TPU v7x, 512 devices: a whole 4x4x16 slice. The times are simulated.
512 devices in a mesh: tm: 64 (over x, z_lo, core), space: 8 (over y, z_hi).
Axes of the slice: x: 4, y: 4, z: 16 (z_hi: 2, z_lo: 8; z = z_hi * 8 + z_lo), core: 2. Of those that a mesh axis runs over, the one named last changes fastest.
Arguments:
- guess: float32 [64, 16, 192, 128], P('tm', 'space'), may hold values from -6 to 6
- source: float32 [64, 16, 192, 128], P('tm', 'space'), may hold values from -4 to 4
- diffusivity: float32 [16, 192, 128], P('space'), may hold values from 0.25 to 4
- initial: float32 [16, 192, 128], P('space'), may hold values from -6 to 6
Outputs:
- states: float32 [64, 16, 192, 128], P('tm', 'space')
All inputs are finite; a program needn't handle non-finite values.
Results may differ from a plain program's by a relative error of at most 0.00002.
Values sent between devices are 32-bit elements; how exact they have to be, the bound alone decides.
No kernel may reach another device: no remote copies, remote signals or barrier semaphores. Data moves between devices by JAX's collectives and lax.ppermute only.
A program may use at most 64 MiB of HBM per device.

v0:
```python
import jax
import jax.numpy as jnp
from jax import lax
from jax.sharding import PartitionSpec as P

SWEEPS = 2


damping = 0.8
step_size = 0.5
coarse_size = 4.0
z_weight = 8.0


def with_halo(cells, sides, width):
    for axis, dim in sides:
        count = lax.axis_size(axis)
        ends = count - 1
        head = lax.slice_in_dim(cells, 0, width, axis=dim)
        tail = lax.slice_in_dim(cells, cells.shape[dim] - width, cells.shape[dim], axis=dim)
        cells = jnp.concatenate(
            [
                lax.ppermute(tail, axis, [(i, (i + 1) % count) for i in range(ends)]),
                cells,
                lax.ppermute(head, axis, [((i + 1) % count, i) for i in range(ends)]),
            ],
            axis=dim,
        )
    return cells


def passed_along(block, axis, distance):
    devices = range(lax.axis_size(axis))
    route = [(i - distance, i) for i in devices if i - distance in devices]
    return lax.ppermute(block, axis, route)


def sweep(field, target, conduct, rate):
    padded = jnp.pad(field, 1)
    cond_pad = jnp.pad(conduct, 1)
    shape_z, shape_y, shape_x = field.shape
    total = jnp.zeros_like(field)
    weighted = jnp.zeros_like(field)
    for axis_pos, weight in ((0, z_weight), (1, 1.0), (2, 1.0)):
        for offset in (0, 2):
            anchor = [1, 1, 1]
            anchor[axis_pos] = offset
            limits = [anchor[0] + shape_z, anchor[1] + shape_y, anchor[2] + shape_x]
            near_field = lax.slice(padded, anchor, limits)
            near_cond = lax.slice(cond_pad, anchor, limits)
            coeff = rate * weight * 0.5 * (conduct + near_cond)
            total = total + coeff
            weighted = weighted + coeff * near_field
    return (1.0 - damping) * field + damping * (target + weighted) / (1.0 + total)


def relax(field, target, conduct, inside, rate):
    for sweep_index in range(SWEEPS):
        field = sweep(field, target, conduct, rate) * inside
    return field


def on_device(guess, source, diffusivity, initial):
    own_guess = guess[0]
    layers = own_guess.shape[0]
    tm_count = lax.axis_size("tm")
    tm_place = lax.axis_index("tm")
    space_count = lax.axis_size("space")
    space_place = lax.axis_index("space")
    position = tm_place % 8
    blocks = tm_count // 8
    extended = with_halo(jnp.stack([diffusivity, source[0]]), (("space", 1),), SWEEPS)
    cond_ext = extended[0]
    force_ext = extended[1]
    depth_rows = jnp.arange(layers + 2 * SWEEPS) + space_place * layers - SWEEPS
    inside_z = ((depth_rows >= 0) & (depth_rows < layers * space_count)).astype(jnp.float32)[
        :, None, None
    ]
    cond_near = lax.slice_in_dim(cond_ext, SWEEPS - 1, SWEEPS + layers + 1, axis=0)
    force_own = lax.slice_in_dim(force_ext, SWEEPS, SWEEPS + layers, axis=0)
    state = own_guess
    fresh = own_guess
    for turn in range(8):
        incoming = passed_along(state, "tm", 1)
        incoming = jnp.where(tm_place == 0, initial, incoming)
        target_pad = jnp.pad(incoming + step_size * force_own, ((1, 1), (0, 0), (0, 0)))
        field = incoming
        for sweep_index in range(SWEEPS):
            field_ext = with_halo(field, (("space", 0),), 1)
            field = sweep(field_ext, target_pad, cond_near, step_size)[1:-1]
        fresh = field
        state = jnp.where(position == 7, own_guess, fresh)
    residual = fresh - own_guess
    payload = jnp.where(position == 7, residual, state)[None]
    regrouped = lax.all_to_all(payload, "tm", split_axis=2, concat_axis=0, tiled=True)
    slab_rows = regrouped.shape[2]
    columns = regrouped.shape[3]
    grouped = regrouped.reshape(blocks, 8, layers, slab_rows, columns)
    residual_slabs = grouped[:, 7]
    cond_pad = jnp.pad(cond_ext, ((0, 0), (SWEEPS, SWEEPS), (0, 0)))
    cond_slab = lax.dynamic_slice_in_dim(cond_pad, tm_place * slab_rows, slab_rows + 2 * SWEEPS, 1)
    across_rows = jnp.arange(slab_rows + 2 * SWEEPS) + tm_place * slab_rows - SWEEPS
    inside_y = ((across_rows >= 0) & (across_rows < slab_rows * tm_count)).astype(jnp.float32)[
        None, :, None
    ]
    inside_both = inside_z * inside_y
    error = residual_slabs[0]
    collected = [error]
    for block in range(1, blocks):
        error_ext = with_halo(error, (("tm", 1), ("space", 0)), SWEEPS)
        relaxed = relax(error_ext, error_ext, cond_slab, inside_both, coarse_size)
        error = relaxed[SWEEPS:-SWEEPS, SWEEPS:-SWEEPS] + residual_slabs[block]
        collected.append(error)
    corrections = jnp.stack(collected)
    outgoing = jnp.concatenate([grouped[:, :7], corrections[:, None]], axis=1)
    outgoing = outgoing.reshape(tm_count, layers, slab_rows, columns)
    returned = lax.all_to_all(outgoing, "tm", split_axis=0, concat_axis=2, tiled=True)[0]
    result = jnp.where(position == 7, own_guess + returned, returned)
    return result[None]


def solution(mesh):
    in_specs = (
        P("tm", "space", None, None),
        P("tm", "space", None, None),
        P("space", None, None),
        P("space", None, None),
    )
    out_specs = P("tm", "space", None, None)
    return jax.shard_map(
        on_device, mesh=mesh, in_specs=in_specs, out_specs=out_specs, check_vma=False
    )
```

profile of v0, /device:TPU:24, one launch (start us, length us, event | category | flops | bytes accessed | tf_op | source)
XLA Modules:
  0.0 905.3 jit_solution(2513424228349008629)
XLA Ops:
  4.5 15.9 %collective-permute-start.4 = (f32[2,2,192,128]{3,1,2,0:T(2,128)S(1)}, f32[2,2,192,128]{3,1,2,0:T(2,128)S(1)}, u32[]{:S(2)}, u32[]{:S(2)}) collective-permute-start(f32[2,2,192,128]{3,1,2,0:T(2,128)S(1)} %pad_maximum_fusion.4), channel_id=1, source_target_pairs={{1,0},{2,1},{3,2},{4,3},{5,4},{6,5},{7,6},{9,8},{10,9},{11,10},{12... | collective-permute-start | bytes 1179656 | tf_op jit(solution)/shard_map/ppermute | solution.py:25
  24.8 13.5 %collective-permute-start.2 = (f32[1,192,128]{2,0,1:T(1,128)S(1)}, f32[1,192,128]{2,0,1:T(1,128)S(1)}, u32[]{:S(2)}, u32[]{:S(2)}) collective-permute-start(f32[1,192,128]{2,0,1:T(1,128)S(1)} %get-tuple-element.102), channel_id=1, source_target_pairs={{1,0},{2,1},{3,2},{4,3},{5,4},{6,5},{7,6},{9,8},{10,9},{11,10},{12... | collective-permute-start | bytes 294920 | tf_op jit(solution)/shard_map/ppermute | solution.py:25
  38.4 32.6 %collective-permute-done.1 = f32[1,192,128]{2,0,1:T(1,128)S(1)} collective-permute-done((f32[1,192,128]{2,0,1:T(1,128)S(1)}, f32[1,192,128]{2,0,1:T(1,128)S(1)}, u32[]{:S(2)}, u32[]{:S(2)}) %collective-permute-start.1) | collective-permute-done | bytes 98336 | tf_op jit(solution)/shard_map/ppermute | solution.py:23
  95.8 19.0 %collective-permute-done.5 = f32[1,192,128]{2,0,1:T(1,128)} collective-permute-done((f32[1,192,128]{2,0,1:T(1,128)}, f32[1,192,128]{2,0,1:T(1,128)}, u32[]{:S(2)}, u32[]{:S(2)}) %collective-permute-start.5) | collective-permute-done | bytes 98336 | tf_op jit(solution)/shard_map/ppermute | solution.py:23
  123.1 13.5 %collective-permute-start.9 = (f32[1,192,128]{2,0,1:T(1,128)S(1)}, f32[1,192,128]{2,0,1:T(1,128)S(1)}, u32[]{:S(2)}, u32[]{:S(2)}) collective-permute-start(f32[1,192,128]{2,0,1:T(1,128)S(1)} %get-tuple-element.100), channel_id=1, source_target_pairs={{1,0},{2,1},{3,2},{4,3},{5,4},{6,5},{7,6},{9,8},{10,9},{11,10},{12... | collective-permute-start | bytes 294920 | tf_op jit(solution)/shard_map/ppermute | solution.py:25
  143.9 15.1 %collective-permute-start.11 = (f32[1,192,128]{2,0,1:T(1,128)S(1)}, f32[1,192,128]{2,0,1:T(1,128)S(1)}, u32[]{:S(2)}, u32[]{:S(2)}) collective-permute-start(f32[1,192,128]{2,0,1:T(1,128)S(1)} %get-tuple-element.81), channel_id=1, source_target_pairs={{1,0},{2,1},{3,2},{4,3},{5,4},{6,5},{7,6},{9,8},{10,9},{11,10},{12... | collective-permute-start | bytes 294920 | tf_op jit(solution)/shard_map/ppermute | solution.py:25
  163.9 33.3 %collective-permute-start.12 = (f32[2,192,128]{2,0,1:T(2,128)S(1)}, f32[2,192,128]{2,0,1:T(2,128)S(1)}, u32[]{:S(2)}, u32[]{:S(2)}) collective-permute-start(f32[2,192,128]{2,0,1:T(2,128)S(1)} %fusion.203), channel_id=1, source_target_pairs={{0,8},{8,16},{16,24},{24,32},{32,40},{40,48},{48,56},{56,64},{64,7... | collective-permute-start | bytes 589832 | tf_op jit(solution)/shard_map/ppermute | solution.py:35
  200.7 13.7 %collective-permute-start.14 = (f32[1,192,128]{2,0,1:T(1,128)S(1)}, f32[1,192,128]{2,0,1:T(1,128)S(1)}, u32[]{:S(2)}, u32[]{:S(2)}) collective-permute-start(f32[1,192,128]{2,0,1:T(1,128)S(1)} %get-tuple-element.98), channel_id=1, source_target_pairs={{1,0},{2,1},{3,2},{4,3},{5,4},{6,5},{7,6},{9,8},{10,9},{11,10},{12... | collective-permute-start | bytes 294920 | tf_op jit(solution)/shard_map/ppermute | solution.py:25
  221.3 14.7 %collective-permute-start.16 = (f32[1,192,128]{2,0,1:T(1,128)S(1)}, f32[1,192,128]{2,0,1:T(1,128)S(1)}, u32[]{:S(2)}, u32[]{:S(2)}) collective-permute-start(f32[1,192,128]{2,0,1:T(1,128)S(1)} %get-tuple-element.76), channel_id=1, source_target_pairs={{1,0},{2,1},{3,2},{4,3},{5,4},{6,5},{7,6},{9,8},{10,9},{11,10},{12... | collective-permute-start | bytes 294920 | tf_op jit(solution)/shard_map/ppermute | solution.py:25
  256.9 13.5 %collective-permute-start.19 = (f32[1,192,128]{2,0,1:T(1,128)S(1)}, f32[1,192,128]{2,0,1:T(1,128)S(1)}, u32[]{:S(2)}, u32[]{:S(2)}) collective-permute-start(f32[1,192,128]{2,0,1:T(1,128)S(1)} %get-tuple-element.96), channel_id=1, source_target_pairs={{1,0},{2,1},{3,2},{4,3},{5,4},{6,5},{7,6},{9,8},{10,9},{11,10},{12... | collective-permute-start | bytes 294920 | tf_op jit(solution)/shard_map/ppermute | solution.py:25
  277.9 14.2 %collective-permute-start.21 = (f32[1,192,128]{2,0,1:T(1,128)S(1)}, f32[1,192,128]{2,0,1:T(1,128)S(1)}, u32[]{:S(2)}, u32[]{:S(2)}) collective-permute-start(f32[1,192,128]{2,0,1:T(1,128)S(1)} %get-tuple-element.71), channel_id=1, source_target_pairs={{1,0},{2,1},{3,2},{4,3},{5,4},{6,5},{7,6},{9,8},{10,9},{11,10},{12... | collective-permute-start | bytes 294920 | tf_op jit(solution)/shard_map/ppermute | solution.py:25
  310.0 19.6 %collective-permute-start.24 = (f32[1,192,128]{2,0,1:T(1,128)S(1)}, f32[1,192,128]{2,0,1:T(1,128)S(1)}, u32[]{:S(2)}, u32[]{:S(2)}) collective-permute-start(f32[1,192,128]{2,0,1:T(1,128)S(1)} %get-tuple-element.94), channel_id=1, source_target_pairs={{1,0},{2,1},{3,2},{4,3},{5,4},{6,5},{7,6},{9,8},{10,9},{11,10},{12... | collective-permute-start | bytes 294920 | tf_op jit(solution)/shard_map/ppermute | solution.py:25
  337.4 14.1 %collective-permute-start.26 = (f32[1,192,128]{2,0,1:T(1,128)S(1)}, f32[1,192,128]{2,0,1:T(1,128)S(1)}, u32[]{:S(2)}, u32[]{:S(2)}) collective-permute-start(f32[1,192,128]{2,0,1:T(1,128)S(1)} %get-tuple-element.66), channel_id=1, source_target_pairs={{1,0},{2,1},{3,2},{4,3},{5,4},{6,5},{7,6},{9,8},{10,9},{11,10},{12... | collective-permute-start | bytes 294920 | tf_op jit(solution)/shard_map/ppermute | solution.py:25
  371.6 15.8 %collective-permute-start.29 = (f32[1,192,128]{2,0,1:T(1,128)S(1)}, f32[1,192,128]{2,0,1:T(1,128)S(1)}, u32[]{:S(2)}, u32[]{:S(2)}) collective-permute-start(f32[1,192,128]{2,0,1:T(1,128)S(1)} %get-tuple-element.92), channel_id=1, source_target_pairs={{1,0},{2,1},{3,2},{4,3},{5,4},{6,5},{7,6},{9,8},{10,9},{11,10},{12... | collective-permute-start | bytes 294920 | tf_op jit(solution)/shard_map/ppermute | solution.py:25
  394.7 14.3 %collective-permute-start.31 = (f32[1,192,128]{2,0,1:T(1,128)S(1)}, f32[1,192,128]{2,0,1:T(1,128)S(1)}, u32[]{:S(2)}, u32[]{:S(2)}) collective-permute-start(f32[1,192,128]{2,0,1:T(1,128)S(1)} %get-tuple-element.61), channel_id=1, source_target_pairs={{1,0},{2,1},{3,2},{4,3},{5,4},{6,5},{7,6},{9,8},{10,9},{11,10},{12... | collective-permute-start | bytes 294920 | tf_op jit(solution)/shard_map/ppermute | solution.py:25
  426.6 13.7 %collective-permute-start.34 = (f32[1,192,128]{2,0,1:T(1,128)S(1)}, f32[1,192,128]{2,0,1:T(1,128)S(1)}, u32[]{:S(2)}, u32[]{:S(2)}) collective-permute-start(f32[1,192,128]{2,0,1:T(1,128)S(1)} %get-tuple-element.90), channel_id=1, source_target_pairs={{1,0},{2,1},{3,2},{4,3},{5,4},{6,5},{7,6},{9,8},{10,9},{11,10},{12... | collective-permute-start | bytes 294920 | tf_op jit(solution)/shard_map/ppermute | solution.py:25
  446.1 15.4 %collective-permute-start.36 = (f32[1,192,128]{2,0,1:T(1,128)S(1)}, f32[1,192,128]{2,0,1:T(1,128)S(1)}, u32[]{:S(2)}, u32[]{:S(2)}) collective-permute-start(f32[1,192,128]{2,0,1:T(1,128)S(1)} %get-tuple-element.56), channel_id=1, source_target_pairs={{1,0},{2,1},{3,2},{4,3},{5,4},{6,5},{7,6},{9,8},{10,9},{11,10},{12... | collective-permute-start | bytes 294920 | tf_op jit(solution)/shard_map/ppermute | solution.py:25
  482.0 18.5 %collective-permute-start.39 = (f32[1,192,128]{2,0,1:T(1,128)S(1)}, f32[1,192,128]{2,0,1:T(1,128)S(1)}, u32[]{:S(2)}, u32[]{:S(2)}) collective-permute-start(f32[1,192,128]{2,0,1:T(1,128)S(1)} %get-tuple-element.88), channel_id=1, source_target_pairs={{1,0},{2,1},{3,2},{4,3},{5,4},{6,5},{7,6},{9,8},{10,9},{11,10},{12... | collective-permute-start | bytes 294920 | tf_op jit(solution)/shard_map/ppermute | solution.py:25
  506.0 14.5 %collective-permute-start.41 = (f32[1,192,128]{2,0,1:T(1,128)S(1)}, f32[1,192,128]{2,0,1:T(1,128)S(1)}, u32[]{:S(2)}, u32[]{:S(2)}) collective-permute-start(f32[1,192,128]{2,0,1:T(1,128)S(1)} %get-tuple-element.51), channel_id=1, source_target_pairs={{1,0},{2,1},{3,2},{4,3},{5,4},{6,5},{7,6},{9,8},{10,9},{11,10},{12... | collective-permute-start | bytes 294920 | tf_op jit(solution)/shard_map/ppermute | solution.py:25
  525.3 47.7 %all-to-all-start = ((f32[1,2,192,128]{3,1,0,2:T(2,128)}), f32[1,2,192,128]{3,1,0,2:T(2,128)S(1)}, u32[]{:S(2)}, u32[]{:S(2)}) async-start(f32[1,2,192,128]{3,1,0,2:T(2,128)} %select_bitcast_fusion), calls=%async_computation | async-start | bytes 393216 | tf_op jit(solution)/shard_map/all_to_all | solution.py:95
  573.5 17.0 %all-to-all-done = f32[1,2,192,128]{3,1,0,2:T(2,128)S(1)} async-done(((f32[1,2,192,128]{3,1,0,2:T(2,128)}), f32[1,2,192,128]{3,1,0,2:T(2,128)S(1)}, u32[]{:S(2)}, u32[]{:S(2)}) %all-to-all-start) | async-done | bytes 196640 | tf_op jit(solution)/shard_map/all_to_all | solution.py:95
  595.0 13.9 %collective-permute-start.45 = (f32[2,7,128]{2,0,1:T(2,128)S(1)}, f32[2,7,128]{2,0,1:T(2,128)S(1)}, u32[]{:S(2)}, u32[]{:S(2)}) collective-permute-start(f32[2,7,128]{2,0,1:T(2,128)S(1)} %pad_maximum_fusion.28), channel_id=1, source_target_pairs={{1,0},{2,1},{3,2},{4,3},{5,4},{6,5},{7,6},{9,8},{10,9},{11,10},{12... | collective-permute-start | bytes 21512 | tf_op jit(solution)/shard_map/ppermute | solution.py:25
  610.8 13.2 %collective-permute-done.44 = f32[2,7,128]{2,0,1:T(2,128)S(1)} collective-permute-done((f32[2,7,128]{2,0,1:T(2,128)S(1)}, f32[2,7,128]{2,0,1:T(2,128)S(1)}, u32[]{:S(2)}, u32[]{:S(2)}) %collective-permute-start.44) | collective-permute-done | bytes 7200 | tf_op jit(solution)/shard_map/ppermute | solution.py:23
  631.2 13.9 %collective-permute-start.49 = (f32[2,7,128]{2,0,1:T(2,128)S(1)}, f32[2,7,128]{2,0,1:T(2,128)S(1)}, u32[]{:S(2)}, u32[]{:S(2)}) collective-permute-start(f32[2,7,128]{2,0,1:T(2,128)S(1)} %pad_maximum_fusion.29), channel_id=1, source_target_pairs={{1,0},{2,1},{3,2},{4,3},{5,4},{6,5},{7,6},{9,8},{10,9},{11,10},{12... | collective-permute-start | bytes 21512 | tf_op jit(solution)/shard_map/ppermute | solution.py:25
  647.0 13.2 %collective-permute-done.48 = f32[2,7,128]{2,0,1:T(2,128)S(1)} collective-permute-done((f32[2,7,128]{2,0,1:T(2,128)S(1)}, f32[2,7,128]{2,0,1:T(2,128)S(1)}, u32[]{:S(2)}, u32[]{:S(2)}) %collective-permute-start.48) | collective-permute-done | bytes 7200 | tf_op jit(solution)/shard_map/ppermute | solution.py:23
  667.4 12.6 %collective-permute-start.53 = (f32[2,7,128]{2,0,1:T(2,128)S(1)}, f32[2,7,128]{2,0,1:T(2,128)S(1)}, u32[]{:S(2)}, u32[]{:S(2)}) collective-permute-start(f32[2,7,128]{2,0,1:T(2,128)S(1)} %pad_maximum_fusion.30), channel_id=1, source_target_pairs={{1,0},{2,1},{3,2},{4,3},{5,4},{6,5},{7,6},{9,8},{10,9},{11,10},{12... | collective-permute-start | bytes 21512 | tf_op jit(solution)/shard_map/ppermute | solution.py:25
  682.0 13.3 %collective-permute-done.52 = f32[2,7,128]{2,0,1:T(2,128)S(1)} collective-permute-done((f32[2,7,128]{2,0,1:T(2,128)S(1)}, f32[2,7,128]{2,0,1:T(2,128)S(1)}, u32[]{:S(2)}, u32[]{:S(2)}) %collective-permute-start.52) | collective-permute-done | bytes 7200 | tf_op jit(solution)/shard_map/ppermute | solution.py:23
  716.9 12.0 %collective-permute-done.56 = f32[2,7,128]{2,0,1:T(2,128)S(1)} collective-permute-done((f32[2,7,128]{2,0,1:T(2,128)S(1)}, f32[2,7,128]{2,0,1:T(2,128)S(1)}, u32[]{:S(2)}, u32[]{:S(2)}) %collective-permute-start.56) | collective-permute-done | bytes 7200 | tf_op jit(solution)/shard_map/ppermute | solution.py:23
  736.0 12.7 %collective-permute-start.61 = (f32[2,7,128]{2,0,1:T(2,128)S(1)}, f32[2,7,128]{2,0,1:T(2,128)S(1)}, u32[]{:S(2)}, u32[]{:S(2)}) collective-permute-start(f32[2,7,128]{2,0,1:T(2,128)S(1)} %pad_maximum_fusion.32), channel_id=1, source_target_pairs={{1,0},{2,1},{3,2},{4,3},{5,4},{6,5},{7,6},{9,8},{10,9},{11,10},{12... | collective-permute-start | bytes 21512 | tf_op jit(solution)/shard_map/ppermute | solution.py:25
  750.6 13.2 %collective-permute-done.60 = f32[2,7,128]{2,0,1:T(2,128)S(1)} collective-permute-done((f32[2,7,128]{2,0,1:T(2,128)S(1)}, f32[2,7,128]{2,0,1:T(2,128)S(1)}, u32[]{:S(2)}, u32[]{:S(2)}) %collective-permute-start.60) | collective-permute-done | bytes 7200 | tf_op jit(solution)/shard_map/ppermute | solution.py:23
  805.9 12.5 %collective-permute-start.68 = (f32[2,7,128]{2,0,1:T(2,128)S(1)}, f32[2,7,128]{2,0,1:T(2,128)S(1)}, u32[]{:S(2)}, u32[]{:S(2)}) collective-permute-start(f32[2,7,128]{2,0,1:T(2,128)S(1)} %pad_maximum_fusion.34), channel_id=1, source_target_pairs={{0,1},{1,2},{2,3},{3,4},{4,5},{5,6},{6,7},{8,9},{9,10},{10,11},{11... | collective-permute-start | bytes 21512 | tf_op jit(solution)/shard_map/ppermute | solution.py:23
  821.4 82.5 %all_to_all.30 = f32[64,2,3,128]{3,1,2,0:T(2,128)S(1)} all-to-all(f32[64,2,3,128]{3,1,2,0:T(2,128)S(1)} %bitcast.124), channel_id=1, replica_groups=mesh['tm'=64,'space'=8] {'tm'}, dimensions={0} | all-to-all | bytes 393216 | tf_op jit(solution)/shard_map/all_to_all | solution.py:117
  (274 shorter events, 300.8 us)
Async XLA Ops:
  1.1 21.2 %collective-permute-start = (f32[2,192,128]{2,0,1:T(2,128)S(1)}, f32[2,192,128]{2,0,1:T(2,128)S(1)}, u32[]{:S(2)}, u32[]{:S(2)}) collective-permute-start(f32[2,192,128]{2,0,1:T(2,128)S(1)} %bitcast.126), channel_id=1, source_target_pairs={{0,8},{8,16},{16,24},{24,32},{32,40},{40,48},{48,56},{56,64},{64,7... | collective-permute-start | bytes 589832 | tf_op jit(solution)/shard_map/ppermute | solution.py:35
  4.5 68.8 %collective-permute-start.4 = (f32[2,2,192,128]{3,1,2,0:T(2,128)S(1)}, f32[2,2,192,128]{3,1,2,0:T(2,128)S(1)}, u32[]{:S(2)}, u32[]{:S(2)}) collective-permute-start(f32[2,2,192,128]{3,1,2,0:T(2,128)S(1)} %pad_maximum_fusion.4), channel_id=1, source_target_pairs={{1,0},{2,1},{3,2},{4,3},{5,4},{6,5},{7,6},{9,8},{10,9},{11,10},{12... | collective-permute-start | bytes 1179656 | tf_op jit(solution)/shard_map/ppermute | solution.py:25
  20.4 53.0 %collective-permute-start.3 = (f32[2,2,192,128]{3,1,2,0:T(2,128)S(1)}, f32[2,2,192,128]{3,1,2,0:T(2,128)S(1)}, u32[]{:S(2)}, u32[]{:S(2)}) collective-permute-start(f32[2,2,192,128]{3,1,2,0:T(2,128)S(1)} %pad_maximum_fusion.4), channel_id=1, source_target_pairs={{0,1},{1,2},{2,3},{3,4},{4,5},{5,6},{6,7},{8,9},{9,10},{10,11},{11... | collective-permute-start | bytes 1179656 | tf_op jit(solution)/shard_map/ppermute | solution.py:23
  22.9 48.0 %collective-permute-start.1 = (f32[1,192,128]{2,0,1:T(1,128)S(1)}, f32[1,192,128]{2,0,1:T(1,128)S(1)}, u32[]{:S(2)}, u32[]{:S(2)}) collective-permute-start(f32[1,192,128]{2,0,1:T(1,128)S(1)} %get-tuple-element.101), channel_id=1, source_target_pairs={{0,1},{1,2},{2,3},{3,4},{4,5},{5,6},{6,7},{8,9},{9,10},{10,11},{11... | collective-permute-start | bytes 294920 | tf_op jit(solution)/shard_map/ppermute | solution.py:23
  24.8 48.2 %collective-permute-start.2 = (f32[1,192,128]{2,0,1:T(1,128)S(1)}, f32[1,192,128]{2,0,1:T(1,128)S(1)}, u32[]{:S(2)}, u32[]{:S(2)}) collective-permute-start(f32[1,192,128]{2,0,1:T(1,128)S(1)} %get-tuple-element.102), channel_id=1, source_target_pairs={{1,0},{2,1},{3,2},{4,3},{5,4},{6,5},{7,6},{9,8},{10,9},{11,10},{12... | collective-permute-start | bytes 294920 | tf_op jit(solution)/shard_map/ppermute | solution.py:25
  78.4 36.4 %collective-permute-start.5 = (f32[1,192,128]{2,0,1:T(1,128)}, f32[1,192,128]{2,0,1:T(1,128)}, u32[]{:S(2)}, u32[]{:S(2)}) collective-permute-start(f32[1,192,128]{2,0,1:T(1,128)} %get-tuple-element.85), channel_id=1, source_target_pairs={{0,1},{1,2},{2,3},{3,4},{4,5},{5,6},{6,7},{8,9},{9,10},{10,11},{11... | collective-permute-start | bytes 294920 | tf_op jit(solution)/shard_map/ppermute | solution.py:23
  89.8 25.0 %collective-permute-start.6 = (f32[1,192,128]{2,0,1:T(1,128)}, f32[1,192,128]{2,0,1:T(1,128)}, u32[]{:S(2)}, u32[]{:S(2)}) collective-permute-start(f32[1,192,128]{2,0,1:T(1,128)} %get-tuple-element.86), channel_id=1, source_target_pairs={{1,0},{2,1},{3,2},{4,3},{5,4},{6,5},{7,6},{9,8},{10,9},{11,10},{12... | collective-permute-start | bytes 294920 | tf_op jit(solution)/shard_map/ppermute | solution.py:25
  123.1 17.5 %collective-permute-start.9 = (f32[1,192,128]{2,0,1:T(1,128)S(1)}, f32[1,192,128]{2,0,1:T(1,128)S(1)}, u32[]{:S(2)}, u32[]{:S(2)}) collective-permute-start(f32[1,192,128]{2,0,1:T(1,128)S(1)} %get-tuple-element.100), channel_id=1, source_target_pairs={{1,0},{2,1},{3,2},{4,3},{5,4},{6,5},{7,6},{9,8},{10,9},{11,10},{12... | collective-permute-start | bytes 294920 | tf_op jit(solution)/shard_map/ppermute | solution.py:25
  142.0 18.3 %collective-permute-start.10 = (f32[1,192,128]{2,0,1:T(1,128)S(1)}, f32[1,192,128]{2,0,1:T(1,128)S(1)}, u32[]{:S(2)}, u32[]{:S(2)}) collective-permute-start(f32[1,192,128]{2,0,1:T(1,128)S(1)} %get-tuple-element.80), channel_id=1, source_target_pairs={{0,1},{1,2},{2,3},{3,4},{4,5},{5,6},{6,7},{8,9},{9,10},{10,11},{11... | collective-permute-start | bytes 294920 | tf_op jit(solution)/shard_map/ppermute | solution.py:23
  143.9 17.3 %collective-permute-start.11 = (f32[1,192,128]{2,0,1:T(1,128)S(1)}, f32[1,192,128]{2,0,1:T(1,128)S(1)}, u32[]{:S(2)}, u32[]{:S(2)}) collective-permute-start(f32[1,192,128]{2,0,1:T(1,128)S(1)} %get-tuple-element.81), channel_id=1, source_target_pairs={{1,0},{2,1},{3,2},{4,3},{5,4},{6,5},{7,6},{9,8},{10,9},{11,10},{12... | collective-permute-start | bytes 294920 | tf_op jit(solution)/shard_map/ppermute | solution.py:25
  163.9 34.4 %collective-permute-start.12 = (f32[2,192,128]{2,0,1:T(2,128)S(1)}, f32[2,192,128]{2,0,1:T(2,128)S(1)}, u32[]{:S(2)}, u32[]{:S(2)}) collective-permute-start(f32[2,192,128]{2,0,1:T(2,128)S(1)} %fusion.203), channel_id=1, source_target_pairs={{0,8},{8,16},{16,24},{24,32},{32,40},{40,48},{48,56},{56,64},{64,7... | collective-permute-start | bytes 589832 | tf_op jit(solution)/shard_map/ppermute | solution.py:35
  200.7 17.2 %collective-permute-start.14 = (f32[1,192,128]{2,0,1:T(1,128)S(1)}, f32[1,192,128]{2,0,1:T(1,128)S(1)}, u32[]{:S(2)}, u32[]{:S(2)}) collective-permute-start(f32[1,192,128]{2,0,1:T(1,128)S(1)} %get-tuple-element.98), channel_id=1, source_target_pairs={{1,0},{2,1},{3,2},{4,3},{5,4},{6,5},{7,6},{9,8},{10,9},{11,10},{12... | collective-permute-start | bytes 294920 | tf_op jit(solution)/shard_map/ppermute | solution.py:25
  219.3 20.3 %collective-permute-start.15 = (f32[1,192,128]{2,0,1:T(1,128)S(1)}, f32[1,192,128]{2,0,1:T(1,128)S(1)}, u32[]{:S(2)}, u32[]{:S(2)}) collective-permute-start(f32[1,192,128]{2,0,1:T(1,128)S(1)} %get-tuple-element.75), channel_id=1, source_target_pairs={{0,1},{1,2},{2,3},{3,4},{4,5},{5,6},{6,7},{8,9},{9,10},{10,11},{11... | collective-permute-start | bytes 294920 | tf_op jit(solution)/shard_map/ppermute | solution.py:23
  221.3 19.3 %collective-permute-start.16 = (f32[1,192,128]{2,0,1:T(1,128)S(1)}, f32[1,192,128]{2,0,1:T(1,128)S(1)}, u32[]{:S(2)}, u32[]{:S(2)}) collective-permute-start(f32[1,192,128]{2,0,1:T(1,128)S(1)} %get-tuple-element.76), channel_id=1, source_target_pairs={{1,0},{2,1},{3,2},{4,3},{5,4},{6,5},{7,6},{9,8},{10,9},{11,10},{12... | collective-permute-start | bytes 294920 | tf_op jit(solution)/shard_map/ppermute | solution.py:25
  255.0 17.9 %collective-permute-start.18 = (f32[1,192,128]{2,0,1:T(1,128)S(1)}, f32[1,192,128]{2,0,1:T(1,128)S(1)}, u32[]{:S(2)}, u32[]{:S(2)}) collective-permute-start(f32[1,192,128]{2,0,1:T(1,128)S(1)} %get-tuple-element.95), channel_id=1, source_target_pairs={{0,1},{1,2},{2,3},{3,4},{4,5},{5,6},{6,7},{8,9},{9,10},{10,11},{11... | collective-permute-start | bytes 294920 | tf_op jit(solution)/shard_map/ppermute | solution.py:23
  256.9 17.7 %collective-permute-start.19 = (f32[1,192,128]{2,0,1:T(1,128)S(1)}, f32[1,192,128]{2,0,1:T(1,128)S(1)}, u32[]{:S(2)}, u32[]{:S(2)}) collective-permute-start(f32[1,192,128]{2,0,1:T(1,128)S(1)} %get-tuple-element.96), channel_id=1, source_target_pairs={{1,0},{2,1},{3,2},{4,3},{5,4},{6,5},{7,6},{9,8},{10,9},{11,10},{12... | collective-permute-start | bytes 294920 | tf_op jit(solution)/shard_map/ppermute | solution.py:25
  275.9 17.0 %collective-permute-start.20 = (f32[1,192,128]{2,0,1:T(1,128)S(1)}, f32[1,192,128]{2,0,1:T(1,128)S(1)}, u32[]{:S(2)}, u32[]{:S(2)}) collective-permute-start(f32[1,192,128]{2,0,1:T(1,128)S(1)} %get-tuple-element.70), channel_id=1, source_target_pairs={{0,1},{1,2},{2,3},{3,4},{4,5},{5,6},{6,7},{8,9},{9,10},{10,11},{11... | collective-permute-start | bytes 294920 | tf_op jit(solution)/shard_map/ppermute | solution.py:23
  277.9 19.0 %collective-permute-start.21 = (f32[1,192,128]{2,0,1:T(1,128)S(1)}, f32[1,192,128]{2,0,1:T(1,128)S(1)}, u32[]{:S(2)}, u32[]{:S(2)}) collective-permute-start(f32[1,192,128]{2,0,1:T(1,128)S(1)} %get-tuple-element.71), channel_id=1, source_target_pairs={{1,0},{2,1},{3,2},{4,3},{5,4},{6,5},{7,6},{9,8},{10,9},{11,10},{12... | collective-permute-start | bytes 294920 | tf_op jit(solution)/shard_map/ppermute | solution.py:25
  308.1 26.1 %collective-permute-start.23 = (f32[1,192,128]{2,0,1:T(1,128)S(1)}, f32[1,192,128]{2,0,1:T(1,128)S(1)}, u32[]{:S(2)}, u32[]{:S(2)}) collective-permute-start(f32[1,192,128]{2,0,1:T(1,128)S(1)} %get-tuple-element.93), channel_id=1, source_target_pairs={{0,1},{1,2},{2,3},{3,4},{4,5},{5,6},{6,7},{8,9},{9,10},{10,11},{11... | collective-permute-start | bytes 294920 | tf_op jit(solution)/shard_map/ppermute | solution.py:23
  310.0 24.1 %collective-permute-start.24 = (f32[1,192,128]{2,0,1:T(1,128)S(1)}, f32[1,192,128]{2,0,1:T(1,128)S(1)}, u32[]{:S(2)}, u32[]{:S(2)}) collective-permute-start(f32[1,192,128]{2,0,1:T(1,128)S(1)} %get-tuple-element.94), channel_id=1, source_target_pairs={{1,0},{2,1},{3,2},{4,3},{5,4},{6,5},{7,6},{9,8},{10,9},{11,10},{12... | collective-permute-start | bytes 294920 | tf_op jit(solution)/shard_map/ppermute | solution.py:25
  335.5 20.8 %collective-permute-start.25 = (f32[1,192,128]{2,0,1:T(1,128)S(1)}, f32[1,192,128]{2,0,1:T(1,128)S(1)}, u32[]{:S(2)}, u32[]{:S(2)}) collective-permute-start(f32[1,192,128]{2,0,1:T(1,128)S(1)} %get-tuple-element.65), channel_id=1, source_target_pairs={{0,1},{1,2},{2,3},{3,4},{4,5},{5,6},{6,7},{8,9},{9,10},{10,11},{11... | collective-permute-start | bytes 294920 | tf_op jit(solution)/shard_map/ppermute | solution.py:23
  337.4 18.9 %collective-permute-start.26 = (f32[1,192,128]{2,0,1:T(1,128)S(1)}, f32[1,192,128]{2,0,1:T(1,128)S(1)}, u32[]{:S(2)}, u32[]{:S(2)}) collective-permute-start(f32[1,192,128]{2,0,1:T(1,128)S(1)} %get-tuple-element.66), channel_id=1, source_target_pairs={{1,0},{2,1},{3,2},{4,3},{5,4},{6,5},{7,6},{9,8},{10,9},{11,10},{12... | collective-permute-start | bytes 294920 | tf_op jit(solution)/shard_map/ppermute | solution.py:25
  369.7 20.7 %collective-permute-start.28 = (f32[1,192,128]{2,0,1:T(1,128)S(1)}, f32[1,192,128]{2,0,1:T(1,128)S(1)}, u32[]{:S(2)}, u32[]{:S(2)}) collective-permute-start(f32[1,192,128]{2,0,1:T(1,128)S(1)} %get-tuple-element.91), channel_id=1, source_target_pairs={{0,1},{1,2},{2,3},{3,4},{4,5},{5,6},{6,7},{8,9},{9,10},{10,11},{11... | collective-permute-start | bytes 294920 | tf_op jit(solution)/shard_map/ppermute | solution.py:23
  371.6 19.8 %collective-permute-start.29 = (f32[1,192,128]{2,0,1:T(1,128)S(1)}, f32[1,192,128]{2,0,1:T(1,128)S(1)}, u32[]{:S(2)}, u32[]{:S(2)}) collective-permute-start(f32[1,192,128]{2,0,1:T(1,128)S(1)} %get-tuple-element.92), channel_id=1, source_target_pairs={{1,0},{2,1},{3,2},{4,3},{5,4},{6,5},{7,6},{9,8},{10,9},{11,10},{12... | collective-permute-start | bytes 294920 | tf_op jit(solution)/shard_map/ppermute | solution.py:25
  392.8 22.0 %collective-permute-start.30 = (f32[1,192,128]{2,0,1:T(1,128)S(1)}, f32[1,192,128]{2,0,1:T(1,128)S(1)}, u32[]{:S(2)}, u32[]{:S(2)}) collective-permute-start(f32[1,192,128]{2,0,1:T(1,128)S(1)} %get-tuple-element.60), channel_id=1, source_target_pairs={{0,1},{1,2},{2,3},{3,4},{4,5},{5,6},{6,7},{8,9},{9,10},{10,11},{11... | collective-permute-start | bytes 294920 | tf_op jit(solution)/shard_map/ppermute | solution.py:23
  394.7 20.1 %collective-permute-start.31 = (f32[1,192,128]{2,0,1:T(1,128)S(1)}, f32[1,192,128]{2,0,1:T(1,128)S(1)}, u32[]{:S(2)}, u32[]{:S(2)}) collective-permute-start(f32[1,192,128]{2,0,1:T(1,128)S(1)} %get-tuple-element.61), channel_id=1, source_target_pairs={{1,0},{2,1},{3,2},{4,3},{5,4},{6,5},{7,6},{9,8},{10,9},{11,10},{12... | collective-permute-start | bytes 294920 | tf_op jit(solution)/shard_map/ppermute | solution.py:25
  444.2 20.3 %collective-permute-start.35 = (f32[1,192,128]{2,0,1:T(1,128)S(1)}, f32[1,192,128]{2,0,1:T(1,128)S(1)}, u32[]{:S(2)}, u32[]{:S(2)}) collective-permute-start(f32[1,192,128]{2,0,1:T(1,128)S(1)} %get-tuple-element.55), channel_id=1, source_target_pairs={{0,1},{1,2},{2,3},{3,4},{4,5},{5,6},{6,7},{8,9},{9,10},{10,11},{11... | collective-permute-start | bytes 294920 | tf_op jit(solution)/shard_map/ppermute | solution.py:23
  446.1 18.5 %collective-permute-start.36 = (f32[1,192,128]{2,0,1:T(1,128)S(1)}, f32[1,192,128]{2,0,1:T(1,128)S(1)}, u32[]{:S(2)}, u32[]{:S(2)}) collective-permute-start(f32[1,192,128]{2,0,1:T(1,128)S(1)} %get-tuple-element.56), channel_id=1, source_target_pairs={{1,0},{2,1},{3,2},{4,3},{5,4},{6,5},{7,6},{9,8},{10,9},{11,10},{12... | collective-permute-start | bytes 294920 | tf_op jit(solution)/shard_map/ppermute | solution.py:25
  480.0 21.1 %collective-permute-start.38 = (f32[1,192,128]{2,0,1:T(1,128)S(1)}, f32[1,192,128]{2,0,1:T(1,128)S(1)}, u32[]{:S(2)}, u32[]{:S(2)}) collective-permute-start(f32[1,192,128]{2,0,1:T(1,128)S(1)} %get-tuple-element.87), channel_id=1, source_target_pairs={{0,1},{1,2},{2,3},{3,4},{4,5},{5,6},{6,7},{8,9},{9,10},{10,11},{11... | collective-permute-start | bytes 294920 | tf_op jit(solution)/shard_map/ppermute | solution.py:23
  482.0 20.7 %collective-permute-start.39 = (f32[1,192,128]{2,0,1:T(1,128)S(1)}, f32[1,192,128]{2,0,1:T(1,128)S(1)}, u32[]{:S(2)}, u32[]{:S(2)}) collective-permute-start(f32[1,192,128]{2,0,1:T(1,128)S(1)} %get-tuple-element.88), channel_id=1, source_target_pairs={{1,0},{2,1},{3,2},{4,3},{5,4},{6,5},{7,6},{9,8},{10,9},{11,10},{12... | collective-permute-start | bytes 294920 | tf_op jit(solution)/shard_map/ppermute | solution.py:25
  504.1 17.0 %collective-permute-start.40 = (f32[1,192,128]{2,0,1:T(1,128)S(1)}, f32[1,192,128]{2,0,1:T(1,128)S(1)}, u32[]{:S(2)}, u32[]{:S(2)}) collective-permute-start(f32[1,192,128]{2,0,1:T(1,128)S(1)} %get-tuple-element.50), channel_id=1, source_target_pairs={{0,1},{1,2},{2,3},{3,4},{4,5},{5,6},{6,7},{8,9},{9,10},{10,11},{11... | collective-permute-start | bytes 294920 | tf_op jit(solution)/shard_map/ppermute | solution.py:23
  525.3 65.1 %all-to-all-start = ((f32[1,2,192,128]{3,1,0,2:T(2,128)}), f32[1,2,192,128]{3,1,0,2:T(2,128)S(1)}, u32[]{:S(2)}, u32[]{:S(2)}) async-start(f32[1,2,192,128]{3,1,0,2:T(2,128)} %select_bitcast_fusion), calls=%async_computation | async-start | bytes 393216 | tf_op jit(solution)/shard_map/all_to_all | solution.py:95
  (54 other events, 760.8 us)
where the time goes:
time: 916 us; the launch traced here: 905 us
  starting transfers between devices  547 us (60%)
  waiting for transfers between devices  225 us (25%)
  blocking collectives  82.5 us (9%)
  other arithmetic  37.3 us (4%)
  local copies, waits for them, and re-layouts  11.1 us (1%)
    ppermute x31, starting transfers between devices, with_halo(): lax.ppermute(head, axis, [((i + 1) % count, i) for i in range(ends)])  331 us
    ppermute x31, waiting for transfers between devices, with_halo(): lax.ppermute(tail, axis, [(i, (i + 1) % count) for i in range(ends)])  162 us
    ppermute x31, starting transfers between devices, with_halo(): lax.ppermute(tail, axis, [(i, (i + 1) % count) for i in range(ends)])  88.5 us
    all_to_all x1, blocking collectives, on_device(): lax.all_to_all(outgoing, 'tm', split_axis=0, concat_axis=2, tiled=True)[0]  82.5 us
    ppermute x8, starting transfers between devices, passed_along(): return lax.ppermute(block, axis, route)  80.1 us
    all_to_all x1, starting transfers between devices, on_device(): lax.all_to_all(payload, 'tm', split_axis=2, concat_axis=0, tiled=True)  47.7 us
    ppermute x31, waiting for transfers between devices, with_halo(): lax.ppermute(head, axis, [((i + 1) % count, i) for i in range(ends)])  39.4 us
  transfers between devices with their start and end apart: 71, of which 50 were waited for; matrix products, arithmetic and copies ran while one was open for 1% of the time, Pallas kernels for 0%

commit v1 on v0

v1 whole, which is shorter than its diff:
```python
import functools

import jax
import jax.numpy as jnp
from jax import lax
from jax.experimental import pallas as pl
from jax.experimental.pallas import tpu as pltpu
from jax.sharding import Mesh, PartitionSpec as P

SWEEPS = 2
F32 = jnp.float32

damping = 0.8
step_size = 0.5
coarse_size = 4.0
z_weight = 8.0

AXES = ("x", "zh", "zl", "core", "y", "zhi")
SIZES = (4, 2, 4, 2, 4, 2)
BLOCK = ("zl", "core", "y", "zhi")
BLOCKS = ("x", "zh")
NB = 8
NZ = 16
ROWS = 8
TILES = 24
CHIPS = 16
SIDE = 8
WIN = 3 * ROWS
LANES = 128


def chip_order(zl, y):
    return zl * 4 + (y if zl % 2 == 0 else 3 - y)


def block_index(zl, core, y, zhi):
    return ((zl * 2 + core) * 4 + y) * 2 + zhi


def neighbours(step):
    place = {chip_order(zl, y): zl * 4 + y for zl in range(4) for y in range(4)}
    return [(place[m], place[m + step]) for m in range(CHIPS) if 0 <= m + step < CHIPS]


def call(body, outs, *args, scratch=(), smem=0, flops=0):
    specs = [pl.BlockSpec(memory_space=pltpu.SMEM)] * smem
    specs += [pl.BlockSpec(memory_space=pltpu.VMEM)] * (len(args) - smem)
    out_specs = [pl.BlockSpec(memory_space=pltpu.VMEM)] * len(outs)
    size = sum(4 * a.size for a in args) + sum(4 * o.size for o in outs)
    return pl.pallas_call(
        body,
        out_shape=list(outs),
        in_specs=specs,
        out_specs=out_specs,
        scratch_shapes=list(scratch),
        compiler_params=pltpu.CompilerParams(vmem_limit_bytes=32 * 1024 * 1024),
        cost_estimate=pl.CostEstimate(flops=flops, bytes_accessed=size, transcendentals=0),
    )(*args)


def sds(*shape):
    return jax.ShapeDtypeStruct(shape, F32)


def scatter_body(j_ref, src_ref, guess_ref, cond_ref, init_ref, out_ref):
    place = j_ref[0]
    zero = jnp.zeros((ROWS, LANES), F32)
    for zl in range(4):
        for y in range(4):
            for zhi in range(2):
                tile = SIDE * zhi + chip_order(zl, y)
                rows = slice(tile * ROWS, (tile + 1) * ROWS)
                for core in range(2):
                    out_ref[block_index(zl, core, y, zhi), 0] = src_ref[core, rows]

    def fill(pick):
        for zl in range(4):
            for y in range(4):
                for zhi in range(2):
                    tile = SIDE * zhi + chip_order(zl, y)
                    for core in range(2):
                        out_ref[block_index(zl, core, y, zhi), 1] = pick(core, tile)

    def tile_of(ref, shift):
        def pick(core, tile):
            at = tile + shift
            if at < 0 or at >= TILES:
                return zero
            return ref[core, at * ROWS : (at + 1) * ROWS]

        return pick

    for where, ref, shift in ((0, cond_ref, 0), (1, cond_ref, 1), (2, cond_ref, -1), (3, init_ref, 0)):
        pl.when(place == where)(functools.partial(fill, tile_of(ref, shift)))
    pl.when(place > 3)(functools.partial(fill, tile_of(guess_ref, 0)))


def pack_body(first, all_ref, g_ref, up_ref, down_ref):
    row = lax.broadcasted_iota(jnp.int32, (ROWS, LANES), 0)
    for z in range(NZ):
        s, p = z // 2, z % 2
        g_ref[z] = all_ref[p, 7, s, 1]
        for phase in range(2):
            f = [all_ref[p, 4 * phase + n, s, 0] for n in range(4)]
            down_ref[2 * phase, z] = jnp.where(row < 7, f[0], pltpu.roll(f[3], 7, 0))
            down_ref[2 * phase + 1, z] = jnp.where(row < 5, f[1], pltpu.roll(f[2], 5, 0))
            up_ref[2 * phase, z] = jnp.where(row >= 1, f[0], pltpu.roll(f[3], 1, 0))
            up_ref[2 * phase + 1, z] = jnp.where(row >= 3, f[1], pltpu.roll(f[2], 3, 0))


def coefficients(rate, all_ref, k_s, co_s):
    zero = jnp.zeros((WIN, LANES), F32)
    for z in range(NZ):
        s, p = z // 2, z % 2
        k_s[z + 1, 0:8] = all_ref[p, 2, s, 1]
        k_s[z + 1, 8:16] = all_ref[p, 0, s, 1]
        k_s[z + 1, 16:24] = all_ref[p, 1, s, 1]
    k_s[0] = zero
    k_s[NZ + 1] = zero
    lane = lax.broadcasted_iota(jnp.int32, (WIN, LANES), 1)
    first = lane == 0
    last = lane == LANES - 1

    def layer(z, carry):
        k = k_s[z + 1]
        side = 0.5 * rate
        tall = 0.5 * rate * z_weight
        c = [
            tall * (k + k_s[z]),
            tall * (k + k_s[z + 2]),
            side * (k + pltpu.roll(k, 1, 0)),
            side * (k + pltpu.roll(k, WIN - 1, 0)),
            side * (k + jnp.where(first, 0.0, pltpu.roll(k, 1, 1))),
            side * (k + jnp.where(last, 0.0, pltpu.roll(k, LANES - 1, 1))),
        ]
        total = ((c[0] + c[1]) + (c[2] + c[3])) + (c[4] + c[5])
        d = jnp.where(k > 0.0, damping / (1.0 + total), 0.0)
        co_s[0, z] = c[0] * d
        co_s[1, z] = c[1] * d
        co_s[2, z] = c[2] * d
        co_s[3, z] = c[3] * d
        co_s[4, z] = jnp.where(first, 0.0, c[4] * d)
        co_s[5, z] = jnp.where(last, 0.0, c[5] * d)
        co_s[6, z] = d
        return carry

    lax.fori_loop(0, NZ, layer, 0)


def one_sweep(src, dst, co_s, db_s):
    for z in range(NZ):
        w = src[z + 1]
        acc = (db_s[z] + (1.0 - damping) * w) + (co_s[0, z] * src[z] + co_s[1, z] * src[z + 2])
        acc = acc + (co_s[2, z] * pltpu.roll(w, 1, 0) + co_s[3, z] * pltpu.roll(w, WIN - 1, 0))
        acc = acc + (co_s[4, z] * pltpu.roll(w, 1, 1) + co_s[5, z] * pltpu.roll(w, LANES - 1, 1))
        dst[z + 1] = acc


def load_window(a_s, own_ref, below_ref, above_ref, b_s):
    zero = jnp.zeros((WIN, LANES), F32)
    for ref in (a_s, b_s):
        ref[0] = zero
        ref[NZ + 1] = zero
    for z in range(NZ):
        a_s[z + 1, 0:8] = below_ref[z]
        a_s[z + 1, 8:16] = own_ref[z]
        a_s[z + 1, 16:24] = above_ref[z]


def fine_body(phase, all_ref, fb_ref, fa_ref, own_ref, below_ref, above_ref, *rest):
    if phase == 0:
        out_ref, end_ref, k_s, co_s, a_s, b_s, db_s = rest
    else:
        out_ref, end_ref, k_s, co_s, a_s, b_s, db_s = rest
    coefficients(step_size, all_ref, k_s, co_s)
    load_window(a_s, own_ref, below_ref, above_ref, b_s)
    for n in range(4):
        tile, turn = ((0, 0), (1, 0), (1, 5), (0, 7))[n]
        for z in range(NZ):
            s, p = z // 2, z % 2
            below = fb_ref[2 * phase + tile, z]
            above = fa_ref[2 * phase + tile, z]
            if turn:
                below = pltpu.roll(below, turn, 0)
                above = pltpu.roll(above, ROWS - turn, 0)
            forcing = jnp.concatenate([below, all_ref[p, 4 * phase + n, s, 0], above], axis=0)
            db_s[z] = co_s[6, z] * (a_s[z + 1] + step_size * forcing)
        one_sweep(a_s, b_s, co_s, db_s)
        one_sweep(b_s, a_s, co_s, db_s)
        for z in range(NZ):
            s, p = z // 2, z % 2
            mine = a_s[z + 1, 8:16]
            if n < 3:
                out_ref[n, z] = mine
            elif phase == 0:
                out_ref[n, z] = mine
                end_ref[z] = mine
            else:
                end_ref[z] = mine - all_ref[p, 7, s, 1]


def coarse_body(steps, all_ref, own_ref, below_ref, above_ref, out_ref, end_ref, k_s, co_s, a_s, b_s, db_s):
    coefficients(coarse_size, all_ref, k_s, co_s)
    load_window(a_s, own_ref, below_ref, above_ref, b_s)
    for n in range(steps):
        for z in range(NZ):
            db_s[z] = co_s[6, z] * a_s[z + 1]
        one_sweep(a_s, b_s, co_s, db_s)
        one_sweep(b_s, a_s, co_s, db_s)
        for z in range(NZ):
            mine = a_s[z + 1, 8:16]
            out_ref[n, z] = mine
            if n == steps - 1:
                end_ref[z] = mine


SWEEP_SCRATCH = (
    pltpu.VMEM((NZ + 2, WIN, LANES), F32),
    pltpu.VMEM((7, NZ, WIN, LANES), F32),
    pltpu.VMEM((NZ + 2, WIN, LANES), F32),
    pltpu.VMEM((NZ + 2, WIN, LANES), F32),
    pltpu.VMEM((NZ, WIN, LANES), F32),
)


def powers_body(place_ref, r_ref, z1_ref, z2_ref, out_ref):
    c, p = place_ref[0], place_ref[1]
    for b in range(NB):

        @pl.when(b == c)
        def _():
            for s in range(8):
                out_ref[b, s] = r_ref[2 * s + p]

        @pl.when((b > c) & (b <= c + 4))
        def _():
            n = jnp.clip(b - c - 1, 0, 3)
            for s in range(8):
                out_ref[b, s] = z1_ref[n, 2 * s + p]

        @pl.when(b > c + 4)
        def _():
            n = jnp.clip(b - c - 5, 0, 2)
            for s in range(8):
                out_ref[b, s] = z2_ref[n, 2 * s + p]

        @pl.when(b < c)
        def _():
            out_ref[b] = jnp.zeros((8, ROWS, LANES), F32)


def collect_body(place_ref, got_ref, v1_ref, v2_ref, out_ref):
    p = place_ref[1]
    for s in range(8):
        total = got_ref[0, s]
        for b in range(1, NB):
            total = total + got_ref[b, s]
        out_ref[7 * 8 + s] = total
        for n in range(4):
            out_ref[n * 8 + s] = v1_ref[n, 2 * s + p]
        for n in range(3):
            out_ref[(4 + n) * 8 + s] = v2_ref[n, 2 * s + p]


def home_body(j_ref, got_ref, guess_ref, out_ref):
    last = j_ref[0] == 7

    def write(add):
        for tile in range(TILES):
            zhi = 0 if tile < TILES // 2 else 1
            m = tile - SIDE * zhi
            zl, y = m // 4, m % 4
            if zl % 2 == 1:
                y = 3 - y
            rows = slice(tile * ROWS, (tile + 1) * ROWS)
            for core in range(2):
                value = got_ref[block_index(zl, core, y, zhi)]
                if add:
                    value = guess_ref[core, rows] + value
                out_ref[core, rows] = value

    pl.when(last)(functools.partial(write, True))
    pl.when(jnp.logical_not(last))(functools.partial(write, False))


def on_device(guess, source, diffusivity, initial):
    guess = guess[0]
    source = source[0]
    core = lax.axis_index("core")
    place = lax.axis_index(("zl", "core"))[None]
    block = lax.axis_index(BLOCKS)
    block_core = jnp.stack([block, core])

    (sent,) = call(scatter_body, [sds(64, 2, ROWS, LANES)], place, source, guess, diffusivity, initial, smem=1)
    strips = lax.all_to_all(sent, BLOCK, 0, 0, tiled=True)
    both = lax.all_gather(strips, "core").reshape(2, 8, 8, 2, ROWS, LANES)

    own_g, f_up, f_down = call(
        functools.partial(pack_body, 0),
        [sds(NZ, ROWS, LANES), sds(4, NZ, ROWS, LANES), sds(4, NZ, ROWS, LANES)],
        both,
    )
    shifted = lax.ppermute(own_g, BLOCKS, [(b, b + 1) for b in range(NB - 1)])

    def exchange(mine):
        below = lax.ppermute(mine, ("zl", "y"), neighbours(1))
        above = lax.ppermute(mine, ("zl", "y"), neighbours(-1))
        return below, above

    f_below = lax.ppermute(f_up, ("zl", "y"), neighbours(1))
    f_above = lax.ppermute(f_down, ("zl", "y"), neighbours(-1))
    first = both[:, 3, :, 1].transpose(1, 0, 2, 3).reshape(NZ, ROWS, LANES)
    v0 = jnp.where(block == 0, first, shifted)
    below, above = exchange(v0)
    sweep_flops = 8 * NZ * WIN * LANES * 15
    v_first, v4 = call(
        functools.partial(fine_body, 0),
        [sds(4, NZ, ROWS, LANES), sds(NZ, ROWS, LANES)],
        both, f_below, f_above, v0, below, above,
        scratch=SWEEP_SCRATCH, flops=sweep_flops,
    )
    below, above = exchange(v4)
    v_second, residual = call(
        functools.partial(fine_body, 1),
        [sds(3, NZ, ROWS, LANES), sds(NZ, ROWS, LANES)],
        both, f_below, f_above, v4, below, above,
        scratch=SWEEP_SCRATCH, flops=sweep_flops,
    )
    below, above = exchange(residual)
    z_first, z4 = call(
        functools.partial(coarse_body, 4),
        [sds(4, NZ, ROWS, LANES), sds(NZ, ROWS, LANES)],
        both, residual, below, above,
        scratch=SWEEP_SCRATCH, flops=sweep_flops,
    )
    below, above = exchange(z4)
    z_second, _ = call(
        functools.partial(coarse_body, 3),
        [sds(3, NZ, ROWS, LANES), sds(NZ, ROWS, LANES)],
        both, z4, below, above,
        scratch=SWEEP_SCRATCH, flops=sweep_flops,
    )
    (outgoing,) = call(powers_body, [sds(NB, 8, ROWS, LANES)], block_core, residual, z_first, z_second, smem=1)
    arrived = lax.all_to_all(outgoing, BLOCKS, 0, 0, tiled=True)
    (back,) = call(collect_body, [sds(64, ROWS, LANES)], block_core, arrived, v_first, v_second, smem=1)
    returned = lax.all_to_all(back, BLOCK, 0, 0, tiled=True)
    (result,) = call(home_body, [sds(2, TILES * ROWS, LANES)], place, returned, guess, smem=1)
    return result[None]


def solution(mesh):
    fine = Mesh(mesh.devices.reshape(SIZES), AXES)
    tm = ("x", "zh", "zl", "core")
    space = ("y", "zhi")
    in_specs = (P(tm, space, None, None), P(tm, space, None, None), P(space, None, None), P(space, None, None))
    out_specs = P(tm, space, None, None)
    return jax.shard_map(on_device, mesh=fine, in_specs=in_specs, out_specs=out_specs, check_vma=False)
```

time: 916 us -> 200 us (0.22)
  the two profiles are of different devices: /device:TPU:24 before, /device:TPU:1 now
where the time goes in v1:
time: 200 us; the launch traced here: 197 us
  blocking collectives  113 us (56%)
  starting transfers between devices  33.4 us (17%)
  waiting for transfers between devices  20.3 us (10%)
  between operations  13.6 us (7%)
  Pallas kernels  12 us (6%)
  local copies, waits for them, and re-layouts  4.95 us (2%)
    all_to_all x1, blocking collectives, on_device(): strips = lax.all_to_all(sent, BLOCK, 0, 0, tiled=True)  52.4 us
    all_to_all x1, blocking collectives, on_device(): returned = lax.all_to_all(back, BLOCK, 0, 0, tiled=True)  46.3 us
    ppermute x4, starting transfers between devices, exchange(): below = lax.ppermute(mine, ('zl', 'y'), neighbours(1))  17.5 us
    all_to_all x1, blocking collectives, on_device(): arrived = lax.all_to_all(outgoing, BLOCKS, 0, 0, tiled=True)  14.4 us
    all_gather x1, waiting for transfers between devices, on_device(): both = lax.all_gather(strips, 'core').reshape(2, 8, 8, 2, ROWS, LANES)  13.4 us
    pallas_call x9, Pallas kernels, call(): pl.pallas_call(body, out_shape=list(outs), in_specs=specs, out_specs=out_...  12 us
    ppermute x1, starting transfers between devices, on_device(): shifted = lax.ppermute(own_g, BLOCKS, [(b, b + 1) for b in range(NB - 1)])  6.37 us
    ppermute x4, starting transfers between devices, exchange(): above = lax.ppermute(mine, ('zl', 'y'), neighbours(-1))  5.17 us
  transfers between devices with their start and end apart: 12, of which 5 were waited for; matrix products, arithmetic and copies ran while one was open for 0% of the time, Pallas kernels for 0%

profile of v1, /device:TPU:1, one launch (start us, length us, event | category | flops | bytes accessed | tf_op | source)
XLA Modules:
  0.0 197.5 jit_solution(7072581668511426670)
XLA Ops:
  6.5 0.9 copy-done.1
  7.5 0.9 copy-done.3
  8.4 0.9 copy-done.4
  9.3 0.9 copy-done.5
  10.3 52.4 %all_to_all.15 = f32[64,2,8,128]{3,2,1,0:T(8,128)} all-to-all(f32[64,2,8,128]{3,2,1,0:T(8,128)S(1)} %shard_map.46), channel_id=1, replica_groups=mesh['x'=4,'zh'=2,'zl'=4,'core'=2,'y'=4,'zhi'=2] {'zl','core','y','zhi'}, dimensions={0} | all-to-all | bytes 1048576 | tf_op jit(solution)/shard_map/all_to_all | solution.py:295
  62.8 13.4 %all-gather.3.cloned.1.call-done = f32[128,2,8,128]{3,2,1,0:T(8,128)} async-done(((f32[64,2,8,128]{3,2,1,0:T(8,128)}), f32[128,2,8,128]{3,2,1,0:T(8,128)}) %all-gather.3.cloned.1.call-update) | async-done | bytes 1048592 | tf_op jit(solution)/shard_map/all_gather | solution.py:296
  76.1 1.2 copy-done
  77.4 6.4 %collective-permute-start.2 = (f32[16,8,128]{2,1,0:T(8,128)S(1)}, f32[16,8,128]{2,1,0:T(8,128)S(1)}, u32[]{:S(2)}, u32[]{:S(2)}) collective-permute-start(f32[16,8,128]{2,1,0:T(8,128)S(1)} %get-tuple-element.17), channel_id=1, source_target_pairs={{0,64},{64,128},{128,192},{192,256},{256,320},{320,384},{384,448},... | collective-permute-start | bytes 196616 | tf_op jit(solution)/shard_map/ppermute | solution.py:303
  83.8 3.1 %collective-permute-start = (f32[4,16,8,128]{3,2,1,0:T(8,128)S(1)}, f32[4,16,8,128]{3,2,1,0:T(8,128)S(1)}, u32[]{:S(2)}, u32[]{:S(2)}) collective-permute-start(f32[4,16,8,128]{3,2,1,0:T(8,128)S(1)} %get-tuple-element.15), channel_id=1, source_target_pairs={{0,2},{2,4},{4,6},{6,22},{22,20},{20,18},{18,16},{16,32},{32,34},{... | collective-permute-start | bytes 786440 | tf_op jit(solution)/shard_map/ppermute | solution.py:310
  87.0 1.3 collective-permute-start.1
  88.3 1.3 collective-permute-start.4
  89.6 4.6 %collective-permute-start.3 = (f32[16,8,128]{2,1,0:T(8,128)S(1)}, f32[16,8,128]{2,1,0:T(8,128)S(1)}, u32[]{:S(2)}, u32[]{:S(2)}) collective-permute-start(f32[16,8,128]{2,1,0:T(8,128)S(1)} %bitcast_select_fusion.own_ref), channel_id=1, source_target_pairs={{0,2},{2,4},{4,6},{6,22},{22,20},{20,18},{18,16},{16,32},{32,34},{... | collective-permute-start | bytes 196616 | tf_op jit(solution)/shard_map/ppermute | solution.py:306
  94.2 3.1 %collective-permute-done.4.above_ref = f32[16,8,128]{2,1,0:T(8,128)S(1)} collective-permute-done((f32[16,8,128]{2,1,0:T(8,128)S(1)}, f32[16,8,128]{2,1,0:T(8,128)S(1)}, u32[]{:S(2)}, u32[]{:S(2)}) %collective-permute-start.4) | collective-permute-done | bytes 65568 | tf_op jit(solution)/shard_map/ppermute | solution.py:307
  97.3 2.4 %shard_map.48 = (f32[4,16,8,128]{3,2,1,0:T(8,128)S(1)}, f32[16,8,128]{2,1,0:T(8,128)S(1)}) custom-call(f32[2,8,8,2,8,128]{5,4,3,2,1,0:T(8,128)S(1)} %bitcast.15, f32[4,16,8,128]{3,2,1,0:T(8,128)S(1)} %collective-permute-done.fb_ref, f32[4,16,8,128]{3,2,1,0:T(8,128)S(1)} %collective-permute-done.1.fa_ref, f32[16,8,128]{2,1,0:T(8,128)S(1)} %bitcast_select_fusion.own_ref, ...), custom_call_target="tpu_custom_call" | custom-call | flops 5898240 | bytes 2097152 | tf_op jit(solution)/shard_map/pallas_call | solution.py:50
  99.8 1.3 collective-permute-start.6
  101.1 4.0 %collective-permute-start.5 = (f32[16,8,128]{2,1,0:T(8,128)S(1)}, f32[16,8,128]{2,1,0:T(8,128)S(1)}, u32[]{:S(2)}, u32[]{:S(2)}) collective-permute-start(f32[16,8,128]{2,1,0:T(8,128)S(1)} %get-tuple-element.18.own_ref), channel_id=1, source_target_pairs={{0,2},{2,4},{4,6},{6,22},{22,20},{20,18},{18,16},{16,32},{32,34},{... | collective-permute-start | bytes 196616 | tf_op jit(solution)/shard_map/ppermute | solution.py:306
  105.1 1.3 collective-permute-done.5.below_ref
  106.4 2.4 %shard_map.49 = (f32[3,16,8,128]{3,2,1,0:T(8,128)S(1)}, f32[16,8,128]{2,1,0:T(8,128)S(1)}) custom-call(f32[2,8,8,2,8,128]{5,4,3,2,1,0:T(8,128)S(1)} %bitcast.16, f32[4,16,8,128]{3,2,1,0:T(8,128)S(1)} %collective-permute-done.fb_ref, f32[4,16,8,128]{3,2,1,0:T(8,128)S(1)} %collective-permute-done.1.fa_ref, f32[16,8,128]{2,1,0:T(8,128)S(1)} %get-tuple-element.18.own_ref, ...), custom_call_target="tpu_custom_call" | custom-call | flops 5898240 | bytes 2031616 | tf_op jit(solution)/shard_map/pallas_call | solution.py:50
  108.8 1.3 collective-permute-start.8
  110.1 4.5 %collective-permute-start.7 = (f32[16,8,128]{2,1,0:T(8,128)S(1)}, f32[16,8,128]{2,1,0:T(8,128)S(1)}, u32[]{:S(2)}, u32[]{:S(2)}) collective-permute-start(f32[16,8,128]{2,1,0:T(8,128)S(1)} %get-tuple-element.19.own_ref.r_ref), channel_id=1, source_target_pairs={{0,2},{2,4},{4,6},{6,22},{22,20},{20,18},{18,16},{16,32},{32,34},{... | collective-permute-start | bytes 196616 | tf_op jit(solution)/shard_map/ppermute | solution.py:306
  114.6 1.3 collective-permute-done.7.below_ref
  115.9 2.3 %shard_map.50 = (f32[4,16,8,128]{3,2,1,0:T(8,128)S(1)}, f32[16,8,128]{2,1,0:T(8,128)S(1)}) custom-call(f32[2,8,8,2,8,128]{5,4,3,2,1,0:T(8,128)S(1)} %bitcast.17, f32[16,8,128]{2,1,0:T(8,128)S(1)} %get-tuple-element.19.own_ref.r_ref, f32[16,8,128]{2,1,0:T(8,128)S(1)} %collective-permute-done.7.below_ref, f32[16,8,128]{2,1,0:T(8,128)S(1)} %collective-permute-done.8.above_ref), custom_call_target="tpu_custom_call" | custom-call | flops 5898240 | bytes 1572864 | tf_op jit(solution)/shard_map/pallas_call | solution.py:50
  118.3 1.3 collective-permute-start.10
  119.6 4.3 %collective-permute-start.9 = (f32[16,8,128]{2,1,0:T(8,128)S(1)}, f32[16,8,128]{2,1,0:T(8,128)S(1)}, u32[]{:S(2)}, u32[]{:S(2)}) collective-permute-start(f32[16,8,128]{2,1,0:T(8,128)S(1)} %get-tuple-element.21.own_ref), channel_id=1, source_target_pairs={{0,2},{2,4},{4,6},{6,22},{22,20},{20,18},{18,16},{16,32},{32,34},{... | collective-permute-start | bytes 196616 | tf_op jit(solution)/shard_map/ppermute | solution.py:306
  123.9 0.1 pad_add_fusion.place_ref
  124.0 1.2 collective-permute-done.9.below_ref
  125.2 2.7 %shard_map.51 = (f32[3,16,8,128]{3,2,1,0:T(8,128)S(1)}, f32[16,8,128]{2,1,0:T(8,128)}) custom-call(f32[2,8,8,2,8,128]{5,4,3,2,1,0:T(8,128)S(1)} %bitcast.18, f32[16,8,128]{2,1,0:T(8,128)S(1)} %get-tuple-element.21.own_ref, f32[16,8,128]{2,1,0:T(8,128)S(1)} %collective-permute-done.9.below_ref, f32[16,8,128]{2,1,0:T(8,128)S(1)} %collective-permute-done.10.above_ref), custom_call_target="tpu_custom_call" | custom-call | flops 5898240 | bytes 1507328 | tf_op jit(solution)/shard_map/pallas_call | solution.py:50
  128.0 0.7 shard_map.52
  128.7 14.4 %all_to_all.16.got_ref = f32[8,8,8,128]{3,2,1,0:T(8,128)S(1)} all-to-all(f32[8,8,8,128]{3,2,1,0:T(8,128)S(1)} %shard_map.52), channel_id=1, replica_groups=mesh['x'=4,'zh'=2,'zl'=4,'core'=2,'y'=4,'zhi'=2] {'x','zh'}, dimensions={0} | all-to-all | bytes 524288 | tf_op jit(solution)/shard_map/all_to_all | solution.py:344
  143.1 0.6 shard_map.53
  143.7 46.3 %all_to_all.17.got_ref = f32[64,8,128]{2,1,0:T(8,128)S(1)} all-to-all(f32[64,8,128]{2,1,0:T(8,128)S(1)} %shard_map.53), channel_id=1, replica_groups=mesh['x'=4,'zh'=2,'zl'=4,'core'=2,'y'=4,'zhi'=2] {'zl','core','y','zhi'}, dimensions={0} | all-to-all | bytes 524288 | tf_op jit(solution)/shard_map/all_to_all | solution.py:346
  189.9 0.7 shard_map.54
  (21 shorter events, 0.2 us)
Async XLA Ops:
  6.5 69.6 %all-gather.3.cloned.1.call-start = ((), (), s32[]{:S(2)}) async-start(), calls=%async_computation.3 | async-start | bytes 1572864 | tf_op jit(solution)/shard_map/all_gather | solution.py:296
  6.5 0.9 copy-start.1
  7.5 0.9 copy-start.3
  8.4 0.9 copy-start.4
  9.3 0.9 copy-start.5
  76.1 1.2 copy-start
  77.4 10.8 %collective-permute-start.2 = (f32[16,8,128]{2,1,0:T(8,128)S(1)}, f32[16,8,128]{2,1,0:T(8,128)S(1)}, u32[]{:S(2)}, u32[]{:S(2)}) collective-permute-start(f32[16,8,128]{2,1,0:T(8,128)S(1)} %get-tuple-element.17), channel_id=1, source_target_pairs={{0,64},{64,128},{128,192},{192,256},{256,320},{320,384},{384,448},... | collective-permute-start | bytes 196616 | tf_op jit(solution)/shard_map/ppermute | solution.py:303
  83.8 13.5 %collective-permute-start = (f32[4,16,8,128]{3,2,1,0:T(8,128)S(1)}, f32[4,16,8,128]{3,2,1,0:T(8,128)S(1)}, u32[]{:S(2)}, u32[]{:S(2)}) collective-permute-start(f32[4,16,8,128]{3,2,1,0:T(8,128)S(1)} %get-tuple-element.15), channel_id=1, source_target_pairs={{0,2},{2,4},{4,6},{6,22},{22,20},{20,18},{18,16},{16,32},{32,34},{... | collective-permute-start | bytes 786440 | tf_op jit(solution)/shard_map/ppermute | solution.py:310
  87.0 10.4 %collective-permute-start.1 = (f32[4,16,8,128]{3,2,1,0:T(8,128)S(1)}, f32[4,16,8,128]{3,2,1,0:T(8,128)S(1)}, u32[]{:S(2)}, u32[]{:S(2)}) collective-permute-start(f32[4,16,8,128]{3,2,1,0:T(8,128)S(1)} %get-tuple-element.16), channel_id=1, source_target_pairs={{2,0},{4,2},{6,4},{22,6},{20,22},{18,20},{16,18},{32,16},{34,32},{... | collective-permute-start | bytes 786440 | tf_op jit(solution)/shard_map/ppermute | solution.py:311
  88.3 9.0 %collective-permute-start.4 = (f32[16,8,128]{2,1,0:T(8,128)S(1)}, f32[16,8,128]{2,1,0:T(8,128)S(1)}, u32[]{:S(2)}, u32[]{:S(2)}) collective-permute-start(f32[16,8,128]{2,1,0:T(8,128)S(1)} %bitcast_select_fusion.own_ref), channel_id=1, source_target_pairs={{2,0},{4,2},{6,4},{22,6},{20,22},{18,20},{16,18},{32,16},{34,32},{... | collective-permute-start | bytes 196616 | tf_op jit(solution)/shard_map/ppermute | solution.py:307
  89.6 7.7 %collective-permute-start.3 = (f32[16,8,128]{2,1,0:T(8,128)S(1)}, f32[16,8,128]{2,1,0:T(8,128)S(1)}, u32[]{:S(2)}, u32[]{:S(2)}) collective-permute-start(f32[16,8,128]{2,1,0:T(8,128)S(1)} %bitcast_select_fusion.own_ref), channel_id=1, source_target_pairs={{0,2},{2,4},{4,6},{6,22},{22,20},{20,18},{18,16},{16,32},{32,34},{... | collective-permute-start | bytes 196616 | tf_op jit(solution)/shard_map/ppermute | solution.py:306
  99.8 5.3 %collective-permute-start.6 = (f32[16,8,128]{2,1,0:T(8,128)S(1)}, f32[16,8,128]{2,1,0:T(8,128)S(1)}, u32[]{:S(2)}, u32[]{:S(2)}) collective-permute-start(f32[16,8,128]{2,1,0:T(8,128)S(1)} %get-tuple-element.18.own_ref), channel_id=1, source_target_pairs={{2,0},{4,2},{6,4},{22,6},{20,22},{18,20},{16,18},{32,16},{34,32},{... | collective-permute-start | bytes 196616 | tf_op jit(solution)/shard_map/ppermute | solution.py:307
  101.1 5.3 %collective-permute-start.5 = (f32[16,8,128]{2,1,0:T(8,128)S(1)}, f32[16,8,128]{2,1,0:T(8,128)S(1)}, u32[]{:S(2)}, u32[]{:S(2)}) collective-permute-start(f32[16,8,128]{2,1,0:T(8,128)S(1)} %get-tuple-element.18.own_ref), channel_id=1, source_target_pairs={{0,2},{2,4},{4,6},{6,22},{22,20},{20,18},{18,16},{16,32},{32,34},{... | collective-permute-start | bytes 196616 | tf_op jit(solution)/shard_map/ppermute | solution.py:306
  108.8 5.8 %collective-permute-start.8 = (f32[16,8,128]{2,1,0:T(8,128)S(1)}, f32[16,8,128]{2,1,0:T(8,128)S(1)}, u32[]{:S(2)}, u32[]{:S(2)}) collective-permute-start(f32[16,8,128]{2,1,0:T(8,128)S(1)} %get-tuple-element.19.own_ref.r_ref), channel_id=1, source_target_pairs={{2,0},{4,2},{6,4},{22,6},{20,22},{18,20},{16,18},{32,16},{34,32},{... | collective-permute-start | bytes 196616 | tf_op jit(solution)/shard_map/ppermute | solution.py:307
  110.1 5.9 %collective-permute-start.7 = (f32[16,8,128]{2,1,0:T(8,128)S(1)}, f32[16,8,128]{2,1,0:T(8,128)S(1)}, u32[]{:S(2)}, u32[]{:S(2)}) collective-permute-start(f32[16,8,128]{2,1,0:T(8,128)S(1)} %get-tuple-element.19.own_ref.r_ref), channel_id=1, source_target_pairs={{0,2},{2,4},{4,6},{6,22},{22,20},{20,18},{18,16},{16,32},{32,34},{... | collective-permute-start | bytes 196616 | tf_op jit(solution)/shard_map/ppermute | solution.py:306
  118.3 5.7 %collective-permute-start.10 = (f32[16,8,128]{2,1,0:T(8,128)S(1)}, f32[16,8,128]{2,1,0:T(8,128)S(1)}, u32[]{:S(2)}, u32[]{:S(2)}) collective-permute-start(f32[16,8,128]{2,1,0:T(8,128)S(1)} %get-tuple-element.21.own_ref), channel_id=1, source_target_pairs={{2,0},{4,2},{6,4},{22,6},{20,22},{18,20},{16,18},{32,16},{34,32},{... | collective-permute-start | bytes 196616 | tf_op jit(solution)/shard_map/ppermute | solution.py:307
  119.6 5.6 %collective-permute-start.9 = (f32[16,8,128]{2,1,0:T(8,128)S(1)}, f32[16,8,128]{2,1,0:T(8,128)S(1)}, u32[]{:S(2)}, u32[]{:S(2)}) collective-permute-start(f32[16,8,128]{2,1,0:T(8,128)S(1)} %get-tuple-element.21.own_ref), channel_id=1, source_target_pairs={{0,2},{2,4},{4,6},{6,22},{22,20},{20,18},{18,16},{16,32},{32,34},{... | collective-permute-start | bytes 196616 | tf_op jit(solution)/shard_map/ppermute | solution.py:306
  143.7 46.3 %copy-start.2 = (f32[1,2,192,128]{3,2,1,0:T(8,128)S(1)}, f32[1,2,192,128]{3,2,1,0:T(8,128)}, u32[]{:S(2)}) copy-start(f32[1,2,192,128]{3,2,1,0:T(8,128)} %param.4) | copy-start | bytes 589828
Sparse Core Ops, SparseCore 0:
  62.9 13.2 all-gather.2

commit v2 on v1

v2 whole, which is shorter than its diff:
```python
import functools

import jax
import jax.numpy as jnp
from jax import lax
from jax.experimental import pallas as pl
from jax.experimental.pallas import tpu as pltpu
from jax.sharding import Mesh, PartitionSpec as P

SWEEPS = 2
F32 = jnp.float32

damping = 0.8
step_size = 0.5
coarse_size = 4.0
z_weight = 8.0

AXES = ("x", "zh", "zl", "core", "y", "zhi")
SIZES = (4, 2, 4, 2, 4, 2)
BLOCK = ("zl", "core", "y", "zhi")
BLOCKS = ("x", "zh")
NB = 8
NZ = 16
ROWS = 8
TILES = 24
CHIPS = 16
SIDE = 8
WIN = 3 * ROWS
LANES = 128


def chip_order(zl, y):
    return zl * 4 + (y if zl % 2 == 0 else 3 - y)


def block_index(zl, core, y, zhi):
    return ((zl * 2 + core) * 4 + y) * 2 + zhi


def neighbours(step):
    place = {chip_order(zl, y): zl * 4 + y for zl in range(4) for y in range(4)}
    return [(place[m], place[m + step]) for m in range(CHIPS) if 0 <= m + step < CHIPS]


def call(body, outs, *args, scratch=(), smem=0, flops=0):
    specs = [pl.BlockSpec(memory_space=pltpu.SMEM)] * smem
    specs += [pl.BlockSpec(memory_space=pltpu.VMEM)] * (len(args) - smem)
    out_specs = [pl.BlockSpec(memory_space=pltpu.VMEM)] * len(outs)
    size = sum(4 * a.size for a in args) + sum(4 * o.size for o in outs)
    return pl.pallas_call(
        body,
        out_shape=list(outs),
        in_specs=specs,
        out_specs=out_specs,
        scratch_shapes=list(scratch),
        compiler_params=pltpu.CompilerParams(vmem_limit_bytes=32 * 1024 * 1024),
        cost_estimate=pl.CostEstimate(flops=flops, bytes_accessed=size, transcendentals=0),
    )(*args)


def sds(*shape):
    return jax.ShapeDtypeStruct(shape, F32)


def scatter_body(j_ref, src_hbm, guess_hbm, cond_hbm, init_hbm, out_ref, src_ref, extra_ref, sems):
    place = j_ref[0]
    zero = jnp.zeros((ROWS, LANES), F32)
    source_copy = pltpu.make_async_copy(src_hbm, src_ref, sems.at[0])
    source_copy.start()

    @pl.when(place < 3)
    def _():
        pltpu.make_async_copy(cond_hbm, extra_ref, sems.at[1]).start()

    @pl.when(place == 3)
    def _():
        pltpu.make_async_copy(init_hbm, extra_ref, sems.at[1]).start()

    @pl.when(place > 3)
    def _():
        pltpu.make_async_copy(guess_hbm, extra_ref, sems.at[1]).start()

    def each():
        for zl in range(4):
            for y in range(4):
                for zhi in range(2):
                    tile = SIDE * zhi + chip_order(zl, y)
                    for core in range(2):
                        yield block_index(zl, core, y, zhi), core, tile

    source_copy.wait()
    for at, core, tile in each():
        out_ref[at, 0] = src_ref[core, tile * ROWS : (tile + 1) * ROWS]
    pltpu.make_async_copy(guess_hbm, extra_ref, sems.at[1]).wait()

    def fill(shift):
        for at, core, tile in each():
            tile = tile + shift
            if 0 <= tile < TILES:
                out_ref[at, 1] = extra_ref[core, tile * ROWS : (tile + 1) * ROWS]
            else:
                out_ref[at, 1] = zero

    pl.when(place == 1)(functools.partial(fill, 1))
    pl.when(place == 2)(functools.partial(fill, -1))
    pl.when((place != 1) & (place != 2))(functools.partial(fill, 0))


def pack_body(core_ref, own_ref, other_ref, f_ref, g_ref, k_ref, first_ref, up_ref, down_ref):
    def order(halves):
        for z in range(NZ):
            s, p = z // 2, z % 2
            half = halves[p]
            for n in range(8):
                f_ref[n, z] = half[n, s, 0]
            g_ref[z] = half[7, s, 1]
            k_ref[z, 0:8] = half[2, s, 1]
            k_ref[z, 8:16] = half[0, s, 1]
            k_ref[z, 16:24] = half[1, s, 1]
            first_ref[z] = half[3, s, 1]

    pl.when(core_ref[0] == 0)(functools.partial(order, (own_ref, other_ref)))
    pl.when(core_ref[0] == 1)(functools.partial(order, (other_ref, own_ref)))
    row = lax.broadcasted_iota(jnp.int32, (ROWS, LANES), 0)
    for z in range(NZ):
        for phase in range(2):
            f = [f_ref[4 * phase + n, z] for n in range(4)]
            down_ref[2 * phase, z] = jnp.where(row < 7, f[0], pltpu.roll(f[3], 7, 0))
            down_ref[2 * phase + 1, z] = jnp.where(row < 5, f[1], pltpu.roll(f[2], 5, 0))
            up_ref[2 * phase, z] = jnp.where(row >= 1, f[0], pltpu.roll(f[3], 1, 0))
            up_ref[2 * phase + 1, z] = jnp.where(row >= 3, f[1], pltpu.roll(f[2], 3, 0))


def coefficients(rate, k_ref, k_s, co_s):
    zero = jnp.zeros((WIN, LANES), F32)
    for z in range(NZ):
        k_s[z + 1] = k_ref[z]
    k_s[0] = zero
    k_s[NZ + 1] = zero
    lane = lax.broadcasted_iota(jnp.int32, (WIN, LANES), 1)
    first = lane == 0
    last = lane == LANES - 1

    def layer(z, carry):
        k = k_s[z + 1]
        side = 0.5 * rate
        tall = 0.5 * rate * z_weight
        c = [
            tall * (k + k_s[z]),
            tall * (k + k_s[z + 2]),
            side * (k + pltpu.roll(k, 1, 0)),
            side * (k + pltpu.roll(k, WIN - 1, 0)),
            side * (k + jnp.where(first, 0.0, pltpu.roll(k, 1, 1))),
            side * (k + jnp.where(last, 0.0, pltpu.roll(k, LANES - 1, 1))),
        ]
        total = ((c[0] + c[1]) + (c[2] + c[3])) + (c[4] + c[5])
        d = jnp.where(k > 0.0, damping / (1.0 + total), 0.0)
        co_s[0, z] = c[0] * d
        co_s[1, z] = c[1] * d
        co_s[2, z] = c[2] * d
        co_s[3, z] = c[3] * d
        co_s[4, z] = jnp.where(first, 0.0, c[4] * d)
        co_s[5, z] = jnp.where(last, 0.0, c[5] * d)
        co_s[6, z] = d
        return carry

    lax.fori_loop(0, NZ, layer, 0)


def one_sweep(src, dst, co_s, db_s):
    for z in range(NZ):
        w = src[z + 1]
        acc = (db_s[z] + (1.0 - damping) * w) + (co_s[0, z] * src[z] + co_s[1, z] * src[z + 2])
        acc = acc + (co_s[2, z] * pltpu.roll(w, 1, 0) + co_s[3, z] * pltpu.roll(w, WIN - 1, 0))
        acc = acc + (co_s[4, z] * pltpu.roll(w, 1, 1) + co_s[5, z] * pltpu.roll(w, LANES - 1, 1))
        dst[z + 1] = acc


def load_window(a_s, own_ref, below_ref, above_ref, b_s):
    zero = jnp.zeros((WIN, LANES), F32)
    for ref in (a_s, b_s):
        ref[0] = zero
        ref[NZ + 1] = zero
    for z in range(NZ):
        a_s[z + 1, 0:8] = below_ref[z]
        a_s[z + 1, 8:16] = own_ref[z]
        a_s[z + 1, 16:24] = above_ref[z]


def fine_steps(phase, f_ref, fb_ref, fa_ref, co_s, a_s, b_s, db_s, keep):
    for n in range(4):
        tile, turn = ((0, 0), (1, 0), (1, 5), (0, 7))[n]
        for z in range(NZ):
            below = fb_ref[2 * phase + tile, z]
            above = fa_ref[2 * phase + tile, z]
            if turn:
                below = pltpu.roll(below, turn, 0)
                above = pltpu.roll(above, ROWS - turn, 0)
            forcing = jnp.concatenate([below, f_ref[4 * phase + n, z], above], axis=0)
            db_s[z] = co_s[6, z] * (a_s[z + 1] + step_size * forcing)
        one_sweep(a_s, b_s, co_s, db_s)
        one_sweep(b_s, a_s, co_s, db_s)
        for z in range(NZ):
            keep(n, z, a_s[z + 1, 8:16])


def early_body(k_ref, f_ref, fb_ref, fa_ref, own_ref, below_ref, above_ref, out_ref, end_ref, k_s, co_s, a_s, b_s, db_s):
    coefficients(step_size, k_ref, k_s, co_s)
    load_window(a_s, own_ref, below_ref, above_ref, b_s)

    def keep(n, z, mine):
        out_ref[n, z] = mine
        if n == 3:
            end_ref[z] = mine

    fine_steps(0, f_ref, fb_ref, fa_ref, co_s, a_s, b_s, db_s, keep)


def late_body(
    core_ref, k_ref, f_ref, fb_ref, fa_ref, own_ref, below_ref, above_ref, g_ref, early_ref,
    out_ref, res_ref, k_s, co_s, a_s, b_s, db_s, late_s,
):
    coefficients(step_size, k_ref, k_s, co_s)
    load_window(a_s, own_ref, below_ref, above_ref, b_s)

    def keep(n, z, mine):
        if n < 3:
            late_s[n, z] = mine
        else:
            res_ref[z] = mine - g_ref[z]

    fine_steps(1, f_ref, fb_ref, fa_ref, co_s, a_s, b_s, db_s, keep)
    core = core_ref[0]
    for y in range(4):
        for zhi in range(2):
            z = 2 * (2 * y + zhi) + core
            for n in range(4):
                out_ref[zhi, n, y] = early_ref[n, z]
            for n in range(3):
                out_ref[zhi, 4 + n, y] = late_s[n, z]


def coarse_steps(steps, co_s, a_s, b_s, db_s, keep):
    for n in range(steps):
        for z in range(NZ):
            db_s[z] = co_s[6, z] * a_s[z + 1]
        one_sweep(a_s, b_s, co_s, db_s)
        one_sweep(b_s, a_s, co_s, db_s)
        for z in range(NZ):
            keep(n, z, a_s[z + 1, 8:16])


def powers_early_body(k_ref, own_ref, below_ref, above_ref, out_ref, end_ref, k_s, co_s, a_s, b_s, db_s):
    coefficients(coarse_size, k_ref, k_s, co_s)
    load_window(a_s, own_ref, below_ref, above_ref, b_s)

    def keep(n, z, mine):
        out_ref[n, z] = mine
        if n == 3:
            end_ref[z] = mine

    coarse_steps(4, co_s, a_s, b_s, db_s, keep)


def powers_late_body(
    place_ref, k_ref, own_ref, below_ref, above_ref, res_ref, early_ref, out_ref, k_s, co_s, a_s, b_s, db_s, pow_s
):
    coefficients(coarse_size, k_ref, k_s, co_s)
    load_window(a_s, own_ref, below_ref, above_ref, b_s)
    for z in range(NZ):
        pow_s[0, z] = res_ref[z]
        for n in range(4):
            pow_s[1 + n, z] = early_ref[n, z]

    def keep(n, z, mine):
        pow_s[5 + n, z] = mine

    coarse_steps(3, co_s, a_s, b_s, db_s, keep)
    c, core = place_ref[0], place_ref[1]
    for b in range(NB):
        power = jnp.clip(b - c, 0, NB - 1)
        live = b >= c
        for y in range(4):
            for zhi in range(2):
                value = pow_s[power, 2 * (2 * y + zhi) + core]
                out_ref[2 * b + zhi, y] = jnp.where(live, value, 0.0)


SWEEP_SCRATCH = (
    pltpu.VMEM((NZ + 2, WIN, LANES), F32),
    pltpu.VMEM((7, NZ, WIN, LANES), F32),
    pltpu.VMEM((NZ + 2, WIN, LANES), F32),
    pltpu.VMEM((NZ + 2, WIN, LANES), F32),
    pltpu.VMEM((NZ, WIN, LANES), F32),
)


def collect_body(got_ref, v_ref, out_ref):
    for side in range(2):
        for y in range(4):
            total = got_ref[side, y]
            for b in range(1, NB):
                total = total + got_ref[2 * b + side, y]
            out_ref[7 * 4 + y, side] = total
            for n in range(7):
                out_ref[n * 4 + y, side] = v_ref[side, n, y]


def home_body(j_ref, got_ref, guess_ref, out_ref):
    last = j_ref[0] == 7

    def write(add):
        for tile in range(TILES):
            zhi = 0 if tile < TILES // 2 else 1
            m = tile - SIDE * zhi
            zl, y = m // 4, m % 4
            if zl % 2 == 1:
                y = 3 - y
            rows = slice(tile * ROWS, (tile + 1) * ROWS)
            for core in range(2):
                value = got_ref[(zl * 2 + core) * 4 + y, zhi]
                if add:
                    value = guess_ref[core, rows] + value
                out_ref[core, rows] = value

    pl.when(last)(functools.partial(write, True))
    pl.when(jnp.logical_not(last))(functools.partial(write, False))


def on_device(guess, source, diffusivity, initial):
    guess = guess[0]
    source = source[0]
    core = lax.axis_index("core")
    place = lax.axis_index(("zl", "core"))[None]
    block = lax.axis_index(BLOCKS)
    block_core = jnp.stack([block, core])

    sent = pl.pallas_call(
        scatter_body,
        out_shape=sds(64, 2, ROWS, LANES),
        in_specs=[pl.BlockSpec(memory_space=pltpu.SMEM)] + [pl.BlockSpec(memory_space=pltpu.HBM)] * 4,
        out_specs=pl.BlockSpec(memory_space=pltpu.VMEM),
        scratch_shapes=[
            pltpu.VMEM((2, TILES * ROWS, LANES), F32),
            pltpu.VMEM((2, TILES * ROWS, LANES), F32),
            pltpu.SemaphoreType.DMA((2,)),
        ],
        compiler_params=pltpu.CompilerParams(vmem_limit_bytes=32 * 1024 * 1024),
    )(place, source, guess, diffusivity, initial)
    strips = lax.all_to_all(sent, BLOCK, 0, 0, tiled=True).reshape(8, 8, 2, ROWS, LANES)
    other = lax.ppermute(strips, "core", [(0, 1), (1, 0)])

    f, g, k, first, f_up, f_down = call(
        pack_body,
        [sds(8, NZ, ROWS, LANES), sds(NZ, ROWS, LANES), sds(NZ, WIN, LANES), sds(NZ, ROWS, LANES)]
        + [sds(4, NZ, ROWS, LANES)] * 2,
        core[None], strips, other, smem=1,
    )

    def exchange(up, down):
        below = lax.ppermute(up, ("zl", "y"), neighbours(1))
        above = lax.ppermute(down, ("zl", "y"), neighbours(-1))
        return below, above

    f_below, f_above = exchange(f_up, f_down)
    shifted = lax.ppermute(g, BLOCKS, [(b, b + 1) for b in range(NB - 1)])
    v0 = jnp.where(block == 0, first, shifted)
    below, above = exchange(v0, v0)
    flops = 8 * NZ * WIN * LANES * 15
    v_early, v4 = call(
        early_body, [sds(4, NZ, ROWS, LANES), sds(NZ, ROWS, LANES)],
        k, f, f_below, f_above, v0, below, above, scratch=SWEEP_SCRATCH, flops=flops,
    )
    below, above = exchange(v4, v4)
    v, residual = call(
        late_body, [sds(2, 7, 4, ROWS, LANES), sds(NZ, ROWS, LANES)],
        core[None], k, f, f_below, f_above, v4, below, above, g, v_early, smem=1,
        scratch=SWEEP_SCRATCH + (pltpu.VMEM((3, NZ, ROWS, LANES), F32),), flops=flops,
    )
    below, above = exchange(residual, residual)
    v = lax.all_to_all(v, "zhi", 0, 0, tiled=True)
    z_early, z4 = call(
        powers_early_body, [sds(4, NZ, ROWS, LANES), sds(NZ, ROWS, LANES)],
        k, residual, below, above, scratch=SWEEP_SCRATCH, flops=flops,
    )
    below, above = exchange(z4, z4)
    (powers,) = call(
        powers_late_body, [sds(2 * NB, 4, ROWS, LANES)],
        block_core, k, z4, below, above, residual, z_early, smem=1,
        scratch=SWEEP_SCRATCH + (pltpu.VMEM((NB, NZ, ROWS, LANES), F32),), flops=flops,
    )
    arrived = lax.all_to_all(powers, BLOCKS + ("zhi",), 0, 0, tiled=True)
    (back,) = call(collect_body, [sds(32, 2, ROWS, LANES)], arrived, v)
    returned = lax.all_to_all(back, ("zl", "core", "y"), 0, 0, tiled=True)
    (result,) = call(home_body, [sds(2, TILES * ROWS, LANES)], place, returned, guess, smem=1)
    return result[None]


def solution(mesh):
    fine = Mesh(mesh.devices.reshape(SIZES), AXES)
    tm = ("x", "zh", "zl", "core")
    space = ("y", "zhi")
    in_specs = (P(tm, space, None, None), P(tm, space, None, None), P(space, None, None), P(space, None, None))
    out_specs = P(tm, space, None, None)
    return jax.shard_map(on_device, mesh=fine, in_specs=in_specs, out_specs=out_specs, check_vma=False)
```

time: 200 us -> 176 us (0.88)
  between operations: 13.6 us -> 0.2 us
  waiting for transfers between devices: 20.3 us -> 16.9 us
  starting transfers between devices: 33.4 us -> 31 us
  blocking collectives: 113 us -> 111 us
    all_gather x1 -> x0, waiting for transfers between devices: 13.4 us -> none  [on_device(): both = lax.all_gather(strips, 'core').reshape(2, 8, 8, 2, ROWS, LANES)]
    ppermute x11 -> x12, waiting for transfers between devices: 6.96 us -> 16.9 us  [the longest x5 15.2 us: exchange(): above = lax.ppermute(down, ('zl', 'y'), neighbours(-1))]
    ppermute x11 -> x12, starting transfers between devices: 33.4 us -> 27.6 us  [the longest x5 15.3 us: exchange(): below = lax.ppermute(up, ('zl', 'y'), neighbours(1))]
    all_to_all x0 -> x1, starting transfers between devices: none -> 3.44 us  [on_device(): v = lax.all_to_all(v, 'zhi', 0, 0, tiled=True)]
    unnamed x12 -> x10, local copies, waits for them, and re-layouts: 4.94 us -> 3.71 us
    pallas_call x9 -> x7, Pallas kernels: 12 us -> 11.4 us  [call(): pl.pallas_call(body, out_shape=list(outs), in_specs=specs, out_specs=out_...]
  transfers between devices with their start and end apart: 12 -> 13, of which waited for: 5 -> 6; matrix products, arithmetic and copies ran while one was open for 0% -> 0% of each run, Pallas kernels for 0% -> 3%
where the time goes in v2:
time: 176 us; the launch traced here: 175 us
  blocking collectives  111 us (63%)
  starting transfers between devices  31 us (18%)
  waiting for transfers between devices  16.9 us (10%)
  Pallas kernels  11.9 us (7%)
  local copies, waits for them, and re-layouts  3.71 us (2%)
    all_to_all x1, blocking collectives, on_device(): lax.all_to_all(sent, BLOCK, 0, 0, tiled=True).reshape(8, 8, 2, ROWS, LANES)  52.3 us
    all_to_all x1, blocking collectives, on_device(): arrived = lax.all_to_all(powers, BLOCKS + ('zhi',), 0, 0, tiled=True)  34.4 us
    all_to_all x1, blocking collectives, on_device(): returned = lax.all_to_all(back, ('zl', 'core', 'y'), 0, 0, tiled=True)  24.7 us
    ppermute x5, starting transfers between devices, exchange(): below = lax.ppermute(up, ('zl', 'y'), neighbours(1))  15.3 us
    ppermute x5, waiting for transfers between devices, exchange(): above = lax.ppermute(down, ('zl', 'y'), neighbours(-1))  15.2 us
    pallas_call x7, Pallas kernels, call(): pl.pallas_call(body, out_shape=list(outs), in_specs=specs, out_specs=out_...  11.4 us
    ppermute x5, starting transfers between devices, exchange(): above = lax.ppermute(down, ('zl', 'y'), neighbours(-1))  6.46 us
    unnamed x10, local copies, waits for them, and re-layouts  3.71 us
  transfers between devices with their start and end apart: 13, of which 6 were waited for; matrix products, arithmetic and copies ran while one was open for 0% of the time, Pallas kernels for 3%

profile of v2, /device:TPU:1, one launch (start us, length us, event | category | flops | bytes accessed | tf_op | source)
XLA Modules:
  0.0 175.3 jit_solution(5829555496672450969)
XLA Ops:
  0.0 0.9 copy-done
  0.9 0.9 copy-done.2
  1.9 0.9 copy-done.3
  2.8 0.9 copy-done.4
  3.7 0.6 shard_map.46
  4.3 52.3 %all_to_all.20 = f32[64,2,8,128]{3,2,1,0:T(8,128)S(1)} all-to-all(f32[64,2,8,128]{3,2,1,0:T(8,128)S(1)} %shard_map.46), channel_id=1, replica_groups=mesh['x'=4,'zh'=2,'zl'=4,'core'=2,'y'=4,'zhi'=2] {'zl','core','y','zhi'}, dimensions={0} | all-to-all | bytes 1048576 | tf_op jit(solution)/shard_map/all_to_all | solution.py:350
  56.6 2.6 %collective-permute-start = (f32[8,8,2,8,128]{4,3,2,1,0:T(8,128)S(1)}, f32[8,8,2,8,128]{4,3,2,1,0:T(8,128)S(1)}, u32[]{:S(2)}, u32[]{:S(2)}) collective-permute-start(f32[8,8,2,8,128]{4,3,2,1,0:T(8,128)S(1)} %bitcast.7), channel_id=1, source_target_pairs={{0,8},{8,0},{1,9},{9,1},{2,10},{10,2},{3,11},{11,3},{4,12},{12,4},... | collective-permute-start | bytes 1572872 | tf_op jit(solution)/shard_map/ppermute | solution.py:351
  59.2 1.5 collective-permute-done.other_ref
  60.8 3.2 %collective-permute-start.3 = (f32[16,8,128]{2,1,0:T(8,128)S(1)}, f32[16,8,128]{2,1,0:T(8,128)S(1)}, u32[]{:S(2)}, u32[]{:S(2)}) collective-permute-start(f32[16,8,128]{2,1,0:T(8,128)S(1)} %get-tuple-element.22.g_ref), channel_id=1, source_target_pairs={{0,64},{64,128},{128,192},{192,256},{256,320},{320,384},{384,448},... | collective-permute-start | bytes 196616 | tf_op jit(solution)/shard_map/ppermute | solution.py:366
  64.0 1.3 collective-permute-start.1
  65.3 1.3 collective-permute-start.2
  66.7 4.0 %collective-permute-start.4 = (f32[16,8,128]{2,1,0:T(8,128)S(1)}, f32[16,8,128]{2,1,0:T(8,128)S(1)}, u32[]{:S(2)}, u32[]{:S(2)}) collective-permute-start(f32[16,8,128]{2,1,0:T(8,128)S(1)} %broadcast_select_fusion.own_ref), channel_id=1, source_target_pairs={{0,2},{2,4},{4,6},{6,22},{22,20},{20,18},{18,16},{16,32},{32,34},{... | collective-permute-start | bytes 196616 | tf_op jit(solution)/shard_map/ppermute | solution.py:361
  70.7 1.3 collective-permute-start.5
  72.0 0.2 collective-permute-done.4.below_ref
  72.1 3.8 %collective-permute-done.5.above_ref = f32[16,8,128]{2,1,0:T(8,128)S(1)} collective-permute-done((f32[16,8,128]{2,1,0:T(8,128)S(1)}, f32[16,8,128]{2,1,0:T(8,128)S(1)}, u32[]{:S(2)}, u32[]{:S(2)}) %collective-permute-start.5) | collective-permute-done | bytes 65568 | tf_op jit(solution)/shard_map/ppermute | solution.py:362
  76.0 2.4 %shard_map.48 = (f32[4,16,8,128]{3,2,1,0:T(8,128)S(1)}, f32[16,8,128]{2,1,0:T(8,128)S(1)}) custom-call(f32[16,24,128]{2,1,0:T(8,128)S(1)} %get-tuple-element.17.k_ref, f32[8,16,8,128]{3,2,1,0:T(8,128)S(1)} %get-tuple-element.18.f_ref, f32[4,16,8,128]{3,2,1,0:T(8,128)S(1)} %collective-permute-done.1.fb_ref, ...), custom_call_target="tpu_custom_call" | custom-call | flops 5898240 | bytes 1769472 | tf_op jit(solution)/shard_map/pallas_call | solution.py:50
  78.4 2.4 %collective-permute-start.6 = (f32[16,8,128]{2,1,0:T(8,128)S(1)}, f32[16,8,128]{2,1,0:T(8,128)S(1)}, u32[]{:S(2)}, u32[]{:S(2)}) collective-permute-start(f32[16,8,128]{2,1,0:T(8,128)S(1)} %get-tuple-element.23.own_ref), channel_id=1, source_target_pairs={{0,2},{2,4},{4,6},{6,22},{22,20},{20,18},{18,16},{16,32},{32,34},{... | collective-permute-start | bytes 196616 | tf_op jit(solution)/shard_map/ppermute | solution.py:361
  80.8 1.3 collective-permute-start.7
  82.1 3.8 %collective-permute-done.7.above_ref = f32[16,8,128]{2,1,0:T(8,128)S(1)} collective-permute-done((f32[16,8,128]{2,1,0:T(8,128)S(1)}, f32[16,8,128]{2,1,0:T(8,128)S(1)}, u32[]{:S(2)}, u32[]{:S(2)}) %collective-permute-start.7) | collective-permute-done | bytes 65568 | tf_op jit(solution)/shard_map/ppermute | solution.py:362
  85.9 3.1 %shard_map.49 = (f32[2,7,4,8,128]{4,3,2,1,0:T(8,128)}, f32[16,8,128]{2,1,0:T(8,128)S(1)}) custom-call(s32[1]{0:T(128)} %bitcast.2.core_ref, f32[16,24,128]{2,1,0:T(8,128)S(1)} %get-tuple-element.17.k_ref, f32[8,16,8,128]{3,2,1,0:T(8,128)S(1)} %get-tuple-element.18.f_ref, f32[4,16,8,128]{3,2,1,0:T(8,128)S(1)} %collective-permute-done.1.fb_ref, ...), custom_call_target="tpu_custom_call" | custom-call | flops 5898240 | bytes 2064388 | tf_op jit(solution)/shard_map/pallas_call | solution.py:50
  88.9 3.4 %all-to-all-start.2 = ((f32[2,7,4,8,128]{4,3,2,1,0:T(8,128)}), f32[2,7,4,8,128]{4,3,2,1,0:T(8,128)S(1)}, u32[]{:S(2)}, u32[]{:S(2)}) async-start(f32[2,7,4,8,128]{4,3,2,1,0:T(8,128)} %get-tuple-element.28), calls=%async_computation.2 | async-start | bytes 458752 | tf_op jit(solution)/shard_map/all_to_all | solution.py:381
  92.4 4.0 %collective-permute-start.8 = (f32[16,8,128]{2,1,0:T(8,128)S(1)}, f32[16,8,128]{2,1,0:T(8,128)S(1)}, u32[]{:S(2)}, u32[]{:S(2)}) collective-permute-start(f32[16,8,128]{2,1,0:T(8,128)S(1)} %get-tuple-element.25.own_ref.res_ref), channel_id=1, source_target_pairs={{0,2},{2,4},{4,6},{6,22},{22,20},{20,18},{18,16},{16,32},{32,34},{... | collective-permute-start | bytes 196616 | tf_op jit(solution)/shard_map/ppermute | solution.py:361
  96.4 1.3 collective-permute-start.9
  97.7 3.7 %collective-permute-done.9.above_ref = f32[16,8,128]{2,1,0:T(8,128)S(1)} collective-permute-done((f32[16,8,128]{2,1,0:T(8,128)S(1)}, f32[16,8,128]{2,1,0:T(8,128)S(1)}, u32[]{:S(2)}, u32[]{:S(2)}) %collective-permute-start.9) | collective-permute-done | bytes 65568 | tf_op jit(solution)/shard_map/ppermute | solution.py:362
  101.4 2.4 %shard_map.50 = (f32[4,16,8,128]{3,2,1,0:T(8,128)S(1)}, f32[16,8,128]{2,1,0:T(8,128)S(1)}) custom-call(f32[16,24,128]{2,1,0:T(8,128)S(1)} %get-tuple-element.17.k_ref, f32[16,8,128]{2,1,0:T(8,128)S(1)} %get-tuple-element.25.own_ref.res_ref, f32[16,8,128]{2,1,0:T(8,128)S(1)} %collective-permute-done.8.below_ref, ...), custom_call_target="tpu_custom_call" | custom-call | flops 5898240 | bytes 720896 | tf_op jit(solution)/shard_map/pallas_call | solution.py:50
  103.8 3.7 %collective-permute-start.10 = (f32[16,8,128]{2,1,0:T(8,128)S(1)}, f32[16,8,128]{2,1,0:T(8,128)S(1)}, u32[]{:S(2)}, u32[]{:S(2)}) collective-permute-start(f32[16,8,128]{2,1,0:T(8,128)S(1)} %get-tuple-element.26.own_ref), channel_id=1, source_target_pairs={{0,2},{2,4},{4,6},{6,22},{22,20},{20,18},{18,16},{16,32},{32,34},{... | collective-permute-start | bytes 196616 | tf_op jit(solution)/shard_map/ppermute | solution.py:361
  107.4 1.3 collective-permute-start.11
  108.8 3.9 %collective-permute-done.11.above_ref = f32[16,8,128]{2,1,0:T(8,128)S(1)} collective-permute-done((f32[16,8,128]{2,1,0:T(8,128)S(1)}, f32[16,8,128]{2,1,0:T(8,128)S(1)}, u32[]{:S(2)}, u32[]{:S(2)}) %collective-permute-start.11) | collective-permute-done | bytes 65568 | tf_op jit(solution)/shard_map/ppermute | solution.py:362
  112.7 2.7 %shard_map.51 = f32[16,4,8,128]{3,2,1,0:T(8,128)S(1)} custom-call(s32[2]{0:T(128)S(1)} %pad_add_fusion.place_ref, f32[16,24,128]{2,1,0:T(8,128)S(1)} %get-tuple-element.17.k_ref, f32[16,8,128]{2,1,0:T(8,128)S(1)} %get-tuple-element.26.own_ref, f32[16,8,128]{2,1,0:T(8,128)S(1)} %collective-permute-done.10.below_ref, ...), custom_call_target="tpu_custom_call" | custom-call | flops 5898240 | bytes 983048 | tf_op jit(solution)/shard_map/pallas_call | solution.py:50
  115.5 34.4 %all_to_all.21.got_ref = f32[16,4,8,128]{3,2,1,0:T(8,128)S(1)} all-to-all(f32[16,4,8,128]{3,2,1,0:T(8,128)S(1)} %shard_map.51), channel_id=1, replica_groups=mesh['x'=4,'zh'=2,'zl'=4,'core'=2,'y'=4,'zhi'=2] {'x','zh','zhi'}, dimensions={0} | all-to-all | bytes 524288 | tf_op jit(solution)/shard_map/all_to_all | solution.py:392
  149.9 24.7 %all_to_all.22.got_ref = f32[32,2,8,128]{3,2,1,0:T(8,128)S(1)} all-to-all(f32[32,2,8,128]{3,2,1,0:T(8,128)S(1)} %shard_map.52), channel_id=1, replica_groups=mesh['x'=4,'zh'=2,'zl'=4,'core'=2,'y'=4,'zhi'=2] {'zl','core','y'}, dimensions={0} | all-to-all | bytes 524288 | tf_op jit(solution)/shard_map/all_to_all | solution.py:394
  174.6 0.7 shard_map.53
  (17 shorter events, 0.3 us)
Async XLA Ops:
  0.0 0.9 copy-start
  0.9 0.9 copy-start.2
  1.9 0.9 copy-start.3
  2.8 0.9 copy-start.4
  56.6 4.1 %collective-permute-start = (f32[8,8,2,8,128]{4,3,2,1,0:T(8,128)S(1)}, f32[8,8,2,8,128]{4,3,2,1,0:T(8,128)S(1)}, u32[]{:S(2)}, u32[]{:S(2)}) collective-permute-start(f32[8,8,2,8,128]{4,3,2,1,0:T(8,128)S(1)} %bitcast.7), channel_id=1, source_target_pairs={{0,8},{8,0},{1,9},{9,1},{2,10},{10,2},{3,11},{11,3},{4,12},{12,4},... | collective-permute-start | bytes 1572872 | tf_op jit(solution)/shard_map/ppermute | solution.py:351
  60.8 5.9 %collective-permute-start.3 = (f32[16,8,128]{2,1,0:T(8,128)S(1)}, f32[16,8,128]{2,1,0:T(8,128)S(1)}, u32[]{:S(2)}, u32[]{:S(2)}) collective-permute-start(f32[16,8,128]{2,1,0:T(8,128)S(1)} %get-tuple-element.22.g_ref), channel_id=1, source_target_pairs={{0,64},{64,128},{128,192},{192,256},{256,320},{320,384},{384,448},... | collective-permute-start | bytes 196616 | tf_op jit(solution)/shard_map/ppermute | solution.py:366
  64.0 11.9 %collective-permute-start.1 = (f32[4,16,8,128]{3,2,1,0:T(8,128)S(1)}, f32[4,16,8,128]{3,2,1,0:T(8,128)S(1)}, u32[]{:S(2)}, u32[]{:S(2)}) collective-permute-start(f32[4,16,8,128]{3,2,1,0:T(8,128)S(1)} %get-tuple-element.19), channel_id=1, source_target_pairs={{0,2},{2,4},{4,6},{6,22},{22,20},{20,18},{18,16},{16,32},{32,34},{... | collective-permute-start | bytes 786440 | tf_op jit(solution)/shard_map/ppermute | solution.py:361
  65.3 10.6 %collective-permute-start.2 = (f32[4,16,8,128]{3,2,1,0:T(8,128)S(1)}, f32[4,16,8,128]{3,2,1,0:T(8,128)S(1)}, u32[]{:S(2)}, u32[]{:S(2)}) collective-permute-start(f32[4,16,8,128]{3,2,1,0:T(8,128)S(1)} %get-tuple-element.20), channel_id=1, source_target_pairs={{2,0},{4,2},{6,4},{22,6},{20,22},{18,20},{16,18},{32,16},{34,32},{... | collective-permute-start | bytes 786440 | tf_op jit(solution)/shard_map/ppermute | solution.py:362
  66.7 5.5 %collective-permute-start.4 = (f32[16,8,128]{2,1,0:T(8,128)S(1)}, f32[16,8,128]{2,1,0:T(8,128)S(1)}, u32[]{:S(2)}, u32[]{:S(2)}) collective-permute-start(f32[16,8,128]{2,1,0:T(8,128)S(1)} %broadcast_select_fusion.own_ref), channel_id=1, source_target_pairs={{0,2},{2,4},{4,6},{6,22},{22,20},{20,18},{18,16},{16,32},{32,34},{... | collective-permute-start | bytes 196616 | tf_op jit(solution)/shard_map/ppermute | solution.py:361
  70.7 5.3 %collective-permute-start.5 = (f32[16,8,128]{2,1,0:T(8,128)S(1)}, f32[16,8,128]{2,1,0:T(8,128)S(1)}, u32[]{:S(2)}, u32[]{:S(2)}) collective-permute-start(f32[16,8,128]{2,1,0:T(8,128)S(1)} %broadcast_select_fusion.own_ref), channel_id=1, source_target_pairs={{2,0},{4,2},{6,4},{22,6},{20,22},{18,20},{16,18},{32,16},{34,32},{... | collective-permute-start | bytes 196616 | tf_op jit(solution)/shard_map/ppermute | solution.py:362
  78.4 3.7 %collective-permute-start.6 = (f32[16,8,128]{2,1,0:T(8,128)S(1)}, f32[16,8,128]{2,1,0:T(8,128)S(1)}, u32[]{:S(2)}, u32[]{:S(2)}) collective-permute-start(f32[16,8,128]{2,1,0:T(8,128)S(1)} %get-tuple-element.23.own_ref), channel_id=1, source_target_pairs={{0,2},{2,4},{4,6},{6,22},{22,20},{20,18},{18,16},{16,32},{32,34},{... | collective-permute-start | bytes 196616 | tf_op jit(solution)/shard_map/ppermute | solution.py:361
  80.8 5.1 %collective-permute-start.7 = (f32[16,8,128]{2,1,0:T(8,128)S(1)}, f32[16,8,128]{2,1,0:T(8,128)S(1)}, u32[]{:S(2)}, u32[]{:S(2)}) collective-permute-start(f32[16,8,128]{2,1,0:T(8,128)S(1)} %get-tuple-element.23.own_ref), channel_id=1, source_target_pairs={{2,0},{4,2},{6,4},{22,6},{20,22},{18,20},{16,18},{32,16},{34,32},{... | collective-permute-start | bytes 196616 | tf_op jit(solution)/shard_map/ppermute | solution.py:362
  88.9 26.5 %all-to-all-start.2 = ((f32[2,7,4,8,128]{4,3,2,1,0:T(8,128)}), f32[2,7,4,8,128]{4,3,2,1,0:T(8,128)S(1)}, u32[]{:S(2)}, u32[]{:S(2)}) async-start(f32[2,7,4,8,128]{4,3,2,1,0:T(8,128)} %get-tuple-element.28), calls=%async_computation.2 | async-start | bytes 458752 | tf_op jit(solution)/shard_map/all_to_all | solution.py:381
  92.4 5.3 %collective-permute-start.8 = (f32[16,8,128]{2,1,0:T(8,128)S(1)}, f32[16,8,128]{2,1,0:T(8,128)S(1)}, u32[]{:S(2)}, u32[]{:S(2)}) collective-permute-start(f32[16,8,128]{2,1,0:T(8,128)S(1)} %get-tuple-element.25.own_ref.res_ref), channel_id=1, source_target_pairs={{0,2},{2,4},{4,6},{6,22},{22,20},{20,18},{18,16},{16,32},{32,34},{... | collective-permute-start | bytes 196616 | tf_op jit(solution)/shard_map/ppermute | solution.py:361
  96.4 5.0 %collective-permute-start.9 = (f32[16,8,128]{2,1,0:T(8,128)S(1)}, f32[16,8,128]{2,1,0:T(8,128)S(1)}, u32[]{:S(2)}, u32[]{:S(2)}) collective-permute-start(f32[16,8,128]{2,1,0:T(8,128)S(1)} %get-tuple-element.25.own_ref.res_ref), channel_id=1, source_target_pairs={{2,0},{4,2},{6,4},{22,6},{20,22},{18,20},{16,18},{32,16},{34,32},{... | collective-permute-start | bytes 196616 | tf_op jit(solution)/shard_map/ppermute | solution.py:362
  103.8 5.0 %collective-permute-start.10 = (f32[16,8,128]{2,1,0:T(8,128)S(1)}, f32[16,8,128]{2,1,0:T(8,128)S(1)}, u32[]{:S(2)}, u32[]{:S(2)}) collective-permute-start(f32[16,8,128]{2,1,0:T(8,128)S(1)} %get-tuple-element.26.own_ref), channel_id=1, source_target_pairs={{0,2},{2,4},{4,6},{6,22},{22,20},{20,18},{18,16},{16,32},{32,34},{... | collective-permute-start | bytes 196616 | tf_op jit(solution)/shard_map/ppermute | solution.py:361
  107.4 5.3 %collective-permute-start.11 = (f32[16,8,128]{2,1,0:T(8,128)S(1)}, f32[16,8,128]{2,1,0:T(8,128)S(1)}, u32[]{:S(2)}, u32[]{:S(2)}) collective-permute-start(f32[16,8,128]{2,1,0:T(8,128)S(1)} %get-tuple-element.26.own_ref), channel_id=1, source_target_pairs={{2,0},{4,2},{6,4},{22,6},{20,22},{18,20},{16,18},{32,16},{34,32},{... | collective-permute-start | bytes 196616 | tf_op jit(solution)/shard_map/ppermute | solution.py:362
  149.9 24.8 %copy-start.1 = (f32[1,2,192,128]{3,2,1,0:T(8,128)S(1)}, f32[1,2,192,128]{3,2,1,0:T(8,128)}, u32[]{:S(2)}) copy-start(f32[1,2,192,128]{3,2,1,0:T(8,128)} %param.4) | copy-start | bytes 589828

commit v3 on v2

v3 whole, which is shorter than its diff:
```python
import functools

import jax
import jax.numpy as jnp
from jax import lax
from jax.experimental import pallas as pl
from jax.experimental.pallas import tpu as pltpu
from jax.sharding import Mesh, PartitionSpec as P

SWEEPS = 2
F32 = jnp.float32

damping = 0.8
step_size = 0.5
coarse_size = 4.0
z_weight = 8.0

AXES = ("x", "zh", "zl", "core", "y", "zhi")
SIZES = (4, 2, 4, 2, 4, 2)
BLOCK = ("zl", "core", "y", "zhi")
BLOCKS = ("x", "zh")
NB = 8
NZ = 16
ROWS = 8
TILES = 24
CHIPS = 16
SIDE = 8
HALO = 2 * ROWS
WIN = ROWS + 2 * HALO
LANES = 128


def chip_order(zl, y):
    return zl * 4 + (y if zl % 2 == 0 else 3 - y)


def block_index(zl, core, y, zhi):
    return ((zl * 2 + core) * 4 + y) * 2 + zhi


def neighbours(step):
    place = {chip_order(zl, y): zl * 4 + y for zl in range(4) for y in range(4)}
    return [(place[m], place[m + step]) for m in range(CHIPS) if 0 <= m + step < CHIPS]


def call(body, outs, *args, scratch=(), smem=0, flops=0):
    specs = [pl.BlockSpec(memory_space=pltpu.SMEM)] * smem
    specs += [pl.BlockSpec(memory_space=pltpu.VMEM)] * (len(args) - smem)
    out_specs = [pl.BlockSpec(memory_space=pltpu.VMEM)] * len(outs)
    size = sum(4 * a.size for a in args) + sum(4 * o.size for o in outs)
    return pl.pallas_call(
        body,
        out_shape=list(outs),
        in_specs=specs,
        out_specs=out_specs,
        scratch_shapes=list(scratch),
        compiler_params=pltpu.CompilerParams(vmem_limit_bytes=32 * 1024 * 1024),
        cost_estimate=pl.CostEstimate(flops=flops, bytes_accessed=size, transcendentals=0),
    )(*args)


def sds(*shape):
    return jax.ShapeDtypeStruct(shape, F32)


def scatter_body(j_ref, src_hbm, guess_hbm, cond_hbm, init_hbm, out_ref, src_ref, extra_ref, sems):
    place = j_ref[0]
    zero = jnp.zeros((ROWS, LANES), F32)
    source_copy = pltpu.make_async_copy(src_hbm, src_ref, sems.at[0])
    source_copy.start()

    @pl.when((place != 3) & (place < 6))
    def _():
        pltpu.make_async_copy(cond_hbm, extra_ref, sems.at[1]).start()

    @pl.when(place == 3)
    def _():
        pltpu.make_async_copy(init_hbm, extra_ref, sems.at[1]).start()

    @pl.when(place > 5)
    def _():
        pltpu.make_async_copy(guess_hbm, extra_ref, sems.at[1]).start()

    def each():
        for zl in range(4):
            for y in range(4):
                for zhi in range(2):
                    tile = SIDE * zhi + chip_order(zl, y)
                    for core in range(2):
                        yield block_index(zl, core, y, zhi), core, tile

    source_copy.wait()
    for at, core, tile in each():
        out_ref[at, 0] = src_ref[core, tile * ROWS : (tile + 1) * ROWS]
    pltpu.make_async_copy(guess_hbm, extra_ref, sems.at[1]).wait()

    def fill(shift):
        for at, core, tile in each():
            tile = tile + shift
            if 0 <= tile < TILES:
                out_ref[at, 1] = extra_ref[core, tile * ROWS : (tile + 1) * ROWS]
            else:
                out_ref[at, 1] = zero

    pl.when(place == 1)(functools.partial(fill, 1))
    pl.when(place == 2)(functools.partial(fill, -1))
    pl.when(place == 4)(functools.partial(fill, 2))
    pl.when(place == 5)(functools.partial(fill, -2))
    pl.when((place == 0) | (place == 3) | (place > 5))(functools.partial(fill, 0))


def pack_body(strip_ref, start_ref, up1_ref, up2_ref, down1_ref, down2_ref):
    row = lax.broadcasted_iota(jnp.int32, (ROWS, LANES), 0)
    for s in range(8):
        start_ref[s] = strip_ref[7, s, 1]
        for n in range(4):
            up1_ref[n, s] = strip_ref[n, s, 0]
            down1_ref[n, s] = strip_ref[n, s, 0]
        for phase, up_ref, down_ref, at in ((0, up2_ref, down2_ref, 0), (1, up1_ref, down1_ref, 4)):
            f = [strip_ref[4 * phase + n, s, 0] for n in range(4)]
            down_ref[at, s] = jnp.where(row < 7, f[0], pltpu.roll(f[3], 7, 0))
            down_ref[at + 1, s] = jnp.where(row < 5, f[1], pltpu.roll(f[2], 5, 0))
            up_ref[at, s] = jnp.where(row >= 1, f[0], pltpu.roll(f[3], 1, 0))
            up_ref[at + 1, s] = jnp.where(row >= 3, f[1], pltpu.roll(f[2], 3, 0))


def in_order(core_ref, body, mine, other):
    pl.when(core_ref[0] == 0)(functools.partial(body, (mine, other)))
    pl.when(core_ref[0] == 1)(functools.partial(body, (other, mine)))


def merge_body(core_ref, block_ref, half_ref, half2_ref, strip_ref, strip2_ref, out_ref):
    first = block_ref[0] == 0

    def body(halves):
        for z in range(NZ):
            half, strip = halves[z % 2]
            out_ref[z] = jnp.where(first, strip[3, z // 2, 1], half[z // 2])

    in_order(core_ref, body, (half_ref, strip_ref), (half2_ref, strip2_ref))


def load_diffusivity(core_ref, mine_ref, other_ref, k_s):
    def body(halves):
        for z in range(NZ):
            half, s = halves[z % 2], z // 2
            for place, at in ((5, 0), (2, 8), (0, 16), (1, 24), (4, 32)):
                k_s[z + 1, at : at + 8] = half[place, s, 1]

    in_order(core_ref, body, mine_ref, other_ref)
    zero = jnp.zeros((WIN, LANES), F32)
    k_s[0] = zero
    k_s[NZ + 1] = zero


def load_sources(core_ref, mine, other, f_s):
    zero = jnp.zeros((ROWS, LANES), F32)

    def body(halves):
        for z in range(NZ):
            (strip, halo), s = halves[z % 2], z // 2
            for n in range(8):
                f_s[n, z, 16:24] = strip[n, s, 0]
            for n in range(4):
                f_s[n, z, 8:16] = halo[n, s]
                f_s[n, z, 24:32] = halo[8 + n, s]
                f_s[4 + n, z, 0:8] = zero
                f_s[4 + n, z, 32:40] = zero
            for first, at, below, above in ((0, 0, 6, 14), (4, 8, 4, 12)):
                low, high = slice(at, at + 8), slice(32 - at, 40 - at)
                f_s[first, z, low] = halo[below, s]
                f_s[first + 1, z, low] = halo[below + 1, s]
                f_s[first + 2, z, low] = pltpu.roll(halo[below + 1, s], 5, 0)
                f_s[first + 3, z, low] = pltpu.roll(halo[below, s], 7, 0)
                f_s[first, z, high] = halo[above, s]
                f_s[first + 1, z, high] = halo[above + 1, s]
                f_s[first + 2, z, high] = pltpu.roll(halo[above + 1, s], 3, 0)
                f_s[first + 3, z, high] = pltpu.roll(halo[above, s], 1, 0)

    in_order(core_ref, body, mine, other)


def load_window(a_s, b_s, own_ref, below2_ref, below1_ref, above1_ref, above2_ref):
    zero = jnp.zeros((WIN, LANES), F32)
    for ref in (a_s, b_s):
        ref[0] = zero
        ref[NZ + 1] = zero
    for z in range(NZ):
        for n, ref in enumerate((below2_ref, below1_ref, own_ref, above1_ref, above2_ref)):
            a_s[z + 1, 8 * n : 8 * n + 8] = ref[z]


def coefficients(rate, k_s, co_s):
    lane = lax.broadcasted_iota(jnp.int32, (WIN, LANES), 1)
    first = lane == 0
    last = lane == LANES - 1

    def layer(z, carry):
        k = k_s[z + 1]
        side = 0.5 * rate
        tall = 0.5 * rate * z_weight
        c = [
            tall * (k + k_s[z]),
            tall * (k + k_s[z + 2]),
            side * (k + pltpu.roll(k, 1, 0)),
            side * (k + pltpu.roll(k, WIN - 1, 0)),
            side * (k + jnp.where(first, 0.0, pltpu.roll(k, 1, 1))),
            side * (k + jnp.where(last, 0.0, pltpu.roll(k, LANES - 1, 1))),
        ]
        total = ((c[0] + c[1]) + (c[2] + c[3])) + (c[4] + c[5])
        d = jnp.where(k > 0.0, damping / (1.0 + total), 0.0)
        co_s[0, z] = c[0] * d
        co_s[1, z] = c[1] * d
        co_s[2, z] = c[2] * d
        co_s[3, z] = c[3] * d
        co_s[4, z] = jnp.where(first, 0.0, c[4] * d)
        co_s[5, z] = jnp.where(last, 0.0, c[5] * d)
        co_s[6, z] = d
        return carry

    lax.fori_loop(0, NZ, layer, 0)


def one_sweep(src, dst, co_s, db_s, rows):
    tall = rows.stop - rows.start
    for z in range(NZ):
        w = src[z + 1, rows]
        acc = (db_s[z, rows] + (1.0 - damping) * w) + (
            co_s[0, z, rows] * src[z, rows] + co_s[1, z, rows] * src[z + 2, rows]
        )
        acc = acc + (
            co_s[2, z, rows] * pltpu.roll(w, 1, 0) + co_s[3, z, rows] * pltpu.roll(w, tall - 1, 0)
        )
        acc = acc + (
            co_s[4, z, rows] * pltpu.roll(w, 1, 1) + co_s[5, z, rows] * pltpu.roll(w, LANES - 1, 1)
        )
        dst[z + 1, rows] = acc


def rows_at(step):
    return slice(0, WIN) if step < 4 else slice(ROWS, WIN - ROWS)


def fine_body(
    core_ref, strip_ref, strip2_ref, halo_ref, halo2_ref, own_ref, below2_ref, below1_ref, above1_ref,
    above2_ref, out_ref, res_ref, k_s, co_s, a_s, b_s, db_s, f_s, v_s,
):
    load_diffusivity(core_ref, strip_ref, strip2_ref, k_s)
    load_sources(core_ref, (strip_ref, halo_ref), (strip2_ref, halo2_ref), f_s)
    load_window(a_s, b_s, own_ref, below2_ref, below1_ref, above1_ref, above2_ref)
    coefficients(step_size, k_s, co_s)
    for n in range(8):
        rows = rows_at(n)
        for z in range(NZ):
            db_s[z, rows] = co_s[6, z, rows] * (a_s[z + 1, rows] + step_size * f_s[n, z, rows])
        one_sweep(a_s, b_s, co_s, db_s, rows)
        one_sweep(b_s, a_s, co_s, db_s, rows)
        for z in range(NZ):
            v_s[n, z] = a_s[z + 1, 16:24]

    def subtract(halves):
        for z in range(NZ):
            res_ref[z] = v_s[7, z] - halves[z % 2][7, z // 2, 1]

    in_order(core_ref, subtract, strip_ref, strip2_ref)
    core = core_ref[0]
    for y in range(4):
        for zhi in range(2):
            for n in range(7):
                out_ref[zhi, n, y] = v_s[n, 2 * (2 * y + zhi) + core]


def powers_body(
    core_ref, place_ref, strip_ref, strip2_ref, own_ref, below2_ref, below1_ref, above1_ref, above2_ref,
    out_ref, k_s, co_s, a_s, b_s, db_s, pow_s,
):
    load_diffusivity(core_ref, strip_ref, strip2_ref, k_s)
    load_window(a_s, b_s, own_ref, below2_ref, below1_ref, above1_ref, above2_ref)
    coefficients(coarse_size, k_s, co_s)
    for z in range(NZ):
        pow_s[0, z] = own_ref[z]
    for n in range(NB - 1):
        rows = rows_at(n)
        for z in range(NZ):
            db_s[z, rows] = co_s[6, z, rows] * a_s[z + 1, rows]
        one_sweep(a_s, b_s, co_s, db_s, rows)
        one_sweep(b_s, a_s, co_s, db_s, rows)
        for z in range(NZ):
            pow_s[1 + n, z] = a_s[z + 1, 16:24]
    core, c = core_ref[0], place_ref[0]
    for b in range(NB):
        power = jnp.clip(b - c, 0, NB - 1)
        live = b >= c
        for y in range(4):
            for zhi in range(2):
                value = pow_s[power, 2 * (2 * y + zhi) + core]
                out_ref[2 * b + zhi, y] = jnp.where(live, value, 0.0)


SWEEP_SCRATCH = (
    pltpu.VMEM((NZ + 2, WIN, LANES), F32),
    pltpu.VMEM((7, NZ, WIN, LANES), F32),
    pltpu.VMEM((NZ + 2, WIN, LANES), F32),
    pltpu.VMEM((NZ + 2, WIN, LANES), F32),
    pltpu.VMEM((NZ, WIN, LANES), F32),
)


def collect_body(got_ref, v_ref, out_ref):
    for side in range(2):
        for y in range(4):
            total = got_ref[side, y]
            for b in range(1, NB):
                total = total + got_ref[2 * b + side, y]
            out_ref[7 * 4 + y, side] = total
            for n in range(7):
                out_ref[n * 4 + y, side] = v_ref[side, n, y]


def home_body(j_ref, got_ref, guess_ref, out_ref):
    last = j_ref[0] == 7

    def write(add):
        for tile in range(TILES):
            zhi = 0 if tile < TILES // 2 else 1
            m = tile - SIDE * zhi
            zl, y = m // 4, m % 4
            if zl % 2 == 1:
                y = 3 - y
            rows = slice(tile * ROWS, (tile + 1) * ROWS)
            for core in range(2):
                value = got_ref[(zl * 2 + core) * 4 + y, zhi]
                if add:
                    value = guess_ref[core, rows] + value
                out_ref[core, rows] = value

    pl.when(last)(functools.partial(write, True))
    pl.when(jnp.logical_not(last))(functools.partial(write, False))


def on_device(guess, source, diffusivity, initial):
    guess = guess[0]
    source = source[0]
    core = lax.axis_index("core")
    place = lax.axis_index(("zl", "core"))[None]
    block = lax.axis_index(BLOCKS)

    sent = pl.pallas_call(
        scatter_body,
        out_shape=sds(64, 2, ROWS, LANES),
        in_specs=[pl.BlockSpec(memory_space=pltpu.SMEM)] + [pl.BlockSpec(memory_space=pltpu.HBM)] * 4,
        out_specs=pl.BlockSpec(memory_space=pltpu.VMEM),
        scratch_shapes=[
            pltpu.VMEM((2, TILES * ROWS, LANES), F32),
            pltpu.VMEM((2, TILES * ROWS, LANES), F32),
            pltpu.SemaphoreType.DMA((2,)),
        ],
        compiler_params=pltpu.CompilerParams(vmem_limit_bytes=60 * 1024 * 1024),
    )(place, source, guess, diffusivity, initial)
    strips = lax.all_to_all(sent, BLOCK, 0, 0, tiled=True).reshape(8, 8, 2, ROWS, LANES)

    def swap(mine):
        return lax.ppermute(mine, "core", [(0, 1), (1, 0)])

    def along(mine, step):
        return lax.ppermute(mine, ("zl", "y"), neighbours(step))

    def exchange(mine):
        return [along(mine, step) for step in (2, 1, -1, -2)]

    half = [sds(8, ROWS, LANES)]
    messages = [sds(6, 8, ROWS, LANES), sds(2, 8, ROWS, LANES)] * 2
    start, up1, up2, down1, down2 = call(pack_body, half + messages, strips)
    shifted = lax.ppermute(start, BLOCKS, [(b, b + 1) for b in range(NB - 1)])
    halos = jnp.concatenate([along(up1, 1), along(up2, 2), along(down1, -1), along(down2, -2)])
    strips2 = swap(strips)
    halos2 = swap(halos)
    (v0,) = call(
        merge_body, [sds(NZ, ROWS, LANES)],
        core[None], block[None], shifted, swap(shifted), strips, strips2, smem=2,
    )
    flops = 16 * NZ * WIN * LANES * 15
    v, residual = call(
        fine_body, [sds(2, 7, 4, ROWS, LANES), sds(NZ, ROWS, LANES)],
        core[None], strips, strips2, halos, halos2, v0, *exchange(v0), smem=1,
        scratch=SWEEP_SCRATCH + (pltpu.VMEM((8, NZ, WIN, LANES), F32), pltpu.VMEM((8, NZ, ROWS, LANES), F32)),
        flops=flops,
    )
    v = lax.all_to_all(v, "zhi", 0, 0, tiled=True)
    (powers,) = call(
        powers_body, [sds(2 * NB, 4, ROWS, LANES)],
        core[None], block[None], strips, strips2, residual, *exchange(residual), smem=2,
        scratch=SWEEP_SCRATCH + (pltpu.VMEM((NB, NZ, ROWS, LANES), F32),), flops=flops,
    )
    arrived = lax.all_to_all(powers, BLOCKS + ("zhi",), 0, 0, tiled=True)
    (back,) = call(collect_body, [sds(32, 2, ROWS, LANES)], arrived, v)
    returned = lax.all_to_all(back, ("zl", "core", "y"), 0, 0, tiled=True)
    (result,) = call(home_body, [sds(2, TILES * ROWS, LANES)], place, returned, guess, smem=1)
    return result[None]


def solution(mesh):
    fine = Mesh(mesh.devices.reshape(SIZES), AXES)
    tm = ("x", "zh", "zl", "core")
    space = ("y", "zhi")
    in_specs = (P(tm, space, None, None), P(tm, space, None, None), P(space, None, None), P(space, None, None))
    out_specs = P(tm, space, None, None)
    return jax.shard_map(on_device, mesh=fine, in_specs=in_specs, out_specs=out_specs, check_vma=False)
```

time: 176 us -> 188 us (1.068)
  starting transfers between devices: 31 us -> 40.9 us
  waiting for transfers between devices: 16.9 us -> 21.4 us
  local copies, waits for them, and re-layouts: 3.71 us -> 0.05 us
    ppermute x12 -> x16, starting transfers between devices: 27.6 us -> 37.4 us  [the longest x12 26.4 us: along(): return lax.ppermute(mine, ('zl', 'y'), neighbours(step))]
    all_to_all x1, blocking collectives: 34.4 us -> 39.4 us  [on_device(): arrived = lax.all_to_all(powers, BLOCKS + ('zhi',), 0, 0, tiled=True)]
    all_to_all x1, blocking collectives: 24.7 us -> 20 us  [on_device(): returned = lax.all_to_all(back, ('zl', 'core', 'y'), 0, 0, tiled=True)]
    ppermute x12 -> x16, waiting for transfers between devices: 16.9 us -> 21.4 us  [the longest x12 19.6 us: along(): return lax.ppermute(mine, ('zl', 'y'), neighbours(step))]
    unnamed x10 -> x5, local copies, waits for them, and re-layouts: 3.71 us -> 0.04 us
    pallas_call x7 -> x6, Pallas kernels: 11.4 us -> 10.4 us  [call(): pl.pallas_call(body, out_shape=list(outs), in_specs=specs, out_specs=out_...]
  transfers between devices with their start and end apart: 13 -> 17, of which waited for: 6 -> 8; matrix products, arithmetic and copies ran while one was open for 0% -> 0% of each run, Pallas kernels for 3% -> 2%
where the time goes in v3:
time: 188 us; the launch traced here: 187 us
  blocking collectives  112 us (60%)
  starting transfers between devices  40.9 us (22%)
  waiting for transfers between devices  21.4 us (11%)
  Pallas kernels  12.3 us (7%)
    all_to_all x1, blocking collectives, on_device(): lax.all_to_all(sent, BLOCK, 0, 0, tiled=True).reshape(8, 8, 2, ROWS, LANES)  52.5 us
    all_to_all x1, blocking collectives, on_device(): arrived = lax.all_to_all(powers, BLOCKS + ('zhi',), 0, 0, tiled=True)  39.4 us
    ppermute x12, starting transfers between devices, along(): return lax.ppermute(mine, ('zl', 'y'), neighbours(step))  26.4 us
    all_to_all x1, blocking collectives, on_device(): returned = lax.all_to_all(back, ('zl', 'core', 'y'), 0, 0, tiled=True)  20 us
    ppermute x12, waiting for transfers between devices, along(): return lax.ppermute(mine, ('zl', 'y'), neighbours(step))  19.6 us
    pallas_call x6, Pallas kernels, call(): pl.pallas_call(body, out_shape=list(outs), in_specs=specs, out_specs=out_...  10.4 us
    ppermute x3, starting transfers between devices, swap(): return lax.ppermute(mine, 'core', [(0, 1), (1, 0)])  8.77 us
  transfers between devices with their start and end apart: 17, of which 8 were waited for; matrix products, arithmetic and copies ran while one was open for 0% of the time, Pallas kernels for 2%

profile of v3, /device:TPU:1, one launch (start us, length us, event | category | flops | bytes accessed | tf_op | source)
XLA Modules:
  0.0 186.8 jit_solution(12109541922085191331)
XLA Ops:
  0.0 1.9 shard_map.46
  1.9 52.5 %all_to_all.20 = f32[64,2,8,128]{3,2,1,0:T(8,128)S(1)} all-to-all(f32[64,2,8,128]{3,2,1,0:T(8,128)} %shard_map.46), channel_id=1, replica_groups=mesh['x'=4,'zh'=2,'zl'=4,'core'=2,'y'=4,'zhi'=2] {'zl','core','y','zhi'}, dimensions={0} | all-to-all | bytes 1048576 | tf_op jit(solution)/shard_map/all_to_all | solution.py:360
  54.4 2.4 %collective-permute-start.1 = (f32[6,8,8,128]{3,2,1,0:T(8,128)S(1)}, f32[6,8,8,128]{3,2,1,0:T(8,128)S(1)}, u32[]{:S(2)}, u32[]{:S(2)}) collective-permute-start(f32[6,8,8,128]{3,2,1,0:T(8,128)S(1)} %get-tuple-element.12), channel_id=1, source_target_pairs={{0,2},{2,4},{4,6},{6,22},{22,20},{20,18},{18,16},{16,32},{32,34},{... | collective-permute-start | bytes 589832 | tf_op jit(solution)/shard_map/ppermute | solution.py:366
  56.8 2.7 %collective-permute-start = (f32[8,8,2,8,128]{4,3,2,1,0:T(8,128)S(1)}, f32[8,8,2,8,128]{4,3,2,1,0:T(8,128)S(1)}, u32[]{:S(2)}, u32[]{:S(2)}) collective-permute-start(f32[8,8,2,8,128]{4,3,2,1,0:T(8,128)S(1)} %bitcast.8), channel_id=1, source_target_pairs={{0,8},{8,0},{1,9},{9,1},{2,10},{10,2},{3,11},{11,3},{4,12},{12,4},... | collective-permute-start | bytes 1572872 | tf_op jit(solution)/shard_map/ppermute | solution.py:363
  59.5 3.4 %collective-permute-start.2 = (f32[2,8,8,128]{3,2,1,0:T(8,128)S(1)}, f32[2,8,8,128]{3,2,1,0:T(8,128)S(1)}, u32[]{:S(2)}, u32[]{:S(2)}) collective-permute-start(f32[2,8,8,128]{3,2,1,0:T(8,128)S(1)} %get-tuple-element.13), channel_id=1, source_target_pairs={{0,4},{2,6},{4,22},{6,20},{22,18},{20,16},{18,32},{16,34},{32,36},... | collective-permute-start | bytes 196616 | tf_op jit(solution)/shard_map/ppermute | solution.py:366
  62.9 1.3 collective-permute-start.3
  64.2 1.3 collective-permute-start.4
  65.6 7.0 %collective-permute-done.3 = f32[6,8,8,128]{3,2,1,0:T(8,128)S(1)} collective-permute-done((f32[6,8,8,128]{3,2,1,0:T(8,128)S(1)}, f32[6,8,8,128]{3,2,1,0:T(8,128)S(1)}, u32[]{:S(2)}, u32[]{:S(2)}) %collective-permute-start.3) | collective-permute-done | bytes 196640 | tf_op jit(solution)/shard_map/ppermute | solution.py:366
  72.6 0.3 collective-permute-done.4
  72.9 3.3 %collective-permute-start.5 = (f32[16,8,8,128]{3,2,1,0:T(8,128)S(1)}, f32[16,8,8,128]{3,2,1,0:T(8,128)S(1)}, u32[]{:S(2)}, u32[]{:S(2)}) collective-permute-start(f32[16,8,8,128]{3,2,1,0:T(8,128)S(1)} %constant_dynamic-update-slice_fusion.halo_ref), channel_id=1, source_target_pairs={{0,8},{8,0},{1,9},{9,1},{2,10},{10,2},{3,11},{11,3},{4,12},{12,4},... | collective-permute-start | bytes 1572872 | tf_op jit(solution)/shard_map/ppermute | solution.py:363
  76.2 2.2 %collective-permute-start.6 = (f32[8,8,128]{2,1,0:T(8,128)S(1)}, f32[8,8,128]{2,1,0:T(8,128)S(1)}, u32[]{:S(2)}, u32[]{:S(2)}) collective-permute-start(f32[8,8,128]{2,1,0:T(8,128)S(1)} %get-tuple-element.16), channel_id=1, source_target_pairs={{0,64},{64,128},{128,192},{192,256},{256,320},{320,384},{384,448},... | collective-permute-start | bytes 98312 | tf_op jit(solution)/shard_map/ppermute | solution.py:374
  78.5 1.0 collective-permute-done.6.half_ref
  79.5 2.8 %collective-permute-start.7 = (f32[8,8,128]{2,1,0:T(8,128)S(1)}, f32[8,8,128]{2,1,0:T(8,128)S(1)}, u32[]{:S(2)}, u32[]{:S(2)}) collective-permute-start(f32[8,8,128]{2,1,0:T(8,128)S(1)} %collective-permute-done.6.half_ref), channel_id=1, source_target_pairs={{0,8},{8,0},{1,9},{9,1},{2,10},{10,2},{3,11},{11,3},{4,12},{12,4},... | collective-permute-start | bytes 98312 | tf_op jit(solution)/shard_map/ppermute | solution.py:363
  82.2 0.8 collective-permute-done.7.half2_ref
  83.1 4.5 %collective-permute-start.8 = (f32[16,8,128]{2,1,0:T(8,128)S(1)}, f32[16,8,128]{2,1,0:T(8,128)S(1)}, u32[]{:S(2)}, u32[]{:S(2)}) collective-permute-start(f32[16,8,128]{2,1,0:T(8,128)S(1)} %shard_map.48.own_ref), channel_id=1, source_target_pairs={{0,4},{2,6},{4,22},{6,20},{22,18},{20,16},{18,32},{16,34},{32,36},... | collective-permute-start | bytes 196616 | tf_op jit(solution)/shard_map/ppermute | solution.py:366
  87.7 1.3 collective-permute-start.9
  89.0 1.3 collective-permute-start.10
  90.3 1.3 collective-permute-start.11
  91.6 2.7 %collective-permute-done.10.above1_ref = f32[16,8,128]{2,1,0:T(8,128)S(1)} collective-permute-done((f32[16,8,128]{2,1,0:T(8,128)S(1)}, f32[16,8,128]{2,1,0:T(8,128)S(1)}, u32[]{:S(2)}, u32[]{:S(2)}) %collective-permute-start.10) | collective-permute-done | bytes 65568 | tf_op jit(solution)/shard_map/ppermute | solution.py:366
  94.3 3.9 %collective-permute-done.11.above2_ref = f32[16,8,128]{2,1,0:T(8,128)S(1)} collective-permute-done((f32[16,8,128]{2,1,0:T(8,128)S(1)}, f32[16,8,128]{2,1,0:T(8,128)S(1)}, u32[]{:S(2)}, u32[]{:S(2)}) %collective-permute-start.11) | collective-permute-done | bytes 65568 | tf_op jit(solution)/shard_map/ppermute | solution.py:366
  98.2 5.5 %shard_map.49 = (f32[2,7,4,8,128]{4,3,2,1,0:T(8,128)}, f32[16,8,128]{2,1,0:T(8,128)S(1)}) custom-call(s32[1]{0:T(128)} %bitcast.1.core_ref, f32[8,8,2,8,128]{4,3,2,1,0:T(8,128)S(1)} %bitcast.10, f32[8,8,2,8,128]{4,3,2,1,0:T(8,128)S(1)} %collective-permute-done.strip2_ref, f32[16,8,8,128]{3,2,1,0:T(8,128)S(1)} %constant_dynamic-update-slice_fusion.halo_ref, ...), custom_call_target="tpu_custom_call" | custom-call | flops 19660800 | bytes 2719748 | tf_op jit(solution)/shard_map/pallas_call | solution.py:51
  103.6 3.4 %all-to-all-start.2 = ((f32[2,7,4,8,128]{4,3,2,1,0:T(8,128)}), f32[2,7,4,8,128]{4,3,2,1,0:T(8,128)S(1)}, u32[]{:S(2)}, u32[]{:S(2)}) async-start(f32[2,7,4,8,128]{4,3,2,1,0:T(8,128)} %get-tuple-element.18), calls=%async_computation.2 | async-start | bytes 458752 | tf_op jit(solution)/shard_map/all_to_all | solution.py:389
  107.1 4.3 %collective-permute-start.12 = (f32[16,8,128]{2,1,0:T(8,128)S(1)}, f32[16,8,128]{2,1,0:T(8,128)S(1)}, u32[]{:S(2)}, u32[]{:S(2)}) collective-permute-start(f32[16,8,128]{2,1,0:T(8,128)S(1)} %get-tuple-element.17.own_ref), channel_id=1, source_target_pairs={{0,4},{2,6},{4,22},{6,20},{22,18},{20,16},{18,32},{16,34},{32,36},... | collective-permute-start | bytes 196616 | tf_op jit(solution)/shard_map/ppermute | solution.py:366
  111.4 2.8 %collective-permute-start.13 = (f32[16,8,128]{2,1,0:T(8,128)S(1)}, f32[16,8,128]{2,1,0:T(8,128)S(1)}, u32[]{:S(2)}, u32[]{:S(2)}) collective-permute-start(f32[16,8,128]{2,1,0:T(8,128)S(1)} %get-tuple-element.17.own_ref), channel_id=1, source_target_pairs={{0,2},{2,4},{4,6},{6,22},{22,20},{20,18},{18,16},{16,32},{32,34},{... | collective-permute-start | bytes 196616 | tf_op jit(solution)/shard_map/ppermute | solution.py:366
  114.1 1.3 collective-permute-start.14
  115.4 1.3 collective-permute-start.15
  116.7 2.4 %collective-permute-done.14.above1_ref = f32[16,8,128]{2,1,0:T(8,128)S(1)} collective-permute-done((f32[16,8,128]{2,1,0:T(8,128)S(1)}, f32[16,8,128]{2,1,0:T(8,128)S(1)}, u32[]{:S(2)}, u32[]{:S(2)}) %collective-permute-start.14) | collective-permute-done | bytes 65568 | tf_op jit(solution)/shard_map/ppermute | solution.py:366
  119.1 3.3 %collective-permute-done.15.above2_ref = f32[16,8,128]{2,1,0:T(8,128)S(1)} collective-permute-done((f32[16,8,128]{2,1,0:T(8,128)S(1)}, f32[16,8,128]{2,1,0:T(8,128)S(1)}, u32[]{:S(2)}, u32[]{:S(2)}) %collective-permute-start.15) | collective-permute-done | bytes 65568 | tf_op jit(solution)/shard_map/ppermute | solution.py:366
  122.5 4.2 %shard_map.50 = f32[16,4,8,128]{3,2,1,0:T(8,128)S(1)} custom-call(s32[1]{0:T(128)} %bitcast.1.core_ref, s32[1]{0:T(128)} %bitcast.2.block_ref.place_ref, f32[8,8,2,8,128]{4,3,2,1,0:T(8,128)S(1)} %bitcast.11, f32[8,8,2,8,128]{4,3,2,1,0:T(8,128)S(1)} %collective-permute-done.strip2_ref, f32[16,8,128]{2,1,0:T(8,128)S(1)} %get-tuple-element.17.own_ref, ...), custom_call_target="tpu_custom_call" | custom-call | flops 19660800 | bytes 1638408 | tf_op jit(solution)/shard_map/pallas_call | solution.py:51
  126.6 39.4 %all_to_all.21.got_ref = f32[16,4,8,128]{3,2,1,0:T(8,128)S(1)} all-to-all(f32[16,4,8,128]{3,2,1,0:T(8,128)S(1)} %shard_map.50), channel_id=1, replica_groups=mesh['x'=4,'zh'=2,'zl'=4,'core'=2,'y'=4,'zhi'=2] {'x','zh','zhi'}, dimensions={0} | all-to-all | bytes 524288 | tf_op jit(solution)/shard_map/all_to_all | solution.py:395
  166.1 20.0 %all_to_all.22.got_ref = f32[32,2,8,128]{3,2,1,0:T(8,128)S(1)} all-to-all(f32[32,2,8,128]{3,2,1,0:T(8,128)S(1)} %shard_map.51), channel_id=1, replica_groups=mesh['x'=4,'zh'=2,'zl'=4,'core'=2,'y'=4,'zhi'=2] {'zl','core','y'}, dimensions={0} | all-to-all | bytes 524288 | tf_op jit(solution)/shard_map/all_to_all | solution.py:397
  186.1 0.7 shard_map.52
  (18 shorter events, 0.2 us)
Async XLA Ops:
  54.4 11.1 %collective-permute-start.1 = (f32[6,8,8,128]{3,2,1,0:T(8,128)S(1)}, f32[6,8,8,128]{3,2,1,0:T(8,128)S(1)}, u32[]{:S(2)}, u32[]{:S(2)}) collective-permute-start(f32[6,8,8,128]{3,2,1,0:T(8,128)S(1)} %get-tuple-element.12), channel_id=1, source_target_pairs={{0,2},{2,4},{4,6},{6,22},{22,20},{20,18},{18,16},{16,32},{32,34},{... | collective-permute-start | bytes 589832 | tf_op jit(solution)/shard_map/ppermute | solution.py:366
  56.8 26.2 %collective-permute-start = (f32[8,8,2,8,128]{4,3,2,1,0:T(8,128)S(1)}, f32[8,8,2,8,128]{4,3,2,1,0:T(8,128)S(1)}, u32[]{:S(2)}, u32[]{:S(2)}) collective-permute-start(f32[8,8,2,8,128]{4,3,2,1,0:T(8,128)S(1)} %bitcast.8), channel_id=1, source_target_pairs={{0,8},{8,0},{1,9},{9,1},{2,10},{10,2},{3,11},{11,3},{4,12},{12,4},... | collective-permute-start | bytes 1572872 | tf_op jit(solution)/shard_map/ppermute | solution.py:363
  59.5 6.1 %collective-permute-start.2 = (f32[2,8,8,128]{3,2,1,0:T(8,128)S(1)}, f32[2,8,8,128]{3,2,1,0:T(8,128)S(1)}, u32[]{:S(2)}, u32[]{:S(2)}) collective-permute-start(f32[2,8,8,128]{3,2,1,0:T(8,128)S(1)} %get-tuple-element.13), channel_id=1, source_target_pairs={{0,4},{2,6},{4,22},{6,20},{22,18},{20,16},{18,32},{16,34},{32,36},... | collective-permute-start | bytes 196616 | tf_op jit(solution)/shard_map/ppermute | solution.py:366
  62.9 9.6 %collective-permute-start.3 = (f32[6,8,8,128]{3,2,1,0:T(8,128)S(1)}, f32[6,8,8,128]{3,2,1,0:T(8,128)S(1)}, u32[]{:S(2)}, u32[]{:S(2)}) collective-permute-start(f32[6,8,8,128]{3,2,1,0:T(8,128)S(1)} %get-tuple-element.14), channel_id=1, source_target_pairs={{2,0},{4,2},{6,4},{22,6},{20,22},{18,20},{16,18},{32,16},{34,32},{... | collective-permute-start | bytes 589832 | tf_op jit(solution)/shard_map/ppermute | solution.py:366
  64.2 8.6 %collective-permute-start.4 = (f32[2,8,8,128]{3,2,1,0:T(8,128)S(1)}, f32[2,8,8,128]{3,2,1,0:T(8,128)S(1)}, u32[]{:S(2)}, u32[]{:S(2)}) collective-permute-start(f32[2,8,8,128]{3,2,1,0:T(8,128)S(1)} %get-tuple-element.15), channel_id=1, source_target_pairs={{4,0},{6,2},{22,4},{20,6},{18,22},{16,20},{32,18},{34,16},{36,32},... | collective-permute-start | bytes 196616 | tf_op jit(solution)/shard_map/ppermute | solution.py:366
  72.9 25.3 %collective-permute-start.5 = (f32[16,8,8,128]{3,2,1,0:T(8,128)S(1)}, f32[16,8,8,128]{3,2,1,0:T(8,128)S(1)}, u32[]{:S(2)}, u32[]{:S(2)}) collective-permute-start(f32[16,8,8,128]{3,2,1,0:T(8,128)S(1)} %constant_dynamic-update-slice_fusion.halo_ref), channel_id=1, source_target_pairs={{0,8},{8,0},{1,9},{9,1},{2,10},{10,2},{3,11},{11,3},{4,12},{12,4},... | collective-permute-start | bytes 1572872 | tf_op jit(solution)/shard_map/ppermute | solution.py:363
  76.2 3.3 %collective-permute-start.6 = (f32[8,8,128]{2,1,0:T(8,128)S(1)}, f32[8,8,128]{2,1,0:T(8,128)S(1)}, u32[]{:S(2)}, u32[]{:S(2)}) collective-permute-start(f32[8,8,128]{2,1,0:T(8,128)S(1)} %get-tuple-element.16), channel_id=1, source_target_pairs={{0,64},{64,128},{128,192},{192,256},{256,320},{320,384},{384,448},... | collective-permute-start | bytes 98312 | tf_op jit(solution)/shard_map/ppermute | solution.py:374
  79.5 3.6 %collective-permute-start.7 = (f32[8,8,128]{2,1,0:T(8,128)S(1)}, f32[8,8,128]{2,1,0:T(8,128)S(1)}, u32[]{:S(2)}, u32[]{:S(2)}) collective-permute-start(f32[8,8,128]{2,1,0:T(8,128)S(1)} %collective-permute-done.6.half_ref), channel_id=1, source_target_pairs={{0,8},{8,0},{1,9},{9,1},{2,10},{10,2},{3,11},{11,3},{4,12},{12,4},... | collective-permute-start | bytes 98312 | tf_op jit(solution)/shard_map/ppermute | solution.py:363
  83.1 8.5 %collective-permute-start.8 = (f32[16,8,128]{2,1,0:T(8,128)S(1)}, f32[16,8,128]{2,1,0:T(8,128)S(1)}, u32[]{:S(2)}, u32[]{:S(2)}) collective-permute-start(f32[16,8,128]{2,1,0:T(8,128)S(1)} %shard_map.48.own_ref), channel_id=1, source_target_pairs={{0,4},{2,6},{4,22},{6,20},{22,18},{20,16},{18,32},{16,34},{32,36},... | collective-permute-start | bytes 196616 | tf_op jit(solution)/shard_map/ppermute | solution.py:366
  87.7 3.9 %collective-permute-start.9 = (f32[16,8,128]{2,1,0:T(8,128)S(1)}, f32[16,8,128]{2,1,0:T(8,128)S(1)}, u32[]{:S(2)}, u32[]{:S(2)}) collective-permute-start(f32[16,8,128]{2,1,0:T(8,128)S(1)} %shard_map.48.own_ref), channel_id=1, source_target_pairs={{0,2},{2,4},{4,6},{6,22},{22,20},{20,18},{18,16},{16,32},{32,34},{... | collective-permute-start | bytes 196616 | tf_op jit(solution)/shard_map/ppermute | solution.py:366
  89.0 5.3 %collective-permute-start.10 = (f32[16,8,128]{2,1,0:T(8,128)S(1)}, f32[16,8,128]{2,1,0:T(8,128)S(1)}, u32[]{:S(2)}, u32[]{:S(2)}) collective-permute-start(f32[16,8,128]{2,1,0:T(8,128)S(1)} %shard_map.48.own_ref), channel_id=1, source_target_pairs={{2,0},{4,2},{6,4},{22,6},{20,22},{18,20},{16,18},{32,16},{34,32},{... | collective-permute-start | bytes 196616 | tf_op jit(solution)/shard_map/ppermute | solution.py:366
  90.3 7.9 %collective-permute-start.11 = (f32[16,8,128]{2,1,0:T(8,128)S(1)}, f32[16,8,128]{2,1,0:T(8,128)S(1)}, u32[]{:S(2)}, u32[]{:S(2)}) collective-permute-start(f32[16,8,128]{2,1,0:T(8,128)S(1)} %shard_map.48.own_ref), channel_id=1, source_target_pairs={{4,0},{6,2},{22,4},{20,6},{18,22},{16,20},{32,18},{34,16},{36,32},... | collective-permute-start | bytes 196616 | tf_op jit(solution)/shard_map/ppermute | solution.py:366
  103.6 23.0 %all-to-all-start.2 = ((f32[2,7,4,8,128]{4,3,2,1,0:T(8,128)}), f32[2,7,4,8,128]{4,3,2,1,0:T(8,128)S(1)}, u32[]{:S(2)}, u32[]{:S(2)}) async-start(f32[2,7,4,8,128]{4,3,2,1,0:T(8,128)} %get-tuple-element.18), calls=%async_computation.2 | async-start | bytes 458752 | tf_op jit(solution)/shard_map/all_to_all | solution.py:389
  107.1 9.6 %collective-permute-start.12 = (f32[16,8,128]{2,1,0:T(8,128)S(1)}, f32[16,8,128]{2,1,0:T(8,128)S(1)}, u32[]{:S(2)}, u32[]{:S(2)}) collective-permute-start(f32[16,8,128]{2,1,0:T(8,128)S(1)} %get-tuple-element.17.own_ref), channel_id=1, source_target_pairs={{0,4},{2,6},{4,22},{6,20},{22,18},{20,16},{18,32},{16,34},{32,36},... | collective-permute-start | bytes 196616 | tf_op jit(solution)/shard_map/ppermute | solution.py:366
  111.4 5.4 %collective-permute-start.13 = (f32[16,8,128]{2,1,0:T(8,128)S(1)}, f32[16,8,128]{2,1,0:T(8,128)S(1)}, u32[]{:S(2)}, u32[]{:S(2)}) collective-permute-start(f32[16,8,128]{2,1,0:T(8,128)S(1)} %get-tuple-element.17.own_ref), channel_id=1, source_target_pairs={{0,2},{2,4},{4,6},{6,22},{22,20},{20,18},{18,16},{16,32},{32,34},{... | collective-permute-start | bytes 196616 | tf_op jit(solution)/shard_map/ppermute | solution.py:366
  114.1 5.0 %collective-permute-start.14 = (f32[16,8,128]{2,1,0:T(8,128)S(1)}, f32[16,8,128]{2,1,0:T(8,128)S(1)}, u32[]{:S(2)}, u32[]{:S(2)}) collective-permute-start(f32[16,8,128]{2,1,0:T(8,128)S(1)} %get-tuple-element.17.own_ref), channel_id=1, source_target_pairs={{2,0},{4,2},{6,4},{22,6},{20,22},{18,20},{16,18},{32,16},{34,32},{... | collective-permute-start | bytes 196616 | tf_op jit(solution)/shard_map/ppermute | solution.py:366
  115.4 7.0 %collective-permute-start.15 = (f32[16,8,128]{2,1,0:T(8,128)S(1)}, f32[16,8,128]{2,1,0:T(8,128)S(1)}, u32[]{:S(2)}, u32[]{:S(2)}) collective-permute-start(f32[16,8,128]{2,1,0:T(8,128)S(1)} %get-tuple-element.17.own_ref), channel_id=1, source_target_pairs={{4,0},{6,2},{22,4},{20,6},{18,22},{16,20},{32,18},{34,16},{36,32},... | collective-permute-start | bytes 196616 | tf_op jit(solution)/shard_map/ppermute | solution.py:366
  166.1 20.0 %copy-start = (f32[1,2,192,128]{3,2,1,0:T(8,128)S(1)}, f32[1,2,192,128]{3,2,1,0:T(8,128)}, u32[]{:S(2)}) copy-start(f32[1,2,192,128]{3,2,1,0:T(8,128)} %param.4) | copy-start | bytes 589828

commit v4 on v2

v4 whole, which is shorter than its diff:
```python
import functools

import jax
import jax.numpy as jnp
from jax import lax
from jax.experimental import pallas as pl
from jax.experimental.pallas import tpu as pltpu
from jax.sharding import Mesh, PartitionSpec as P

SWEEPS = 2
F32 = jnp.float32

damping = 0.8
step_size = 0.5
coarse_size = 4.0
z_weight = 8.0

AXES = ("x", "zh", "zl", "core", "y", "zhi")
SIZES = (4, 2, 4, 2, 4, 2)
BLOCK = ("zl", "core", "y", "zhi")
BLOCKS = ("x", "zh")
NB = 8
NZ = 16
ROWS = 8
TILES = 24
CHIPS = 16
SIDE = 8
FINE = 3 * ROWS
WIDE = 5 * ROWS
LANES = 128


def chip_order(zl, y):
    return zl * 4 + (y if zl % 2 == 0 else 3 - y)


def block_index(zl, core, y, zhi):
    return ((zl * 2 + core) * 4 + y) * 2 + zhi


def neighbours(step):
    place = {chip_order(zl, y): zl * 4 + y for zl in range(4) for y in range(4)}
    return [(place[m], place[m + step]) for m in range(CHIPS) if 0 <= m + step < CHIPS]


def call(body, outs, *args, scratch=(), smem=0, flops=0):
    specs = [pl.BlockSpec(memory_space=pltpu.SMEM)] * smem
    specs += [pl.BlockSpec(memory_space=pltpu.VMEM)] * (len(args) - smem)
    out_specs = [pl.BlockSpec(memory_space=pltpu.VMEM)] * len(outs)
    size = sum(4 * a.size for a in args) + sum(4 * o.size for o in outs)
    return pl.pallas_call(
        body,
        out_shape=list(outs),
        in_specs=specs,
        out_specs=out_specs,
        scratch_shapes=list(scratch),
        compiler_params=pltpu.CompilerParams(vmem_limit_bytes=32 * 1024 * 1024),
        cost_estimate=pl.CostEstimate(flops=flops, bytes_accessed=size, transcendentals=0),
    )(*args)


def sds(*shape):
    return jax.ShapeDtypeStruct(shape, F32)


def scatter_body(j_ref, src_hbm, guess_hbm, cond_hbm, init_hbm, out_ref, src_ref, extra_ref, sems):
    place = j_ref[0]
    zero = jnp.zeros((ROWS, LANES), F32)
    source_copy = pltpu.make_async_copy(src_hbm, src_ref, sems.at[0])
    source_copy.start()

    @pl.when(place < 3)
    def _():
        pltpu.make_async_copy(cond_hbm, extra_ref, sems.at[1]).start()

    @pl.when((place > 2) & (place < 6))
    def _():
        pltpu.make_async_copy(init_hbm, extra_ref, sems.at[1]).start()

    @pl.when(place > 5)
    def _():
        pltpu.make_async_copy(guess_hbm, extra_ref, sems.at[1]).start()

    def each():
        for zl in range(4):
            for y in range(4):
                for zhi in range(2):
                    tile = SIDE * zhi + chip_order(zl, y)
                    for core in range(2):
                        yield block_index(zl, core, y, zhi), core, tile

    source_copy.wait()
    for at, core, tile in each():
        out_ref[at, 0] = src_ref[core, tile * ROWS : (tile + 1) * ROWS]
    pltpu.make_async_copy(guess_hbm, extra_ref, sems.at[1]).wait()

    def fill(shift):
        for at, core, tile in each():
            tile = tile + shift
            if 0 <= tile < TILES:
                out_ref[at, 1] = extra_ref[core, tile * ROWS : (tile + 1) * ROWS]
            else:
                out_ref[at, 1] = zero

    pl.when((place == 1) | (place == 4))(functools.partial(fill, 1))
    pl.when((place == 2) | (place == 5))(functools.partial(fill, -1))
    pl.when((place == 0) | (place == 3) | (place > 5))(functools.partial(fill, 0))


def pack_body(core_ref, own_ref, other_ref, f_ref, g_ref, k_ref, first_ref, up_ref, down_ref):
    def order(halves):
        for z in range(NZ):
            half, s = halves[z % 2], z // 2
            for n in range(8):
                f_ref[n, z] = half[n, s, 0]
            g_ref[z] = half[7, s, 1]
            for n, place in enumerate((2, 0, 1)):
                k_ref[z, 8 * n : 8 * n + 8] = half[place, s, 1]
                first_ref[z, 8 * n : 8 * n + 8] = half[3 + place, s, 1]
            up_ref[4, z] = half[2, s, 1]
            down_ref[4, z] = half[1, s, 1]

    pl.when(core_ref[0] == 0)(functools.partial(order, (own_ref, other_ref)))
    pl.when(core_ref[0] == 1)(functools.partial(order, (other_ref, own_ref)))
    row = lax.broadcasted_iota(jnp.int32, (ROWS, LANES), 0)
    for z in range(NZ):
        for phase in range(2):
            f = [f_ref[4 * phase + n, z] for n in range(4)]
            down_ref[2 * phase, z] = jnp.where(row < 7, f[0], pltpu.roll(f[3], 7, 0))
            down_ref[2 * phase + 1, z] = jnp.where(row < 5, f[1], pltpu.roll(f[2], 5, 0))
            up_ref[2 * phase, z] = jnp.where(row >= 1, f[0], pltpu.roll(f[3], 1, 0))
            up_ref[2 * phase + 1, z] = jnp.where(row >= 3, f[1], pltpu.roll(f[2], 3, 0))


def load_window(a_s, b_s, tiles):
    zero = jnp.zeros((a_s.shape[1], LANES), F32)
    for ref in (a_s, b_s):
        ref[0] = zero
        ref[NZ + 1] = zero
    for z in range(NZ):
        for n, tile in enumerate(tiles):
            a_s[z + 1, 8 * n : 8 * n + 8] = tile[z]


def load_diffusivity(k_s, parts):
    zero = jnp.zeros((k_s.shape[1], LANES), F32)
    k_s[0] = zero
    k_s[NZ + 1] = zero
    for z in range(NZ):
        at = 0
        for part in parts:
            tile = part(z)
            k_s[z + 1, at : at + tile.shape[0]] = tile
            at += tile.shape[0]


def coefficients(rate, k_s, co_s):
    tall_win = k_s.shape[1]
    lane = lax.broadcasted_iota(jnp.int32, (tall_win, LANES), 1)
    first = lane == 0
    last = lane == LANES - 1

    def layer(z, carry):
        k = k_s[z + 1]
        side = 0.5 * rate
        tall = 0.5 * rate * z_weight
        c = [
            tall * (k + k_s[z]),
            tall * (k + k_s[z + 2]),
            side * (k + pltpu.roll(k, 1, 0)),
            side * (k + pltpu.roll(k, tall_win - 1, 0)),
            side * (k + jnp.where(first, 0.0, pltpu.roll(k, 1, 1))),
            side * (k + jnp.where(last, 0.0, pltpu.roll(k, LANES - 1, 1))),
        ]
        total = ((c[0] + c[1]) + (c[2] + c[3])) + (c[4] + c[5])
        d = jnp.where(k > 0.0, damping / (1.0 + total), 0.0)
        co_s[0, z] = c[0] * d
        co_s[1, z] = c[1] * d
        co_s[2, z] = c[2] * d
        co_s[3, z] = c[3] * d
        co_s[4, z] = jnp.where(first, 0.0, c[4] * d)
        co_s[5, z] = jnp.where(last, 0.0, c[5] * d)
        co_s[6, z] = d
        return carry

    lax.fori_loop(0, NZ, layer, 0)


def one_sweep(src, dst, co_s, db_s, rows):
    tall = rows.stop - rows.start
    for z in range(NZ):
        w = src[z + 1, rows]
        acc = (db_s[z, rows] + (1.0 - damping) * w) + (
            co_s[0, z, rows] * src[z, rows] + co_s[1, z, rows] * src[z + 2, rows]
        )
        acc = acc + (
            co_s[2, z, rows] * pltpu.roll(w, 1, 0) + co_s[3, z, rows] * pltpu.roll(w, tall - 1, 0)
        )
        acc = acc + (
            co_s[4, z, rows] * pltpu.roll(w, 1, 1) + co_s[5, z, rows] * pltpu.roll(w, LANES - 1, 1)
        )
        dst[z + 1, rows] = acc


def fine_steps(phase, f_ref, fb_ref, fa_ref, co_s, a_s, b_s, db_s, keep):
    rows = slice(0, FINE)
    for n in range(4):
        tile, turn = ((0, 0), (1, 0), (1, 5), (0, 7))[n]
        for z in range(NZ):
            below = fb_ref[2 * phase + tile, z]
            above = fa_ref[2 * phase + tile, z]
            if turn:
                below = pltpu.roll(below, turn, 0)
                above = pltpu.roll(above, ROWS - turn, 0)
            forcing = jnp.concatenate([below, f_ref[4 * phase + n, z], above], axis=0)
            db_s[z] = co_s[6, z] * (a_s[z + 1] + step_size * forcing)
        one_sweep(a_s, b_s, co_s, db_s, rows)
        one_sweep(b_s, a_s, co_s, db_s, rows)
        for z in range(NZ):
            keep(n, z, a_s[z + 1, 8:16])


def early_body(
    block_ref, k_ref, f_ref, fb_ref, fa_ref, first_ref, below_ref, own_ref, above_ref,
    out_ref, end_ref, k_s, co_s, a_s, b_s, db_s,
):
    load_diffusivity(k_s, [lambda z: k_ref[z]])
    coefficients(step_size, k_s, co_s)
    load_window(a_s, b_s, (below_ref, own_ref, above_ref))

    @pl.when(block_ref[0] == 0)
    def _():
        for z in range(NZ):
            a_s[z + 1] = first_ref[z]

    def keep(n, z, mine):
        out_ref[n, z] = mine
        if n == 3:
            end_ref[z] = mine

    fine_steps(0, f_ref, fb_ref, fa_ref, co_s, a_s, b_s, db_s, keep)


def late_body(
    k_ref, f_ref, fb_ref, fa_ref, below_ref, own_ref, above_ref, g_ref,
    out_ref, res_ref, k_s, co_s, a_s, b_s, db_s,
):
    load_diffusivity(k_s, [lambda z: k_ref[z]])
    coefficients(step_size, k_s, co_s)
    load_window(a_s, b_s, (below_ref, own_ref, above_ref))

    def keep(n, z, mine):
        if n < 3:
            out_ref[n, z] = mine
        else:
            res_ref[z] = mine - g_ref[z]

    fine_steps(1, f_ref, fb_ref, fa_ref, co_s, a_s, b_s, db_s, keep)


def powers_body(
    core_ref, block_ref, k_ref, fb_ref, fa_ref, below2_ref, below1_ref, own_ref, above1_ref, above2_ref,
    out_ref, k_s, co_s, a_s, b_s, db_s, pow_s,
):
    load_diffusivity(k_s, [lambda z: fb_ref[4, z], lambda z: k_ref[z], lambda z: fa_ref[4, z]])
    coefficients(coarse_size, k_s, co_s)
    load_window(a_s, b_s, (below2_ref, below1_ref, own_ref, above1_ref, above2_ref))
    for z in range(NZ):
        pow_s[0, z] = own_ref[z]
    for n in range(NB - 1):
        rows = slice(0, WIDE) if n < 4 else slice(ROWS, WIDE - ROWS)
        for z in range(NZ):
            db_s[z, rows] = co_s[6, z, rows] * a_s[z + 1, rows]
        one_sweep(a_s, b_s, co_s, db_s, rows)
        one_sweep(b_s, a_s, co_s, db_s, rows)
        for z in range(NZ):
            pow_s[1 + n, z] = a_s[z + 1, 16:24]
    core, c = core_ref[0], block_ref[0]
    for b in range(NB):
        power = jnp.clip(b - c, 0, NB - 1)
        live = b >= c
        for s in range(8):
            out_ref[b, s] = jnp.where(live, pow_s[power, 2 * s + core], 0.0)


def sweep_scratch(window):
    return (
        pltpu.VMEM((NZ + 2, window, LANES), F32),
        pltpu.VMEM((7, NZ, window, LANES), F32),
        pltpu.VMEM((NZ + 2, window, LANES), F32),
        pltpu.VMEM((NZ + 2, window, LANES), F32),
        pltpu.VMEM((NZ, window, LANES), F32),
    )


def collect_body(core_ref, got_ref, early_ref, late_ref, out_ref):
    core = core_ref[0]
    for s in range(8):
        total = got_ref[0, s]
        for b in range(1, NB):
            total = total + got_ref[b, s]
        out_ref[7 * 8 + s] = total
        for n in range(4):
            out_ref[n * 8 + s] = early_ref[n, 2 * s + core]
        for n in range(3):
            out_ref[(4 + n) * 8 + s] = late_ref[n, 2 * s + core]


def home_body(j_ref, got_ref, guess_ref, out_ref):
    last = j_ref[0] == 7

    def write(add):
        for tile in range(TILES):
            zhi = 0 if tile < TILES // 2 else 1
            m = tile - SIDE * zhi
            zl, y = m // 4, m % 4
            if zl % 2 == 1:
                y = 3 - y
            rows = slice(tile * ROWS, (tile + 1) * ROWS)
            for core in range(2):
                value = got_ref[block_index(zl, core, y, zhi)]
                if add:
                    value = guess_ref[core, rows] + value
                out_ref[core, rows] = value

    pl.when(last)(functools.partial(write, True))
    pl.when(jnp.logical_not(last))(functools.partial(write, False))


def on_device(guess, source, diffusivity, initial):
    guess = guess[0]
    source = source[0]
    core = lax.axis_index("core")
    place = lax.axis_index(("zl", "core"))[None]
    block = lax.axis_index(BLOCKS)

    sent = pl.pallas_call(
        scatter_body,
        out_shape=sds(64, 2, ROWS, LANES),
        in_specs=[pl.BlockSpec(memory_space=pltpu.SMEM)] + [pl.BlockSpec(memory_space=pltpu.HBM)] * 4,
        out_specs=pl.BlockSpec(memory_space=pltpu.VMEM),
        scratch_shapes=[
            pltpu.VMEM((2, TILES * ROWS, LANES), F32),
            pltpu.VMEM((2, TILES * ROWS, LANES), F32),
            pltpu.SemaphoreType.DMA((2,)),
        ],
        compiler_params=pltpu.CompilerParams(vmem_limit_bytes=60 * 1024 * 1024),
    )(place, source, guess, diffusivity, initial)
    strips = lax.all_to_all(sent, BLOCK, 0, 0, tiled=True).reshape(8, 8, 2, ROWS, LANES)

    strips2 = lax.ppermute(strips, "core", [(0, 1), (1, 0)])
    full = sds(NZ, ROWS, LANES)
    f, g, k, first, f_up, f_down = call(
        pack_body,
        [sds(8, NZ, ROWS, LANES), full] + [sds(NZ, FINE, LANES)] * 2 + [sds(5, NZ, ROWS, LANES)] * 2,
        core[None], strips, strips2, smem=1,
    )

    def along(mine, step):
        return lax.ppermute(mine, ("zl", "y"), neighbours(step))

    def onward(mine, step):
        route = [(16 * b + i, 16 * (b + 1) + j) for b in range(NB - 1) for i, j in neighbours(step)]
        return lax.ppermute(mine, BLOCKS + ("zl", "y"), route)

    v0 = [onward(g, step) for step in (1, 0, -1)]
    f_below, f_above = along(f_up, 1), along(f_down, -1)
    flops = 8 * NZ * FINE * LANES * 15
    v_early, v4 = call(
        early_body, [sds(4, NZ, ROWS, LANES), full],
        block[None], k, f, f_below, f_above, first, *v0, smem=1, scratch=sweep_scratch(FINE), flops=flops,
    )
    v_late, residual = call(
        late_body, [sds(3, NZ, ROWS, LANES), full],
        k, f, f_below, f_above, along(v4, 1), v4, along(v4, -1), g, scratch=sweep_scratch(FINE), flops=flops,
    )
    (powers,) = call(
        powers_body, [sds(NB, 8, ROWS, LANES)],
        core[None], block[None], k, f_below, f_above,
        along(residual, 2), along(residual, 1), residual, along(residual, -1), along(residual, -2), smem=2,
        scratch=sweep_scratch(WIDE) + (pltpu.VMEM((NB, NZ, ROWS, LANES), F32),), flops=3 * flops,
    )
    arrived = lax.all_to_all(powers, BLOCKS, 0, 0, tiled=True)
    (back,) = call(collect_body, [sds(64, ROWS, LANES)], core[None], arrived, v_early, v_late, smem=1)
    returned = lax.all_to_all(back, BLOCK, 0, 0, tiled=True)
    (result,) = call(home_body, [sds(2, TILES * ROWS, LANES)], place, returned, guess, smem=1)
    return result[None]


def solution(mesh):
    fine = Mesh(mesh.devices.reshape(SIZES), AXES)
    tm = ("x", "zh", "zl", "core")
    space = ("y", "zhi")
    in_specs = (P(tm, space, None, None), P(tm, space, None, None), P(space, None, None), P(space, None, None))
    out_specs = P(tm, space, None, None)
    return jax.shard_map(on_device, mesh=fine, in_specs=in_specs, out_specs=out_specs, check_vma=False)
```

time: 176 us -> 174 us (0.989); the launches traced: 175 us -> 171 us
  waiting for transfers between devices: 16.9 us -> 5.4 us
  starting transfers between devices: 31 us -> 38.6 us
  blocking collectives: 111 us -> 116 us
  local copies, waits for them, and re-layouts: 3.71 us -> 0.01 us
    ppermute x12, waiting for transfers between devices: 16.9 us -> 5.4 us  [the longest x8 2.6 us: along(): return lax.ppermute(mine, ('zl', 'y'), neighbours(step))]
    ppermute x12, starting transfers between devices: 27.6 us -> 38.6 us  [the longest x8 22.2 us: along(): return lax.ppermute(mine, ('zl', 'y'), neighbours(step))]
    all_to_all x2, blocking collectives: 59.1 us -> 63.1 us  [the longest x1 38.4 us: on_device(): returned = lax.all_to_all(back, BLOCK, 0, 0, tiled=True)]
    unnamed x10 -> x2, local copies, waits for them, and re-layouts: 3.71 us -> 0.01 us
    all_to_all x1 -> x0, starting transfers between devices: 3.44 us -> none  [on_device(): v = lax.all_to_all(v, 'zhi', 0, 0, tiled=True)]
    pallas_call x7 -> x6, Pallas kernels: 11.4 us -> 9.75 us  [call(): pl.pallas_call(body, out_shape=list(outs), in_specs=specs, out_specs=out_...]
  transfers between devices with their start and end apart: 13 -> 12, of which waited for: 6 -> 4; matrix products, arithmetic and copies ran while one was open for 0% -> 0% of each run, Pallas kernels for 3% -> 0%
where the time goes in v4:
time: 174 us; the launch traced here: 171 us
  blocking collectives  116 us (67%)
  starting transfers between devices  38.6 us (22%)
  Pallas kernels  11.6 us (7%)
  waiting for transfers between devices  5.4 us (3%)
    all_to_all x1, blocking collectives, on_device(): lax.all_to_all(sent, BLOCK, 0, 0, tiled=True).reshape(8, 8, 2, ROWS, LANES)  52.5 us
    all_to_all x1, blocking collectives, on_device(): returned = lax.all_to_all(back, BLOCK, 0, 0, tiled=True)  38.4 us
    all_to_all x1, blocking collectives, on_device(): arrived = lax.all_to_all(powers, BLOCKS, 0, 0, tiled=True)  24.7 us
    ppermute x8, starting transfers between devices, along(): return lax.ppermute(mine, ('zl', 'y'), neighbours(step))  22.2 us
    ppermute x3, starting transfers between devices, onward(): return lax.ppermute(mine, BLOCKS + ('zl', 'y'), route)  13.8 us
    pallas_call x6, Pallas kernels, call(): pl.pallas_call(body, out_shape=list(outs), in_specs=specs, out_specs=out_...  9.75 us
  transfers between devices with their start and end apart: 12, of which 4 were waited for; matrix products, arithmetic and copies ran while one was open for 0% of the time, Pallas kernels for 0%

profile of v4, /device:TPU:1, one launch (start us, length us, event | category | flops | bytes accessed | tf_op | source)
XLA Modules:
  0.0 171.4 jit_solution(13022713168950042173)
XLA Ops:
  0.0 1.9 %shard_map.46 = f32[64,2,8,128]{3,2,1,0:T(8,128)} custom-call(s32[1]{0:T(128)} %bitcast.j_ref, f32[2,192,128]{2,1,0:T(8,128)} %bitcast.11, f32[2,192,128]{2,1,0:T(8,128)} %bitcast.9, f32[2,192,128]{2,1,0:T(8,128)} %cond_hbm.1, f32[2,192,128]{2,1,0:T(8,128)} %init_hbm.1), custom_call_target="tpu_custom_call" | custom-call | tf_op jit(solution)/shard_map/pallas_call | solution.py:337
  1.9 52.5 %all_to_all.15 = f32[64,2,8,128]{3,2,1,0:T(8,128)S(1)} all-to-all(f32[64,2,8,128]{3,2,1,0:T(8,128)} %shard_map.46), channel_id=1, replica_groups=mesh['x'=4,'zh'=2,'zl'=4,'core'=2,'y'=4,'zhi'=2] {'zl','core','y','zhi'}, dimensions={0} | all-to-all | bytes 1048576 | tf_op jit(solution)/shard_map/all_to_all | solution.py:349
  54.4 2.6 %collective-permute-start = (f32[8,8,2,8,128]{4,3,2,1,0:T(8,128)S(1)}, f32[8,8,2,8,128]{4,3,2,1,0:T(8,128)S(1)}, u32[]{:S(2)}, u32[]{:S(2)}) collective-permute-start(f32[8,8,2,8,128]{4,3,2,1,0:T(8,128)S(1)} %bitcast.7), channel_id=1, source_target_pairs={{0,8},{8,0},{1,9},{9,1},{2,10},{10,2},{3,11},{11,3},{4,12},{12,4},... | collective-permute-start | bytes 1572872 | tf_op jit(solution)/shard_map/ppermute | solution.py:351
  57.0 1.5 collective-permute-done.other_ref
  58.5 0.1 shard_map.47
  58.6 2.2 %collective-permute-start.1 = (f32[5,16,8,128]{3,2,1,0:T(8,128)S(1)}, f32[5,16,8,128]{3,2,1,0:T(8,128)S(1)}, u32[]{:S(2)}, u32[]{:S(2)}) collective-permute-start(f32[5,16,8,128]{3,2,1,0:T(8,128)S(1)} %get-tuple-element.16), channel_id=1, source_target_pairs={{0,2},{2,4},{4,6},{6,22},{22,20},{20,18},{18,16},{16,32},{32,34},{... | collective-permute-start | bytes 983048 | tf_op jit(solution)/shard_map/ppermute | solution.py:360
  60.8 1.3 collective-permute-start.2
  62.1 0.7 collective-permute-start.5
  62.8 2.9 %collective-permute-start.4 = (f32[16,8,128]{2,1,0:T(8,128)S(1)}, f32[16,8,128]{2,1,0:T(8,128)S(1)}, u32[]{:S(2)}, u32[]{:S(2)}) collective-permute-start(f32[16,8,128]{2,1,0:T(8,128)S(1)} %get-tuple-element.20.g_ref), channel_id=1, source_target_pairs={{0,64},{2,66},{4,68},{6,70},{22,86},{20,84},{18,82},{16,80},{32,96... | collective-permute-start | bytes 196616 | tf_op jit(solution)/shard_map/ppermute | solution.py:364
  65.8 10.2 %collective-permute-start.3 = (f32[16,8,128]{2,1,0:T(8,128)S(1)}, f32[16,8,128]{2,1,0:T(8,128)S(1)}, u32[]{:S(2)}, u32[]{:S(2)}) collective-permute-start(f32[16,8,128]{2,1,0:T(8,128)S(1)} %get-tuple-element.20.g_ref), channel_id=1, source_target_pairs={{0,66},{2,68},{4,70},{6,86},{22,84},{20,82},{18,80},{16,96},{32,98... | collective-permute-start | bytes 196616 | tf_op jit(solution)/shard_map/ppermute | solution.py:364
  76.0 0.0 collective-permute-done.5.above_ref
  76.0 1.3 collective-permute-done.3.below_ref
  77.3 0.0 collective-permute-done.1.fb_ref
  77.3 0.0 collective-permute-done.2.fa_ref
  77.3 2.6 %shard_map.48 = (f32[4,16,8,128]{3,2,1,0:T(8,128)S(1)}, f32[16,8,128]{2,1,0:T(8,128)S(1)}) custom-call(s32[1]{0:T(128)} %bitcast.2.block_ref, f32[16,24,128]{2,1,0:T(8,128)S(1)} %get-tuple-element.15.k_ref, f32[8,16,8,128]{3,2,1,0:T(8,128)S(1)} %get-tuple-element.18.f_ref, f32[5,16,8,128]{3,2,1,0:T(8,128)S(1)} %collective-permute-done.1.fb_ref, ...), custom_call_target="tpu_custom_call" | custom-call | flops 5898240 | bytes 2097156 | tf_op jit(solution)/shard_map/pallas_call | solution.py:51
  80.0 1.3 collective-permute-start.7
  81.3 4.1 %collective-permute-start.6 = (f32[16,8,128]{2,1,0:T(8,128)S(1)}, f32[16,8,128]{2,1,0:T(8,128)S(1)}, u32[]{:S(2)}, u32[]{:S(2)}) collective-permute-start(f32[16,8,128]{2,1,0:T(8,128)S(1)} %get-tuple-element.21.own_ref), channel_id=1, source_target_pairs={{0,2},{2,4},{4,6},{6,22},{22,20},{20,18},{18,16},{16,32},{32,34},{... | collective-permute-start | bytes 196616 | tf_op jit(solution)/shard_map/ppermute | solution.py:360
  85.4 0.0 collective-permute-done.7.above_ref
  85.4 1.3 collective-permute-done.6.below_ref
  86.7 2.4 %shard_map.49 = (f32[3,16,8,128]{3,2,1,0:T(8,128)S(1)}, f32[16,8,128]{2,1,0:T(8,128)S(1)}) custom-call(f32[16,24,128]{2,1,0:T(8,128)S(1)} %get-tuple-element.15.k_ref, f32[8,16,8,128]{3,2,1,0:T(8,128)S(1)} %get-tuple-element.18.f_ref, f32[5,16,8,128]{3,2,1,0:T(8,128)S(1)} %collective-permute-done.1.fb_ref, ...), custom_call_target="tpu_custom_call" | custom-call | flops 5898240 | bytes 1900544 | tf_op jit(solution)/shard_map/pallas_call | solution.py:51
  89.1 1.3 collective-permute-start.11
  90.4 1.3 collective-permute-start.10
  91.7 4.6 %collective-permute-start.9 = (f32[16,8,128]{2,1,0:T(8,128)S(1)}, f32[16,8,128]{2,1,0:T(8,128)S(1)}, u32[]{:S(2)}, u32[]{:S(2)}) collective-permute-start(f32[16,8,128]{2,1,0:T(8,128)S(1)} %get-tuple-element.22.own_ref), channel_id=1, source_target_pairs={{0,2},{2,4},{4,6},{6,22},{22,20},{20,18},{18,16},{16,32},{32,34},{... | collective-permute-start | bytes 196616 | tf_op jit(solution)/shard_map/ppermute | solution.py:360
  96.3 6.1 %collective-permute-start.8 = (f32[16,8,128]{2,1,0:T(8,128)S(1)}, f32[16,8,128]{2,1,0:T(8,128)S(1)}, u32[]{:S(2)}, u32[]{:S(2)}) collective-permute-start(f32[16,8,128]{2,1,0:T(8,128)S(1)} %get-tuple-element.22.own_ref), channel_id=1, source_target_pairs={{0,4},{2,6},{4,22},{6,20},{22,18},{20,16},{18,32},{16,34},{32,36},... | collective-permute-start | bytes 196616 | tf_op jit(solution)/shard_map/ppermute | solution.py:360
  102.5 0.0 collective-permute-done.10.above1_ref
  102.5 0.0 collective-permute-done.9.below1_ref
  102.5 1.3 collective-permute-done.8.below2_ref
  103.8 3.8 %shard_map.50 = f32[8,8,8,128]{3,2,1,0:T(8,128)S(1)} custom-call(s32[1]{0:T(128)} %bitcast.1.core_ref, s32[1]{0:T(128)} %bitcast.2.block_ref, f32[16,24,128]{2,1,0:T(8,128)S(1)} %get-tuple-element.15.k_ref, f32[5,16,8,128]{3,2,1,0:T(8,128)S(1)} %collective-permute-done.1.fb_ref, f32[5,16,8,128]{3,2,1,0:T(8,128)S(1)} %collective-permute-done.2.fa_ref, ...), custom_call_target="tpu_custom_call" | custom-call | flops 17694720 | bytes 1441800 | tf_op jit(solution)/shard_map/pallas_call | solution.py:51
  107.6 24.7 %all_to_all.16.got_ref = f32[8,8,8,128]{3,2,1,0:T(8,128)S(1)} all-to-all(f32[8,8,8,128]{3,2,1,0:T(8,128)S(1)} %shard_map.50), channel_id=1, replica_groups=mesh['x'=4,'zh'=2,'zl'=4,'core'=2,'y'=4,'zhi'=2] {'x','zh'}, dimensions={0} | all-to-all | bytes 524288 | tf_op jit(solution)/shard_map/all_to_all | solution.py:383
  132.3 0.0 copy-start
  132.3 38.4 %all_to_all.17.got_ref = f32[64,8,128]{2,1,0:T(8,128)S(1)} all-to-all(f32[64,8,128]{2,1,0:T(8,128)S(1)} %shard_map.51), channel_id=1, replica_groups=mesh['x'=4,'zh'=2,'zl'=4,'core'=2,'y'=4,'zhi'=2] {'zl','core','y','zhi'}, dimensions={0} | all-to-all | bytes 524288 | tf_op jit(solution)/shard_map/all_to_all | solution.py:385
  170.7 0.7 shard_map.52
  (4 shorter events, 0.0 us)
Async XLA Ops:
  54.4 4.1 %collective-permute-start = (f32[8,8,2,8,128]{4,3,2,1,0:T(8,128)S(1)}, f32[8,8,2,8,128]{4,3,2,1,0:T(8,128)S(1)}, u32[]{:S(2)}, u32[]{:S(2)}) collective-permute-start(f32[8,8,2,8,128]{4,3,2,1,0:T(8,128)S(1)} %bitcast.7), channel_id=1, source_target_pairs={{0,8},{8,0},{1,9},{9,1},{2,10},{10,2},{3,11},{11,3},{4,12},{12,4},... | collective-permute-start | bytes 1572872 | tf_op jit(solution)/shard_map/ppermute | solution.py:351
  58.6 18.7 %collective-permute-start.1 = (f32[5,16,8,128]{3,2,1,0:T(8,128)S(1)}, f32[5,16,8,128]{3,2,1,0:T(8,128)S(1)}, u32[]{:S(2)}, u32[]{:S(2)}) collective-permute-start(f32[5,16,8,128]{3,2,1,0:T(8,128)S(1)} %get-tuple-element.16), channel_id=1, source_target_pairs={{0,2},{2,4},{4,6},{6,22},{22,20},{20,18},{18,16},{16,32},{32,34},{... | collective-permute-start | bytes 983048 | tf_op jit(solution)/shard_map/ppermute | solution.py:360
  60.8 16.5 %collective-permute-start.2 = (f32[5,16,8,128]{3,2,1,0:T(8,128)S(1)}, f32[5,16,8,128]{3,2,1,0:T(8,128)S(1)}, u32[]{:S(2)}, u32[]{:S(2)}) collective-permute-start(f32[5,16,8,128]{3,2,1,0:T(8,128)S(1)} %get-tuple-element.17), channel_id=1, source_target_pairs={{2,0},{4,2},{6,4},{22,6},{20,22},{18,20},{16,18},{32,16},{34,32},{... | collective-permute-start | bytes 983048 | tf_op jit(solution)/shard_map/ppermute | solution.py:360
  62.1 13.9 %collective-permute-start.5 = (f32[16,8,128]{2,1,0:T(8,128)S(1)}, f32[16,8,128]{2,1,0:T(8,128)S(1)}, u32[]{:S(2)}, u32[]{:S(2)}) collective-permute-start(f32[16,8,128]{2,1,0:T(8,128)S(1)} %get-tuple-element.20.g_ref), channel_id=1, source_target_pairs={{2,64},{4,66},{6,68},{22,70},{20,86},{18,84},{16,82},{32,80},{34,9... | collective-permute-start | bytes 196616 | tf_op jit(solution)/shard_map/ppermute | solution.py:364
  62.8 13.2 %collective-permute-start.4 = (f32[16,8,128]{2,1,0:T(8,128)S(1)}, f32[16,8,128]{2,1,0:T(8,128)S(1)}, u32[]{:S(2)}, u32[]{:S(2)}) collective-permute-start(f32[16,8,128]{2,1,0:T(8,128)S(1)} %get-tuple-element.20.g_ref), channel_id=1, source_target_pairs={{0,64},{2,66},{4,68},{6,70},{22,86},{20,84},{18,82},{16,80},{32,96... | collective-permute-start | bytes 196616 | tf_op jit(solution)/shard_map/ppermute | solution.py:364
  65.8 11.6 %collective-permute-start.3 = (f32[16,8,128]{2,1,0:T(8,128)S(1)}, f32[16,8,128]{2,1,0:T(8,128)S(1)}, u32[]{:S(2)}, u32[]{:S(2)}) collective-permute-start(f32[16,8,128]{2,1,0:T(8,128)S(1)} %get-tuple-element.20.g_ref), channel_id=1, source_target_pairs={{0,66},{2,68},{4,70},{6,86},{22,84},{20,82},{18,80},{16,96},{32,98... | collective-permute-start | bytes 196616 | tf_op jit(solution)/shard_map/ppermute | solution.py:364
  80.0 5.4 %collective-permute-start.7 = (f32[16,8,128]{2,1,0:T(8,128)S(1)}, f32[16,8,128]{2,1,0:T(8,128)S(1)}, u32[]{:S(2)}, u32[]{:S(2)}) collective-permute-start(f32[16,8,128]{2,1,0:T(8,128)S(1)} %get-tuple-element.21.own_ref), channel_id=1, source_target_pairs={{2,0},{4,2},{6,4},{22,6},{20,22},{18,20},{16,18},{32,16},{34,32},{... | collective-permute-start | bytes 196616 | tf_op jit(solution)/shard_map/ppermute | solution.py:360
  81.3 5.4 %collective-permute-start.6 = (f32[16,8,128]{2,1,0:T(8,128)S(1)}, f32[16,8,128]{2,1,0:T(8,128)S(1)}, u32[]{:S(2)}, u32[]{:S(2)}) collective-permute-start(f32[16,8,128]{2,1,0:T(8,128)S(1)} %get-tuple-element.21.own_ref), channel_id=1, source_target_pairs={{0,2},{2,4},{4,6},{6,22},{22,20},{20,18},{18,16},{16,32},{32,34},{... | collective-permute-start | bytes 196616 | tf_op jit(solution)/shard_map/ppermute | solution.py:360
  89.1 13.3 %collective-permute-start.11 = (f32[16,8,128]{2,1,0:T(8,128)S(1)}, f32[16,8,128]{2,1,0:T(8,128)S(1)}, u32[]{:S(2)}, u32[]{:S(2)}) collective-permute-start(f32[16,8,128]{2,1,0:T(8,128)S(1)} %get-tuple-element.22.own_ref), channel_id=1, source_target_pairs={{4,0},{6,2},{22,4},{20,6},{18,22},{16,20},{32,18},{34,16},{36,32},... | collective-permute-start | bytes 196616 | tf_op jit(solution)/shard_map/ppermute | solution.py:360
  90.4 12.0 %collective-permute-start.10 = (f32[16,8,128]{2,1,0:T(8,128)S(1)}, f32[16,8,128]{2,1,0:T(8,128)S(1)}, u32[]{:S(2)}, u32[]{:S(2)}) collective-permute-start(f32[16,8,128]{2,1,0:T(8,128)S(1)} %get-tuple-element.22.own_ref), channel_id=1, source_target_pairs={{2,0},{4,2},{6,4},{22,6},{20,22},{18,20},{16,18},{32,16},{34,32},{... | collective-permute-start | bytes 196616 | tf_op jit(solution)/shard_map/ppermute | solution.py:360
  91.7 10.8 %collective-permute-start.9 = (f32[16,8,128]{2,1,0:T(8,128)S(1)}, f32[16,8,128]{2,1,0:T(8,128)S(1)}, u32[]{:S(2)}, u32[]{:S(2)}) collective-permute-start(f32[16,8,128]{2,1,0:T(8,128)S(1)} %get-tuple-element.22.own_ref), channel_id=1, source_target_pairs={{0,2},{2,4},{4,6},{6,22},{22,20},{20,18},{18,16},{16,32},{32,34},{... | collective-permute-start | bytes 196616 | tf_op jit(solution)/shard_map/ppermute | solution.py:360
  96.3 7.4 %collective-permute-start.8 = (f32[16,8,128]{2,1,0:T(8,128)S(1)}, f32[16,8,128]{2,1,0:T(8,128)S(1)}, u32[]{:S(2)}, u32[]{:S(2)}) collective-permute-start(f32[16,8,128]{2,1,0:T(8,128)S(1)} %get-tuple-element.22.own_ref), channel_id=1, source_target_pairs={{0,4},{2,6},{4,22},{6,20},{22,18},{20,16},{18,32},{16,34},{32,36},... | collective-permute-start | bytes 196616 | tf_op jit(solution)/shard_map/ppermute | solution.py:360
  132.3 38.4 %copy-start = (f32[1,2,192,128]{3,2,1,0:T(8,128)S(1)}, f32[1,2,192,128]{3,2,1,0:T(8,128)}, u32[]{:S(2)}) copy-start(f32[1,2,192,128]{3,2,1,0:T(8,128)} %param.4) | copy-start | bytes 589828

commit v5 on v4

--- a/solution.py
+++ b/solution.py
@@ -359,16 +359,12 @@
     def along(mine, step):
         return lax.ppermute(mine, ("zl", "y"), neighbours(step))
 
-    def onward(mine, step):
-        route = [(16 * b + i, 16 * (b + 1) + j) for b in range(NB - 1) for i, j in neighbours(step)]
-        return lax.ppermute(mine, BLOCKS + ("zl", "y"), route)
-
-    v0 = [onward(g, step) for step in (1, 0, -1)]
+    v0 = lax.ppermute(g, BLOCKS, [(b, b + 1) for b in range(NB - 1)])
     f_below, f_above = along(f_up, 1), along(f_down, -1)
     flops = 8 * NZ * FINE * LANES * 15
     v_early, v4 = call(
         early_body, [sds(4, NZ, ROWS, LANES), full],
-        block[None], k, f, f_below, f_above, first, *v0, smem=1, scratch=sweep_scratch(FINE), flops=flops,
+        block[None], k, f, f_below, f_above, first, along(v0, 1), v0, along(v0, -1), smem=1, scratch=sweep_scratch(FINE), flops=flops,
     )
     v_late, residual = call(
         late_body, [sds(3, NZ, ROWS, LANES), full],

time: 174 us -> 171 us (0.983)
  starting transfers between devices: 38.6 us -> 35.2 us
  blocking collectives: 116 us -> 114 us
    ppermute x3 -> x1, starting transfers between devices: 13.8 us -> 2.31 us  [on_device(): v0 = lax.ppermute(g, BLOCKS, [(b, b + 1) for b in range(NB - 1)])]
    ppermute x8 -> x10, starting transfers between devices: 22.2 us -> 30.4 us  [along(): return lax.ppermute(mine, ('zl', 'y'), neighbours(step))]
    all_to_all x1, blocking collectives: 24.7 us -> 20.8 us  [on_device(): arrived = lax.all_to_all(powers, BLOCKS, 0, 0, tiled=True)]
    all_to_all x1, blocking collectives: 38.4 us -> 40.5 us  [on_device(): returned = lax.all_to_all(back, BLOCK, 0, 0, tiled=True)]
    ppermute x8 -> x10, waiting for transfers between devices: 2.6 us -> 3.9 us  [along(): return lax.ppermute(mine, ('zl', 'y'), neighbours(step))]
  transfers between devices with their start and end apart: 12 -> 12, of which waited for: 4 -> 6; matrix products, arithmetic and copies ran while one was open for 0% -> 0% of each run, Pallas kernels for 0% -> 0%
where the time goes in v5:
time: 171 us; the launch traced here: 168 us
  blocking collectives  114 us (67%)
  starting transfers between devices  35.2 us (21%)
  Pallas kernels  11.6 us (7%)
  waiting for transfers between devices  6.73 us (4%)
    all_to_all x1, blocking collectives, on_device(): lax.all_to_all(sent, BLOCK, 0, 0, tiled=True).reshape(8, 8, 2, ROWS, LANES)  52.5 us
    all_to_all x1, blocking collectives, on_device(): returned = lax.all_to_all(back, BLOCK, 0, 0, tiled=True)  40.5 us
    ppermute x10, starting transfers between devices, along(): return lax.ppermute(mine, ('zl', 'y'), neighbours(step))  30.4 us
    all_to_all x1, blocking collectives, on_device(): arrived = lax.all_to_all(powers, BLOCKS, 0, 0, tiled=True)  20.8 us
    pallas_call x6, Pallas kernels, call(): pl.pallas_call(body, out_shape=list(outs), in_specs=specs, out_specs=out_...  9.75 us
    ppermute x10, waiting for transfers between devices, along(): return lax.ppermute(mine, ('zl', 'y'), neighbours(step))  3.9 us
  transfers between devices with their start and end apart: 12, of which 6 were waited for; matrix products, arithmetic and copies ran while one was open for 0% of the time, Pallas kernels for 0%

profile of v5, /device:TPU:1, one launch (start us, length us, event | category | flops | bytes accessed | tf_op | source)
XLA Modules:
  0.0 167.5 jit_solution(13483440167057381637)
XLA Ops:
  0.0 1.9 %shard_map.46 = f32[64,2,8,128]{3,2,1,0:T(8,128)} custom-call(s32[1]{0:T(128)} %bitcast.j_ref, f32[2,192,128]{2,1,0:T(8,128)} %bitcast.11, f32[2,192,128]{2,1,0:T(8,128)} %bitcast.9, f32[2,192,128]{2,1,0:T(8,128)} %cond_hbm.1, f32[2,192,128]{2,1,0:T(8,128)} %init_hbm.1), custom_call_target="tpu_custom_call" | custom-call | tf_op jit(solution)/shard_map/pallas_call | solution.py:337
  1.9 52.5 %all_to_all.15 = f32[64,2,8,128]{3,2,1,0:T(8,128)S(1)} all-to-all(f32[64,2,8,128]{3,2,1,0:T(8,128)} %shard_map.46), channel_id=1, replica_groups=mesh['x'=4,'zh'=2,'zl'=4,'core'=2,'y'=4,'zhi'=2] {'zl','core','y','zhi'}, dimensions={0} | all-to-all | bytes 1048576 | tf_op jit(solution)/shard_map/all_to_all | solution.py:349
  54.4 2.6 %collective-permute-start = (f32[8,8,2,8,128]{4,3,2,1,0:T(8,128)S(1)}, f32[8,8,2,8,128]{4,3,2,1,0:T(8,128)S(1)}, u32[]{:S(2)}, u32[]{:S(2)}) collective-permute-start(f32[8,8,2,8,128]{4,3,2,1,0:T(8,128)S(1)} %bitcast.7), channel_id=1, source_target_pairs={{0,8},{8,0},{1,9},{9,1},{2,10},{10,2},{3,11},{11,3},{4,12},{12,4},... | collective-permute-start | bytes 1572872 | tf_op jit(solution)/shard_map/ppermute | solution.py:351
  57.0 1.5 collective-permute-done.other_ref
  58.5 0.1 shard_map.47
  58.6 2.2 %collective-permute-start.1 = (f32[5,16,8,128]{3,2,1,0:T(8,128)S(1)}, f32[5,16,8,128]{3,2,1,0:T(8,128)S(1)}, u32[]{:S(2)}, u32[]{:S(2)}) collective-permute-start(f32[5,16,8,128]{3,2,1,0:T(8,128)S(1)} %get-tuple-element.16), channel_id=1, source_target_pairs={{0,2},{2,4},{4,6},{6,22},{22,20},{20,18},{18,16},{16,32},{32,34},{... | collective-permute-start | bytes 983048 | tf_op jit(solution)/shard_map/ppermute | solution.py:360
  60.8 1.3 collective-permute-start.2
  62.1 2.3 %collective-permute-start.3 = (f32[16,8,128]{2,1,0:T(8,128)S(1)}, f32[16,8,128]{2,1,0:T(8,128)S(1)}, u32[]{:S(2)}, u32[]{:S(2)}) collective-permute-start(f32[16,8,128]{2,1,0:T(8,128)S(1)} %get-tuple-element.20.g_ref), channel_id=1, source_target_pairs={{0,64},{64,128},{128,192},{192,256},{256,320},{320,384},{384,448},... | collective-permute-start | bytes 196616 | tf_op jit(solution)/shard_map/ppermute | solution.py:362
  64.5 1.3 collective-permute-done.3.own_ref
  65.8 1.3 collective-permute-start.5
  67.1 4.6 %collective-permute-start.4 = (f32[16,8,128]{2,1,0:T(8,128)S(1)}, f32[16,8,128]{2,1,0:T(8,128)S(1)}, u32[]{:S(2)}, u32[]{:S(2)}) collective-permute-start(f32[16,8,128]{2,1,0:T(8,128)S(1)} %collective-permute-done.3.own_ref), channel_id=1, source_target_pairs={{0,2},{2,4},{4,6},{6,22},{22,20},{20,18},{18,16},{16,32},{32,34},{... | collective-permute-start | bytes 196616 | tf_op jit(solution)/shard_map/ppermute | solution.py:360
  71.7 1.1 collective-permute-done.5.above_ref
  72.7 0.3 collective-permute-done.4.below_ref
  73.0 0.0 collective-permute-done.1.fb_ref
  73.0 0.0 collective-permute-done.2.fa_ref
  73.0 2.6 %shard_map.48 = (f32[4,16,8,128]{3,2,1,0:T(8,128)S(1)}, f32[16,8,128]{2,1,0:T(8,128)S(1)}) custom-call(s32[1]{0:T(128)} %bitcast.2.block_ref, f32[16,24,128]{2,1,0:T(8,128)S(1)} %get-tuple-element.15.k_ref, f32[8,16,8,128]{3,2,1,0:T(8,128)S(1)} %get-tuple-element.18.f_ref, f32[5,16,8,128]{3,2,1,0:T(8,128)S(1)} %collective-permute-done.1.fb_ref, ...), custom_call_target="tpu_custom_call" | custom-call | flops 5898240 | bytes 2097156 | tf_op jit(solution)/shard_map/pallas_call | solution.py:51
  75.7 1.3 collective-permute-start.7
  77.0 4.6 %collective-permute-start.6 = (f32[16,8,128]{2,1,0:T(8,128)S(1)}, f32[16,8,128]{2,1,0:T(8,128)S(1)}, u32[]{:S(2)}, u32[]{:S(2)}) collective-permute-start(f32[16,8,128]{2,1,0:T(8,128)S(1)} %get-tuple-element.21.own_ref), channel_id=1, source_target_pairs={{0,2},{2,4},{4,6},{6,22},{22,20},{20,18},{18,16},{16,32},{32,34},{... | collective-permute-start | bytes 196616 | tf_op jit(solution)/shard_map/ppermute | solution.py:360
  81.6 0.0 collective-permute-done.7.above_ref
  81.6 1.3 collective-permute-done.6.below_ref
  82.9 2.4 %shard_map.49 = (f32[3,16,8,128]{3,2,1,0:T(8,128)S(1)}, f32[16,8,128]{2,1,0:T(8,128)S(1)}) custom-call(f32[16,24,128]{2,1,0:T(8,128)S(1)} %get-tuple-element.15.k_ref, f32[8,16,8,128]{3,2,1,0:T(8,128)S(1)} %get-tuple-element.18.f_ref, f32[5,16,8,128]{3,2,1,0:T(8,128)S(1)} %collective-permute-done.1.fb_ref, ...), custom_call_target="tpu_custom_call" | custom-call | flops 5898240 | bytes 1900544 | tf_op jit(solution)/shard_map/pallas_call | solution.py:51
  85.3 1.3 collective-permute-start.11
  86.6 1.3 collective-permute-start.10
  87.9 6.0 %collective-permute-start.9 = (f32[16,8,128]{2,1,0:T(8,128)S(1)}, f32[16,8,128]{2,1,0:T(8,128)S(1)}, u32[]{:S(2)}, u32[]{:S(2)}) collective-permute-start(f32[16,8,128]{2,1,0:T(8,128)S(1)} %get-tuple-element.22.own_ref), channel_id=1, source_target_pairs={{0,2},{2,4},{4,6},{6,22},{22,20},{20,18},{18,16},{16,32},{32,34},{... | collective-permute-start | bytes 196616 | tf_op jit(solution)/shard_map/ppermute | solution.py:360
  93.9 6.5 %collective-permute-start.8 = (f32[16,8,128]{2,1,0:T(8,128)S(1)}, f32[16,8,128]{2,1,0:T(8,128)S(1)}, u32[]{:S(2)}, u32[]{:S(2)}) collective-permute-start(f32[16,8,128]{2,1,0:T(8,128)S(1)} %get-tuple-element.22.own_ref), channel_id=1, source_target_pairs={{0,4},{2,6},{4,22},{6,20},{22,18},{20,16},{18,32},{16,34},{32,36},... | collective-permute-start | bytes 196616 | tf_op jit(solution)/shard_map/ppermute | solution.py:360
  100.4 0.0 collective-permute-done.10.above1_ref
  100.4 1.3 collective-permute-done.8.below2_ref
  101.7 3.8 %shard_map.50 = f32[8,8,8,128]{3,2,1,0:T(8,128)S(1)} custom-call(s32[1]{0:T(128)} %bitcast.1.core_ref, s32[1]{0:T(128)} %bitcast.2.block_ref, f32[16,24,128]{2,1,0:T(8,128)S(1)} %get-tuple-element.15.k_ref, f32[5,16,8,128]{3,2,1,0:T(8,128)S(1)} %collective-permute-done.1.fb_ref, f32[5,16,8,128]{3,2,1,0:T(8,128)S(1)} %collective-permute-done.2.fa_ref, ...), custom_call_target="tpu_custom_call" | custom-call | flops 17694720 | bytes 1441800 | tf_op jit(solution)/shard_map/pallas_call | solution.py:51
  105.5 20.8 %all_to_all.16.got_ref = f32[8,8,8,128]{3,2,1,0:T(8,128)S(1)} all-to-all(f32[8,8,8,128]{3,2,1,0:T(8,128)S(1)} %shard_map.50), channel_id=1, replica_groups=mesh['x'=4,'zh'=2,'zl'=4,'core'=2,'y'=4,'zhi'=2] {'x','zh'}, dimensions={0} | all-to-all | bytes 524288 | tf_op jit(solution)/shard_map/all_to_all | solution.py:379
  126.3 0.0 copy-start
  126.3 40.5 %all_to_all.17.got_ref = f32[64,8,128]{2,1,0:T(8,128)S(1)} all-to-all(f32[64,8,128]{2,1,0:T(8,128)S(1)} %shard_map.51), channel_id=1, replica_groups=mesh['x'=4,'zh'=2,'zl'=4,'core'=2,'y'=4,'zhi'=2] {'zl','core','y','zhi'}, dimensions={0} | all-to-all | bytes 524288 | tf_op jit(solution)/shard_map/all_to_all | solution.py:381
  166.8 0.7 shard_map.52
  (4 shorter events, 0.0 us)
Async XLA Ops:
  54.4 4.1 %collective-permute-start = (f32[8,8,2,8,128]{4,3,2,1,0:T(8,128)S(1)}, f32[8,8,2,8,128]{4,3,2,1,0:T(8,128)S(1)}, u32[]{:S(2)}, u32[]{:S(2)}) collective-permute-start(f32[8,8,2,8,128]{4,3,2,1,0:T(8,128)S(1)} %bitcast.7), channel_id=1, source_target_pairs={{0,8},{8,0},{1,9},{9,1},{2,10},{10,2},{3,11},{11,3},{4,12},{12,4},... | collective-permute-start | bytes 1572872 | tf_op jit(solution)/shard_map/ppermute | solution.py:351
  58.6 14.4 %collective-permute-start.1 = (f32[5,16,8,128]{3,2,1,0:T(8,128)S(1)}, f32[5,16,8,128]{3,2,1,0:T(8,128)S(1)}, u32[]{:S(2)}, u32[]{:S(2)}) collective-permute-start(f32[5,16,8,128]{3,2,1,0:T(8,128)S(1)} %get-tuple-element.16), channel_id=1, source_target_pairs={{0,2},{2,4},{4,6},{6,22},{22,20},{20,18},{18,16},{16,32},{32,34},{... | collective-permute-start | bytes 983048 | tf_op jit(solution)/shard_map/ppermute | solution.py:360
  60.8 12.2 %collective-permute-start.2 = (f32[5,16,8,128]{3,2,1,0:T(8,128)S(1)}, f32[5,16,8,128]{3,2,1,0:T(8,128)S(1)}, u32[]{:S(2)}, u32[]{:S(2)}) collective-permute-start(f32[5,16,8,128]{3,2,1,0:T(8,128)S(1)} %get-tuple-element.17), channel_id=1, source_target_pairs={{2,0},{4,2},{6,4},{22,6},{20,22},{18,20},{16,18},{32,16},{34,32},{... | collective-permute-start | bytes 983048 | tf_op jit(solution)/shard_map/ppermute | solution.py:360
  62.1 3.6 %collective-permute-start.3 = (f32[16,8,128]{2,1,0:T(8,128)S(1)}, f32[16,8,128]{2,1,0:T(8,128)S(1)}, u32[]{:S(2)}, u32[]{:S(2)}) collective-permute-start(f32[16,8,128]{2,1,0:T(8,128)S(1)} %get-tuple-element.20.g_ref), channel_id=1, source_target_pairs={{0,64},{64,128},{128,192},{192,256},{256,320},{320,384},{384,448},... | collective-permute-start | bytes 196616 | tf_op jit(solution)/shard_map/ppermute | solution.py:362
  65.8 7.0 %collective-permute-start.5 = (f32[16,8,128]{2,1,0:T(8,128)S(1)}, f32[16,8,128]{2,1,0:T(8,128)S(1)}, u32[]{:S(2)}, u32[]{:S(2)}) collective-permute-start(f32[16,8,128]{2,1,0:T(8,128)S(1)} %collective-permute-done.3.own_ref), channel_id=1, source_target_pairs={{2,0},{4,2},{6,4},{22,6},{20,22},{18,20},{16,18},{32,16},{34,32},{... | collective-permute-start | bytes 196616 | tf_op jit(solution)/shard_map/ppermute | solution.py:360
  67.1 5.9 %collective-permute-start.4 = (f32[16,8,128]{2,1,0:T(8,128)S(1)}, f32[16,8,128]{2,1,0:T(8,128)S(1)}, u32[]{:S(2)}, u32[]{:S(2)}) collective-permute-start(f32[16,8,128]{2,1,0:T(8,128)S(1)} %collective-permute-done.3.own_ref), channel_id=1, source_target_pairs={{0,2},{2,4},{4,6},{6,22},{22,20},{20,18},{18,16},{16,32},{32,34},{... | collective-permute-start | bytes 196616 | tf_op jit(solution)/shard_map/ppermute | solution.py:360
  75.7 5.9 %collective-permute-start.7 = (f32[16,8,128]{2,1,0:T(8,128)S(1)}, f32[16,8,128]{2,1,0:T(8,128)S(1)}, u32[]{:S(2)}, u32[]{:S(2)}) collective-permute-start(f32[16,8,128]{2,1,0:T(8,128)S(1)} %get-tuple-element.21.own_ref), channel_id=1, source_target_pairs={{2,0},{4,2},{6,4},{22,6},{20,22},{18,20},{16,18},{32,16},{34,32},{... | collective-permute-start | bytes 196616 | tf_op jit(solution)/shard_map/ppermute | solution.py:360
  77.0 5.9 %collective-permute-start.6 = (f32[16,8,128]{2,1,0:T(8,128)S(1)}, f32[16,8,128]{2,1,0:T(8,128)S(1)}, u32[]{:S(2)}, u32[]{:S(2)}) collective-permute-start(f32[16,8,128]{2,1,0:T(8,128)S(1)} %get-tuple-element.21.own_ref), channel_id=1, source_target_pairs={{0,2},{2,4},{4,6},{6,22},{22,20},{20,18},{18,16},{16,32},{32,34},{... | collective-permute-start | bytes 196616 | tf_op jit(solution)/shard_map/ppermute | solution.py:360
  85.3 15.1 %collective-permute-start.11 = (f32[16,8,128]{2,1,0:T(8,128)S(1)}, f32[16,8,128]{2,1,0:T(8,128)S(1)}, u32[]{:S(2)}, u32[]{:S(2)}) collective-permute-start(f32[16,8,128]{2,1,0:T(8,128)S(1)} %get-tuple-element.22.own_ref), channel_id=1, source_target_pairs={{4,0},{6,2},{22,4},{20,6},{18,22},{16,20},{32,18},{34,16},{36,32},... | collective-permute-start | bytes 196616 | tf_op jit(solution)/shard_map/ppermute | solution.py:360
  86.6 13.8 %collective-permute-start.10 = (f32[16,8,128]{2,1,0:T(8,128)S(1)}, f32[16,8,128]{2,1,0:T(8,128)S(1)}, u32[]{:S(2)}, u32[]{:S(2)}) collective-permute-start(f32[16,8,128]{2,1,0:T(8,128)S(1)} %get-tuple-element.22.own_ref), channel_id=1, source_target_pairs={{2,0},{4,2},{6,4},{22,6},{20,22},{18,20},{16,18},{32,16},{34,32},{... | collective-permute-start | bytes 196616 | tf_op jit(solution)/shard_map/ppermute | solution.py:360
  87.9 12.5 %collective-permute-start.9 = (f32[16,8,128]{2,1,0:T(8,128)S(1)}, f32[16,8,128]{2,1,0:T(8,128)S(1)}, u32[]{:S(2)}, u32[]{:S(2)}) collective-permute-start(f32[16,8,128]{2,1,0:T(8,128)S(1)} %get-tuple-element.22.own_ref), channel_id=1, source_target_pairs={{0,2},{2,4},{4,6},{6,22},{22,20},{20,18},{18,16},{16,32},{32,34},{... | collective-permute-start | bytes 196616 | tf_op jit(solution)/shard_map/ppermute | solution.py:360
  93.9 7.8 %collective-permute-start.8 = (f32[16,8,128]{2,1,0:T(8,128)S(1)}, f32[16,8,128]{2,1,0:T(8,128)S(1)}, u32[]{:S(2)}, u32[]{:S(2)}) collective-permute-start(f32[16,8,128]{2,1,0:T(8,128)S(1)} %get-tuple-element.22.own_ref), channel_id=1, source_target_pairs={{0,4},{2,6},{4,22},{6,20},{22,18},{20,16},{18,32},{16,34},{32,36},... | collective-permute-start | bytes 196616 | tf_op jit(solution)/shard_map/ppermute | solution.py:360
  126.3 40.5 %copy-start = (f32[1,2,192,128]{3,2,1,0:T(8,128)S(1)}, f32[1,2,192,128]{3,2,1,0:T(8,128)}, u32[]{:S(2)}) copy-start(f32[1,2,192,128]{3,2,1,0:T(8,128)} %param.4) | copy-start | bytes 589828

commit v6 on v2

v6 whole, which is shorter than its diff:
```python
import functools

import jax
import jax.numpy as jnp
from jax import lax
from jax.experimental import pallas as pl
from jax.experimental.pallas import tpu as pltpu
from jax.sharding import Mesh, PartitionSpec as P

F32 = jnp.float32

damping = 0.8
step_size = 0.5
coarse_size = 4.0
z_weight = 8.0

AXES = ("x", "zh", "zl", "core", "y", "zhi")
SIZES = (4, 2, 4, 2, 4, 2)
BLOCK = ("zl", "core", "y", "zhi")
BLOCKS = ("x", "zh")
NB = 8
NZ = 16
NY = 192
CHIPS = 16
STRIP = NY // CHIPS
PAIR = 2 * STRIP
LANES = 128
LOW, OWN, HIGH, WIN = 4, 16, 28, 40


def chip_order(zl, y):
    return zl * 4 + (y if zl % 2 == 0 else 3 - y)


def neighbours(step):
    place = {chip_order(zl, y): zl * 4 + y for zl in range(4) for y in range(4)}
    return [(place[m], place[m + step]) for m in range(CHIPS) if 0 <= m + step < CHIPS]


def at(z, first, last):
    return slice((z % 2) * STRIP + first, (z % 2) * STRIP + last)


def call(body, outs, *args, scratch=(), smem=0, flops=0):
    specs = [pl.BlockSpec(memory_space=pltpu.SMEM)] * smem
    specs += [pl.BlockSpec(memory_space=pltpu.VMEM)] * (len(args) - smem)
    out_specs = [pl.BlockSpec(memory_space=pltpu.VMEM)] * len(outs)
    size = sum(4 * a.size for a in args) + sum(4 * o.size for o in outs)
    return pl.pallas_call(
        body,
        out_shape=list(outs),
        in_specs=specs,
        out_specs=out_specs,
        scratch_shapes=list(scratch),
        compiler_params=pltpu.CompilerParams(vmem_limit_bytes=32 * 1024 * 1024),
        cost_estimate=pl.CostEstimate(flops=flops, bytes_accessed=size, transcendentals=0),
    )(*args)


def sds(*shape):
    return jax.ShapeDtypeStruct(shape, F32)


def scatter_body(j_ref, block_ref, src_hbm, prev_hbm, cond_hbm, init_hbm, out_ref, src_ref, extra_ref, sems):
    place = j_ref[0]
    zero = jnp.zeros((STRIP, LANES), F32)
    source_copy = pltpu.make_async_copy(src_hbm, src_ref, sems.at[0])
    source_copy.start()

    @pl.when(place < 7)
    def _():
        pltpu.make_async_copy(cond_hbm, extra_ref, sems.at[1]).start()

    @pl.when((place == 7) & (block_ref[0] == 0))
    def _():
        pltpu.make_async_copy(init_hbm, extra_ref, sems.at[1]).start()

    @pl.when((place == 7) & (block_ref[0] > 0))
    def _():
        pltpu.make_async_copy(prev_hbm, extra_ref, sems.at[1]).start()

    def each():
        for zl in range(4):
            for y in range(4):
                for zhi in range(2):
                    for core in range(2):
                        yield ((zl * 2 + core) * 4 + y) * 2 + zhi, core, chip_order(zl, y)

    source_copy.wait()
    for to, core, m in each():
        out_ref[to, 0:STRIP] = src_ref[core, m * STRIP : (m + 1) * STRIP]
    pltpu.make_async_copy(cond_hbm, extra_ref, sems.at[1]).wait()

    def fill(shift):
        for to, core, m in each():
            m = m + shift
            if 0 <= m < CHIPS:
                out_ref[to, STRIP:PAIR] = extra_ref[core, m * STRIP : (m + 1) * STRIP]
            else:
                out_ref[to, STRIP:PAIR] = zero

    pl.when(place == 1)(functools.partial(fill, 1))
    pl.when(place == 2)(functools.partial(fill, -1))
    pl.when((place != 1) & (place != 2))(functools.partial(fill, 0))


def pack_body(core_ref, own_ref, other_ref, f_ref, k_ref, up_ref, down_ref):
    def order(halves):
        for z in range(NZ):
            half, s = halves[z % 2], z // 2
            for n in range(8):
                f_ref[n, z] = half[n, s, 0:STRIP]
            start = half[7, s, STRIP:PAIR]
            up_ref[0, s, at(z, 0, STRIP)] = start
            down_ref[0, s, at(z, 0, STRIP)] = start
            k_ref[z, 0:LOW] = jnp.zeros((LOW, LANES), F32)
            k_ref[z, LOW:OWN] = half[2, s, STRIP:PAIR]
            k_ref[z, OWN:HIGH] = half[0, s, STRIP:PAIR]
            k_ref[z, HIGH:WIN] = half[1, s, STRIP:PAIR]

    pl.when(core_ref[0] == 0)(functools.partial(order, (own_ref, other_ref)))
    pl.when(core_ref[0] == 1)(functools.partial(order, (other_ref, own_ref)))
    for z in range(NZ):
        s = z // 2
        for n in range(3):
            rows = 11 - 2 * n
            early, late = f_ref[n, z], f_ref[5 - n, z]
            down_ref[1 + n, s, at(z, 0, rows)] = early[0:rows]
            down_ref[1 + n, s, at(z, rows, STRIP)] = late[0 : STRIP - rows]
            up_ref[1 + n, s, at(z, STRIP - rows, STRIP)] = early[STRIP - rows : STRIP]
            up_ref[1 + n, s, at(z, 0, STRIP - rows)] = late[rows:STRIP]


def clear_ends(*refs):
    zero = jnp.zeros((WIN, LANES), F32)
    for ref in refs:
        ref[0] = zero
        ref[NZ + 1] = zero


def load_window(a_s, below, own, above):
    zero = jnp.zeros((LOW, LANES), F32)
    for z in range(NZ):
        a_s[z + 1, 0:LOW] = zero
        a_s[z + 1, LOW:OWN] = below(z)
        a_s[z + 1, OWN:HIGH] = own(z)
        a_s[z + 1, HIGH:WIN] = above(z)


def strips_of(ref, field):
    return lambda z: ref[field, z // 2, at(z, 0, STRIP)]


def coefficients(rate, k_ref, k_s, co_s):
    clear_ends(k_s)
    for z in range(NZ):
        k_s[z + 1] = k_ref[z]
    lane = lax.broadcasted_iota(jnp.int32, (WIN, LANES), 1)
    first = lane == 0
    last = lane == LANES - 1

    def layer(z, carry):
        k = k_s[z + 1]
        side = 0.5 * rate
        tall = 0.5 * rate * z_weight
        c = [
            tall * (k + k_s[z]),
            tall * (k + k_s[z + 2]),
            side * (k + pltpu.roll(k, 1, 0)),
            side * (k + pltpu.roll(k, WIN - 1, 0)),
            side * (k + jnp.where(first, 0.0, pltpu.roll(k, 1, 1))),
            side * (k + jnp.where(last, 0.0, pltpu.roll(k, LANES - 1, 1))),
        ]
        total = ((c[0] + c[1]) + (c[2] + c[3])) + (c[4] + c[5])
        d = jnp.where(k > 0.0, damping / (1.0 + total), 0.0)
        co_s[0, z] = c[0] * d
        co_s[1, z] = c[1] * d
        co_s[2, z] = c[2] * d
        co_s[3, z] = c[3] * d
        co_s[4, z] = jnp.where(first, 0.0, c[4] * d)
        co_s[5, z] = jnp.where(last, 0.0, c[5] * d)
        co_s[6, z] = d
        return carry

    lax.fori_loop(0, NZ, layer, 0)


def one_sweep(src, dst, co_s, db_s):
    for z in range(NZ):
        w = src[z + 1]
        acc = (db_s[z] + (1.0 - damping) * w) + (co_s[0, z] * src[z] + co_s[1, z] * src[z + 2])
        acc = acc + (co_s[2, z] * pltpu.roll(w, 1, 0) + co_s[3, z] * pltpu.roll(w, WIN - 1, 0))
        acc = acc + (co_s[4, z] * pltpu.roll(w, 1, 1) + co_s[5, z] * pltpu.roll(w, LANES - 1, 1))
        dst[z + 1] = acc


def step(a_s, b_s, co_s, db_s, forcing=None):
    for z in range(NZ):
        target = a_s[z + 1]
        if forcing is not None:
            target = target + step_size * forcing[z]
        db_s[z] = co_s[6, z] * target
    one_sweep(a_s, b_s, co_s, db_s)
    one_sweep(b_s, a_s, co_s, db_s)


def early_body(k_ref, f_ref, own_ref, below_ref, above_ref, out_ref, next_ref, k_s, co_s, a_s, b_s, db_s, f_s):
    coefficients(step_size, k_ref, k_s, co_s)
    clear_ends(a_s, b_s)
    load_window(a_s, strips_of(below_ref, 0), strips_of(own_ref, 0), strips_of(above_ref, 0))
    for n in range(3):
        rows = 11 - 2 * n
        for z in range(NZ):
            s = z // 2
            for m in (n, 5 - n):
                f_s[m, z] = jnp.zeros((WIN, LANES), F32)
                f_s[m, z, OWN:HIGH] = f_ref[m, z]
            f_s[n, z, OWN - rows : OWN] = below_ref[1 + n, s, at(z, STRIP - rows, STRIP)]
            f_s[n, z, HIGH : HIGH + rows] = above_ref[1 + n, s, at(z, 0, rows)]
            f_s[5 - n, z, OWN - STRIP + rows : OWN] = below_ref[1 + n, s, at(z, 0, STRIP - rows)]
            f_s[5 - n, z, HIGH : HIGH + STRIP - rows] = above_ref[1 + n, s, at(z, rows, STRIP)]
    for n in range(6):
        step(a_s, b_s, co_s, db_s, f_s.at[n])
        for z in range(NZ):
            out_ref[n, z] = a_s[z + 1, OWN:HIGH]
    for z in range(NZ):
        next_ref[0, z // 2, at(z, 0, STRIP)] = a_s[z + 1, OWN:HIGH]
        for n in range(2):
            next_ref[1 + n, z // 2, at(z, 0, STRIP)] = f_ref[6 + n, z]


def late_body(
    block_ref, k_ref, own_ref, below_ref, above_ref, start_ref, start_below_ref, start_above_ref,
    out_ref, pow_ref, next_ref, k_s, co_s, a_s, b_s, db_s, f_s, y_s,
):
    coefficients(step_size, k_ref, k_s, co_s)
    clear_ends(a_s, b_s)
    load_window(a_s, strips_of(below_ref, 0), strips_of(own_ref, 0), strips_of(above_ref, 0))
    for n in range(2):
        load_window(f_s, strips_of(below_ref, 1 + n), strips_of(own_ref, 1 + n), strips_of(above_ref, 1 + n))
        step(a_s, b_s, co_s, db_s, f_s.at[pl.ds(1, NZ)])
        if n == 0:
            for z in range(NZ):
                out_ref[z] = a_s[z + 1, OWN:HIGH]
    for z in range(NZ):
        y_s[z] = a_s[z + 1]
    coefficients(coarse_size, k_ref, k_s, co_s)
    load_window(a_s, strips_of(start_below_ref, 0), strips_of(start_ref, 0), strips_of(start_above_ref, 0))
    step(a_s, b_s, co_s, db_s)
    later = block_ref[0] > 0
    for z in range(NZ):
        a_s[z + 1] = y_s[z] - jnp.where(later, a_s[z + 1], 0.0)
    for n in range(5):
        if n > 0:
            step(a_s, b_s, co_s, db_s)
        for z in range(NZ):
            pow_ref[n, z] = a_s[z + 1, OWN:HIGH]
    for z in range(NZ):
        next_ref[0, z // 2, at(z, 0, STRIP)] = a_s[z + 1, OWN:HIGH]


def powers_body(
    core_ref, side_ref, block_ref, k_ref, own_ref, below_ref, above_ref, early_ref,
    out_ref, k_s, co_s, a_s, b_s, db_s, pow_s,
):
    coefficients(coarse_size, k_ref, k_s, co_s)
    clear_ends(a_s, b_s)
    load_window(a_s, strips_of(below_ref, 0), strips_of(own_ref, 0), strips_of(above_ref, 0))
    for n in range(5):
        for z in range(NZ):
            pow_s[n, z] = early_ref[n, z]
    for n in range(3):
        step(a_s, b_s, co_s, db_s)
        for z in range(NZ):
            pow_s[5 + n, z] = a_s[z + 1, OWN:HIGH]
    c = block_ref[0]
    for b in range(NB):
        power = jnp.clip(b - c, 0, NB - 1)
        live = b >= c
        for y in range(4):
            value = pow_s[power, 2 * (2 * y + side_ref[0]) + core_ref[0]]
            out_ref[b, y * STRIP : (y + 1) * STRIP] = jnp.where(live, value, 0.0)


SWEEP_SCRATCH = (
    pltpu.VMEM((NZ + 2, WIN, LANES), F32),
    pltpu.VMEM((7, NZ, WIN, LANES), F32),
    pltpu.VMEM((NZ + 2, WIN, LANES), F32),
    pltpu.VMEM((NZ + 2, WIN, LANES), F32),
    pltpu.VMEM((NZ, WIN, LANES), F32),
)


def collect_body(core_ref, side_ref, got_ref, early_ref, late_ref, out_ref):
    for y in range(4):
        z = 2 * (2 * y + side_ref[0]) + core_ref[0]
        rows = slice(y * STRIP, (y + 1) * STRIP)
        total = got_ref[0, rows]
        for b in range(1, NB):
            total = total + got_ref[b, rows]
        out_ref[7 * 4 + y, 0:STRIP] = total
        for n in range(6):
            out_ref[n * 4 + y, 0:STRIP] = early_ref[n, z]
        out_ref[6 * 4 + y, 0:STRIP] = late_ref[z]
        for n in range(8):
            out_ref[n * 4 + y, STRIP:16] = jnp.zeros((16 - STRIP, LANES), F32)


def home_body(got_ref, out_ref):
    for zl in range(4):
        for y in range(4):
            m = chip_order(zl, y)
            for core in range(2):
                out_ref[core, m * STRIP : (m + 1) * STRIP] = got_ref[(zl * 2 + core) * 4 + y, 0:STRIP]


def on_device(guess, source, diffusivity, initial):
    guess = guess[0]
    source = source[0]
    core = lax.axis_index("core")[None]
    side = lax.axis_index("zhi")[None]
    place = lax.axis_index(("zl", "core"))[None]
    block = lax.axis_index(BLOCKS)[None]

    previous = lax.ppermute(guess, BLOCKS + ("zl", "core"), [(8 * b + 7, 8 * b + 15) for b in range(NB - 1)])
    sent = pl.pallas_call(
        scatter_body,
        out_shape=sds(64, PAIR, LANES),
        in_specs=[pl.BlockSpec(memory_space=pltpu.SMEM)] * 2 + [pl.BlockSpec(memory_space=pltpu.HBM)] * 4,
        out_specs=pl.BlockSpec(memory_space=pltpu.VMEM),
        scratch_shapes=[
            pltpu.VMEM((2, NY, LANES), F32),
            pltpu.VMEM((2, NY, LANES), F32),
            pltpu.SemaphoreType.DMA((2,)),
        ],
        compiler_params=pltpu.CompilerParams(vmem_limit_bytes=60 * 1024 * 1024),
    )(place, block, source, previous, diffusivity, initial)
    strips = lax.all_to_all(sent, BLOCK, 0, 0, tiled=True).reshape(8, 8, PAIR, LANES)
    strips2 = lax.ppermute(strips, "core", [(0, 1), (1, 0)])

    f, k, f_up, f_down = call(
        pack_body,
        [sds(8, NZ, STRIP, LANES), sds(NZ, WIN, LANES)] + [sds(4, 8, PAIR, LANES)] * 2,
        core, strips, strips2, smem=1,
    )

    def exchange(up, down):
        below = lax.ppermute(up, ("zl", "y"), neighbours(1))
        above = lax.ppermute(down, ("zl", "y"), neighbours(-1))
        return below, above

    flops = NZ * WIN * LANES * 15
    window = pltpu.VMEM((NZ, WIN, LANES), F32)
    f_below, f_above = exchange(f_up, f_down)
    v_early, state = call(
        early_body, [sds(6, NZ, STRIP, LANES), sds(3, 8, PAIR, LANES)],
        k, f, f_up, f_below, f_above, flops=12 * flops,
        scratch=SWEEP_SCRATCH + (pltpu.VMEM((6, NZ, WIN, LANES), F32),),
    )
    below, above = exchange(state, state)
    v_late, first_powers, last = call(
        late_body, [sds(NZ, STRIP, LANES), sds(5, NZ, STRIP, LANES), sds(1, 8, PAIR, LANES)],
        block, k, state, below, above, f_up, f_below, f_above, smem=1, flops=14 * flops,
        scratch=SWEEP_SCRATCH + (pltpu.VMEM((NZ + 2, WIN, LANES), F32), window),
    )
    below, above = exchange(last, last)
    (powers,) = call(
        powers_body, [sds(NB, 4 * STRIP, LANES)],
        core, side, block, k, last, below, above, first_powers, smem=3, flops=6 * flops,
        scratch=SWEEP_SCRATCH + (pltpu.VMEM((NB, NZ, STRIP, LANES), F32),),
    )
    arrived = lax.all_to_all(powers, BLOCKS, 0, 0, tiled=True)
    (back,) = call(collect_body, [sds(32, 16, LANES)], core, side, arrived, v_early, v_late, smem=2)
    returned = lax.all_to_all(back, ("zl", "core", "y"), 0, 0, tiled=True)
    (result,) = call(home_body, [sds(2, NY, LANES)], returned)
    return result[None]


def solution(mesh):
    fine = Mesh(mesh.devices.reshape(SIZES), AXES)
    tm = ("x", "zh", "zl", "core")
    space = ("y", "zhi")
    in_specs = (P(tm, space, None, None), P(tm, space, None, None), P(space, None, None), P(space, None, None))
    out_specs = P(tm, space, None, None)
    return jax.shard_map(on_device, mesh=fine, in_specs=in_specs, out_specs=out_specs, check_vma=False)
```

time: 176 us -> 166 us (0.943)
  starting transfers between devices: 31 us -> 21.6 us
  Pallas kernels: 11.9 us -> 16.4 us
  local copies, waits for them, and re-layouts: 3.71 us -> 0.67 us
    ppermute x5 -> x3, waiting for transfers between devices: 15.2 us -> 10.8 us  [exchange(): above = lax.ppermute(down, ('zl', 'y'), neighbours(-1))]
    all_to_all x1 -> x0, starting transfers between devices: 3.44 us -> none  [on_device(): v = lax.all_to_all(v, 'zhi', 0, 0, tiled=True)]
    ppermute x5 -> x3, waiting for transfers between devices: 0.2 us -> 3.32 us  [exchange(): below = lax.ppermute(up, ('zl', 'y'), neighbours(1))]
    unnamed x10 -> x2, local copies, waits for them, and re-layouts: 3.71 us -> 0.67 us
    pallas_call x7 -> x6, Pallas kernels: 11.4 us -> 14.4 us  [call(): pl.pallas_call(body, out_shape=list(outs), in_specs=specs, out_specs=out_...]
    all_to_all x2, blocking collectives: 86.7 us -> 84.1 us  [the longest x1 56.8 us: on_device(): lax.all_to_all(sent, BLOCK, 0, 0, tiled=True).reshape(8, 8, PAIR, LANES)]
    ppermute x5 -> x3, starting transfers between devices: 6.46 us -> 3.88 us  [exchange(): above = lax.ppermute(down, ('zl', 'y'), neighbours(-1))]
    all_to_all x1, blocking collectives: 24.7 us -> 27 us  [on_device(): returned = lax.all_to_all(back, ('zl', 'core', 'y'), 0, 0, tiled=True)]
  transfers between devices with their start and end apart: 13 -> 8, of which waited for: 6 -> 7; matrix products, arithmetic and copies ran while one was open for 0% -> 0% of each run, Pallas kernels for 3% -> 0%
where the time goes in v6:
time: 166 us
  blocking collectives  111 us (67%)
  starting transfers between devices  21.6 us (13%)
  Pallas kernels  16.4 us (10%)
  waiting for transfers between devices  16 us (10%)
    all_to_all x1, blocking collectives, on_device(): lax.all_to_all(sent, BLOCK, 0, 0, tiled=True).reshape(8, 8, PAIR, LANES)  56.8 us
    all_to_all x1, blocking collectives, on_device(): arrived = lax.all_to_all(powers, BLOCKS, 0, 0, tiled=True)  27.3 us
    all_to_all x1, blocking collectives, on_device(): returned = lax.all_to_all(back, ('zl', 'core', 'y'), 0, 0, tiled=True)  27 us
    pallas_call x6, Pallas kernels, call(): pl.pallas_call(body, out_shape=list(outs), in_specs=specs, out_specs=out_...  14.4 us
    ppermute x3, starting transfers between devices, exchange(): below = lax.ppermute(up, ('zl', 'y'), neighbours(1))  13.5 us
    ppermute x3, waiting for transfers between devices, exchange(): above = lax.ppermute(down, ('zl', 'y'), neighbours(-1))  10.8 us
    ppermute x3, starting transfers between devices, exchange(): above = lax.ppermute(down, ('zl', 'y'), neighbours(-1))  3.88 us
    ppermute x1, starting transfers between devices, on_device(): strips2 = lax.ppermute(strips, 'core', [(0, 1), (1, 0)])  3.54 us
  transfers between devices with their start and end apart: 8, of which 7 were waited for; matrix products, arithmetic and copies ran while one was open for 0% of the time, Pallas kernels for 0%

profile of v6, /device:TPU:1, one launch (start us, length us, event | category | flops | bytes accessed | tf_op | source)
XLA Modules:
  0.0 165.9 jit_solution(7096276639457338575)
XLA Ops:
  0.0 0.7 collective-permute-start
  0.7 0.0 collective-permute-done.prev_hbm
  0.7 0.0 copy-start
  0.7 0.7 copy-done
  1.4 2.0 %shard_map.46 = f32[64,24,128]{2,1,0:T(8,128)} custom-call(s32[1]{0:T(128)} %bitcast.3.j_ref, s32[1]{0:T(128)} %bitcast.2.block_ref, f32[2,192,128]{2,1,0:T(8,128)} %bitcast.10, f32[2,192,128]{2,1,0:T(8,128)} %copy-done, f32[2,192,128]{2,1,0:T(8,128)} %cond_hbm.1, f32[2,192,128]{2,1,0:T(8,128)} %init_hbm.1), custom_call_target="tpu_custom_call" | custom-call | tf_op jit(solution)/shard_map/pallas_call | solution.py:326
  3.3 56.8 %all_to_all.15 = f32[64,24,128]{2,1,0:T(8,128)S(1)} all-to-all(f32[64,24,128]{2,1,0:T(8,128)} %shard_map.46), channel_id=1, replica_groups=mesh['x'=4,'zh'=2,'zl'=4,'core'=2,'y'=4,'zhi'=2] {'zl','core','y','zhi'}, dimensions={0} | all-to-all | bytes 1572864 | tf_op jit(solution)/shard_map/all_to_all | solution.py:338
  60.2 3.5 %collective-permute-start.1 = (f32[8,8,24,128]{3,2,1,0:T(8,128)S(1)}, f32[8,8,24,128]{3,2,1,0:T(8,128)S(1)}, u32[]{:S(2)}, u32[]{:S(2)}) collective-permute-start(f32[8,8,24,128]{3,2,1,0:T(8,128)S(1)} %bitcast.8), channel_id=1, source_target_pairs={{0,8},{8,0},{1,9},{9,1},{2,10},{10,2},{3,11},{11,3},{4,12},{12,4},... | collective-permute-start | bytes 2359304 | tf_op jit(solution)/shard_map/ppermute | solution.py:339
  63.7 1.9 %collective-permute-done.1.other_ref = f32[8,8,24,128]{3,2,1,0:T(8,128)S(1)} collective-permute-done((f32[8,8,24,128]{3,2,1,0:T(8,128)S(1)}, f32[8,8,24,128]{3,2,1,0:T(8,128)S(1)}, u32[]{:S(2)}, u32[]{:S(2)}) %collective-permute-start.1) | collective-permute-done | bytes 786464 | tf_op jit(solution)/shard_map/ppermute | solution.py:339
  65.6 0.2 shard_map.47
  65.8 1.3 collective-permute-start.3
  67.1 4.0 %collective-permute-start.2 = (f32[4,8,24,128]{3,2,1,0:T(8,128)S(1)}, f32[4,8,24,128]{3,2,1,0:T(8,128)S(1)}, u32[]{:S(2)}, u32[]{:S(2)}) collective-permute-start(f32[4,8,24,128]{3,2,1,0:T(8,128)S(1)} %get-tuple-element.16.own_ref.start_ref), channel_id=1, source_target_pairs={{0,2},{2,4},{4,6},{6,22},{22,20},{20,18},{18,16},{16,32},{32,34},{... | collective-permute-start | bytes 1179656 | tf_op jit(solution)/shard_map/ppermute | solution.py:348
  71.1 6.9 %collective-permute-done.3.above_ref.start_above_ref = f32[4,8,24,128]{3,2,1,0:T(8,128)S(1)} collective-permute-done((f32[4,8,24,128]{3,2,1,0:T(8,128)S(1)}, f32[4,8,24,128]{3,2,1,0:T(8,128)S(1)}, u32[]{:S(2)}, u32[]{:S(2)}) %collective-permute-start.3) | collective-permute-done | bytes 393248 | tf_op jit(solution)/shard_map/ppermute | solution.py:349
  78.0 0.9 collective-permute-done.2.below_ref.start_below_ref
  78.9 4.3 %shard_map.48 = (f32[6,16,12,128]{3,2,1,0:T(8,128)S(1)}, f32[3,8,24,128]{3,2,1,0:T(8,128)S(1)}) custom-call(f32[16,40,128]{2,1,0:T(8,128)S(1)} %get-tuple-element.14.k_ref, f32[8,16,12,128]{3,2,1,0:T(8,128)S(1)} %get-tuple-element.15.f_ref, f32[4,8,24,128]{3,2,1,0:T(8,128)S(1)} %get-tuple-element.16.own_ref.start_ref, ...), custom_call_target="tpu_custom_call" | custom-call | flops 14745600 | bytes 3178496 | tf_op jit(solution)/shard_map/pallas_call | solution.py:49
  83.2 1.3 collective-permute-start.5
  84.5 4.8 %collective-permute-start.4 = (f32[3,8,24,128]{3,2,1,0:T(8,128)S(1)}, f32[3,8,24,128]{3,2,1,0:T(8,128)S(1)}, u32[]{:S(2)}, u32[]{:S(2)}) collective-permute-start(f32[3,8,24,128]{3,2,1,0:T(8,128)S(1)} %get-tuple-element.18.own_ref), channel_id=1, source_target_pairs={{0,2},{2,4},{4,6},{6,22},{22,20},{20,18},{18,16},{16,32},{32,34},{... | collective-permute-start | bytes 884744 | tf_op jit(solution)/shard_map/ppermute | solution.py:348
  89.3 3.8 %collective-permute-done.5.above_ref = f32[3,8,24,128]{3,2,1,0:T(8,128)S(1)} collective-permute-done((f32[3,8,24,128]{3,2,1,0:T(8,128)S(1)}, f32[3,8,24,128]{3,2,1,0:T(8,128)S(1)}, u32[]{:S(2)}, u32[]{:S(2)}) %collective-permute-start.5) | collective-permute-done | bytes 294944 | tf_op jit(solution)/shard_map/ppermute | solution.py:349
  93.1 0.9 collective-permute-done.4.below_ref
  94.0 6.2 %shard_map.49 = (f32[16,12,128]{2,1,0:T(8,128)S(1)}, f32[5,16,12,128]{3,2,1,0:T(8,128)S(1)}, f32[1,8,24,128]{3,2,1,0:T(8,128)S(1)}) custom-call(s32[1]{0:T(128)} %bitcast.2.block_ref, f32[16,40,128]{2,1,0:T(8,128)S(1)} %get-tuple-element.14.k_ref, f32[3,8,24,128]{3,2,1,0:T(8,128)S(1)} %get-tuple-element.18.own_ref, ...), custom_call_target="tpu_custom_call" | custom-call | flops 17203200 | bytes 3080196 | tf_op jit(solution)/shard_map/pallas_call | solution.py:49
  100.3 1.3 collective-permute-start.7
  101.6 4.7 %collective-permute-start.6 = (f32[1,8,24,128]{3,2,1,0:T(8,128)S(1)}, f32[1,8,24,128]{3,2,1,0:T(8,128)S(1)}, u32[]{:S(2)}, u32[]{:S(2)}) collective-permute-start(f32[1,8,24,128]{3,2,1,0:T(8,128)S(1)} %get-tuple-element.19.own_ref), channel_id=1, source_target_pairs={{0,2},{2,4},{4,6},{6,22},{22,20},{20,18},{18,16},{16,32},{32,34},{... | collective-permute-start | bytes 294920 | tf_op jit(solution)/shard_map/ppermute | solution.py:348
  106.3 0.1 collective-permute-done.7.above_ref
  106.4 1.6 collective-permute-done.6.below_ref
  107.9 2.9 %shard_map.50 = f32[8,48,128]{2,1,0:T(8,128)S(1)} custom-call(s32[1]{0:T(128)} %bitcast.core_ref, s32[1]{0:T(128)} %bitcast.1.side_ref, s32[1]{0:T(128)} %bitcast.2.block_ref, f32[16,40,128]{2,1,0:T(8,128)S(1)} %get-tuple-element.14.k_ref, f32[1,8,24,128]{3,2,1,0:T(8,128)S(1)} %get-tuple-element.19.own_ref, ...), custom_call_target="tpu_custom_call" | custom-call | flops 7372800 | bytes 1310732 | tf_op jit(solution)/shard_map/pallas_call | solution.py:49
  110.8 27.3 %all_to_all.16.got_ref = f32[8,48,128]{2,1,0:T(8,128)S(1)} all-to-all(f32[8,48,128]{2,1,0:T(8,128)S(1)} %shard_map.50), channel_id=1, replica_groups=mesh['x'=4,'zh'=2,'zl'=4,'core'=2,'y'=4,'zhi'=2] {'x','zh'}, dimensions={0} | all-to-all | bytes 393216 | tf_op jit(solution)/shard_map/all_to_all | solution.py:372
  138.2 27.0 %all_to_all.17.got_ref = f32[32,16,128]{2,1,0:T(8,128)S(1)} all-to-all(f32[32,16,128]{2,1,0:T(8,128)S(1)} %shard_map.51), channel_id=1, replica_groups=mesh['x'=4,'zh'=2,'zl'=4,'core'=2,'y'=4,'zhi'=2] {'zl','core','y'}, dimensions={0} | all-to-all | bytes 524288 | tf_op jit(solution)/shard_map/all_to_all | solution.py:374
  165.2 0.7 shard_map.52
  (1 shorter events, 0.0 us)
Async XLA Ops:
  0.0 0.7 collective-permute-start
  0.7 0.7 copy-start
  60.2 5.4 %collective-permute-start.1 = (f32[8,8,24,128]{3,2,1,0:T(8,128)S(1)}, f32[8,8,24,128]{3,2,1,0:T(8,128)S(1)}, u32[]{:S(2)}, u32[]{:S(2)}) collective-permute-start(f32[8,8,24,128]{3,2,1,0:T(8,128)S(1)} %bitcast.8), channel_id=1, source_target_pairs={{0,8},{8,0},{1,9},{9,1},{2,10},{10,2},{3,11},{11,3},{4,12},{12,4},... | collective-permute-start | bytes 2359304 | tf_op jit(solution)/shard_map/ppermute | solution.py:339
  65.8 12.2 %collective-permute-start.3 = (f32[4,8,24,128]{3,2,1,0:T(8,128)S(1)}, f32[4,8,24,128]{3,2,1,0:T(8,128)S(1)}, u32[]{:S(2)}, u32[]{:S(2)}) collective-permute-start(f32[4,8,24,128]{3,2,1,0:T(8,128)S(1)} %get-tuple-element.17), channel_id=1, source_target_pairs={{2,0},{4,2},{6,4},{22,6},{20,22},{18,20},{16,18},{32,16},{34,32},{... | collective-permute-start | bytes 1179656 | tf_op jit(solution)/shard_map/ppermute | solution.py:349
  67.1 11.8 %collective-permute-start.2 = (f32[4,8,24,128]{3,2,1,0:T(8,128)S(1)}, f32[4,8,24,128]{3,2,1,0:T(8,128)S(1)}, u32[]{:S(2)}, u32[]{:S(2)}) collective-permute-start(f32[4,8,24,128]{3,2,1,0:T(8,128)S(1)} %get-tuple-element.16.own_ref.start_ref), channel_id=1, source_target_pairs={{0,2},{2,4},{4,6},{6,22},{22,20},{20,18},{18,16},{16,32},{32,34},{... | collective-permute-start | bytes 1179656 | tf_op jit(solution)/shard_map/ppermute | solution.py:348
  83.2 9.9 %collective-permute-start.5 = (f32[3,8,24,128]{3,2,1,0:T(8,128)S(1)}, f32[3,8,24,128]{3,2,1,0:T(8,128)S(1)}, u32[]{:S(2)}, u32[]{:S(2)}) collective-permute-start(f32[3,8,24,128]{3,2,1,0:T(8,128)S(1)} %get-tuple-element.18.own_ref), channel_id=1, source_target_pairs={{2,0},{4,2},{6,4},{22,6},{20,22},{18,20},{16,18},{32,16},{34,32},{... | collective-permute-start | bytes 884744 | tf_op jit(solution)/shard_map/ppermute | solution.py:349
  84.5 9.5 %collective-permute-start.4 = (f32[3,8,24,128]{3,2,1,0:T(8,128)S(1)}, f32[3,8,24,128]{3,2,1,0:T(8,128)S(1)}, u32[]{:S(2)}, u32[]{:S(2)}) collective-permute-start(f32[3,8,24,128]{3,2,1,0:T(8,128)S(1)} %get-tuple-element.18.own_ref), channel_id=1, source_target_pairs={{0,2},{2,4},{4,6},{6,22},{22,20},{20,18},{18,16},{16,32},{32,34},{... | collective-permute-start | bytes 884744 | tf_op jit(solution)/shard_map/ppermute | solution.py:348
  100.3 6.1 %collective-permute-start.7 = (f32[1,8,24,128]{3,2,1,0:T(8,128)S(1)}, f32[1,8,24,128]{3,2,1,0:T(8,128)S(1)}, u32[]{:S(2)}, u32[]{:S(2)}) collective-permute-start(f32[1,8,24,128]{3,2,1,0:T(8,128)S(1)} %get-tuple-element.19.own_ref), channel_id=1, source_target_pairs={{2,0},{4,2},{6,4},{22,6},{20,22},{18,20},{16,18},{32,16},{34,32},{... | collective-permute-start | bytes 294920 | tf_op jit(solution)/shard_map/ppermute | solution.py:349
  101.6 6.4 %collective-permute-start.6 = (f32[1,8,24,128]{3,2,1,0:T(8,128)S(1)}, f32[1,8,24,128]{3,2,1,0:T(8,128)S(1)}, u32[]{:S(2)}, u32[]{:S(2)}) collective-permute-start(f32[1,8,24,128]{3,2,1,0:T(8,128)S(1)} %get-tuple-element.19.own_ref), channel_id=1, source_target_pairs={{0,2},{2,4},{4,6},{6,22},{22,20},{20,18},{18,16},{16,32},{32,34},{... | collective-permute-start | bytes 294920 | tf_op jit(solution)/shard_map/ppermute | solution.py:348

commit v7 on v6

--- a/solution.py
+++ b/solution.py
@@ -61,23 +61,23 @@
     return jax.ShapeDtypeStruct(shape, F32)
 
 
-def scatter_body(j_ref, block_ref, src_hbm, prev_hbm, cond_hbm, init_hbm, out_ref, src_ref, extra_ref, sems):
+def scatter_body(
+    j_ref, block_ref, src_hbm, prev6_hbm, prev7_hbm, cond_hbm, init_hbm, out_ref, src_ref, extra_ref, sems
+):
     place = j_ref[0]
-    zero = jnp.zeros((STRIP, LANES), F32)
     source_copy = pltpu.make_async_copy(src_hbm, src_ref, sems.at[0])
     source_copy.start()
-
-    @pl.when(place < 7)
-    def _():
-        pltpu.make_async_copy(cond_hbm, extra_ref, sems.at[1]).start()
-
-    @pl.when((place == 7) & (block_ref[0] == 0))
-    def _():
-        pltpu.make_async_copy(init_hbm, extra_ref, sems.at[1]).start()
-
-    @pl.when((place == 7) & (block_ref[0] > 0))
-    def _():
-        pltpu.make_async_copy(prev_hbm, extra_ref, sems.at[1]).start()
+    first = block_ref[0] == 0
+    for live, field in (
+        (place < 6, cond_hbm),
+        ((place > 5) & first, init_hbm),
+        ((place == 6) & jnp.logical_not(first), prev6_hbm),
+        ((place == 7) & jnp.logical_not(first), prev7_hbm),
+    ):
+
+        @pl.when(live)
+        def _(field=field):
+            pltpu.make_async_copy(field, extra_ref, sems.at[1]).start()
 
     def each():
         for zl in range(4):
@@ -88,35 +88,41 @@
 
     source_copy.wait()
     for to, core, m in each():
-        out_ref[to, 0:STRIP] = src_ref[core, m * STRIP : (m + 1) * STRIP]
+        for r in range(6):
+            row = m * STRIP + 2 * r
+            out_ref[to, r] = src_ref[core, row : row + 2]
     pltpu.make_async_copy(cond_hbm, extra_ref, sems.at[1]).wait()
 
-    def fill(shift):
+    def fill(shift, half):
         for to, core, m in each():
             m = m + shift
-            if 0 <= m < CHIPS:
-                out_ref[to, STRIP:PAIR] = extra_ref[core, m * STRIP : (m + 1) * STRIP]
-            else:
-                out_ref[to, STRIP:PAIR] = zero
-
-    pl.when(place == 1)(functools.partial(fill, 1))
-    pl.when(place == 2)(functools.partial(fill, -1))
-    pl.when((place != 1) & (place != 2))(functools.partial(fill, 0))
+            for r in range(3):
+                row = m * STRIP + 6 * half + 2 * r
+                if 0 <= m < CHIPS:
+                    out_ref[to, 6 + r] = extra_ref[core, row : row + 2]
+                else:
+                    out_ref[to, 6 + r] = jnp.zeros((2, LANES), F32)
+
+    for half in range(2):
+        pl.when((place == half) | (place == 6 + half))(functools.partial(fill, 0, half))
+        pl.when(place == 2 + half)(functools.partial(fill, 1, half))
+        pl.when(place == 4 + half)(functools.partial(fill, -1, half))
 
 
 def pack_body(core_ref, own_ref, other_ref, f_ref, k_ref, up_ref, down_ref):
     def order(halves):
         for z in range(NZ):
             half, s = halves[z % 2], z // 2
-            for n in range(8):
-                f_ref[n, z] = half[n, s, 0:STRIP]
-            start = half[7, s, STRIP:PAIR]
-            up_ref[0, s, at(z, 0, STRIP)] = start
-            down_ref[0, s, at(z, 0, STRIP)] = start
             k_ref[z, 0:LOW] = jnp.zeros((LOW, LANES), F32)
-            k_ref[z, LOW:OWN] = half[2, s, STRIP:PAIR]
-            k_ref[z, OWN:HIGH] = half[0, s, STRIP:PAIR]
-            k_ref[z, HIGH:WIN] = half[1, s, STRIP:PAIR]
+            for r in range(6):
+                for n in range(8):
+                    f_ref[n, z, 2 * r : 2 * r + 2] = half[n, s, r]
+                part, extra = r // 3, 6 + r % 3
+                start = half[6 + part, s, extra]
+                up_ref[0, s, at(z, 2 * r, 2 * r + 2)] = start
+                down_ref[0, s, at(z, 2 * r, 2 * r + 2)] = start
+                for place, base in ((4, LOW), (0, OWN), (2, HIGH)):
+                    k_ref[z, base + 2 * r : base + 2 * r + 2] = half[place + part, s, extra]
 
     pl.when(core_ref[0] == 0)(functools.partial(order, (own_ref, other_ref)))
     pl.when(core_ref[0] == 1)(functools.partial(order, (other_ref, own_ref)))
@@ -185,23 +191,31 @@
     lax.fori_loop(0, NZ, layer, 0)
 
 
-def one_sweep(src, dst, co_s, db_s):
-    for z in range(NZ):
-        w = src[z + 1]
-        acc = (db_s[z] + (1.0 - damping) * w) + (co_s[0, z] * src[z] + co_s[1, z] * src[z + 2])
-        acc = acc + (co_s[2, z] * pltpu.roll(w, 1, 0) + co_s[3, z] * pltpu.roll(w, WIN - 1, 0))
-        acc = acc + (co_s[4, z] * pltpu.roll(w, 1, 1) + co_s[5, z] * pltpu.roll(w, LANES - 1, 1))
-        dst[z + 1] = acc
-
-
-def step(a_s, b_s, co_s, db_s, forcing=None):
-    for z in range(NZ):
-        target = a_s[z + 1]
+def one_sweep(src, dst, co_s, db_s, rows):
+    tall = rows.stop - rows.start
+    for z in range(NZ):
+        w = src[z + 1, rows]
+        acc = (db_s[z, rows] + (1.0 - damping) * w) + (
+            co_s[0, z, rows] * src[z, rows] + co_s[1, z, rows] * src[z + 2, rows]
+        )
+        acc = acc + (
+            co_s[2, z, rows] * pltpu.roll(w, 1, 0) + co_s[3, z, rows] * pltpu.roll(w, tall - 1, 0)
+        )
+        acc = acc + (
+            co_s[4, z, rows] * pltpu.roll(w, 1, 1) + co_s[5, z, rows] * pltpu.roll(w, LANES - 1, 1)
+        )
+        dst[z + 1, rows] = acc
+
+
+def step(halo, a_s, b_s, co_s, db_s, forcing=None):
+    rows = slice(8, 32) if halo <= 4 else slice(8, WIN) if halo <= 8 else slice(0, WIN)
+    for z in range(NZ):
+        target = a_s[z + 1, rows]
         if forcing is not None:
-            target = target + step_size * forcing[z]
-        db_s[z] = co_s[6, z] * target
-    one_sweep(a_s, b_s, co_s, db_s)
-    one_sweep(b_s, a_s, co_s, db_s)
+            target = target + step_size * forcing[z, rows]
+        db_s[z, rows] = co_s[6, z, rows] * target
+    one_sweep(a_s, b_s, co_s, db_s, rows)
+    one_sweep(b_s, a_s, co_s, db_s, rows)
 
 
 def early_body(k_ref, f_ref, own_ref, below_ref, above_ref, out_ref, next_ref, k_s, co_s, a_s, b_s, db_s, f_s):
@@ -220,7 +234,7 @@
             f_s[5 - n, z, OWN - STRIP + rows : OWN] = below_ref[1 + n, s, at(z, 0, STRIP - rows)]
             f_s[5 - n, z, HIGH : HIGH + STRIP - rows] = above_ref[1 + n, s, at(z, rows, STRIP)]
     for n in range(6):
-        step(a_s, b_s, co_s, db_s, f_s.at[n])
+        step(12 - 2 * n, a_s, b_s, co_s, db_s, f_s.at[n])
         for z in range(NZ):
             out_ref[n, z] = a_s[z + 1, OWN:HIGH]
     for z in range(NZ):
@@ -238,7 +252,7 @@
     load_window(a_s, strips_of(below_ref, 0), strips_of(own_ref, 0), strips_of(above_ref, 0))
     for n in range(2):
         load_window(f_s, strips_of(below_ref, 1 + n), strips_of(own_ref, 1 + n), strips_of(above_ref, 1 + n))
-        step(a_s, b_s, co_s, db_s, f_s.at[pl.ds(1, NZ)])
+        step(12 - 2 * n, a_s, b_s, co_s, db_s, f_s.at[pl.ds(1, NZ)])
         if n == 0:
             for z in range(NZ):
                 out_ref[z] = a_s[z + 1, OWN:HIGH]
@@ -246,13 +260,13 @@
         y_s[z] = a_s[z + 1]
     coefficients(coarse_size, k_ref, k_s, co_s)
     load_window(a_s, strips_of(start_below_ref, 0), strips_of(start_ref, 0), strips_of(start_above_ref, 0))
-    step(a_s, b_s, co_s, db_s)
+    step(10, a_s, b_s, co_s, db_s)
     later = block_ref[0] > 0
     for z in range(NZ):
         a_s[z + 1] = y_s[z] - jnp.where(later, a_s[z + 1], 0.0)
     for n in range(5):
         if n > 0:
-            step(a_s, b_s, co_s, db_s)
+            step(10 - 2 * n, a_s, b_s, co_s, db_s)
         for z in range(NZ):
             pow_ref[n, z] = a_s[z + 1, OWN:HIGH]
     for z in range(NZ):
@@ -270,7 +284,7 @@
         for z in range(NZ):
             pow_s[n, z] = early_ref[n, z]
     for n in range(3):
-        step(a_s, b_s, co_s, db_s)
+        step(6 - 2 * n, a_s, b_s, co_s, db_s)
         for z in range(NZ):
             pow_s[5 + n, z] = a_s[z + 1, OWN:HIGH]
     c = block_ref[0]
@@ -322,11 +336,13 @@
     place = lax.axis_index(("zl", "core"))[None]
     block = lax.axis_index(BLOCKS)[None]
 
-    previous = lax.ppermute(guess, BLOCKS + ("zl", "core"), [(8 * b + 7, 8 * b + 15) for b in range(NB - 1)])
+    def onward(place):
+        return lax.ppermute(guess, BLOCKS + ("zl", "core"), [(8 * b + 7, 8 * b + 8 + place) for b in range(NB - 1)])
+
     sent = pl.pallas_call(
         scatter_body,
-        out_shape=sds(64, PAIR, LANES),
-        in_specs=[pl.BlockSpec(memory_space=pltpu.SMEM)] * 2 + [pl.BlockSpec(memory_space=pltpu.HBM)] * 4,
+        out_shape=sds(64, 9, 2, LANES),
+        in_specs=[pl.BlockSpec(memory_space=pltpu.SMEM)] * 2 + [pl.BlockSpec(memory_space=pl.ANY)] * 5,
         out_specs=pl.BlockSpec(memory_space=pltpu.VMEM),
         scratch_shapes=[
             pltpu.VMEM((2, NY, LANES), F32),
@@ -334,8 +350,8 @@
             pltpu.SemaphoreType.DMA((2,)),
         ],
         compiler_params=pltpu.CompilerParams(vmem_limit_bytes=60 * 1024 * 1024),
-    )(place, block, source, previous, diffusivity, initial)
-    strips = lax.all_to_all(sent, BLOCK, 0, 0, tiled=True).reshape(8, 8, PAIR, LANES)
+    )(place, block, source, onward(6), onward(7), diffusivity, initial)
+    strips = lax.all_to_all(sent, BLOCK, 0, 0, tiled=True).reshape(8, 8, 9, 2, LANES)
     strips2 = lax.ppermute(strips, "core", [(0, 1), (1, 0)])
 
     f, k, f_up, f_down = call(

time: 166 us -> 159 us (0.958)
  blocking collectives: 111 us -> 104 us
  starting transfers between devices: 21.6 us -> 23.3 us
    all_to_all x1, blocking collectives: 56.8 us -> 49.3 us  [on_device(): lax.all_to_all(sent, BLOCK, 0, 0, tiled=True).reshape(8, 8, 9, 2, LANES)]
  transfers between devices with their start and end apart: 8 -> 9, of which waited for: 7 -> 7; matrix products, arithmetic and copies ran while one was open for 0% -> 0% of each run, Pallas kernels for 0% -> 0%
where the time goes in v7:
time: 159 us
  blocking collectives  104 us (65%)
  starting transfers between devices  23.3 us (15%)
  waiting for transfers between devices  15.7 us (10%)
  Pallas kernels  15.1 us (9%)
    all_to_all x1, blocking collectives, on_device(): lax.all_to_all(sent, BLOCK, 0, 0, tiled=True).reshape(8, 8, 9, 2, LANES)  49.3 us
    all_to_all x1, blocking collectives, on_device(): arrived = lax.all_to_all(powers, BLOCKS, 0, 0, tiled=True)  27.4 us
    all_to_all x1, blocking collectives, on_device(): returned = lax.all_to_all(back, ('zl', 'core', 'y'), 0, 0, tiled=True)  26.9 us
    ppermute x3, starting transfers between devices, exchange(): below = lax.ppermute(up, ('zl', 'y'), neighbours(1))  13.5 us
    pallas_call x6, Pallas kernels, call(): pl.pallas_call(body, out_shape=list(outs), in_specs=specs, out_specs=out_...  13.2 us
    ppermute x3, waiting for transfers between devices, exchange(): above = lax.ppermute(down, ('zl', 'y'), neighbours(-1))  10.8 us
    ppermute x1, starting transfers between devices, on_device(): strips2 = lax.ppermute(strips, 'core', [(0, 1), (1, 0)])  4.57 us
    ppermute x3, starting transfers between devices, exchange(): above = lax.ppermute(down, ('zl', 'y'), neighbours(-1))  3.88 us
  transfers between devices with their start and end apart: 9, of which 7 were waited for; matrix products, arithmetic and copies ran while one was open for 0% of the time, Pallas kernels for 0%

profile of v7, /device:TPU:1, one launch (start us, length us, event | category | flops | bytes accessed | tf_op | source)
XLA Modules:
  0.0 158.6 jit_solution(5174674208025699609)
XLA Ops:
  0.0 0.7 collective-permute-start.1
  0.7 0.7 collective-permute-start
  1.4 0.0 collective-permute-done.1.prev7_hbm
  1.4 0.0 copy-start
  1.4 0.0 collective-permute-done.prev6_hbm
  1.4 0.0 copy-start.1
  1.4 0.7 copy-done
  2.1 0.1 copy-done.1
  2.1 1.9 %shard_map.46 = f32[64,9,2,128]{3,2,1,0:T(2,128)} custom-call(s32[1]{0:T(128)} %bitcast.3.j_ref, s32[1]{0:T(128)} %bitcast.2.block_ref, f32[2,192,128]{2,1,0:T(8,128)} %bitcast.10, f32[2,192,128]{2,1,0:T(8,128)} %copy-done.1, f32[2,192,128]{2,1,0:T(8,128)} %copy-done, f32[2,192,128]{2,1,0:T(8,128)} %cond_hbm.1, f32[2,192,128]{2,1,0:T(8,128)} %init_hbm.1), custom_call_target="tpu_custom_call" | custom-call | tf_op jit(solution)/shard_map/pallas_call | solution.py:342
  4.1 49.3 %all_to_all.15 = f32[64,9,2,128]{3,2,1,0:T(2,128)S(1)} all-to-all(f32[64,9,2,128]{3,2,1,0:T(2,128)} %shard_map.46), channel_id=1, replica_groups=mesh['x'=4,'zh'=2,'zl'=4,'core'=2,'y'=4,'zhi'=2] {'zl','core','y','zhi'}, dimensions={0} | all-to-all | bytes 1179648 | tf_op jit(solution)/shard_map/all_to_all | solution.py:354
  53.3 4.6 %collective-permute-start.2 = (f32[8,8,9,2,128]{4,3,2,1,0:T(2,128)S(1)}, f32[8,8,9,2,128]{4,3,2,1,0:T(2,128)S(1)}, u32[]{:S(2)}, u32[]{:S(2)}) collective-permute-start(f32[8,8,9,2,128]{4,3,2,1,0:T(2,128)S(1)} %bitcast.8), channel_id=1, source_target_pairs={{0,8},{8,0},{1,9},{9,1},{2,10},{10,2},{3,11},{11,3},{4,12},{12,4},... | collective-permute-start | bytes 1769480 | tf_op jit(solution)/shard_map/ppermute | solution.py:355
  57.9 1.6 %collective-permute-done.2.other_ref = f32[8,8,9,2,128]{4,3,2,1,0:T(2,128)S(1)} collective-permute-done((f32[8,8,9,2,128]{4,3,2,1,0:T(2,128)S(1)}, f32[8,8,9,2,128]{4,3,2,1,0:T(2,128)S(1)}, u32[]{:S(2)}, u32[]{:S(2)}) %collective-permute-start.2) | collective-permute-done | bytes 589856 | tf_op jit(solution)/shard_map/ppermute | solution.py:355
  59.5 0.3 shard_map.47
  59.8 1.3 collective-permute-start.4
  61.1 4.0 %collective-permute-start.3 = (f32[4,8,24,128]{3,2,1,0:T(8,128)S(1)}, f32[4,8,24,128]{3,2,1,0:T(8,128)S(1)}, u32[]{:S(2)}, u32[]{:S(2)}) collective-permute-start(f32[4,8,24,128]{3,2,1,0:T(8,128)S(1)} %get-tuple-element.16.own_ref.start_ref), channel_id=1, source_target_pairs={{0,2},{2,4},{4,6},{6,22},{22,20},{20,18},{18,16},{16,32},{32,34},{... | collective-permute-start | bytes 1179656 | tf_op jit(solution)/shard_map/ppermute | solution.py:364
  65.1 6.9 %collective-permute-done.4.above_ref.start_above_ref = f32[4,8,24,128]{3,2,1,0:T(8,128)S(1)} collective-permute-done((f32[4,8,24,128]{3,2,1,0:T(8,128)S(1)}, f32[4,8,24,128]{3,2,1,0:T(8,128)S(1)}, u32[]{:S(2)}, u32[]{:S(2)}) %collective-permute-start.4) | collective-permute-done | bytes 393248 | tf_op jit(solution)/shard_map/ppermute | solution.py:365
  72.0 0.9 collective-permute-done.3.below_ref.start_below_ref
  72.9 3.9 %shard_map.48 = (f32[6,16,12,128]{3,2,1,0:T(8,128)S(1)}, f32[3,8,24,128]{3,2,1,0:T(8,128)S(1)}) custom-call(f32[16,40,128]{2,1,0:T(8,128)S(1)} %get-tuple-element.14.k_ref, f32[8,16,12,128]{3,2,1,0:T(8,128)S(1)} %get-tuple-element.15.f_ref, f32[4,8,24,128]{3,2,1,0:T(8,128)S(1)} %get-tuple-element.16.own_ref.start_ref, ...), custom_call_target="tpu_custom_call" | custom-call | flops 14745600 | bytes 3178496 | tf_op jit(solution)/shard_map/pallas_call | solution.py:49
  76.8 1.3 collective-permute-start.6
  78.1 4.8 %collective-permute-start.5 = (f32[3,8,24,128]{3,2,1,0:T(8,128)S(1)}, f32[3,8,24,128]{3,2,1,0:T(8,128)S(1)}, u32[]{:S(2)}, u32[]{:S(2)}) collective-permute-start(f32[3,8,24,128]{3,2,1,0:T(8,128)S(1)} %get-tuple-element.18.own_ref), channel_id=1, source_target_pairs={{0,2},{2,4},{4,6},{6,22},{22,20},{20,18},{18,16},{16,32},{32,34},{... | collective-permute-start | bytes 884744 | tf_op jit(solution)/shard_map/ppermute | solution.py:364
  82.8 3.8 %collective-permute-done.6.above_ref = f32[3,8,24,128]{3,2,1,0:T(8,128)S(1)} collective-permute-done((f32[3,8,24,128]{3,2,1,0:T(8,128)S(1)}, f32[3,8,24,128]{3,2,1,0:T(8,128)S(1)}, u32[]{:S(2)}, u32[]{:S(2)}) %collective-permute-start.6) | collective-permute-done | bytes 294944 | tf_op jit(solution)/shard_map/ppermute | solution.py:365
  86.7 0.9 collective-permute-done.5.below_ref
  87.6 5.9 %shard_map.49 = (f32[16,12,128]{2,1,0:T(8,128)S(1)}, f32[5,16,12,128]{3,2,1,0:T(8,128)S(1)}, f32[1,8,24,128]{3,2,1,0:T(8,128)S(1)}) custom-call(s32[1]{0:T(128)} %bitcast.2.block_ref, f32[16,40,128]{2,1,0:T(8,128)S(1)} %get-tuple-element.14.k_ref, f32[3,8,24,128]{3,2,1,0:T(8,128)S(1)} %get-tuple-element.18.own_ref, ...), custom_call_target="tpu_custom_call" | custom-call | flops 17203200 | bytes 3080196 | tf_op jit(solution)/shard_map/pallas_call | solution.py:49
  93.4 1.3 collective-permute-start.8
  94.7 4.7 %collective-permute-start.7 = (f32[1,8,24,128]{3,2,1,0:T(8,128)S(1)}, f32[1,8,24,128]{3,2,1,0:T(8,128)S(1)}, u32[]{:S(2)}, u32[]{:S(2)}) collective-permute-start(f32[1,8,24,128]{3,2,1,0:T(8,128)S(1)} %get-tuple-element.19.own_ref), channel_id=1, source_target_pairs={{0,2},{2,4},{4,6},{6,22},{22,20},{20,18},{18,16},{16,32},{32,34},{... | collective-permute-start | bytes 294920 | tf_op jit(solution)/shard_map/ppermute | solution.py:364
  99.5 0.1 collective-permute-done.8.above_ref
  99.6 1.6 collective-permute-done.7.below_ref
  101.1 2.4 %shard_map.50 = f32[8,48,128]{2,1,0:T(8,128)S(1)} custom-call(s32[1]{0:T(128)} %bitcast.core_ref, s32[1]{0:T(128)} %bitcast.1.side_ref, s32[1]{0:T(128)} %bitcast.2.block_ref, f32[16,40,128]{2,1,0:T(8,128)S(1)} %get-tuple-element.14.k_ref, f32[1,8,24,128]{3,2,1,0:T(8,128)S(1)} %get-tuple-element.19.own_ref, ...), custom_call_target="tpu_custom_call" | custom-call | flops 7372800 | bytes 1310732 | tf_op jit(solution)/shard_map/pallas_call | solution.py:49
  103.5 27.4 %all_to_all.16.got_ref = f32[8,48,128]{2,1,0:T(8,128)S(1)} all-to-all(f32[8,48,128]{2,1,0:T(8,128)S(1)} %shard_map.50), channel_id=1, replica_groups=mesh['x'=4,'zh'=2,'zl'=4,'core'=2,'y'=4,'zhi'=2] {'x','zh'}, dimensions={0} | all-to-all | bytes 393216 | tf_op jit(solution)/shard_map/all_to_all | solution.py:388
  131.0 26.9 %all_to_all.17.got_ref = f32[32,16,128]{2,1,0:T(8,128)S(1)} all-to-all(f32[32,16,128]{2,1,0:T(8,128)S(1)} %shard_map.51), channel_id=1, replica_groups=mesh['x'=4,'zh'=2,'zl'=4,'core'=2,'y'=4,'zhi'=2] {'zl','core','y'}, dimensions={0} | all-to-all | bytes 524288 | tf_op jit(solution)/shard_map/all_to_all | solution.py:390
  157.9 0.7 shard_map.52
  (1 shorter events, 0.0 us)
Async XLA Ops:
  0.0 1.4 collective-permute-start.1
  0.7 0.7 collective-permute-start
  1.4 0.7 copy-start
  1.4 0.7 copy-start.1
  53.3 6.2 %collective-permute-start.2 = (f32[8,8,9,2,128]{4,3,2,1,0:T(2,128)S(1)}, f32[8,8,9,2,128]{4,3,2,1,0:T(2,128)S(1)}, u32[]{:S(2)}, u32[]{:S(2)}) collective-permute-start(f32[8,8,9,2,128]{4,3,2,1,0:T(2,128)S(1)} %bitcast.8), channel_id=1, source_target_pairs={{0,8},{8,0},{1,9},{9,1},{2,10},{10,2},{3,11},{11,3},{4,12},{12,4},... | collective-permute-start | bytes 1769480 | tf_op jit(solution)/shard_map/ppermute | solution.py:355
  59.8 12.2 %collective-permute-start.4 = (f32[4,8,24,128]{3,2,1,0:T(8,128)S(1)}, f32[4,8,24,128]{3,2,1,0:T(8,128)S(1)}, u32[]{:S(2)}, u32[]{:S(2)}) collective-permute-start(f32[4,8,24,128]{3,2,1,0:T(8,128)S(1)} %get-tuple-element.17), channel_id=1, source_target_pairs={{2,0},{4,2},{6,4},{22,6},{20,22},{18,20},{16,18},{32,16},{34,32},{... | collective-permute-start | bytes 1179656 | tf_op jit(solution)/shard_map/ppermute | solution.py:365
  61.1 11.8 %collective-permute-start.3 = (f32[4,8,24,128]{3,2,1,0:T(8,128)S(1)}, f32[4,8,24,128]{3,2,1,0:T(8,128)S(1)}, u32[]{:S(2)}, u32[]{:S(2)}) collective-permute-start(f32[4,8,24,128]{3,2,1,0:T(8,128)S(1)} %get-tuple-element.16.own_ref.start_ref), channel_id=1, source_target_pairs={{0,2},{2,4},{4,6},{6,22},{22,20},{20,18},{18,16},{16,32},{32,34},{... | collective-permute-start | bytes 1179656 | tf_op jit(solution)/shard_map/ppermute | solution.py:364
  76.8 9.9 %collective-permute-start.6 = (f32[3,8,24,128]{3,2,1,0:T(8,128)S(1)}, f32[3,8,24,128]{3,2,1,0:T(8,128)S(1)}, u32[]{:S(2)}, u32[]{:S(2)}) collective-permute-start(f32[3,8,24,128]{3,2,1,0:T(8,128)S(1)} %get-tuple-element.18.own_ref), channel_id=1, source_target_pairs={{2,0},{4,2},{6,4},{22,6},{20,22},{18,20},{16,18},{32,16},{34,32},{... | collective-permute-start | bytes 884744 | tf_op jit(solution)/shard_map/ppermute | solution.py:365
  78.1 9.5 %collective-permute-start.5 = (f32[3,8,24,128]{3,2,1,0:T(8,128)S(1)}, f32[3,8,24,128]{3,2,1,0:T(8,128)S(1)}, u32[]{:S(2)}, u32[]{:S(2)}) collective-permute-start(f32[3,8,24,128]{3,2,1,0:T(8,128)S(1)} %get-tuple-element.18.own_ref), channel_id=1, source_target_pairs={{0,2},{2,4},{4,6},{6,22},{22,20},{20,18},{18,16},{16,32},{32,34},{... | collective-permute-start | bytes 884744 | tf_op jit(solution)/shard_map/ppermute | solution.py:364
  93.4 6.1 %collective-permute-start.8 = (f32[1,8,24,128]{3,2,1,0:T(8,128)S(1)}, f32[1,8,24,128]{3,2,1,0:T(8,128)S(1)}, u32[]{:S(2)}, u32[]{:S(2)}) collective-permute-start(f32[1,8,24,128]{3,2,1,0:T(8,128)S(1)} %get-tuple-element.19.own_ref), channel_id=1, source_target_pairs={{2,0},{4,2},{6,4},{22,6},{20,22},{18,20},{16,18},{32,16},{34,32},{... | collective-permute-start | bytes 294920 | tf_op jit(solution)/shard_map/ppermute | solution.py:365
  94.7 6.4 %collective-permute-start.7 = (f32[1,8,24,128]{3,2,1,0:T(8,128)S(1)}, f32[1,8,24,128]{3,2,1,0:T(8,128)S(1)}, u32[]{:S(2)}, u32[]{:S(2)}) collective-permute-start(f32[1,8,24,128]{3,2,1,0:T(8,128)S(1)} %get-tuple-element.19.own_ref), channel_id=1, source_target_pairs={{0,2},{2,4},{4,6},{6,22},{22,20},{20,18},{18,16},{16,32},{32,34},{... | collective-permute-start | bytes 294920 | tf_op jit(solution)/shard_map/ppermute | solution.py:364

commit v8 on v7

--- a/solution.py
+++ b/solution.py
@@ -32,9 +32,15 @@
     return zl * 4 + (y if zl % 2 == 0 else 3 - y)
 
 
-def neighbours(step):
-    place = {chip_order(zl, y): zl * 4 + y for zl in range(4) for y in range(4)}
-    return [(place[m], place[m + step]) for m in range(CHIPS) if 0 <= m + step < CHIPS]
+def neighbour_route():
+    place = {chip_order(zl, y): (zl, y) for zl in range(4) for y in range(4)}
+    route = []
+    for core, step in ((0, 1), (1, -1)):
+        for m in range(CHIPS):
+            if 0 <= m + step < CHIPS:
+                (zl, y), (to_zl, to_y) = place[m], place[m + step]
+                route.append(((zl * 2 + core) * 4 + y, (to_zl * 2 + core) * 4 + to_y))
+    return route
 
 
 def at(z, first, last):
@@ -61,56 +67,50 @@
     return jax.ShapeDtypeStruct(shape, F32)
 
 
-def scatter_body(
-    j_ref, block_ref, src_hbm, prev6_hbm, prev7_hbm, cond_hbm, init_hbm, out_ref, src_ref, extra_ref, sems
-):
-    place = j_ref[0]
-    source_copy = pltpu.make_async_copy(src_hbm, src_ref, sems.at[0])
-    source_copy.start()
-    first = block_ref[0] == 0
-    for live, field in (
-        (place < 6, cond_hbm),
-        ((place > 5) & first, init_hbm),
-        ((place == 6) & jnp.logical_not(first), prev6_hbm),
-        ((place == 7) & jnp.logical_not(first), prev7_hbm),
-    ):
-
-        @pl.when(live)
-        def _(field=field):
-            pltpu.make_async_copy(field, extra_ref, sems.at[1]).start()
-
-    def each():
-        for zl in range(4):
-            for y in range(4):
-                for zhi in range(2):
-                    for core in range(2):
-                        yield ((zl * 2 + core) * 4 + y) * 2 + zhi, core, chip_order(zl, y)
-
-    source_copy.wait()
-    for to, core, m in each():
+def targets():
+    for zl in range(4):
+        for y in range(4):
+            for zhi in range(2):
+                for core in range(2):
+                    yield ((zl * 2 + core) * 4 + y) * 2 + zhi, core, chip_order(zl, y)
+
+
+def source_body(src_ref, out_ref):
+    for to, core, m in targets():
         for r in range(6):
             row = m * STRIP + 2 * r
             out_ref[to, r] = src_ref[core, row : row + 2]
-    pltpu.make_async_copy(cond_hbm, extra_ref, sems.at[1]).wait()
-
-    def fill(shift, half):
-        for to, core, m in each():
+
+
+def extra_body(j_ref, block_ref, prev6_ref, prev7_ref, cond_ref, init_ref, base_ref, out_ref):
+    place = j_ref[0]
+    first = block_ref[0] == 0
+    later = jnp.logical_not(first)
+
+    def fill(ref, shift, half):
+        for to, core, m in targets():
             m = m + shift
             for r in range(3):
                 row = m * STRIP + 6 * half + 2 * r
                 if 0 <= m < CHIPS:
-                    out_ref[to, 6 + r] = extra_ref[core, row : row + 2]
+                    out_ref[to, 6 + r] = ref[core, row : row + 2]
                 else:
                     out_ref[to, 6 + r] = jnp.zeros((2, LANES), F32)
 
-    for half in range(2):
-        pl.when((place == half) | (place == 6 + half))(functools.partial(fill, 0, half))
-        pl.when(place == 2 + half)(functools.partial(fill, 1, half))
-        pl.when(place == 4 + half)(functools.partial(fill, -1, half))
-
-
-def pack_body(core_ref, own_ref, other_ref, f_ref, k_ref, up_ref, down_ref):
-    def order(halves):
+    for half, prev_ref in ((0, prev6_ref), (1, prev7_ref)):
+        for n, shift in enumerate((0, 1, -1)):
+            pl.when(place == 2 * n + half)(functools.partial(fill, cond_ref, shift, half))
+        pl.when((place == 6 + half) & first)(functools.partial(fill, init_ref, 0, half))
+        pl.when((place == 6 + half) & later)(functools.partial(fill, prev_ref, 0, half))
+
+
+def by_core(core_ref, body, mine, other):
+    pl.when(core_ref[0] == 0)(functools.partial(body, mine, other))
+    pl.when(core_ref[0] == 1)(functools.partial(body, other, mine))
+
+
+def pack_body(core_ref, own_ref, other_ref, f_ref, k_ref, start_ref, out_ref):
+    def order(*halves):
         for z in range(NZ):
             half, s = halves[z % 2], z // 2
             k_ref[z, 0:LOW] = jnp.zeros((LOW, LANES), F32)
@@ -119,22 +119,28 @@
                     f_ref[n, z, 2 * r : 2 * r + 2] = half[n, s, r]
                 part, extra = r // 3, 6 + r % 3
                 start = half[6 + part, s, extra]
-                up_ref[0, s, at(z, 2 * r, 2 * r + 2)] = start
-                down_ref[0, s, at(z, 2 * r, 2 * r + 2)] = start
+                start_ref[0, s, at(z, 2 * r, 2 * r + 2)] = start
+                out_ref[0, s, at(z, 2 * r, 2 * r + 2)] = start
                 for place, base in ((4, LOW), (0, OWN), (2, HIGH)):
                     k_ref[z, base + 2 * r : base + 2 * r + 2] = half[place + part, s, extra]
 
-    pl.when(core_ref[0] == 0)(functools.partial(order, (own_ref, other_ref)))
-    pl.when(core_ref[0] == 1)(functools.partial(order, (other_ref, own_ref)))
-    for z in range(NZ):
-        s = z // 2
-        for n in range(3):
-            rows = 11 - 2 * n
-            early, late = f_ref[n, z], f_ref[5 - n, z]
-            down_ref[1 + n, s, at(z, 0, rows)] = early[0:rows]
-            down_ref[1 + n, s, at(z, rows, STRIP)] = late[0 : STRIP - rows]
-            up_ref[1 + n, s, at(z, STRIP - rows, STRIP)] = early[STRIP - rows : STRIP]
-            up_ref[1 + n, s, at(z, 0, STRIP - rows)] = late[rows:STRIP]
+    by_core(core_ref, order, own_ref, other_ref)
+
+    @pl.when(core_ref[0] == 0)
+    def _():
+        for z in range(NZ):
+            for n in range(3):
+                rows = 11 - 2 * n
+                out_ref[1 + n, z // 2, at(z, STRIP - rows, STRIP)] = f_ref[n, z, STRIP - rows : STRIP]
+                out_ref[1 + n, z // 2, at(z, 0, STRIP - rows)] = f_ref[5 - n, z, rows:STRIP]
+
+    @pl.when(core_ref[0] == 1)
+    def _():
+        for z in range(NZ):
+            for n in range(3):
+                rows = 11 - 2 * n
+                out_ref[1 + n, z // 2, at(z, 0, rows)] = f_ref[n, z, 0:rows]
+                out_ref[1 + n, z // 2, at(z, rows, STRIP)] = f_ref[5 - n, z, 0 : STRIP - rows]
 
 
 def clear_ends(*refs):
@@ -144,17 +150,16 @@
         ref[NZ + 1] = zero
 
 
-def load_window(a_s, below, own, above):
-    zero = jnp.zeros((LOW, LANES), F32)
-    for z in range(NZ):
-        a_s[z + 1, 0:LOW] = zero
-        a_s[z + 1, LOW:OWN] = below(z)
-        a_s[z + 1, OWN:HIGH] = own(z)
-        a_s[z + 1, HIGH:WIN] = above(z)
-
-
-def strips_of(ref, field):
-    return lambda z: ref[field, z // 2, at(z, 0, STRIP)]
+def load_window(core_ref, a_s, field, own_ref, got_ref, got2_ref):
+    def load(below_ref, above_ref):
+        zero = jnp.zeros((LOW, LANES), F32)
+        for z in range(NZ):
+            a_s[z + 1, 0:LOW] = zero
+            a_s[z + 1, LOW:OWN] = below_ref[field, z // 2, at(z, 0, STRIP)]
+            a_s[z + 1, OWN:HIGH] = own_ref[field, z // 2, at(z, 0, STRIP)]
+            a_s[z + 1, HIGH:WIN] = above_ref[field, z // 2, at(z, 0, STRIP)]
+
+    by_core(core_ref, load, got_ref, got2_ref)
 
 
 def coefficients(rate, k_ref, k_s, co_s):
@@ -218,21 +223,28 @@
     one_sweep(b_s, a_s, co_s, db_s, rows)
 
 
-def early_body(k_ref, f_ref, own_ref, below_ref, above_ref, out_ref, next_ref, k_s, co_s, a_s, b_s, db_s, f_s):
+def early_body(
+    core_ref, k_ref, f_ref, own_ref, got_ref, got2_ref, out_ref, next_ref, k_s, co_s, a_s, b_s, db_s, f_s
+):
     coefficients(step_size, k_ref, k_s, co_s)
     clear_ends(a_s, b_s)
-    load_window(a_s, strips_of(below_ref, 0), strips_of(own_ref, 0), strips_of(above_ref, 0))
-    for n in range(3):
-        rows = 11 - 2 * n
-        for z in range(NZ):
-            s = z // 2
-            for m in (n, 5 - n):
-                f_s[m, z] = jnp.zeros((WIN, LANES), F32)
-                f_s[m, z, OWN:HIGH] = f_ref[m, z]
-            f_s[n, z, OWN - rows : OWN] = below_ref[1 + n, s, at(z, STRIP - rows, STRIP)]
-            f_s[n, z, HIGH : HIGH + rows] = above_ref[1 + n, s, at(z, 0, rows)]
-            f_s[5 - n, z, OWN - STRIP + rows : OWN] = below_ref[1 + n, s, at(z, 0, STRIP - rows)]
-            f_s[5 - n, z, HIGH : HIGH + STRIP - rows] = above_ref[1 + n, s, at(z, rows, STRIP)]
+    load_window(core_ref, a_s, 0, own_ref, got_ref, got2_ref)
+    for n in range(6):
+        for z in range(NZ):
+            f_s[n, z] = jnp.zeros((WIN, LANES), F32)
+            f_s[n, z, OWN:HIGH] = f_ref[n, z]
+
+    def halos(below_ref, above_ref):
+        for n in range(3):
+            rows = 11 - 2 * n
+            for z in range(NZ):
+                s = z // 2
+                f_s[n, z, OWN - rows : OWN] = below_ref[1 + n, s, at(z, STRIP - rows, STRIP)]
+                f_s[n, z, HIGH : HIGH + rows] = above_ref[1 + n, s, at(z, 0, rows)]
+                f_s[5 - n, z, OWN - STRIP + rows : OWN] = below_ref[1 + n, s, at(z, 0, STRIP - rows)]
+                f_s[5 - n, z, HIGH : HIGH + STRIP - rows] = above_ref[1 + n, s, at(z, rows, STRIP)]
+
+    by_core(core_ref, halos, got_ref, got2_ref)
     for n in range(6):
         step(12 - 2 * n, a_s, b_s, co_s, db_s, f_s.at[n])
         for z in range(NZ):
@@ -244,14 +256,14 @@
 
 
 def late_body(
-    block_ref, k_ref, own_ref, below_ref, above_ref, start_ref, start_below_ref, start_above_ref,
+    core_ref, block_ref, k_ref, own_ref, got_ref, got2_ref, start_ref, start_got_ref, start_got2_ref,
     out_ref, pow_ref, next_ref, k_s, co_s, a_s, b_s, db_s, f_s, y_s,
 ):
     coefficients(step_size, k_ref, k_s, co_s)
     clear_ends(a_s, b_s)
-    load_window(a_s, strips_of(below_ref, 0), strips_of(own_ref, 0), strips_of(above_ref, 0))
+    load_window(core_ref, a_s, 0, own_ref, got_ref, got2_ref)
     for n in range(2):
-        load_window(f_s, strips_of(below_ref, 1 + n), strips_of(own_ref, 1 + n), strips_of(above_ref, 1 + n))
+        load_window(core_ref, f_s, 1 + n, own_ref, got_ref, got2_ref)
         step(12 - 2 * n, a_s, b_s, co_s, db_s, f_s.at[pl.ds(1, NZ)])
         if n == 0:
             for z in range(NZ):
@@ -259,7 +271,7 @@
     for z in range(NZ):
         y_s[z] = a_s[z + 1]
     coefficients(coarse_size, k_ref, k_s, co_s)
-    load_window(a_s, strips_of(start_below_ref, 0), strips_of(start_ref, 0), strips_of(start_above_ref, 0))
+    load_window(core_ref, a_s, 0, start_ref, start_got_ref, start_got2_ref)
     step(10, a_s, b_s, co_s, db_s)
     later = block_ref[0] > 0
     for z in range(NZ):
@@ -274,12 +286,12 @@
 
 
 def powers_body(
-    core_ref, side_ref, block_ref, k_ref, own_ref, below_ref, above_ref, early_ref,
+    core_ref, side_ref, block_ref, k_ref, own_ref, got_ref, got2_ref, early_ref,
     out_ref, k_s, co_s, a_s, b_s, db_s, pow_s,
 ):
     coefficients(coarse_size, k_ref, k_s, co_s)
     clear_ends(a_s, b_s)
-    load_window(a_s, strips_of(below_ref, 0), strips_of(own_ref, 0), strips_of(above_ref, 0))
+    load_window(core_ref, a_s, 0, own_ref, got_ref, got2_ref)
     for n in range(5):
         for z in range(NZ):
             pow_s[n, z] = early_ref[n, z]
@@ -339,50 +351,47 @@
     def onward(place):
         return lax.ppermute(guess, BLOCKS + ("zl", "core"), [(8 * b + 7, 8 * b + 8 + place) for b in range(NB - 1)])
 
+    prev6, prev7 = onward(6), onward(7)
+    (base,) = call(source_body, [sds(64, 9, 2, LANES)], source)
+    vmem = pl.BlockSpec(memory_space=pltpu.VMEM)
     sent = pl.pallas_call(
-        scatter_body,
+        extra_body,
         out_shape=sds(64, 9, 2, LANES),
-        in_specs=[pl.BlockSpec(memory_space=pltpu.SMEM)] * 2 + [pl.BlockSpec(memory_space=pl.ANY)] * 5,
-        out_specs=pl.BlockSpec(memory_space=pltpu.VMEM),
-        scratch_shapes=[
-            pltpu.VMEM((2, NY, LANES), F32),
-            pltpu.VMEM((2, NY, LANES), F32),
-            pltpu.SemaphoreType.DMA((2,)),
-        ],
-        compiler_params=pltpu.CompilerParams(vmem_limit_bytes=60 * 1024 * 1024),
-    )(place, block, source, onward(6), onward(7), diffusivity, initial)
+        in_specs=[pl.BlockSpec(memory_space=pltpu.SMEM)] * 2 + [vmem] * 5,
+        out_specs=vmem,
+        input_output_aliases={6: 0},
+        compiler_params=pltpu.CompilerParams(vmem_limit_bytes=32 * 1024 * 1024),
+    )(place, block, prev6, prev7, diffusivity, initial, base)
     strips = lax.all_to_all(sent, BLOCK, 0, 0, tiled=True).reshape(8, 8, 9, 2, LANES)
-    strips2 = lax.ppermute(strips, "core", [(0, 1), (1, 0)])
-
-    f, k, f_up, f_down = call(
+
+    def swap(mine):
+        return lax.ppermute(mine, "core", [(0, 1), (1, 0)])
+
+    def exchange(mine):
+        got = lax.ppermute(mine, ("zl", "core", "y"), neighbour_route())
+        return got, swap(got)
+
+    f, k, start, message = call(
         pack_body,
-        [sds(8, NZ, STRIP, LANES), sds(NZ, WIN, LANES)] + [sds(4, 8, PAIR, LANES)] * 2,
-        core, strips, strips2, smem=1,
+        [sds(8, NZ, STRIP, LANES), sds(NZ, WIN, LANES), sds(1, 8, PAIR, LANES), sds(4, 8, PAIR, LANES)],
+        core, strips, swap(strips), smem=1,
     )
-
-    def exchange(up, down):
-        below = lax.ppermute(up, ("zl", "y"), neighbours(1))
-        above = lax.ppermute(down, ("zl", "y"), neighbours(-1))
-        return below, above
-
     flops = NZ * WIN * LANES * 15
     window = pltpu.VMEM((NZ, WIN, LANES), F32)
-    f_below, f_above = exchange(f_up, f_down)
+    got, got2 = exchange(message)
     v_early, state = call(
         early_body, [sds(6, NZ, STRIP, LANES), sds(3, 8, PAIR, LANES)],
-        k, f, f_up, f_below, f_above, flops=12 * flops,
+        core, k, f, start, got, got2, smem=1, flops=12 * flops,
         scratch=SWEEP_SCRATCH + (pltpu.VMEM((6, NZ, WIN, LANES), F32),),
     )
-    below, above = exchange(state, state)
     v_late, first_powers, last = call(
         late_body, [sds(NZ, STRIP, LANES), sds(5, NZ, STRIP, LANES), sds(1, 8, PAIR, LANES)],
-        block, k, state, below, above, f_up, f_below, f_above, smem=1, flops=14 * flops,
+        core, block, k, state, *exchange(state), start, got, got2, smem=2, flops=14 * flops,
         scratch=SWEEP_SCRATCH + (pltpu.VMEM((NZ + 2, WIN, LANES), F32), window),
     )
-    below, above = exchange(last, last)
     (powers,) = call(
         powers_body, [sds(NB, 4 * STRIP, LANES)],
-        core, side, block, k, last, below, above, first_powers, smem=3, flops=6 * flops,
+        core, side, block, k, last, *exchange(last), first_powers, smem=3, flops=6 * flops,
         scratch=SWEEP_SCRATCH + (pltpu.VMEM((NB, NZ, STRIP, LANES), F32),),
     )
     arrived = lax.all_to_all(powers, BLOCKS, 0, 0, tiled=True)

time: 159 us -> 157 us (0.987)
  waiting for transfers between devices: 15.7 us -> 23.2 us
  starting transfers between devices: 23.3 us -> 16.3 us
  blocking collectives: 104 us -> 101 us
    ppermute x7, waiting for transfers between devices: 15.7 us -> 23.2 us  [the longest x3 17.4 us: exchange(): got = lax.ppermute(mine, ('zl', 'core', 'y'), neighbour_route())]
    ppermute x7, starting transfers between devices: 21.9 us -> 15 us  [the longest x4 11.1 us: swap(): return lax.ppermute(mine, 'core', [(0, 1), (1, 0)])]
    all_to_all x1, blocking collectives: 49.3 us -> 47.2 us  [on_device(): lax.all_to_all(sent, BLOCK, 0, 0, tiled=True).reshape(8, 8, 9, 2, LANES)]
    pallas_call x1, Pallas kernels: 1.93 us -> 0.07 us  [on_device(): pl.pallas_call(extra_body, out_shape=sds(64, 9, 2, LANES), in_specs=[pl.B...]
    all_to_all x1, blocking collectives: 26.9 us -> 25.2 us  [on_device(): returned = lax.all_to_all(back, ('zl', 'core', 'y'), 0, 0, tiled=True)]
    pallas_call x6 -> x7, Pallas kernels: 13.2 us -> 13.7 us  [call(): pl.pallas_call(body, out_shape=list(outs), in_specs=specs, out_specs=out_...]
where the time goes in v8:
time: 157 us; the launch traced here: 156 us
  blocking collectives  101 us (64%)
  waiting for transfers between devices  23.2 us (15%)
  starting transfers between devices  16.3 us (10%)
  Pallas kernels  13.7 us (9%)
  local copies, waits for them, and re-layouts  1.8 us (1%)
    all_to_all x1, blocking collectives, on_device(): lax.all_to_all(sent, BLOCK, 0, 0, tiled=True).reshape(8, 8, 9, 2, LANES)  47.2 us
    all_to_all x1, blocking collectives, on_device(): arrived = lax.all_to_all(powers, BLOCKS, 0, 0, tiled=True)  28.6 us
    all_to_all x1, blocking collectives, on_device(): returned = lax.all_to_all(back, ('zl', 'core', 'y'), 0, 0, tiled=True)  25.2 us
    ppermute x3, waiting for transfers between devices, exchange(): got = lax.ppermute(mine, ('zl', 'core', 'y'), neighbour_route())  17.4 us
    pallas_call x7, Pallas kernels, call(): pl.pallas_call(body, out_shape=list(outs), in_specs=specs, out_specs=out_...  13.7 us
    ppermute x4, starting transfers between devices, swap(): return lax.ppermute(mine, 'core', [(0, 1), (1, 0)])  11.1 us
    ppermute x4, waiting for transfers between devices, swap(): return lax.ppermute(mine, 'core', [(0, 1), (1, 0)])  5.77 us
    ppermute x3, starting transfers between devices, exchange(): got = lax.ppermute(mine, ('zl', 'core', 'y'), neighbour_route())  3.88 us
  transfers between devices with their start and end apart: 9, of which 7 were waited for; matrix products, arithmetic and copies ran while one was open for 0% of the time, Pallas kernels for 0%

profile of v8, /device:TPU:1, one launch (start us, length us, event | category | flops | bytes accessed | tf_op | source)
XLA Modules:
  0.0 156.2 jit_solution(3388682796586275938)
XLA Ops:
  0.0 0.7 collective-permute-start.1
  0.7 0.7 collective-permute-start
  1.4 0.0 copy-start.2
  1.4 0.9 copy-done.2
  2.3 0.1 shard_map.46.base_ref
  2.4 0.0 collective-permute-done.1.prev7_ref
  2.4 0.0 collective-permute-done.prev6_ref
  2.4 0.8 copy-done
  3.2 0.1 copy-done.1
  3.3 0.1 shard_map.47
  3.4 47.2 %all_to_all.15 = f32[64,9,2,128]{3,2,1,0:T(2,128)S(1)} all-to-all(f32[64,9,2,128]{3,2,1,0:T(2,128)S(1)} %shard_map.47), channel_id=1, replica_groups=mesh['x'=4,'zh'=2,'zl'=4,'core'=2,'y'=4,'zhi'=2] {'zl','core','y','zhi'}, dimensions={0} | all-to-all | bytes 1179648 | tf_op jit(solution)/shard_map/all_to_all | solution.py:365
  50.6 4.6 %collective-permute-start.2 = (f32[8,8,9,2,128]{4,3,2,1,0:T(2,128)S(1)}, f32[8,8,9,2,128]{4,3,2,1,0:T(2,128)S(1)}, u32[]{:S(2)}, u32[]{:S(2)}) collective-permute-start(f32[8,8,9,2,128]{4,3,2,1,0:T(2,128)S(1)} %bitcast.8), channel_id=1, source_target_pairs={{0,8},{8,0},{1,9},{9,1},{2,10},{10,2},{3,11},{11,3},{4,12},{12,4},... | collective-permute-start | bytes 1769480 | tf_op jit(solution)/shard_map/ppermute | solution.py:368
  55.1 1.6 %collective-permute-done.2.other_ref = f32[8,8,9,2,128]{4,3,2,1,0:T(2,128)S(1)} collective-permute-done((f32[8,8,9,2,128]{4,3,2,1,0:T(2,128)S(1)}, f32[8,8,9,2,128]{4,3,2,1,0:T(2,128)S(1)}, u32[]{:S(2)}, u32[]{:S(2)}) %collective-permute-start.2) | collective-permute-done | bytes 589856 | tf_op jit(solution)/shard_map/ppermute | solution.py:368
  56.8 0.3 shard_map.48
  57.0 1.3 collective-permute-start.3
  58.3 7.2 %collective-permute-done.3.got_ref.start_got_ref = f32[4,8,24,128]{3,2,1,0:T(8,128)S(1)} collective-permute-done((f32[4,8,24,128]{3,2,1,0:T(8,128)S(1)}, f32[4,8,24,128]{3,2,1,0:T(8,128)S(1)}, u32[]{:S(2)}, u32[]{:S(2)}) %collective-permute-start.3) | collective-permute-done | bytes 393248 | tf_op jit(solution)/shard_map/ppermute | solution.py:371
  65.5 1.9 %collective-permute-start.4 = (f32[4,8,24,128]{3,2,1,0:T(8,128)S(1)}, f32[4,8,24,128]{3,2,1,0:T(8,128)S(1)}, u32[]{:S(2)}, u32[]{:S(2)}) collective-permute-start(f32[4,8,24,128]{3,2,1,0:T(8,128)S(1)} %collective-permute-done.3.got_ref.start_got_ref), channel_id=1, source_target_pairs={{0,8},{8,0},{1,9},{9,1},{2,10},{10,2},{3,11},{11,3},{4,12},{12,4},... | collective-permute-start | bytes 1179656 | tf_op jit(solution)/shard_map/ppermute | solution.py:368
  67.5 1.7 %collective-permute-done.4.got2_ref.start_got2_ref = f32[4,8,24,128]{3,2,1,0:T(8,128)S(1)} collective-permute-done((f32[4,8,24,128]{3,2,1,0:T(8,128)S(1)}, f32[4,8,24,128]{3,2,1,0:T(8,128)S(1)}, u32[]{:S(2)}, u32[]{:S(2)}) %collective-permute-start.4) | collective-permute-done | bytes 393248 | tf_op jit(solution)/shard_map/ppermute | solution.py:368
  69.2 4.1 %shard_map.49 = (f32[6,16,12,128]{3,2,1,0:T(8,128)S(1)}, f32[3,8,24,128]{3,2,1,0:T(8,128)S(1)}) custom-call(s32[1]{0:T(128)} %bitcast.core_ref, f32[16,40,128]{2,1,0:T(8,128)S(1)} %get-tuple-element.14.k_ref, f32[8,16,12,128]{3,2,1,0:T(8,128)S(1)} %get-tuple-element.15.f_ref, f32[1,8,24,128]{3,2,1,0:T(8,128)S(1)} %get-tuple-element.16.own_ref.start_ref, ...), custom_call_target="tpu_custom_call" | custom-call | flops 14745600 | bytes 2883588 | tf_op jit(solution)/shard_map/pallas_call | solution.py:55
  73.3 1.3 collective-permute-start.5
  74.6 6.2 %collective-permute-done.5.got_ref = f32[3,8,24,128]{3,2,1,0:T(8,128)S(1)} collective-permute-done((f32[3,8,24,128]{3,2,1,0:T(8,128)S(1)}, f32[3,8,24,128]{3,2,1,0:T(8,128)S(1)}, u32[]{:S(2)}, u32[]{:S(2)}) %collective-permute-start.5) | collective-permute-done | bytes 294944 | tf_op jit(solution)/shard_map/ppermute | solution.py:371
  80.7 1.9 %collective-permute-start.6 = (f32[3,8,24,128]{3,2,1,0:T(8,128)S(1)}, f32[3,8,24,128]{3,2,1,0:T(8,128)S(1)}, u32[]{:S(2)}, u32[]{:S(2)}) collective-permute-start(f32[3,8,24,128]{3,2,1,0:T(8,128)S(1)} %collective-permute-done.5.got_ref), channel_id=1, source_target_pairs={{0,8},{8,0},{1,9},{9,1},{2,10},{10,2},{3,11},{11,3},{4,12},{12,4},... | collective-permute-start | bytes 884744 | tf_op jit(solution)/shard_map/ppermute | solution.py:368
  82.7 1.5 collective-permute-done.6.got2_ref
  84.2 6.0 %shard_map.50 = (f32[16,12,128]{2,1,0:T(8,128)S(1)}, f32[5,16,12,128]{3,2,1,0:T(8,128)S(1)}, f32[1,8,24,128]{3,2,1,0:T(8,128)S(1)}) custom-call(s32[1]{0:T(128)} %bitcast.core_ref, s32[1]{0:T(128)} %bitcast.2.block_ref, f32[16,40,128]{2,1,0:T(8,128)S(1)} %get-tuple-element.14.k_ref, f32[3,8,24,128]{3,2,1,0:T(8,128)S(1)} %get-tuple-element.18.own_ref, ...), custom_call_target="tpu_custom_call" | custom-call | flops 17203200 | bytes 2785288 | tf_op jit(solution)/shard_map/pallas_call | solution.py:55
  90.2 1.3 collective-permute-start.7
  91.5 4.1 %collective-permute-done.7.got_ref = f32[1,8,24,128]{3,2,1,0:T(8,128)S(1)} collective-permute-done((f32[1,8,24,128]{3,2,1,0:T(8,128)S(1)}, f32[1,8,24,128]{3,2,1,0:T(8,128)S(1)}, u32[]{:S(2)}, u32[]{:S(2)}) %collective-permute-start.7) | collective-permute-done | bytes 98336 | tf_op jit(solution)/shard_map/ppermute | solution.py:371
  95.6 2.7 %collective-permute-start.8 = (f32[1,8,24,128]{3,2,1,0:T(8,128)S(1)}, f32[1,8,24,128]{3,2,1,0:T(8,128)S(1)}, u32[]{:S(2)}, u32[]{:S(2)}) collective-permute-start(f32[1,8,24,128]{3,2,1,0:T(8,128)S(1)} %collective-permute-done.7.got_ref), channel_id=1, source_target_pairs={{0,8},{8,0},{1,9},{9,1},{2,10},{10,2},{3,11},{11,3},{4,12},{12,4},... | collective-permute-start | bytes 294920 | tf_op jit(solution)/shard_map/ppermute | solution.py:368
  98.3 0.9 collective-permute-done.8.got2_ref
  99.2 2.5 %shard_map.51 = f32[8,48,128]{2,1,0:T(8,128)S(1)} custom-call(s32[1]{0:T(128)} %bitcast.core_ref, s32[1]{0:T(128)} %bitcast.1.side_ref, s32[1]{0:T(128)} %bitcast.2.block_ref, f32[16,40,128]{2,1,0:T(8,128)S(1)} %get-tuple-element.14.k_ref, f32[1,8,24,128]{3,2,1,0:T(8,128)S(1)} %get-tuple-element.19.own_ref, ...), custom_call_target="tpu_custom_call" | custom-call | flops 7372800 | bytes 1310732 | tf_op jit(solution)/shard_map/pallas_call | solution.py:55
  101.7 28.6 %all_to_all.16.got_ref = f32[8,48,128]{2,1,0:T(8,128)S(1)} all-to-all(f32[8,48,128]{2,1,0:T(8,128)S(1)} %shard_map.51), channel_id=1, replica_groups=mesh['x'=4,'zh'=2,'zl'=4,'core'=2,'y'=4,'zhi'=2] {'x','zh'}, dimensions={0} | all-to-all | bytes 393216 | tf_op jit(solution)/shard_map/all_to_all | solution.py:397
  130.4 25.2 %all_to_all.17.got_ref = f32[32,16,128]{2,1,0:T(8,128)S(1)} all-to-all(f32[32,16,128]{2,1,0:T(8,128)S(1)} %shard_map.52), channel_id=1, replica_groups=mesh['x'=4,'zh'=2,'zl'=4,'core'=2,'y'=4,'zhi'=2] {'zl','core','y'}, dimensions={0} | all-to-all | bytes 524288 | tf_op jit(solution)/shard_map/all_to_all | solution.py:399
  155.5 0.7 shard_map.53
  (3 shorter events, 0.0 us)
Async XLA Ops:
  0.0 2.4 %collective-permute-start.1 = (f32[2,192,128]{2,1,0:T(8,128)}, f32[2,192,128]{2,1,0:T(8,128)S(1)}, u32[]{:S(2)}, u32[]{:S(2)}) collective-permute-start(f32[2,192,128]{2,1,0:T(8,128)} %bitcast.11), channel_id=1, source_target_pairs={{56,120},{120,184},{184,248},{248,312},{312,376},{376,440},{440,50... | collective-permute-start | bytes 589832 | tf_op jit(solution)/shard_map/ppermute | solution.py:352
  0.7 1.8 %collective-permute-start = (f32[2,192,128]{2,1,0:T(8,128)}, f32[2,192,128]{2,1,0:T(8,128)S(1)}, u32[]{:S(2)}, u32[]{:S(2)}) collective-permute-start(f32[2,192,128]{2,1,0:T(8,128)} %bitcast.12), channel_id=1, source_target_pairs={{56,112},{120,176},{184,240},{248,304},{312,368},{376,432},{440,49... | collective-permute-start | bytes 589832 | tf_op jit(solution)/shard_map/ppermute | solution.py:352
  1.4 0.9 copy-start.2
  2.3 0.9 copy-start
  2.3 1.0 copy-start.1
  50.6 6.2 %collective-permute-start.2 = (f32[8,8,9,2,128]{4,3,2,1,0:T(2,128)S(1)}, f32[8,8,9,2,128]{4,3,2,1,0:T(2,128)S(1)}, u32[]{:S(2)}, u32[]{:S(2)}) collective-permute-start(f32[8,8,9,2,128]{4,3,2,1,0:T(2,128)S(1)} %bitcast.8), channel_id=1, source_target_pairs={{0,8},{8,0},{1,9},{9,1},{2,10},{10,2},{3,11},{11,3},{4,12},{12,4},... | collective-permute-start | bytes 1769480 | tf_op jit(solution)/shard_map/ppermute | solution.py:368
  57.0 8.5 %collective-permute-start.3 = (f32[4,8,24,128]{3,2,1,0:T(8,128)S(1)}, f32[4,8,24,128]{3,2,1,0:T(8,128)S(1)}, u32[]{:S(2)}, u32[]{:S(2)}) collective-permute-start(f32[4,8,24,128]{3,2,1,0:T(8,128)S(1)} %get-tuple-element.17), channel_id=1, source_target_pairs={{0,2},{2,4},{4,6},{6,22},{22,20},{20,18},{18,16},{16,32},{32,34},{... | collective-permute-start | bytes 1179656 | tf_op jit(solution)/shard_map/ppermute | solution.py:371
  65.5 3.6 %collective-permute-start.4 = (f32[4,8,24,128]{3,2,1,0:T(8,128)S(1)}, f32[4,8,24,128]{3,2,1,0:T(8,128)S(1)}, u32[]{:S(2)}, u32[]{:S(2)}) collective-permute-start(f32[4,8,24,128]{3,2,1,0:T(8,128)S(1)} %collective-permute-done.3.got_ref.start_got_ref), channel_id=1, source_target_pairs={{0,8},{8,0},{1,9},{9,1},{2,10},{10,2},{3,11},{11,3},{4,12},{12,4},... | collective-permute-start | bytes 1179656 | tf_op jit(solution)/shard_map/ppermute | solution.py:368
  73.3 7.5 %collective-permute-start.5 = (f32[3,8,24,128]{3,2,1,0:T(8,128)S(1)}, f32[3,8,24,128]{3,2,1,0:T(8,128)S(1)}, u32[]{:S(2)}, u32[]{:S(2)}) collective-permute-start(f32[3,8,24,128]{3,2,1,0:T(8,128)S(1)} %get-tuple-element.18.own_ref), channel_id=1, source_target_pairs={{0,2},{2,4},{4,6},{6,22},{22,20},{20,18},{18,16},{16,32},{32,34},{... | collective-permute-start | bytes 884744 | tf_op jit(solution)/shard_map/ppermute | solution.py:371
  80.7 3.5 %collective-permute-start.6 = (f32[3,8,24,128]{3,2,1,0:T(8,128)S(1)}, f32[3,8,24,128]{3,2,1,0:T(8,128)S(1)}, u32[]{:S(2)}, u32[]{:S(2)}) collective-permute-start(f32[3,8,24,128]{3,2,1,0:T(8,128)S(1)} %collective-permute-done.5.got_ref), channel_id=1, source_target_pairs={{0,8},{8,0},{1,9},{9,1},{2,10},{10,2},{3,11},{11,3},{4,12},{12,4},... | collective-permute-start | bytes 884744 | tf_op jit(solution)/shard_map/ppermute | solution.py:368
  90.2 5.4 %collective-permute-start.7 = (f32[1,8,24,128]{3,2,1,0:T(8,128)S(1)}, f32[1,8,24,128]{3,2,1,0:T(8,128)S(1)}, u32[]{:S(2)}, u32[]{:S(2)}) collective-permute-start(f32[1,8,24,128]{3,2,1,0:T(8,128)S(1)} %get-tuple-element.19.own_ref), channel_id=1, source_target_pairs={{0,2},{2,4},{4,6},{6,22},{22,20},{20,18},{18,16},{16,32},{32,34},{... | collective-permute-start | bytes 294920 | tf_op jit(solution)/shard_map/ppermute | solution.py:371
  95.6 3.6 %collective-permute-start.8 = (f32[1,8,24,128]{3,2,1,0:T(8,128)S(1)}, f32[1,8,24,128]{3,2,1,0:T(8,128)S(1)}, u32[]{:S(2)}, u32[]{:S(2)}) collective-permute-start(f32[1,8,24,128]{3,2,1,0:T(8,128)S(1)} %collective-permute-done.7.got_ref), channel_id=1, source_target_pairs={{0,8},{8,0},{1,9},{9,1},{2,10},{10,2},{3,11},{11,3},{4,12},{12,4},... | collective-permute-start | bytes 294920 | tf_op jit(solution)/shard_map/ppermute | solution.py:368

commit v9 on v8

--- a/solution.py
+++ b/solution.py
@@ -82,7 +82,7 @@
             out_ref[to, r] = src_ref[core, row : row + 2]
 
 
-def extra_body(j_ref, block_ref, prev6_ref, prev7_ref, cond_ref, init_ref, base_ref, out_ref):
+def extra_body(j_ref, block_ref, prev0_ref, prev1_ref, cond_ref, init_ref, base_ref, out_ref):
     place = j_ref[0]
     first = block_ref[0] == 0
     later = jnp.logical_not(first)
@@ -97,11 +97,11 @@
                 else:
                     out_ref[to, 6 + r] = jnp.zeros((2, LANES), F32)
 
-    for half, prev_ref in ((0, prev6_ref), (1, prev7_ref)):
+    for half, prev_ref in ((0, prev0_ref), (1, prev1_ref)):
         for n, shift in enumerate((0, 1, -1)):
-            pl.when(place == 2 * n + half)(functools.partial(fill, cond_ref, shift, half))
-        pl.when((place == 6 + half) & first)(functools.partial(fill, init_ref, 0, half))
-        pl.when((place == 6 + half) & later)(functools.partial(fill, prev_ref, 0, half))
+            pl.when(place == 2 + 2 * n + half)(functools.partial(fill, cond_ref, shift, half))
+        pl.when((place == half) & first)(functools.partial(fill, init_ref, 0, half))
+        pl.when((place == half) & later)(functools.partial(fill, prev_ref, 0, half))
 
 
 def by_core(core_ref, body, mine, other):
@@ -109,7 +109,9 @@
     pl.when(core_ref[0] == 1)(functools.partial(body, other, mine))
 
 
-def pack_body(core_ref, own_ref, other_ref, f_ref, k_ref, start_ref, out_ref):
+def pack_body(core_ref, flip_ref, own_ref, other_ref, f_ref, k_ref, start_ref, out_ref):
+    flip = flip_ref[0]
+
     def order(*halves):
         for z in range(NZ):
             half, s = halves[z % 2], z // 2
@@ -118,10 +120,10 @@
                 for n in range(8):
                     f_ref[n, z, 2 * r : 2 * r + 2] = half[n, s, r]
                 part, extra = r // 3, 6 + r % 3
-                start = half[6 + part, s, extra]
+                start = half[part, s + (1 - 2 * (s % 2)) * flip, extra]
                 start_ref[0, s, at(z, 2 * r, 2 * r + 2)] = start
                 out_ref[0, s, at(z, 2 * r, 2 * r + 2)] = start
-                for place, base in ((4, LOW), (0, OWN), (2, HIGH)):
+                for place, base in ((6, LOW), (2, OWN), (4, HIGH)):
                     k_ref[z, base + 2 * r : base + 2 * r + 2] = half[place + part, s, extra]
 
     by_core(core_ref, order, own_ref, other_ref)
@@ -162,10 +164,7 @@
     by_core(core_ref, load, got_ref, got2_ref)
 
 
-def coefficients(rate, k_ref, k_s, co_s):
-    clear_ends(k_s)
-    for z in range(NZ):
-        k_s[z + 1] = k_ref[z]
+def coefficients(rate, k_s, co_s):
     lane = lax.broadcasted_iota(jnp.int32, (WIN, LANES), 1)
     first = lane == 0
     last = lane == LANES - 1
@@ -196,13 +195,20 @@
     lax.fori_loop(0, NZ, layer, 0)
 
 
+def coefficients_body(k_ref, fine_ref, coarse_ref, k_s):
+    clear_ends(k_s)
+    for z in range(NZ):
+        k_s[z + 1] = k_ref[z]
+    coefficients(step_size, k_s, fine_ref)
+    coefficients(coarse_size, k_s, coarse_ref)
+
+
 def one_sweep(src, dst, co_s, db_s, rows):
     tall = rows.stop - rows.start
-    for z in range(NZ):
-        w = src[z + 1, rows]
-        acc = (db_s[z, rows] + (1.0 - damping) * w) + (
-            co_s[0, z, rows] * src[z, rows] + co_s[1, z, rows] * src[z + 2, rows]
-        )
+    under, w = src[0, rows], src[1, rows]
+    for z in range(NZ):
+        over = src[z + 2, rows]
+        acc = (db_s[z, rows] + (1.0 - damping) * w) + (co_s[0, z, rows] * under + co_s[1, z, rows] * over)
         acc = acc + (
             co_s[2, z, rows] * pltpu.roll(w, 1, 0) + co_s[3, z, rows] * pltpu.roll(w, tall - 1, 0)
         )
@@ -210,6 +216,7 @@
             co_s[4, z, rows] * pltpu.roll(w, 1, 1) + co_s[5, z, rows] * pltpu.roll(w, LANES - 1, 1)
         )
         dst[z + 1, rows] = acc
+        under, w = w, over
 
 
 def step(halo, a_s, b_s, co_s, db_s, forcing=None):
@@ -224,9 +231,8 @@
 
 
 def early_body(
-    core_ref, k_ref, f_ref, own_ref, got_ref, got2_ref, out_ref, next_ref, k_s, co_s, a_s, b_s, db_s, f_s
+    core_ref, co_s, f_ref, own_ref, got_ref, got2_ref, out_ref, next_ref, a_s, b_s, db_s, f_s
 ):
-    coefficients(step_size, k_ref, k_s, co_s)
     clear_ends(a_s, b_s)
     load_window(core_ref, a_s, 0, own_ref, got_ref, got2_ref)
     for n in range(6):
@@ -255,27 +261,29 @@
             next_ref[1 + n, z // 2, at(z, 0, STRIP)] = f_ref[6 + n, z]
 
 
+def start_body(core_ref, block_ref, co_s, own_ref, got_ref, got2_ref, out_ref, a_s, b_s, db_s):
+    clear_ends(a_s, b_s)
+    load_window(core_ref, a_s, 0, own_ref, got_ref, got2_ref)
+    step(10, a_s, b_s, co_s, db_s)
+    later = block_ref[0] > 0
+    for z in range(NZ):
+        out_ref[z] = jnp.where(later, a_s[z + 1], 0.0)
+
+
 def late_body(
-    core_ref, block_ref, k_ref, own_ref, got_ref, got2_ref, start_ref, start_got_ref, start_got2_ref,
-    out_ref, pow_ref, next_ref, k_s, co_s, a_s, b_s, db_s, f_s, y_s,
+    core_ref, fine_s, co_s, own_ref, got_ref, got2_ref, start_ref,
+    out_ref, pow_ref, next_ref, a_s, b_s, db_s, f_s,
 ):
-    coefficients(step_size, k_ref, k_s, co_s)
     clear_ends(a_s, b_s)
     load_window(core_ref, a_s, 0, own_ref, got_ref, got2_ref)
     for n in range(2):
         load_window(core_ref, f_s, 1 + n, own_ref, got_ref, got2_ref)
-        step(12 - 2 * n, a_s, b_s, co_s, db_s, f_s.at[pl.ds(1, NZ)])
+        step(12 - 2 * n, a_s, b_s, fine_s, db_s, f_s.at[pl.ds(1, NZ)])
         if n == 0:
             for z in range(NZ):
                 out_ref[z] = a_s[z + 1, OWN:HIGH]
     for z in range(NZ):
-        y_s[z] = a_s[z + 1]
-    coefficients(coarse_size, k_ref, k_s, co_s)
-    load_window(core_ref, a_s, 0, start_ref, start_got_ref, start_got2_ref)
-    step(10, a_s, b_s, co_s, db_s)
-    later = block_ref[0] > 0
-    for z in range(NZ):
-        a_s[z + 1] = y_s[z] - jnp.where(later, a_s[z + 1], 0.0)
+        a_s[z + 1] = a_s[z + 1] - start_ref[z]
     for n in range(5):
         if n > 0:
             step(10 - 2 * n, a_s, b_s, co_s, db_s)
@@ -286,10 +294,9 @@
 
 
 def powers_body(
-    core_ref, side_ref, block_ref, k_ref, own_ref, got_ref, got2_ref, early_ref,
-    out_ref, k_s, co_s, a_s, b_s, db_s, pow_s,
+    core_ref, side_ref, block_ref, co_s, own_ref, got_ref, got2_ref, early_ref,
+    out_ref, a_s, b_s, db_s, pow_s,
 ):
-    coefficients(coarse_size, k_ref, k_s, co_s)
     clear_ends(a_s, b_s)
     load_window(core_ref, a_s, 0, own_ref, got_ref, got2_ref)
     for n in range(5):
@@ -309,8 +316,6 @@
 
 
 SWEEP_SCRATCH = (
-    pltpu.VMEM((NZ + 2, WIN, LANES), F32),
-    pltpu.VMEM((7, NZ, WIN, LANES), F32),
     pltpu.VMEM((NZ + 2, WIN, LANES), F32),
     pltpu.VMEM((NZ + 2, WIN, LANES), F32),
     pltpu.VMEM((NZ, WIN, LANES), F32),
@@ -349,9 +354,16 @@
     block = lax.axis_index(BLOCKS)[None]
 
     def onward(place):
-        return lax.ppermute(guess, BLOCKS + ("zl", "core"), [(8 * b + 7, 8 * b + 8 + place) for b in range(NB - 1)])
-
-    prev6, prev7 = onward(6), onward(7)
+        route = []
+        for b in range(NB - 1):
+            for y in range(4):
+                for zhi in range(2):
+                    to = zhi if b % 2 == 0 else 1 - zhi
+                    route.append((((b * 8 + 7) * 4 + y) * 2 + zhi, (((b + 1) * 8 + place) * 4 + y) * 2 + to))
+        return lax.ppermute(guess, AXES, route)
+
+    prev0, prev1 = onward(0), onward(1)
+    flip = ((block > 0) & (block % 2 == 0)).astype(jnp.int32)
     (base,) = call(source_body, [sds(64, 9, 2, LANES)], source)
     vmem = pl.BlockSpec(memory_space=pltpu.VMEM)
     sent = pl.pallas_call(
@@ -361,37 +373,47 @@
         out_specs=vmem,
         input_output_aliases={6: 0},
         compiler_params=pltpu.CompilerParams(vmem_limit_bytes=32 * 1024 * 1024),
-    )(place, block, prev6, prev7, diffusivity, initial, base)
+    )(place, block, prev0, prev1, diffusivity, initial, base)
     strips = lax.all_to_all(sent, BLOCK, 0, 0, tiled=True).reshape(8, 8, 9, 2, LANES)
 
     def swap(mine):
         return lax.ppermute(mine, "core", [(0, 1), (1, 0)])
 
-    def exchange(mine):
+    def exchange(mine, beside):
         got = lax.ppermute(mine, ("zl", "core", "y"), neighbour_route())
-        return got, swap(got)
+        got, beside = lax.optimization_barrier((got, beside))
+        return got, swap(got), beside
 
     f, k, start, message = call(
         pack_body,
         [sds(8, NZ, STRIP, LANES), sds(NZ, WIN, LANES), sds(1, 8, PAIR, LANES), sds(4, 8, PAIR, LANES)],
-        core, strips, swap(strips), smem=1,
+        core, flip, strips, swap(strips), smem=2,
     )
     flops = NZ * WIN * LANES * 15
-    window = pltpu.VMEM((NZ, WIN, LANES), F32)
-    got, got2 = exchange(message)
+    both_rates = call(
+        coefficients_body, [sds(7, NZ, WIN, LANES)] * 2, k, flops=6 * flops,
+        scratch=(pltpu.VMEM((NZ + 2, WIN, LANES), F32),),
+    )
+    got, got2, (fine, coarse) = exchange(message, both_rates)
     v_early, state = call(
         early_body, [sds(6, NZ, STRIP, LANES), sds(3, 8, PAIR, LANES)],
-        core, k, f, start, got, got2, smem=1, flops=12 * flops,
+        core, fine, f, start, got, got2, smem=1, flops=12 * flops,
         scratch=SWEEP_SCRATCH + (pltpu.VMEM((6, NZ, WIN, LANES), F32),),
     )
+    (start_g,) = call(
+        start_body, [sds(NZ, WIN, LANES)],
+        core, block, coarse, start, got, got2, smem=2, flops=2 * flops, scratch=SWEEP_SCRATCH,
+    )
+    state_got, state_got2, start_g = exchange(state, start_g)
     v_late, first_powers, last = call(
         late_body, [sds(NZ, STRIP, LANES), sds(5, NZ, STRIP, LANES), sds(1, 8, PAIR, LANES)],
-        core, block, k, state, *exchange(state), start, got, got2, smem=2, flops=14 * flops,
-        scratch=SWEEP_SCRATCH + (pltpu.VMEM((NZ + 2, WIN, LANES), F32), window),
-    )
+        core, fine, coarse, state, state_got, state_got2, start_g, smem=1, flops=12 * flops,
+        scratch=SWEEP_SCRATCH + (pltpu.VMEM((NZ + 2, WIN, LANES), F32),),
+    )
+    last_got, last_got2, _ = exchange(last, ())
     (powers,) = call(
         powers_body, [sds(NB, 4 * STRIP, LANES)],
-        core, side, block, k, last, *exchange(last), first_powers, smem=3, flops=6 * flops,
+        core, side, block, coarse, last, last_got, last_got2, first_powers, smem=3, flops=6 * flops,
         scratch=SWEEP_SCRATCH + (pltpu.VMEM((NB, NZ, STRIP, LANES), F32),),
     )
     arrived = lax.all_to_all(powers, BLOCKS, 0, 0, tiled=True)

time: 157 us -> 153 us (0.975)
  waiting for transfers between devices: 23.2 us -> 19.6 us
  local copies, waits for them, and re-layouts: 1.8 us -> 4.69 us
  Pallas kernels: 13.7 us -> 11.3 us
    ppermute x3, waiting for transfers between devices: 17.4 us -> 13.9 us  [exchange(): got = lax.ppermute(mine, ('zl', 'core', 'y'), neighbour_route())]
    unnamed x6 -> x10, local copies, waits for them, and re-layouts: 1.8 us -> 4.69 us
    pallas_call x7 -> x9, Pallas kernels: 13.7 us -> 11.3 us  [call(): pl.pallas_call(body, out_shape=list(outs), in_specs=specs, out_specs=out_...]
  transfers between devices with their start and end apart: 9 -> 9, of which waited for: 7 -> 7; matrix products, arithmetic and copies ran while one was open for 0% -> 0% of each run, Pallas kernels for 0% -> 2%
where the time goes in v9:
time: 153 us
  blocking collectives  101 us (66%)
  waiting for transfers between devices  19.6 us (13%)
  starting transfers between devices  16.3 us (11%)
  Pallas kernels  11.3 us (7%)
  local copies, waits for them, and re-layouts  4.69 us (3%)
    all_to_all x1, blocking collectives, on_device(): lax.all_to_all(sent, BLOCK, 0, 0, tiled=True).reshape(8, 8, 9, 2, LANES)  46.7 us
    all_to_all x1, blocking collectives, on_device(): arrived = lax.all_to_all(powers, BLOCKS, 0, 0, tiled=True)  28.6 us
    all_to_all x1, blocking collectives, on_device(): returned = lax.all_to_all(back, ('zl', 'core', 'y'), 0, 0, tiled=True)  25.2 us
    ppermute x3, waiting for transfers between devices, exchange(): got = lax.ppermute(mine, ('zl', 'core', 'y'), neighbour_route())  13.9 us
    pallas_call x9, Pallas kernels, call(): pl.pallas_call(body, out_shape=list(outs), in_specs=specs, out_specs=out_...  11.3 us
    ppermute x4, starting transfers between devices, swap(): return lax.ppermute(mine, 'core', [(0, 1), (1, 0)])  11.1 us
    ppermute x4, waiting for transfers between devices, swap(): return lax.ppermute(mine, 'core', [(0, 1), (1, 0)])  5.75 us
    unnamed x10, local copies, waits for them, and re-layouts  4.69 us
  transfers between devices with their start and end apart: 9, of which 7 were waited for; matrix products, arithmetic and copies ran while one was open for 0% of the time, Pallas kernels for 2%

profile of v9, /device:TPU:1, one launch (start us, length us, event | category | flops | bytes accessed | tf_op | source)
XLA Modules:
  0.0 152.7 jit_solution(7278509075273477502)
XLA Ops:
  0.0 0.7 collective-permute-start.1
  0.7 0.7 collective-permute-start
  1.4 0.9 copy-done.4
  2.3 0.1 shard_map.46.base_ref
  2.4 0.9 copy-done.2
  3.4 0.9 copy-done.3
  4.3 46.7 %all_to_all.15 = f32[64,9,2,128]{3,2,1,0:T(2,128)S(1)} all-to-all(f32[64,9,2,128]{3,2,1,0:T(2,128)S(1)} %shard_map.47), channel_id=1, replica_groups=mesh['x'=4,'zh'=2,'zl'=4,'core'=2,'y'=4,'zhi'=2] {'zl','core','y','zhi'}, dimensions={0} | all-to-all | bytes 1179648 | tf_op jit(solution)/shard_map/all_to_all | solution.py:377
  51.1 4.6 %collective-permute-start.2 = (f32[8,8,9,2,128]{4,3,2,1,0:T(2,128)S(1)}, f32[8,8,9,2,128]{4,3,2,1,0:T(2,128)S(1)}, u32[]{:S(2)}, u32[]{:S(2)}) collective-permute-start(f32[8,8,9,2,128]{4,3,2,1,0:T(2,128)S(1)} %bitcast.8), channel_id=1, source_target_pairs={{0,8},{8,0},{1,9},{9,1},{2,10},{10,2},{3,11},{11,3},{4,12},{12,4},... | collective-permute-start | bytes 1769480 | tf_op jit(solution)/shard_map/ppermute | solution.py:380
  55.7 1.6 %collective-permute-done.2.other_ref = f32[8,8,9,2,128]{4,3,2,1,0:T(2,128)S(1)} collective-permute-done((f32[8,8,9,2,128]{4,3,2,1,0:T(2,128)S(1)}, f32[8,8,9,2,128]{4,3,2,1,0:T(2,128)S(1)}, u32[]{:S(2)}, u32[]{:S(2)}) %collective-permute-start.2) | collective-permute-done | bytes 589856 | tf_op jit(solution)/shard_map/ppermute | solution.py:380
  57.2 0.3 shard_map.48
  57.5 1.3 collective-permute-start.3
  58.8 3.1 %shard_map.49 = (f32[7,16,40,128]{3,2,1,0:T(8,128)S(1)}, f32[7,16,40,128]{3,2,1,0:T(8,128)S(1)}) custom-call(f32[16,40,128]{2,1,0:T(8,128)S(1)} %get-tuple-element.22.k_ref), custom_call_target="tpu_custom_call" | custom-call | flops 7372800 | bytes 4915200 | tf_op jit(solution)/shard_map/pallas_call | solution.py:55
  61.9 4.1 %collective-permute-done.3.got_ref = f32[4,8,24,128]{3,2,1,0:T(8,128)S(1)} collective-permute-done((f32[4,8,24,128]{3,2,1,0:T(8,128)S(1)}, f32[4,8,24,128]{3,2,1,0:T(8,128)S(1)}, u32[]{:S(2)}, u32[]{:S(2)}) %collective-permute-start.3) | collective-permute-done | bytes 393248 | tf_op jit(solution)/shard_map/ppermute | solution.py:383
  66.0 1.9 %collective-permute-start.4 = (f32[4,8,24,128]{3,2,1,0:T(8,128)S(1)}, f32[4,8,24,128]{3,2,1,0:T(8,128)S(1)}, u32[]{:S(2)}, u32[]{:S(2)}) collective-permute-start(f32[4,8,24,128]{3,2,1,0:T(8,128)S(1)} %collective-permute-done.3.got_ref), channel_id=1, source_target_pairs={{0,8},{8,0},{1,9},{9,1},{2,10},{10,2},{3,11},{11,3},{4,12},{12,4},... | collective-permute-start | bytes 1179656 | tf_op jit(solution)/shard_map/ppermute | solution.py:380
  68.0 1.7 %collective-permute-done.4.got2_ref = f32[4,8,24,128]{3,2,1,0:T(8,128)S(1)} collective-permute-done((f32[4,8,24,128]{3,2,1,0:T(8,128)S(1)}, f32[4,8,24,128]{3,2,1,0:T(8,128)S(1)}, u32[]{:S(2)}, u32[]{:S(2)}) %collective-permute-start.4) | collective-permute-done | bytes 393248 | tf_op jit(solution)/shard_map/ppermute | solution.py:380
  69.6 3.1 %shard_map.50 = (f32[6,16,12,128]{3,2,1,0:T(8,128)S(1)}, f32[3,8,24,128]{3,2,1,0:T(8,128)S(1)}) custom-call(s32[1]{0:T(128)} %bitcast.core_ref, f32[7,16,40,128]{3,2,1,0:T(8,128)S(1)} %get-tuple-element.26.co_s.fine_s, f32[8,16,12,128]{3,2,1,0:T(8,128)S(1)} %get-tuple-element.27.f_ref, f32[1,8,24,128]{3,2,1,0:T(8,128)S(1)} %get-tuple-element.28.own_ref, ...), custom_call_target="tpu_custom_call" | custom-call | flops 14745600 | bytes 4849668 | tf_op jit(solution)/shard_map/pallas_call | solution.py:55
  72.8 1.3 collective-permute-start.5
  74.1 0.5 shard_map.51.start_ref
  74.5 5.7 %collective-permute-done.5.got_ref = f32[3,8,24,128]{3,2,1,0:T(8,128)S(1)} collective-permute-done((f32[3,8,24,128]{3,2,1,0:T(8,128)S(1)}, f32[3,8,24,128]{3,2,1,0:T(8,128)S(1)}, u32[]{:S(2)}, u32[]{:S(2)}) %collective-permute-start.5) | collective-permute-done | bytes 294944 | tf_op jit(solution)/shard_map/ppermute | solution.py:383
  80.2 1.9 %collective-permute-start.6 = (f32[3,8,24,128]{3,2,1,0:T(8,128)S(1)}, f32[3,8,24,128]{3,2,1,0:T(8,128)S(1)}, u32[]{:S(2)}, u32[]{:S(2)}) collective-permute-start(f32[3,8,24,128]{3,2,1,0:T(8,128)S(1)} %collective-permute-done.5.got_ref), channel_id=1, source_target_pairs={{0,8},{8,0},{1,9},{9,1},{2,10},{10,2},{3,11},{11,3},{4,12},{12,4},... | collective-permute-start | bytes 884744 | tf_op jit(solution)/shard_map/ppermute | solution.py:380
  82.1 1.5 %collective-permute-done.6.got2_ref = f32[3,8,24,128]{3,2,1,0:T(8,128)S(1)} collective-permute-done((f32[3,8,24,128]{3,2,1,0:T(8,128)S(1)}, f32[3,8,24,128]{3,2,1,0:T(8,128)S(1)}, u32[]{:S(2)}, u32[]{:S(2)}) %collective-permute-start.6) | collective-permute-done | bytes 294944 | tf_op jit(solution)/shard_map/ppermute | solution.py:380
  83.7 2.6 %shard_map.52 = (f32[16,12,128]{2,1,0:T(8,128)S(1)}, f32[5,16,12,128]{3,2,1,0:T(8,128)S(1)}, f32[1,8,24,128]{3,2,1,0:T(8,128)S(1)}) custom-call(s32[1]{0:T(128)} %bitcast.core_ref, f32[7,16,40,128]{3,2,1,0:T(8,128)S(1)} %get-tuple-element.26.co_s.fine_s, f32[7,16,40,128]{3,2,1,0:T(8,128)S(1)} %get-tuple-element.25.co_s, ...), custom_call_target="tpu_custom_call" | custom-call | flops 14745600 | bytes 6488068 | tf_op jit(solution)/shard_map/pallas_call | solution.py:55
  86.3 0.8 copy-done
  87.1 1.3 collective-permute-start.7
  88.4 4.1 %collective-permute-done.7.got_ref = f32[1,8,24,128]{3,2,1,0:T(8,128)S(1)} collective-permute-done((f32[1,8,24,128]{3,2,1,0:T(8,128)S(1)}, f32[1,8,24,128]{3,2,1,0:T(8,128)S(1)}, u32[]{:S(2)}, u32[]{:S(2)}) %collective-permute-start.7) | collective-permute-done | bytes 98336 | tf_op jit(solution)/shard_map/ppermute | solution.py:383
  92.4 2.7 %collective-permute-start.8 = (f32[1,8,24,128]{3,2,1,0:T(8,128)S(1)}, f32[1,8,24,128]{3,2,1,0:T(8,128)S(1)}, u32[]{:S(2)}, u32[]{:S(2)}) collective-permute-start(f32[1,8,24,128]{3,2,1,0:T(8,128)S(1)} %collective-permute-done.7.got_ref), channel_id=1, source_target_pairs={{0,8},{8,0},{1,9},{9,1},{2,10},{10,2},{3,11},{11,3},{4,12},{12,4},... | collective-permute-start | bytes 294920 | tf_op jit(solution)/shard_map/ppermute | solution.py:380
  95.2 0.9 collective-permute-done.8.got2_ref
  96.1 1.1 copy-done.1
  97.2 0.9 shard_map.53
  98.1 28.6 %all_to_all.16.got_ref = f32[8,48,128]{2,1,0:T(8,128)S(1)} all-to-all(f32[8,48,128]{2,1,0:T(8,128)S(1)} %shard_map.53), channel_id=1, replica_groups=mesh['x'=4,'zh'=2,'zl'=4,'core'=2,'y'=4,'zhi'=2] {'x','zh'}, dimensions={0} | all-to-all | bytes 393216 | tf_op jit(solution)/shard_map/all_to_all | solution.py:419
  126.8 25.2 %all_to_all.17.got_ref = f32[32,16,128]{2,1,0:T(8,128)S(1)} all-to-all(f32[32,16,128]{2,1,0:T(8,128)S(1)} %shard_map.54), channel_id=1, replica_groups=mesh['x'=4,'zh'=2,'zl'=4,'core'=2,'y'=4,'zhi'=2] {'zl','core','y'}, dimensions={0} | all-to-all | bytes 524288 | tf_op jit(solution)/shard_map/all_to_all | solution.py:421
  152.0 0.7 shard_map.55
  (9 shorter events, 0.1 us)
Async XLA Ops:
  0.0 2.4 %collective-permute-start.1 = (f32[2,192,128]{2,1,0:T(8,128)}, f32[2,192,128]{2,1,0:T(8,128)S(1)}, u32[]{:S(2)}, u32[]{:S(2)}) collective-permute-start(f32[2,192,128]{2,1,0:T(8,128)} %bitcast.11), channel_id=1, source_target_pairs={{56,72},{57,73},{58,74},{59,75},{60,76},{61,77},{62,78},{63,79},{1... | collective-permute-start | bytes 589832 | tf_op jit(solution)/shard_map/ppermute | solution.py:363
  0.7 1.7 %collective-permute-start = (f32[2,192,128]{2,1,0:T(8,128)}, f32[2,192,128]{2,1,0:T(8,128)S(1)}, u32[]{:S(2)}, u32[]{:S(2)}) collective-permute-start(f32[2,192,128]{2,1,0:T(8,128)} %bitcast.12), channel_id=1, source_target_pairs={{56,64},{57,65},{58,66},{59,67},{60,68},{61,69},{62,70},{63,71},{1... | collective-permute-start | bytes 589832 | tf_op jit(solution)/shard_map/ppermute | solution.py:363
  1.4 0.9 copy-start.4
  2.4 0.9 copy-start.2
  3.4 0.9 copy-start.3
  51.1 6.2 %collective-permute-start.2 = (f32[8,8,9,2,128]{4,3,2,1,0:T(2,128)S(1)}, f32[8,8,9,2,128]{4,3,2,1,0:T(2,128)S(1)}, u32[]{:S(2)}, u32[]{:S(2)}) collective-permute-start(f32[8,8,9,2,128]{4,3,2,1,0:T(2,128)S(1)} %bitcast.8), channel_id=1, source_target_pairs={{0,8},{8,0},{1,9},{9,1},{2,10},{10,2},{3,11},{11,3},{4,12},{12,4},... | collective-permute-start | bytes 1769480 | tf_op jit(solution)/shard_map/ppermute | solution.py:380
  57.5 8.5 %collective-permute-start.3 = (f32[4,8,24,128]{3,2,1,0:T(8,128)S(1)}, f32[4,8,24,128]{3,2,1,0:T(8,128)S(1)}, u32[]{:S(2)}, u32[]{:S(2)}) collective-permute-start(f32[4,8,24,128]{3,2,1,0:T(8,128)S(1)} %get-tuple-element.21), channel_id=1, source_target_pairs={{0,2},{2,4},{4,6},{6,22},{22,20},{20,18},{18,16},{16,32},{32,34},{... | collective-permute-start | bytes 1179656 | tf_op jit(solution)/shard_map/ppermute | solution.py:383
  66.0 3.6 %collective-permute-start.4 = (f32[4,8,24,128]{3,2,1,0:T(8,128)S(1)}, f32[4,8,24,128]{3,2,1,0:T(8,128)S(1)}, u32[]{:S(2)}, u32[]{:S(2)}) collective-permute-start(f32[4,8,24,128]{3,2,1,0:T(8,128)S(1)} %collective-permute-done.3.got_ref), channel_id=1, source_target_pairs={{0,8},{8,0},{1,9},{9,1},{2,10},{10,2},{3,11},{11,3},{4,12},{12,4},... | collective-permute-start | bytes 1179656 | tf_op jit(solution)/shard_map/ppermute | solution.py:380
  72.8 7.5 %collective-permute-start.5 = (f32[3,8,24,128]{3,2,1,0:T(8,128)S(1)}, f32[3,8,24,128]{3,2,1,0:T(8,128)S(1)}, u32[]{:S(2)}, u32[]{:S(2)}) collective-permute-start(f32[3,8,24,128]{3,2,1,0:T(8,128)S(1)} %get-tuple-element.30.own_ref), channel_id=1, source_target_pairs={{0,2},{2,4},{4,6},{6,22},{22,20},{20,18},{18,16},{16,32},{32,34},{... | collective-permute-start | bytes 884744 | tf_op jit(solution)/shard_map/ppermute | solution.py:383
  80.2 3.5 %collective-permute-start.6 = (f32[3,8,24,128]{3,2,1,0:T(8,128)S(1)}, f32[3,8,24,128]{3,2,1,0:T(8,128)S(1)}, u32[]{:S(2)}, u32[]{:S(2)}) collective-permute-start(f32[3,8,24,128]{3,2,1,0:T(8,128)S(1)} %collective-permute-done.5.got_ref), channel_id=1, source_target_pairs={{0,8},{8,0},{1,9},{9,1},{2,10},{10,2},{3,11},{11,3},{4,12},{12,4},... | collective-permute-start | bytes 884744 | tf_op jit(solution)/shard_map/ppermute | solution.py:380
  86.3 0.8 copy-start
  87.1 5.3 %collective-permute-start.7 = (f32[1,8,24,128]{3,2,1,0:T(8,128)S(1)}, f32[1,8,24,128]{3,2,1,0:T(8,128)S(1)}, u32[]{:S(2)}, u32[]{:S(2)}) collective-permute-start(f32[1,8,24,128]{3,2,1,0:T(8,128)S(1)} %get-tuple-element.33.own_ref), channel_id=1, source_target_pairs={{0,2},{2,4},{4,6},{6,22},{22,20},{20,18},{18,16},{16,32},{32,34},{... | collective-permute-start | bytes 294920 | tf_op jit(solution)/shard_map/ppermute | solution.py:383
  92.4 3.6 %collective-permute-start.8 = (f32[1,8,24,128]{3,2,1,0:T(8,128)S(1)}, f32[1,8,24,128]{3,2,1,0:T(8,128)S(1)}, u32[]{:S(2)}, u32[]{:S(2)}) collective-permute-start(f32[1,8,24,128]{3,2,1,0:T(8,128)S(1)} %collective-permute-done.7.got_ref), channel_id=1, source_target_pairs={{0,8},{8,0},{1,9},{9,1},{2,10},{10,2},{3,11},{11,3},{4,12},{12,4},... | collective-permute-start | bytes 294920 | tf_op jit(solution)/shard_map/ppermute | solution.py:380
  96.1 1.1 copy-start.1

commit v10 on v9

--- a/solution.py
+++ b/solution.py
@@ -58,7 +58,7 @@
         in_specs=specs,
         out_specs=out_specs,
         scratch_shapes=list(scratch),
-        compiler_params=pltpu.CompilerParams(vmem_limit_bytes=32 * 1024 * 1024),
+        compiler_params=pltpu.CompilerParams(vmem_limit_bytes=12 * 1024 * 1024),
         cost_estimate=pl.CostEstimate(flops=flops, bytes_accessed=size, transcendentals=0),
     )(*args)
 
@@ -75,17 +75,21 @@
                     yield ((zl * 2 + core) * 4 + y) * 2 + zhi, core, chip_order(zl, y)
 
 
-def source_body(src_ref, out_ref):
+def halves_body(guess_ref, half0_ref, half1_ref):
+    for core in range(2):
+        for m in range(CHIPS):
+            for r in range(3):
+                row = m * STRIP + 2 * r
+                half0_ref[core, m, r] = guess_ref[core, row : row + 2]
+                half1_ref[core, m, r] = guess_ref[core, row + 6 : row + 8]
+
+
+def home_fields_body(j_ref, src_ref, cond_ref, init_ref, out_ref):
+    place = j_ref[0]
     for to, core, m in targets():
         for r in range(6):
             row = m * STRIP + 2 * r
             out_ref[to, r] = src_ref[core, row : row + 2]
-
-
-def extra_body(j_ref, block_ref, prev0_ref, prev1_ref, cond_ref, init_ref, base_ref, out_ref):
-    place = j_ref[0]
-    first = block_ref[0] == 0
-    later = jnp.logical_not(first)
 
     def fill(ref, shift, half):
         for to, core, m in targets():
@@ -97,11 +101,20 @@
                 else:
                     out_ref[to, 6 + r] = jnp.zeros((2, LANES), F32)
 
-    for half, prev_ref in ((0, prev0_ref), (1, prev1_ref)):
+    for half in range(2):
+        pl.when(place == half)(functools.partial(fill, init_ref, 0, half))
         for n, shift in enumerate((0, 1, -1)):
             pl.when(place == 2 + 2 * n + half)(functools.partial(fill, cond_ref, shift, half))
-        pl.when((place == half) & first)(functools.partial(fill, init_ref, 0, half))
-        pl.when((place == half) & later)(functools.partial(fill, prev_ref, 0, half))
+
+
+def previous_body(j_ref, block_ref, prev0_ref, prev1_ref, base_ref, out_ref):
+    for half, prev_ref in ((0, prev0_ref), (1, prev1_ref)):
+
+        @pl.when((j_ref[0] == half) & (block_ref[0] > 0))
+        def _(prev_ref=prev_ref):
+            for to, core, m in targets():
+                for r in range(3):
+                    out_ref[to, 6 + r] = prev_ref[core, m, r]
 
 
 def by_core(core_ref, body, mine, other):
@@ -353,27 +366,28 @@
     place = lax.axis_index(("zl", "core"))[None]
     block = lax.axis_index(BLOCKS)[None]
 
-    def onward(place):
+    def onward(mine, place):
         route = []
         for b in range(NB - 1):
             for y in range(4):
                 for zhi in range(2):
                     to = zhi if b % 2 == 0 else 1 - zhi
                     route.append((((b * 8 + 7) * 4 + y) * 2 + zhi, (((b + 1) * 8 + place) * 4 + y) * 2 + to))
-        return lax.ppermute(guess, AXES, route)
-
-    prev0, prev1 = onward(0), onward(1)
+        return lax.ppermute(mine, AXES, route)
+
+    half0, half1 = call(halves_body, [sds(2, CHIPS, 3, 2, LANES)] * 2, guess)
+    prev0, prev1 = onward(half0, 0), onward(half1, 1)
     flip = ((block > 0) & (block % 2 == 0)).astype(jnp.int32)
-    (base,) = call(source_body, [sds(64, 9, 2, LANES)], source)
+    (base,) = call(home_fields_body, [sds(64, 9, 2, LANES)], place, source, diffusivity, initial, smem=1)
     vmem = pl.BlockSpec(memory_space=pltpu.VMEM)
     sent = pl.pallas_call(
-        extra_body,
+        previous_body,
         out_shape=sds(64, 9, 2, LANES),
-        in_specs=[pl.BlockSpec(memory_space=pltpu.SMEM)] * 2 + [vmem] * 5,
+        in_specs=[pl.BlockSpec(memory_space=pltpu.SMEM)] * 2 + [vmem] * 3,
         out_specs=vmem,
-        input_output_aliases={6: 0},
-        compiler_params=pltpu.CompilerParams(vmem_limit_bytes=32 * 1024 * 1024),
-    )(place, block, prev0, prev1, diffusivity, initial, base)
+        input_output_aliases={4: 0},
+        compiler_params=pltpu.CompilerParams(vmem_limit_bytes=12 * 1024 * 1024),
+    )(place, block, prev0, prev1, base)
     strips = lax.all_to_all(sent, BLOCK, 0, 0, tiled=True).reshape(8, 8, 9, 2, LANES)
 
     def swap(mine):

time: 153 us -> 150 us (0.980)
  blocking collectives: 101 us -> 97 us
    all_to_all x1, blocking collectives: 28.6 us -> 22.3 us  [on_device(): arrived = lax.all_to_all(powers, BLOCKS, 0, 0, tiled=True)]
    all_to_all x1, blocking collectives: 46.7 us -> 50 us  [on_device(): lax.all_to_all(sent, BLOCK, 0, 0, tiled=True).reshape(8, 8, 9, 2, LANES)]
    unnamed x10 -> x12, local copies, waits for them, and re-layouts: 4.69 us -> 5.63 us
    pallas_call x9 -> x10, Pallas kernels: 11.3 us -> 11.4 us  [call(): pl.pallas_call(body, out_shape=list(outs), in_specs=specs, out_specs=out_...]
  transfers between devices with their start and end apart: 9 -> 9, of which waited for: 7 -> 7; matrix products, arithmetic and copies ran while one was open for 0% -> 0% of each run, Pallas kernels for 2% -> 3%
where the time goes in v10:
time: 150 us
  blocking collectives  97 us (65%)
  waiting for transfers between devices  20.4 us (14%)
  starting transfers between devices  15.1 us (10%)
  Pallas kernels  11.4 us (8%)
  local copies, waits for them, and re-layouts  5.63 us (4%)
    all_to_all x1, blocking collectives, on_device(): lax.all_to_all(sent, BLOCK, 0, 0, tiled=True).reshape(8, 8, 9, 2, LANES)  50 us
    all_to_all x1, blocking collectives, on_device(): returned = lax.all_to_all(back, ('zl', 'core', 'y'), 0, 0, tiled=True)  24.6 us
    all_to_all x1, blocking collectives, on_device(): arrived = lax.all_to_all(powers, BLOCKS, 0, 0, tiled=True)  22.3 us
    ppermute x3, waiting for transfers between devices, exchange(): got = lax.ppermute(mine, ('zl', 'core', 'y'), neighbour_route())  15 us
    pallas_call x10, Pallas kernels, call(): pl.pallas_call(body, out_shape=list(outs), in_specs=specs, out_specs=out_...  11.4 us
    ppermute x4, starting transfers between devices, swap(): return lax.ppermute(mine, 'core', [(0, 1), (1, 0)])  9.92 us
    unnamed x12, local copies, waits for them, and re-layouts  5.63 us
    ppermute x4, waiting for transfers between devices, swap(): return lax.ppermute(mine, 'core', [(0, 1), (1, 0)])  5.39 us
  transfers between devices with their start and end apart: 9, of which 7 were waited for; matrix products, arithmetic and copies ran while one was open for 0% of the time, Pallas kernels for 3%

profile of v10, /device:TPU:1, one launch (start us, length us, event | category | flops | bytes accessed | tf_op | source)
XLA Modules:
  0.0 149.7 jit_solution(16768958528044875419)
XLA Ops:
  0.0 0.9 copy-done.2
  1.0 0.7 collective-permute-start
  1.7 0.7 collective-permute-start.1
  2.4 0.9 copy-done.3
  3.3 0.9 copy-done.4
  4.2 0.9 copy-done.5
  5.4 50.0 %all_to_all.15 = f32[64,9,2,128]{3,2,1,0:T(2,128)S(1)} all-to-all(f32[64,9,2,128]{3,2,1,0:T(2,128)S(1)} %shard_map.48), channel_id=1, replica_groups=mesh['x'=4,'zh'=2,'zl'=4,'core'=2,'y'=4,'zhi'=2] {'zl','core','y','zhi'}, dimensions={0} | all-to-all | bytes 1179648 | tf_op jit(solution)/shard_map/all_to_all | solution.py:391
  55.4 2.6 %collective-permute-start.2 = (f32[8,8,9,2,128]{4,3,2,1,0:T(2,128)S(1)}, f32[8,8,9,2,128]{4,3,2,1,0:T(2,128)S(1)}, u32[]{:S(2)}, u32[]{:S(2)}) collective-permute-start(f32[8,8,9,2,128]{4,3,2,1,0:T(2,128)S(1)} %bitcast.8), channel_id=1, source_target_pairs={{0,8},{8,0},{1,9},{9,1},{2,10},{10,2},{3,11},{11,3},{4,12},{12,4},... | collective-permute-start | bytes 1769480 | tf_op jit(solution)/shard_map/ppermute | solution.py:394
  58.0 1.6 %collective-permute-done.2.other_ref = f32[8,8,9,2,128]{4,3,2,1,0:T(2,128)S(1)} collective-permute-done((f32[8,8,9,2,128]{4,3,2,1,0:T(2,128)S(1)}, f32[8,8,9,2,128]{4,3,2,1,0:T(2,128)S(1)}, u32[]{:S(2)}, u32[]{:S(2)}) %collective-permute-start.2) | collective-permute-done | bytes 589856 | tf_op jit(solution)/shard_map/ppermute | solution.py:394
  59.6 0.3 shard_map.49
  59.9 1.3 collective-permute-start.3
  61.2 3.1 %shard_map.50 = (f32[7,16,40,128]{3,2,1,0:T(8,128)S(1)}, f32[7,16,40,128]{3,2,1,0:T(8,128)S(1)}) custom-call(f32[16,40,128]{2,1,0:T(8,128)S(1)} %get-tuple-element.26.k_ref), custom_call_target="tpu_custom_call" | custom-call | flops 7372800 | bytes 4915200 | tf_op jit(solution)/shard_map/pallas_call | solution.py:55
  64.2 4.1 %collective-permute-done.3.got_ref = f32[4,8,24,128]{3,2,1,0:T(8,128)S(1)} collective-permute-done((f32[4,8,24,128]{3,2,1,0:T(8,128)S(1)}, f32[4,8,24,128]{3,2,1,0:T(8,128)S(1)}, u32[]{:S(2)}, u32[]{:S(2)}) %collective-permute-start.3) | collective-permute-done | bytes 393248 | tf_op jit(solution)/shard_map/ppermute | solution.py:397
  68.4 1.9 %collective-permute-start.4 = (f32[4,8,24,128]{3,2,1,0:T(8,128)S(1)}, f32[4,8,24,128]{3,2,1,0:T(8,128)S(1)}, u32[]{:S(2)}, u32[]{:S(2)}) collective-permute-start(f32[4,8,24,128]{3,2,1,0:T(8,128)S(1)} %collective-permute-done.3.got_ref), channel_id=1, source_target_pairs={{0,8},{8,0},{1,9},{9,1},{2,10},{10,2},{3,11},{11,3},{4,12},{12,4},... | collective-permute-start | bytes 1179656 | tf_op jit(solution)/shard_map/ppermute | solution.py:394
  70.3 1.7 %collective-permute-done.4.got2_ref = f32[4,8,24,128]{3,2,1,0:T(8,128)S(1)} collective-permute-done((f32[4,8,24,128]{3,2,1,0:T(8,128)S(1)}, f32[4,8,24,128]{3,2,1,0:T(8,128)S(1)}, u32[]{:S(2)}, u32[]{:S(2)}) %collective-permute-start.4) | collective-permute-done | bytes 393248 | tf_op jit(solution)/shard_map/ppermute | solution.py:394
  72.0 3.1 %shard_map.51 = (f32[6,16,12,128]{3,2,1,0:T(8,128)S(1)}, f32[3,8,24,128]{3,2,1,0:T(8,128)S(1)}) custom-call(s32[1]{0:T(128)} %bitcast.core_ref, f32[7,16,40,128]{3,2,1,0:T(8,128)S(1)} %get-tuple-element.30.co_s.fine_s, f32[8,16,12,128]{3,2,1,0:T(8,128)S(1)} %get-tuple-element.31.f_ref, f32[1,8,24,128]{3,2,1,0:T(8,128)S(1)} %get-tuple-element.32.own_ref, ...), custom_call_target="tpu_custom_call" | custom-call | flops 14745600 | bytes 4849668 | tf_op jit(solution)/shard_map/pallas_call | solution.py:55
  75.1 1.3 collective-permute-start.5
  76.4 0.5 shard_map.52.start_ref
  76.9 6.0 %collective-permute-done.5.got_ref = f32[3,8,24,128]{3,2,1,0:T(8,128)S(1)} collective-permute-done((f32[3,8,24,128]{3,2,1,0:T(8,128)S(1)}, f32[3,8,24,128]{3,2,1,0:T(8,128)S(1)}, u32[]{:S(2)}, u32[]{:S(2)}) %collective-permute-start.5) | collective-permute-done | bytes 294944 | tf_op jit(solution)/shard_map/ppermute | solution.py:397
  82.9 2.7 %collective-permute-start.6 = (f32[3,8,24,128]{3,2,1,0:T(8,128)S(1)}, f32[3,8,24,128]{3,2,1,0:T(8,128)S(1)}, u32[]{:S(2)}, u32[]{:S(2)}) collective-permute-start(f32[3,8,24,128]{3,2,1,0:T(8,128)S(1)} %collective-permute-done.5.got_ref), channel_id=1, source_target_pairs={{0,8},{8,0},{1,9},{9,1},{2,10},{10,2},{3,11},{11,3},{4,12},{12,4},... | collective-permute-start | bytes 884744 | tf_op jit(solution)/shard_map/ppermute | solution.py:394
  85.6 1.2 collective-permute-done.6.got2_ref
  86.8 2.6 %shard_map.53 = (f32[16,12,128]{2,1,0:T(8,128)S(1)}, f32[5,16,12,128]{3,2,1,0:T(8,128)S(1)}, f32[1,8,24,128]{3,2,1,0:T(8,128)S(1)}) custom-call(s32[1]{0:T(128)} %bitcast.core_ref, f32[7,16,40,128]{3,2,1,0:T(8,128)S(1)} %get-tuple-element.30.co_s.fine_s, f32[7,16,40,128]{3,2,1,0:T(8,128)S(1)} %get-tuple-element.29.co_s, ...), custom_call_target="tpu_custom_call" | custom-call | flops 14745600 | bytes 6488068 | tf_op jit(solution)/shard_map/pallas_call | solution.py:55
  89.3 0.8 copy-done
  90.2 1.3 collective-permute-start.7
  91.5 4.8 %collective-permute-done.7.got_ref = f32[1,8,24,128]{3,2,1,0:T(8,128)S(1)} collective-permute-done((f32[1,8,24,128]{3,2,1,0:T(8,128)S(1)}, f32[1,8,24,128]{3,2,1,0:T(8,128)S(1)}, u32[]{:S(2)}, u32[]{:S(2)}) %collective-permute-start.7) | collective-permute-done | bytes 98336 | tf_op jit(solution)/shard_map/ppermute | solution.py:397
  96.3 2.8 %collective-permute-start.8 = (f32[1,8,24,128]{3,2,1,0:T(8,128)S(1)}, f32[1,8,24,128]{3,2,1,0:T(8,128)S(1)}, u32[]{:S(2)}, u32[]{:S(2)}) collective-permute-start(f32[1,8,24,128]{3,2,1,0:T(8,128)S(1)} %collective-permute-done.7.got_ref), channel_id=1, source_target_pairs={{0,8},{8,0},{1,9},{9,1},{2,10},{10,2},{3,11},{11,3},{4,12},{12,4},... | collective-permute-start | bytes 294920 | tf_op jit(solution)/shard_map/ppermute | solution.py:394
  99.0 0.9 collective-permute-done.8.got2_ref
  100.0 1.1 copy-done.1
  101.1 0.9 shard_map.54
  102.0 22.3 %all_to_all.16.got_ref = f32[8,48,128]{2,1,0:T(8,128)S(1)} all-to-all(f32[8,48,128]{2,1,0:T(8,128)S(1)} %shard_map.54), channel_id=1, replica_groups=mesh['x'=4,'zh'=2,'zl'=4,'core'=2,'y'=4,'zhi'=2] {'x','zh'}, dimensions={0} | all-to-all | bytes 393216 | tf_op jit(solution)/shard_map/all_to_all | solution.py:433
  124.4 24.6 %all_to_all.17.got_ref = f32[32,16,128]{2,1,0:T(8,128)S(1)} all-to-all(f32[32,16,128]{2,1,0:T(8,128)S(1)} %shard_map.55), channel_id=1, replica_groups=mesh['x'=4,'zh'=2,'zl'=4,'core'=2,'y'=4,'zhi'=2] {'zl','core','y'}, dimensions={0} | all-to-all | bytes 524288 | tf_op jit(solution)/shard_map/all_to_all | solution.py:435
  149.0 0.7 shard_map.56
  (12 shorter events, 0.3 us)
Async XLA Ops:
  0.0 0.9 copy-start.2
  1.0 4.3 %collective-permute-start = (f32[2,16,3,2,128]{4,3,2,1,0:T(2,128)S(1)}, f32[2,16,3,2,128]{4,3,2,1,0:T(2,128)S(1)}, u32[]{:S(2)}, u32[]{:S(2)}) collective-permute-start(f32[2,16,3,2,128]{4,3,2,1,0:T(2,128)S(1)} %get-tuple-element.23), channel_id=1, source_target_pairs={{56,64},{57,65},{58,66},{59,67},{60,68},{61,69},{62,70},{63,71},{1... | collective-permute-start | bytes 294920 | tf_op jit(solution)/shard_map/ppermute | solution.py:376
  1.7 3.7 %collective-permute-start.1 = (f32[2,16,3,2,128]{4,3,2,1,0:T(2,128)S(1)}, f32[2,16,3,2,128]{4,3,2,1,0:T(2,128)S(1)}, u32[]{:S(2)}, u32[]{:S(2)}) collective-permute-start(f32[2,16,3,2,128]{4,3,2,1,0:T(2,128)S(1)} %get-tuple-element.24), channel_id=1, source_target_pairs={{56,72},{57,73},{58,74},{59,75},{60,76},{61,77},{62,78},{63,79},{1... | collective-permute-start | bytes 294920 | tf_op jit(solution)/shard_map/ppermute | solution.py:376
  2.3 0.9 copy-start.3
  3.3 0.9 copy-start.4
  4.2 0.9 copy-start.5
  55.4 4.2 %collective-permute-start.2 = (f32[8,8,9,2,128]{4,3,2,1,0:T(2,128)S(1)}, f32[8,8,9,2,128]{4,3,2,1,0:T(2,128)S(1)}, u32[]{:S(2)}, u32[]{:S(2)}) collective-permute-start(f32[8,8,9,2,128]{4,3,2,1,0:T(2,128)S(1)} %bitcast.8), channel_id=1, source_target_pairs={{0,8},{8,0},{1,9},{9,1},{2,10},{10,2},{3,11},{11,3},{4,12},{12,4},... | collective-permute-start | bytes 1769480 | tf_op jit(solution)/shard_map/ppermute | solution.py:394
  59.9 8.5 %collective-permute-start.3 = (f32[4,8,24,128]{3,2,1,0:T(8,128)S(1)}, f32[4,8,24,128]{3,2,1,0:T(8,128)S(1)}, u32[]{:S(2)}, u32[]{:S(2)}) collective-permute-start(f32[4,8,24,128]{3,2,1,0:T(8,128)S(1)} %get-tuple-element.25), channel_id=1, source_target_pairs={{0,2},{2,4},{4,6},{6,22},{22,20},{20,18},{18,16},{16,32},{32,34},{... | collective-permute-start | bytes 1179656 | tf_op jit(solution)/shard_map/ppermute | solution.py:397
  68.4 3.6 %collective-permute-start.4 = (f32[4,8,24,128]{3,2,1,0:T(8,128)S(1)}, f32[4,8,24,128]{3,2,1,0:T(8,128)S(1)}, u32[]{:S(2)}, u32[]{:S(2)}) collective-permute-start(f32[4,8,24,128]{3,2,1,0:T(8,128)S(1)} %collective-permute-done.3.got_ref), channel_id=1, source_target_pairs={{0,8},{8,0},{1,9},{9,1},{2,10},{10,2},{3,11},{11,3},{4,12},{12,4},... | collective-permute-start | bytes 1179656 | tf_op jit(solution)/shard_map/ppermute | solution.py:394
  75.1 7.8 %collective-permute-start.5 = (f32[3,8,24,128]{3,2,1,0:T(8,128)S(1)}, f32[3,8,24,128]{3,2,1,0:T(8,128)S(1)}, u32[]{:S(2)}, u32[]{:S(2)}) collective-permute-start(f32[3,8,24,128]{3,2,1,0:T(8,128)S(1)} %get-tuple-element.34.own_ref), channel_id=1, source_target_pairs={{0,2},{2,4},{4,6},{6,22},{22,20},{20,18},{18,16},{16,32},{32,34},{... | collective-permute-start | bytes 884744 | tf_op jit(solution)/shard_map/ppermute | solution.py:397
  82.9 3.9 %collective-permute-start.6 = (f32[3,8,24,128]{3,2,1,0:T(8,128)S(1)}, f32[3,8,24,128]{3,2,1,0:T(8,128)S(1)}, u32[]{:S(2)}, u32[]{:S(2)}) collective-permute-start(f32[3,8,24,128]{3,2,1,0:T(8,128)S(1)} %collective-permute-done.5.got_ref), channel_id=1, source_target_pairs={{0,8},{8,0},{1,9},{9,1},{2,10},{10,2},{3,11},{11,3},{4,12},{12,4},... | collective-permute-start | bytes 884744 | tf_op jit(solution)/shard_map/ppermute | solution.py:394
  89.3 0.9 copy-start
  90.2 6.1 %collective-permute-start.7 = (f32[1,8,24,128]{3,2,1,0:T(8,128)S(1)}, f32[1,8,24,128]{3,2,1,0:T(8,128)S(1)}, u32[]{:S(2)}, u32[]{:S(2)}) collective-permute-start(f32[1,8,24,128]{3,2,1,0:T(8,128)S(1)} %get-tuple-element.37.own_ref), channel_id=1, source_target_pairs={{0,2},{2,4},{4,6},{6,22},{22,20},{20,18},{18,16},{16,32},{32,34},{... | collective-permute-start | bytes 294920 | tf_op jit(solution)/shard_map/ppermute | solution.py:397
  96.3 3.7 %collective-permute-start.8 = (f32[1,8,24,128]{3,2,1,0:T(8,128)S(1)}, f32[1,8,24,128]{3,2,1,0:T(8,128)S(1)}, u32[]{:S(2)}, u32[]{:S(2)}) collective-permute-start(f32[1,8,24,128]{3,2,1,0:T(8,128)S(1)} %collective-permute-done.7.got_ref), channel_id=1, source_target_pairs={{0,8},{8,0},{1,9},{9,1},{2,10},{10,2},{3,11},{11,3},{4,12},{12,4},... | collective-permute-start | bytes 294920 | tf_op jit(solution)/shard_map/ppermute | solution.py:394
  100.0 1.1 copy-start.1

commit v11 on v10

--- a/solution.py
+++ b/solution.py
@@ -24,7 +24,9 @@
 CHIPS = 16
 STRIP = NY // CHIPS
 PAIR = 2 * STRIP
+HALF = STRIP // 2
 LANES = 128
+LAYERS = [(y, p) for y in range(4) for p in range(2)]
 LOW, OWN, HIGH, WIN = 4, 16, 28, 40
 
 
@@ -307,11 +309,19 @@
 
 
 def powers_body(
-    core_ref, side_ref, block_ref, co_s, own_ref, got_ref, got2_ref, early_ref,
-    out_ref, a_s, b_s, db_s, pow_s,
+    core_ref, side_ref, block_ref, co_s, own_ref, got_ref, early_ref, out_ref, a_s, b_s, db_s, pow_s
 ):
     clear_ends(a_s, b_s)
-    load_window(core_ref, a_s, 0, own_ref, got_ref, got2_ref)
+    for z in range(NZ):
+        a_s[z + 1] = jnp.zeros((WIN, LANES), F32)
+        a_s[z + 1, OWN:HIGH] = own_ref[0, z // 2, at(z, 0, STRIP)]
+
+    def halo(rows):
+        for z in range(NZ):
+            a_s[z + 1, rows] = got_ref[0, z // 2, at(z, 0, STRIP)]
+
+    pl.when(core_ref[0] == 0)(functools.partial(halo, slice(LOW, OWN)))
+    pl.when(core_ref[0] == 1)(functools.partial(halo, slice(HIGH, WIN)))
     for n in range(5):
         for z in range(NZ):
             pow_s[n, z] = early_ref[n, z]
@@ -320,12 +330,17 @@
         for z in range(NZ):
             pow_s[5 + n, z] = a_s[z + 1, OWN:HIGH]
     c = block_ref[0]
-    for b in range(NB):
-        power = jnp.clip(b - c, 0, NB - 1)
-        live = b >= c
-        for y in range(4):
-            value = pow_s[power, 2 * (2 * y + side_ref[0]) + core_ref[0]]
-            out_ref[b, y * STRIP : (y + 1) * STRIP] = jnp.where(live, value, 0.0)
+
+    def send(rows):
+        for b in range(NB):
+            power = jnp.clip(b - c, 0, NB - 1)
+            live = b >= c
+            for n, (y, p) in enumerate(LAYERS):
+                value = pow_s[power, 2 * (2 * y + side_ref[0]) + p, rows]
+                out_ref[b, n * HALF : (n + 1) * HALF] = jnp.where(live, value, 0.0)
+
+    for core in range(2):
+        pl.when(core_ref[0] == core)(functools.partial(send, slice(core * HALF, (core + 1) * HALF)))
 
 
 SWEEP_SCRATCH = (
@@ -336,26 +351,31 @@
 
 
 def collect_body(core_ref, side_ref, got_ref, early_ref, late_ref, out_ref):
-    for y in range(4):
-        z = 2 * (2 * y + side_ref[0]) + core_ref[0]
-        rows = slice(y * STRIP, (y + 1) * STRIP)
-        total = got_ref[0, rows]
-        for b in range(1, NB):
-            total = total + got_ref[b, rows]
-        out_ref[7 * 4 + y, 0:STRIP] = total
-        for n in range(6):
-            out_ref[n * 4 + y, 0:STRIP] = early_ref[n, z]
-        out_ref[6 * 4 + y, 0:STRIP] = late_ref[z]
-        for n in range(8):
-            out_ref[n * 4 + y, STRIP:16] = jnp.zeros((16 - STRIP, LANES), F32)
+    def fill(rows):
+        for n, (y, p) in enumerate(LAYERS):
+            z = 2 * (2 * y + side_ref[0]) + p
+            mine, to = slice(n * HALF, (n + 1) * HALF), slice(p * HALF, (p + 1) * HALF)
+            total = got_ref[0, mine]
+            for b in range(1, NB):
+                total = total + got_ref[b, mine]
+            out_ref[7 * 4 + y, to] = total
+            for t in range(6):
+                out_ref[t * 4 + y, to] = early_ref[t, z, rows]
+            out_ref[6 * 4 + y, to] = late_ref[z, rows]
+
+    for core in range(2):
+        pl.when(core_ref[0] == core)(functools.partial(fill, slice(core * HALF, (core + 1) * HALF)))
+    for n in range(32):
+        out_ref[n, STRIP:16] = jnp.zeros((16 - STRIP, LANES), F32)
 
 
 def home_body(got_ref, out_ref):
     for zl in range(4):
         for y in range(4):
-            m = chip_order(zl, y)
             for core in range(2):
-                out_ref[core, m * STRIP : (m + 1) * STRIP] = got_ref[(zl * 2 + core) * 4 + y, 0:STRIP]
+                row = chip_order(zl, y) * STRIP + core * HALF
+                for p in range(2):
+                    out_ref[p, row : row + HALF] = got_ref[(zl * 2 + core) * 4 + y, p * HALF : (p + 1) * HALF]
 
 
 def on_device(guess, source, diffusivity, initial):
@@ -393,8 +413,11 @@
     def swap(mine):
         return lax.ppermute(mine, "core", [(0, 1), (1, 0)])
 
+    def from_neighbour(mine):
+        return lax.ppermute(mine, ("zl", "core", "y"), neighbour_route())
+
     def exchange(mine, beside):
-        got = lax.ppermute(mine, ("zl", "core", "y"), neighbour_route())
+        got = from_neighbour(mine)
         got, beside = lax.optimization_barrier((got, beside))
         return got, swap(got), beside
 
@@ -424,10 +447,9 @@
         core, fine, coarse, state, state_got, state_got2, start_g, smem=1, flops=12 * flops,
         scratch=SWEEP_SCRATCH + (pltpu.VMEM((NZ + 2, WIN, LANES), F32),),
     )
-    last_got, last_got2, _ = exchange(last, ())
     (powers,) = call(
         powers_body, [sds(NB, 4 * STRIP, LANES)],
-        core, side, block, coarse, last, last_got, last_got2, first_powers, smem=3, flops=6 * flops,
+        core, side, block, coarse, last, from_neighbour(last), first_powers, smem=3, flops=6 * flops,
         scratch=SWEEP_SCRATCH + (pltpu.VMEM((NB, NZ, STRIP, LANES), F32),),
     )
     arrived = lax.all_to_all(powers, BLOCKS, 0, 0, tiled=True)

time: 150 us -> 147 us (0.980)
  starting transfers between devices: 15.1 us -> 12.4 us
    ppermute x4 -> x3, starting transfers between devices: 9.92 us -> 7.16 us  [swap(): return lax.ppermute(mine, 'core', [(0, 1), (1, 0)])]
    ppermute x4 -> x3, waiting for transfers between devices: 5.39 us -> 4.47 us  [swap(): return lax.ppermute(mine, 'core', [(0, 1), (1, 0)])]
  transfers between devices with their start and end apart: 9 -> 8, of which waited for: 7 -> 6; matrix products, arithmetic and copies ran while one was open for 0% -> 0% of each run, Pallas kernels for 3% -> 3%
where the time goes in v11:
time: 147 us; the launch traced here: 146 us
  blocking collectives  97.3 us (66%)
  waiting for transfers between devices  19.4 us (13%)
  starting transfers between devices  12.4 us (8%)
  Pallas kernels  11.5 us (8%)
  local copies, waits for them, and re-layouts  5.62 us (4%)
    all_to_all x1, blocking collectives, on_device(): lax.all_to_all(sent, BLOCK, 0, 0, tiled=True).reshape(8, 8, 9, 2, LANES)  50 us
    all_to_all x1, blocking collectives, on_device(): returned = lax.all_to_all(back, ('zl', 'core', 'y'), 0, 0, tiled=True)  25 us
    all_to_all x1, blocking collectives, on_device(): arrived = lax.all_to_all(powers, BLOCKS, 0, 0, tiled=True)  22.3 us
    ppermute x3, waiting for transfers between devices, from_neighbour(): return lax.ppermute(mine, ('zl', 'core', 'y'), neighbour_route())  15 us
    pallas_call x10, Pallas kernels, call(): pl.pallas_call(body, out_shape=list(outs), in_specs=specs, out_specs=out_...  11.5 us
    ppermute x3, starting transfers between devices, swap(): return lax.ppermute(mine, 'core', [(0, 1), (1, 0)])  7.16 us
    unnamed x12, local copies, waits for them, and re-layouts  5.62 us
    ppermute x3, waiting for transfers between devices, swap(): return lax.ppermute(mine, 'core', [(0, 1), (1, 0)])  4.47 us
  transfers between devices with their start and end apart: 8, of which 6 were waited for; matrix products, arithmetic and copies ran while one was open for 0% of the time, Pallas kernels for 3%

profile of v11, /device:TPU:1, one launch (start us, length us, event | category | flops | bytes accessed | tf_op | source)
XLA Modules:
  0.0 146.4 jit_solution(16274642813779362264)
XLA Ops:
  0.0 0.9 copy-done.2
  1.0 0.7 collective-permute-start
  1.7 0.7 collective-permute-start.1
  2.4 0.9 copy-done.3
  3.3 0.9 copy-done.4
  4.2 0.9 copy-done.5
  5.1 0.2 shard_map.47.base_ref
  5.4 50.0 %all_to_all.15 = f32[64,9,2,128]{3,2,1,0:T(2,128)S(1)} all-to-all(f32[64,9,2,128]{3,2,1,0:T(2,128)S(1)} %shard_map.48), channel_id=1, replica_groups=mesh['x'=4,'zh'=2,'zl'=4,'core'=2,'y'=4,'zhi'=2] {'zl','core','y','zhi'}, dimensions={0} | all-to-all | bytes 1179648 | tf_op jit(solution)/shard_map/all_to_all | solution.py:411
  55.4 2.6 %collective-permute-start.2 = (f32[8,8,9,2,128]{4,3,2,1,0:T(2,128)S(1)}, f32[8,8,9,2,128]{4,3,2,1,0:T(2,128)S(1)}, u32[]{:S(2)}, u32[]{:S(2)}) collective-permute-start(f32[8,8,9,2,128]{4,3,2,1,0:T(2,128)S(1)} %bitcast.8), channel_id=1, source_target_pairs={{0,8},{8,0},{1,9},{9,1},{2,10},{10,2},{3,11},{11,3},{4,12},{12,4},... | collective-permute-start | bytes 1769480 | tf_op jit(solution)/shard_map/ppermute | solution.py:414
  58.0 1.6 %collective-permute-done.2.other_ref = f32[8,8,9,2,128]{4,3,2,1,0:T(2,128)S(1)} collective-permute-done((f32[8,8,9,2,128]{4,3,2,1,0:T(2,128)S(1)}, f32[8,8,9,2,128]{4,3,2,1,0:T(2,128)S(1)}, u32[]{:S(2)}, u32[]{:S(2)}) %collective-permute-start.2) | collective-permute-done | bytes 589856 | tf_op jit(solution)/shard_map/ppermute | solution.py:414
  59.6 0.3 shard_map.49
  59.9 1.3 collective-permute-start.3
  61.2 3.1 %shard_map.50 = (f32[7,16,40,128]{3,2,1,0:T(8,128)S(1)}, f32[7,16,40,128]{3,2,1,0:T(8,128)S(1)}) custom-call(f32[16,40,128]{2,1,0:T(8,128)S(1)} %get-tuple-element.26.k_ref), custom_call_target="tpu_custom_call" | custom-call | flops 7372800 | bytes 4915200 | tf_op jit(solution)/shard_map/pallas_call | solution.py:57
  64.2 4.1 %collective-permute-done.3.got_ref = f32[4,8,24,128]{3,2,1,0:T(8,128)S(1)} collective-permute-done((f32[4,8,24,128]{3,2,1,0:T(8,128)S(1)}, f32[4,8,24,128]{3,2,1,0:T(8,128)S(1)}, u32[]{:S(2)}, u32[]{:S(2)}) %collective-permute-start.3) | collective-permute-done | bytes 393248 | tf_op jit(solution)/shard_map/ppermute | solution.py:417
  68.4 1.9 %collective-permute-start.4 = (f32[4,8,24,128]{3,2,1,0:T(8,128)S(1)}, f32[4,8,24,128]{3,2,1,0:T(8,128)S(1)}, u32[]{:S(2)}, u32[]{:S(2)}) collective-permute-start(f32[4,8,24,128]{3,2,1,0:T(8,128)S(1)} %collective-permute-done.3.got_ref), channel_id=1, source_target_pairs={{0,8},{8,0},{1,9},{9,1},{2,10},{10,2},{3,11},{11,3},{4,12},{12,4},... | collective-permute-start | bytes 1179656 | tf_op jit(solution)/shard_map/ppermute | solution.py:414
  70.3 1.7 %collective-permute-done.4.got2_ref = f32[4,8,24,128]{3,2,1,0:T(8,128)S(1)} collective-permute-done((f32[4,8,24,128]{3,2,1,0:T(8,128)S(1)}, f32[4,8,24,128]{3,2,1,0:T(8,128)S(1)}, u32[]{:S(2)}, u32[]{:S(2)}) %collective-permute-start.4) | collective-permute-done | bytes 393248 | tf_op jit(solution)/shard_map/ppermute | solution.py:414
  72.0 3.1 %shard_map.51 = (f32[6,16,12,128]{3,2,1,0:T(8,128)S(1)}, f32[3,8,24,128]{3,2,1,0:T(8,128)S(1)}) custom-call(s32[1]{0:T(128)} %bitcast.core_ref, f32[7,16,40,128]{3,2,1,0:T(8,128)S(1)} %get-tuple-element.30.co_s.fine_s, f32[8,16,12,128]{3,2,1,0:T(8,128)S(1)} %get-tuple-element.31.f_ref, f32[1,8,24,128]{3,2,1,0:T(8,128)S(1)} %get-tuple-element.32.own_ref, ...), custom_call_target="tpu_custom_call" | custom-call | flops 14745600 | bytes 4849668 | tf_op jit(solution)/shard_map/pallas_call | solution.py:57
  75.1 1.3 collective-permute-start.5
  76.4 0.5 shard_map.52.start_ref
  76.9 6.0 %collective-permute-done.5.got_ref = f32[3,8,24,128]{3,2,1,0:T(8,128)S(1)} collective-permute-done((f32[3,8,24,128]{3,2,1,0:T(8,128)S(1)}, f32[3,8,24,128]{3,2,1,0:T(8,128)S(1)}, u32[]{:S(2)}, u32[]{:S(2)}) %collective-permute-start.5) | collective-permute-done | bytes 294944 | tf_op jit(solution)/shard_map/ppermute | solution.py:417
  82.9 2.7 %collective-permute-start.6 = (f32[3,8,24,128]{3,2,1,0:T(8,128)S(1)}, f32[3,8,24,128]{3,2,1,0:T(8,128)S(1)}, u32[]{:S(2)}, u32[]{:S(2)}) collective-permute-start(f32[3,8,24,128]{3,2,1,0:T(8,128)S(1)} %collective-permute-done.5.got_ref), channel_id=1, source_target_pairs={{0,8},{8,0},{1,9},{9,1},{2,10},{10,2},{3,11},{11,3},{4,12},{12,4},... | collective-permute-start | bytes 884744 | tf_op jit(solution)/shard_map/ppermute | solution.py:414
  85.6 1.2 collective-permute-done.6.got2_ref
  86.8 2.6 %shard_map.53 = (f32[16,12,128]{2,1,0:T(8,128)S(1)}, f32[5,16,12,128]{3,2,1,0:T(8,128)S(1)}, f32[1,8,24,128]{3,2,1,0:T(8,128)S(1)}) custom-call(s32[1]{0:T(128)} %bitcast.core_ref, f32[7,16,40,128]{3,2,1,0:T(8,128)S(1)} %get-tuple-element.30.co_s.fine_s, f32[7,16,40,128]{3,2,1,0:T(8,128)S(1)} %get-tuple-element.29.co_s, ...), custom_call_target="tpu_custom_call" | custom-call | flops 14745600 | bytes 6488068 | tf_op jit(solution)/shard_map/pallas_call | solution.py:57
  89.3 0.8 copy-done
  90.2 1.3 collective-permute-start.7
  91.5 4.8 %collective-permute-done.7.got_ref = f32[1,8,24,128]{3,2,1,0:T(8,128)S(1)} collective-permute-done((f32[1,8,24,128]{3,2,1,0:T(8,128)S(1)}, f32[1,8,24,128]{3,2,1,0:T(8,128)S(1)}, u32[]{:S(2)}, u32[]{:S(2)}) %collective-permute-start.7) | collective-permute-done | bytes 98336 | tf_op jit(solution)/shard_map/ppermute | solution.py:417
  96.3 1.1 copy-done.1
  97.4 1.0 shard_map.54
  98.3 22.3 %all_to_all.16.got_ref = f32[8,48,128]{2,1,0:T(8,128)S(1)} all-to-all(f32[8,48,128]{2,1,0:T(8,128)S(1)} %shard_map.54), channel_id=1, replica_groups=mesh['x'=4,'zh'=2,'zl'=4,'core'=2,'y'=4,'zhi'=2] {'x','zh'}, dimensions={0} | all-to-all | bytes 393216 | tf_op jit(solution)/shard_map/all_to_all | solution.py:455
  120.7 0.1 shard_map.55
  120.7 25.0 %all_to_all.17.got_ref = f32[32,16,128]{2,1,0:T(8,128)S(1)} all-to-all(f32[32,16,128]{2,1,0:T(8,128)S(1)} %shard_map.55), channel_id=1, replica_groups=mesh['x'=4,'zh'=2,'zl'=4,'core'=2,'y'=4,'zhi'=2] {'zl','core','y'}, dimensions={0} | all-to-all | bytes 524288 | tf_op jit(solution)/shard_map/all_to_all | solution.py:457
  145.7 0.7 shard_map.56
  (10 shorter events, 0.1 us)
Async XLA Ops:
  0.0 0.9 copy-start.2
  1.0 4.3 %collective-permute-start = (f32[2,16,3,2,128]{4,3,2,1,0:T(2,128)S(1)}, f32[2,16,3,2,128]{4,3,2,1,0:T(2,128)S(1)}, u32[]{:S(2)}, u32[]{:S(2)}) collective-permute-start(f32[2,16,3,2,128]{4,3,2,1,0:T(2,128)S(1)} %get-tuple-element.23), channel_id=1, source_target_pairs={{56,64},{57,65},{58,66},{59,67},{60,68},{61,69},{62,70},{63,71},{1... | collective-permute-start | bytes 294920 | tf_op jit(solution)/shard_map/ppermute | solution.py:396
  1.7 3.7 %collective-permute-start.1 = (f32[2,16,3,2,128]{4,3,2,1,0:T(2,128)S(1)}, f32[2,16,3,2,128]{4,3,2,1,0:T(2,128)S(1)}, u32[]{:S(2)}, u32[]{:S(2)}) collective-permute-start(f32[2,16,3,2,128]{4,3,2,1,0:T(2,128)S(1)} %get-tuple-element.24), channel_id=1, source_target_pairs={{56,72},{57,73},{58,74},{59,75},{60,76},{61,77},{62,78},{63,79},{1... | collective-permute-start | bytes 294920 | tf_op jit(solution)/shard_map/ppermute | solution.py:396
  2.3 0.9 copy-start.3
  3.3 0.9 copy-start.4
  4.2 0.9 copy-start.5
  55.4 4.2 %collective-permute-start.2 = (f32[8,8,9,2,128]{4,3,2,1,0:T(2,128)S(1)}, f32[8,8,9,2,128]{4,3,2,1,0:T(2,128)S(1)}, u32[]{:S(2)}, u32[]{:S(2)}) collective-permute-start(f32[8,8,9,2,128]{4,3,2,1,0:T(2,128)S(1)} %bitcast.8), channel_id=1, source_target_pairs={{0,8},{8,0},{1,9},{9,1},{2,10},{10,2},{3,11},{11,3},{4,12},{12,4},... | collective-permute-start | bytes 1769480 | tf_op jit(solution)/shard_map/ppermute | solution.py:414
  59.9 8.5 %collective-permute-start.3 = (f32[4,8,24,128]{3,2,1,0:T(8,128)S(1)}, f32[4,8,24,128]{3,2,1,0:T(8,128)S(1)}, u32[]{:S(2)}, u32[]{:S(2)}) collective-permute-start(f32[4,8,24,128]{3,2,1,0:T(8,128)S(1)} %get-tuple-element.25), channel_id=1, source_target_pairs={{0,2},{2,4},{4,6},{6,22},{22,20},{20,18},{18,16},{16,32},{32,34},{... | collective-permute-start | bytes 1179656 | tf_op jit(solution)/shard_map/ppermute | solution.py:417
  68.4 3.6 %collective-permute-start.4 = (f32[4,8,24,128]{3,2,1,0:T(8,128)S(1)}, f32[4,8,24,128]{3,2,1,0:T(8,128)S(1)}, u32[]{:S(2)}, u32[]{:S(2)}) collective-permute-start(f32[4,8,24,128]{3,2,1,0:T(8,128)S(1)} %collective-permute-done.3.got_ref), channel_id=1, source_target_pairs={{0,8},{8,0},{1,9},{9,1},{2,10},{10,2},{3,11},{11,3},{4,12},{12,4},... | collective-permute-start | bytes 1179656 | tf_op jit(solution)/shard_map/ppermute | solution.py:414
  75.1 7.8 %collective-permute-start.5 = (f32[3,8,24,128]{3,2,1,0:T(8,128)S(1)}, f32[3,8,24,128]{3,2,1,0:T(8,128)S(1)}, u32[]{:S(2)}, u32[]{:S(2)}) collective-permute-start(f32[3,8,24,128]{3,2,1,0:T(8,128)S(1)} %get-tuple-element.34.own_ref), channel_id=1, source_target_pairs={{0,2},{2,4},{4,6},{6,22},{22,20},{20,18},{18,16},{16,32},{32,34},{... | collective-permute-start | bytes 884744 | tf_op jit(solution)/shard_map/ppermute | solution.py:417
  82.9 3.9 %collective-permute-start.6 = (f32[3,8,24,128]{3,2,1,0:T(8,128)S(1)}, f32[3,8,24,128]{3,2,1,0:T(8,128)S(1)}, u32[]{:S(2)}, u32[]{:S(2)}) collective-permute-start(f32[3,8,24,128]{3,2,1,0:T(8,128)S(1)} %collective-permute-done.5.got_ref), channel_id=1, source_target_pairs={{0,8},{8,0},{1,9},{9,1},{2,10},{10,2},{3,11},{11,3},{4,12},{12,4},... | collective-permute-start | bytes 884744 | tf_op jit(solution)/shard_map/ppermute | solution.py:414
  89.3 0.8 copy-start
  90.2 6.1 %collective-permute-start.7 = (f32[1,8,24,128]{3,2,1,0:T(8,128)S(1)}, f32[1,8,24,128]{3,2,1,0:T(8,128)S(1)}, u32[]{:S(2)}, u32[]{:S(2)}) collective-permute-start(f32[1,8,24,128]{3,2,1,0:T(8,128)S(1)} %get-tuple-element.37.own_ref), channel_id=1, source_target_pairs={{0,2},{2,4},{4,6},{6,22},{22,20},{20,18},{18,16},{16,32},{32,34},{... | collective-permute-start | bytes 294920 | tf_op jit(solution)/shard_map/ppermute | solution.py:417
  96.3 1.1 copy-start.1

commit v12 on v11

--- a/solution.py
+++ b/solution.py
@@ -286,8 +286,8 @@
 
 
 def late_body(
-    core_ref, fine_s, co_s, own_ref, got_ref, got2_ref, start_ref,
-    out_ref, pow_ref, next_ref, a_s, b_s, db_s, f_s,
+    core_ref, side_ref, fine_s, co_s, own_ref, got_ref, got2_ref, start_ref,
+    out_ref, pow_ref, next_ref, a_s, b_s, db_s, f_s, pow_s,
 ):
     clear_ends(a_s, b_s)
     load_window(core_ref, a_s, 0, own_ref, got_ref, got2_ref)
@@ -303,13 +303,19 @@
         if n > 0:
             step(10 - 2 * n, a_s, b_s, co_s, db_s)
         for z in range(NZ):
-            pow_ref[n, z] = a_s[z + 1, OWN:HIGH]
+            pow_s[n, z] = a_s[z + 1, OWN:HIGH]
     for z in range(NZ):
         next_ref[0, z // 2, at(z, 0, STRIP)] = a_s[z + 1, OWN:HIGH]
 
+    def send(m, z, rows):
+        for n in range(5):
+            pow_ref[n, m * HALF : (m + 1) * HALF] = pow_s[n, z, rows]
+
+    cut(core_ref, side_ref, send)
+
 
 def powers_body(
-    core_ref, side_ref, block_ref, co_s, own_ref, got_ref, early_ref, out_ref, a_s, b_s, db_s, pow_s
+    core_ref, side_ref, block_ref, co_s, own_ref, got_ref, early_ref, out_ref, a_s, b_s, db_s, pow_s, late_s
 ):
     clear_ends(a_s, b_s)
     for z in range(NZ):
@@ -323,24 +329,29 @@
     pl.when(core_ref[0] == 0)(functools.partial(halo, slice(LOW, OWN)))
     pl.when(core_ref[0] == 1)(functools.partial(halo, slice(HIGH, WIN)))
     for n in range(5):
-        for z in range(NZ):
-            pow_s[n, z] = early_ref[n, z]
+        pow_s[n] = early_ref[n]
     for n in range(3):
         step(6 - 2 * n, a_s, b_s, co_s, db_s)
         for z in range(NZ):
-            pow_s[5 + n, z] = a_s[z + 1, OWN:HIGH]
-    c = block_ref[0]
-
-    def send(rows):
-        for b in range(NB):
-            power = jnp.clip(b - c, 0, NB - 1)
-            live = b >= c
-            for n, (y, p) in enumerate(LAYERS):
-                value = pow_s[power, 2 * (2 * y + side_ref[0]) + p, rows]
-                out_ref[b, n * HALF : (n + 1) * HALF] = jnp.where(live, value, 0.0)
+            late_s[n, z] = a_s[z + 1, OWN:HIGH]
+
+    def send(m, z, rows):
+        for n in range(3):
+            pow_s[5 + n, m * HALF : (m + 1) * HALF] = late_s[n, z, rows]
+
+    cut(core_ref, side_ref, send)
+    for b in range(NB):
+        power = jnp.clip(b - block_ref[0], 0, NB - 1)
+        out_ref[b] = jnp.where(b >= block_ref[0], pow_s[power], 0.0)
+
+
+def cut(core_ref, side_ref, body):
+    def each(rows):
+        for n, (y, p) in enumerate(LAYERS):
+            body(n, 2 * (2 * y + side_ref[0]) + p, rows)
 
     for core in range(2):
-        pl.when(core_ref[0] == core)(functools.partial(send, slice(core * HALF, (core + 1) * HALF)))
+        pl.when(core_ref[0] == core)(functools.partial(each, slice(core * HALF, (core + 1) * HALF)))
 
 
 SWEEP_SCRATCH = (
@@ -351,31 +362,27 @@
 
 
 def collect_body(core_ref, side_ref, got_ref, early_ref, late_ref, out_ref):
-    def fill(rows):
-        for n, (y, p) in enumerate(LAYERS):
-            z = 2 * (2 * y + side_ref[0]) + p
-            mine, to = slice(n * HALF, (n + 1) * HALF), slice(p * HALF, (p + 1) * HALF)
-            total = got_ref[0, mine]
-            for b in range(1, NB):
-                total = total + got_ref[b, mine]
-            out_ref[7 * 4 + y, to] = total
-            for t in range(6):
-                out_ref[t * 4 + y, to] = early_ref[t, z, rows]
-            out_ref[6 * 4 + y, to] = late_ref[z, rows]
-
-    for core in range(2):
-        pl.when(core_ref[0] == core)(functools.partial(fill, slice(core * HALF, (core + 1) * HALF)))
-    for n in range(32):
-        out_ref[n, STRIP:16] = jnp.zeros((16 - STRIP, LANES), F32)
+    def fill(n, z, rows):
+        y, p = LAYERS[n]
+        total = got_ref[0, n * HALF : (n + 1) * HALF]
+        for b in range(1, NB):
+            total = total + got_ref[b, n * HALF : (n + 1) * HALF]
+        states = [early_ref[t, z, rows] for t in range(6)] + [late_ref[z, rows], total]
+        for t in range(8):
+            for r in range(3):
+                out_ref[t * 4 + y, 3 * p + r] = states[t][2 * r : 2 * r + 2]
+
+    cut(core_ref, side_ref, fill)
 
 
 def home_body(got_ref, out_ref):
     for zl in range(4):
         for y in range(4):
             for core in range(2):
-                row = chip_order(zl, y) * STRIP + core * HALF
                 for p in range(2):
-                    out_ref[p, row : row + HALF] = got_ref[(zl * 2 + core) * 4 + y, p * HALF : (p + 1) * HALF]
+                    for r in range(3):
+                        row = chip_order(zl, y) * STRIP + core * HALF + 2 * r
+                        out_ref[p, row : row + 2] = got_ref[(zl * 2 + core) * 4 + y, 3 * p + r]
 
 
 def on_device(guess, source, diffusivity, initial):
@@ -443,17 +450,17 @@
     )
     state_got, state_got2, start_g = exchange(state, start_g)
     v_late, first_powers, last = call(
-        late_body, [sds(NZ, STRIP, LANES), sds(5, NZ, STRIP, LANES), sds(1, 8, PAIR, LANES)],
-        core, fine, coarse, state, state_got, state_got2, start_g, smem=1, flops=12 * flops,
-        scratch=SWEEP_SCRATCH + (pltpu.VMEM((NZ + 2, WIN, LANES), F32),),
+        late_body, [sds(NZ, STRIP, LANES), sds(5, 8 * HALF, LANES), sds(1, 8, PAIR, LANES)],
+        core, side, fine, coarse, state, state_got, state_got2, start_g, smem=2, flops=12 * flops,
+        scratch=SWEEP_SCRATCH + (pltpu.VMEM((NZ + 2, WIN, LANES), F32), pltpu.VMEM((5, NZ, STRIP, LANES), F32)),
     )
     (powers,) = call(
-        powers_body, [sds(NB, 4 * STRIP, LANES)],
+        powers_body, [sds(NB, 8 * HALF, LANES)],
         core, side, block, coarse, last, from_neighbour(last), first_powers, smem=3, flops=6 * flops,
-        scratch=SWEEP_SCRATCH + (pltpu.VMEM((NB, NZ, STRIP, LANES), F32),),
+        scratch=SWEEP_SCRATCH + (pltpu.VMEM((NB, 8 * HALF, LANES), F32), pltpu.VMEM((3, NZ, STRIP, LANES), F32)),
     )
     arrived = lax.all_to_all(powers, BLOCKS, 0, 0, tiled=True)
-    (back,) = call(collect_body, [sds(32, 16, LANES)], core, side, arrived, v_early, v_late, smem=2)
+    (back,) = call(collect_body, [sds(32, 6, 2, LANES)], core, side, arrived, v_early, v_late, smem=2)
     returned = lax.all_to_all(back, ("zl", "core", "y"), 0, 0, tiled=True)
     (result,) = call(home_body, [sds(2, NY, LANES)], returned)
     return result[None]

time: 147 us -> 149 us (1.014)
  local copies, waits for them, and re-layouts: 5.62 us -> 7.72 us
  blocking collectives: 97.3 us -> 95.7 us
    unnamed x12 -> x16, local copies, waits for them, and re-layouts: 5.62 us -> 7.72 us
    all_to_all x1, blocking collectives: 25 us -> 23.3 us  [on_device(): returned = lax.all_to_all(back, ('zl', 'core', 'y'), 0, 0, tiled=True)]
where the time goes in v12:
time: 149 us; the launch traced here: 148 us
  blocking collectives  95.7 us (64%)
  waiting for transfers between devices  20 us (13%)
  Pallas kernels  12.6 us (8%)
  starting transfers between devices  12.3 us (8%)
  local copies, waits for them, and re-layouts  7.72 us (5%)
    all_to_all x1, blocking collectives, on_device(): lax.all_to_all(sent, BLOCK, 0, 0, tiled=True).reshape(8, 8, 9, 2, LANES)  50 us
    all_to_all x1, blocking collectives, on_device(): returned = lax.all_to_all(back, ('zl', 'core', 'y'), 0, 0, tiled=True)  23.3 us
    all_to_all x1, blocking collectives, on_device(): arrived = lax.all_to_all(powers, BLOCKS, 0, 0, tiled=True)  22.3 us
    ppermute x3, waiting for transfers between devices, from_neighbour(): return lax.ppermute(mine, ('zl', 'core', 'y'), neighbour_route())  15.2 us
    pallas_call x10, Pallas kernels, call(): pl.pallas_call(body, out_shape=list(outs), in_specs=specs, out_specs=out_...  12.6 us
    unnamed x16, local copies, waits for them, and re-layouts  7.72 us
    ppermute x3, starting transfers between devices, swap(): return lax.ppermute(mine, 'core', [(0, 1), (1, 0)])  7.06 us
    ppermute x3, waiting for transfers between devices, swap(): return lax.ppermute(mine, 'core', [(0, 1), (1, 0)])  4.81 us
  transfers between devices with their start and end apart: 8, of which 6 were waited for; matrix products, arithmetic and copies ran while one was open for 0% of the time, Pallas kernels for 3%

profile of v12, /device:TPU:1, one launch (start us, length us, event | category | flops | bytes accessed | tf_op | source)
XLA Modules:
  0.0 148.4 jit_solution(3713426020766202645)
XLA Ops:
  0.0 0.9 copy-done.4
  1.0 0.7 collective-permute-start
  1.7 0.7 collective-permute-start.1
  2.4 0.9 copy-done.5
  3.3 0.9 copy-done.6
  4.2 0.9 copy-done.7
  5.1 0.2 shard_map.47.base_ref
  5.4 50.0 %all_to_all.15 = f32[64,9,2,128]{3,2,1,0:T(2,128)S(1)} all-to-all(f32[64,9,2,128]{3,2,1,0:T(2,128)S(1)} %shard_map.48), channel_id=1, replica_groups=mesh['x'=4,'zh'=2,'zl'=4,'core'=2,'y'=4,'zhi'=2] {'zl','core','y','zhi'}, dimensions={0} | all-to-all | bytes 1179648 | tf_op jit(solution)/shard_map/all_to_all | solution.py:418
  55.4 2.6 %collective-permute-start.2 = (f32[8,8,9,2,128]{4,3,2,1,0:T(2,128)S(1)}, f32[8,8,9,2,128]{4,3,2,1,0:T(2,128)S(1)}, u32[]{:S(2)}, u32[]{:S(2)}) collective-permute-start(f32[8,8,9,2,128]{4,3,2,1,0:T(2,128)S(1)} %bitcast.8), channel_id=1, source_target_pairs={{0,8},{8,0},{1,9},{9,1},{2,10},{10,2},{3,11},{11,3},{4,12},{12,4},... | collective-permute-start | bytes 1769480 | tf_op jit(solution)/shard_map/ppermute | solution.py:421
  58.0 1.6 %collective-permute-done.2.other_ref = f32[8,8,9,2,128]{4,3,2,1,0:T(2,128)S(1)} collective-permute-done((f32[8,8,9,2,128]{4,3,2,1,0:T(2,128)S(1)}, f32[8,8,9,2,128]{4,3,2,1,0:T(2,128)S(1)}, u32[]{:S(2)}, u32[]{:S(2)}) %collective-permute-start.2) | collective-permute-done | bytes 589856 | tf_op jit(solution)/shard_map/ppermute | solution.py:421
  59.6 0.3 shard_map.49
  59.9 1.3 collective-permute-start.3
  61.2 3.1 %shard_map.50 = (f32[7,16,40,128]{3,2,1,0:T(8,128)S(1)}, f32[7,16,40,128]{3,2,1,0:T(8,128)S(1)}) custom-call(f32[16,40,128]{2,1,0:T(8,128)S(1)} %get-tuple-element.26.k_ref), custom_call_target="tpu_custom_call" | custom-call | flops 7372800 | bytes 4915200 | tf_op jit(solution)/shard_map/pallas_call | solution.py:57
  64.2 4.1 %collective-permute-done.3.got_ref = f32[4,8,24,128]{3,2,1,0:T(8,128)S(1)} collective-permute-done((f32[4,8,24,128]{3,2,1,0:T(8,128)S(1)}, f32[4,8,24,128]{3,2,1,0:T(8,128)S(1)}, u32[]{:S(2)}, u32[]{:S(2)}) %collective-permute-start.3) | collective-permute-done | bytes 393248 | tf_op jit(solution)/shard_map/ppermute | solution.py:424
  68.4 1.9 %collective-permute-start.4 = (f32[4,8,24,128]{3,2,1,0:T(8,128)S(1)}, f32[4,8,24,128]{3,2,1,0:T(8,128)S(1)}, u32[]{:S(2)}, u32[]{:S(2)}) collective-permute-start(f32[4,8,24,128]{3,2,1,0:T(8,128)S(1)} %collective-permute-done.3.got_ref), channel_id=1, source_target_pairs={{0,8},{8,0},{1,9},{9,1},{2,10},{10,2},{3,11},{11,3},{4,12},{12,4},... | collective-permute-start | bytes 1179656 | tf_op jit(solution)/shard_map/ppermute | solution.py:421
  70.3 1.7 %collective-permute-done.4.got2_ref = f32[4,8,24,128]{3,2,1,0:T(8,128)S(1)} collective-permute-done((f32[4,8,24,128]{3,2,1,0:T(8,128)S(1)}, f32[4,8,24,128]{3,2,1,0:T(8,128)S(1)}, u32[]{:S(2)}, u32[]{:S(2)}) %collective-permute-start.4) | collective-permute-done | bytes 393248 | tf_op jit(solution)/shard_map/ppermute | solution.py:421
  72.0 3.1 %shard_map.51 = (f32[6,16,12,128]{3,2,1,0:T(8,128)S(1)}, f32[3,8,24,128]{3,2,1,0:T(8,128)S(1)}) custom-call(s32[1]{0:T(128)} %bitcast.core_ref, f32[7,16,40,128]{3,2,1,0:T(8,128)S(1)} %get-tuple-element.30.co_s.fine_s, f32[8,16,12,128]{3,2,1,0:T(8,128)S(1)} %get-tuple-element.31.f_ref, f32[1,8,24,128]{3,2,1,0:T(8,128)S(1)} %get-tuple-element.32.own_ref, ...), custom_call_target="tpu_custom_call" | custom-call | flops 14745600 | bytes 4849668 | tf_op jit(solution)/shard_map/pallas_call | solution.py:57
  75.1 1.4 copy-done
  76.5 1.3 collective-permute-start.5
  77.8 0.5 shard_map.52.start_ref
  78.3 6.1 %collective-permute-done.5.got_ref = f32[3,8,24,128]{3,2,1,0:T(8,128)} collective-permute-done((f32[3,8,24,128]{3,2,1,0:T(8,128)S(1)}, f32[3,8,24,128]{3,2,1,0:T(8,128)}, u32[]{:S(2)}, u32[]{:S(2)}) %collective-permute-start.5) | collective-permute-done | bytes 294944 | tf_op jit(solution)/shard_map/ppermute | solution.py:424
  84.4 2.6 %collective-permute-start.6 = (f32[3,8,24,128]{3,2,1,0:T(8,128)}, f32[3,8,24,128]{3,2,1,0:T(8,128)}, u32[]{:S(2)}, u32[]{:S(2)}) collective-permute-start(f32[3,8,24,128]{3,2,1,0:T(8,128)} %collective-permute-done.5.got_ref), channel_id=1, source_target_pairs={{0,8},{8,0},{1,9},{9,1},{2,10},{10,2},{3,11},{11,3},{4,12},{12,4},... | collective-permute-start | bytes 884744 | tf_op jit(solution)/shard_map/ppermute | solution.py:421
  87.0 1.5 %collective-permute-done.6.got2_ref = f32[3,8,24,128]{3,2,1,0:T(8,128)} collective-permute-done((f32[3,8,24,128]{3,2,1,0:T(8,128)}, f32[3,8,24,128]{3,2,1,0:T(8,128)}, u32[]{:S(2)}, u32[]{:S(2)}) %collective-permute-start.6) | collective-permute-done | bytes 294944 | tf_op jit(solution)/shard_map/ppermute | solution.py:421
  88.5 1.6 %copy-done.1 = f32[7,16,40,128]{3,2,1,0:T(8,128)S(1)} copy-done((f32[7,16,40,128]{3,2,1,0:T(8,128)S(1)}, f32[7,16,40,128]{3,2,1,0:T(8,128)}, u32[]{:S(2)}) %copy-start.1) | copy-done | bytes 2293784
  90.2 1.0 copy-done.3
  91.1 3.7 %shard_map.53 = (f32[16,12,128]{2,1,0:T(8,128)S(1)}, f32[5,48,128]{2,1,0:T(8,128)S(1)}, f32[1,8,24,128]{3,2,1,0:T(8,128)S(1)}) custom-call(s32[1]{0:T(128)} %bitcast.core_ref, s32[1]{0:T(128)} %bitcast.1.side_ref, f32[7,16,40,128]{3,2,1,0:T(8,128)S(1)} %copy-done.1, f32[7,16,40,128]{3,2,1,0:T(8,128)S(1)} %get-tuple-element.29.co_s, ...), custom_call_target="tpu_custom_call" | custom-call | flops 14745600 | bytes 6119432 | tf_op jit(solution)/shard_map/pallas_call | solution.py:57
  94.8 1.3 collective-permute-start.7
  96.1 4.9 %collective-permute-done.7.got_ref = f32[1,8,24,128]{3,2,1,0:T(8,128)S(1)} collective-permute-done((f32[1,8,24,128]{3,2,1,0:T(8,128)S(1)}, f32[1,8,24,128]{3,2,1,0:T(8,128)S(1)}, u32[]{:S(2)}, u32[]{:S(2)}) %collective-permute-start.7) | collective-permute-done | bytes 98336 | tf_op jit(solution)/shard_map/ppermute | solution.py:424
  101.0 0.9 shard_map.54
  102.0 22.3 %all_to_all.16.got_ref = f32[8,48,128]{2,1,0:T(8,128)S(1)} all-to-all(f32[8,48,128]{2,1,0:T(8,128)S(1)} %shard_map.54), channel_id=1, replica_groups=mesh['x'=4,'zh'=2,'zl'=4,'core'=2,'y'=4,'zhi'=2] {'x','zh'}, dimensions={0} | all-to-all | bytes 393216 | tf_op jit(solution)/shard_map/all_to_all | solution.py:462
  124.4 23.3 %all_to_all.17.got_ref = f32[32,6,2,128]{3,2,1,0:T(2,128)S(1)} all-to-all(f32[32,6,2,128]{3,2,1,0:T(2,128)S(1)} %shard_map.55), channel_id=1, replica_groups=mesh['x'=4,'zh'=2,'zl'=4,'core'=2,'y'=4,'zhi'=2] {'zl','core','y'}, dimensions={0} | all-to-all | bytes 393216 | tf_op jit(solution)/shard_map/all_to_all | solution.py:464
  147.7 0.7 shard_map.56
  (14 shorter events, 0.1 us)
Async XLA Ops:
  0.0 0.9 copy-start.4
  1.0 4.3 %collective-permute-start = (f32[2,16,3,2,128]{4,3,2,1,0:T(2,128)S(1)}, f32[2,16,3,2,128]{4,3,2,1,0:T(2,128)S(1)}, u32[]{:S(2)}, u32[]{:S(2)}) collective-permute-start(f32[2,16,3,2,128]{4,3,2,1,0:T(2,128)S(1)} %get-tuple-element.23), channel_id=1, source_target_pairs={{56,64},{57,65},{58,66},{59,67},{60,68},{61,69},{62,70},{63,71},{1... | collective-permute-start | bytes 294920 | tf_op jit(solution)/shard_map/ppermute | solution.py:403
  1.7 3.7 %collective-permute-start.1 = (f32[2,16,3,2,128]{4,3,2,1,0:T(2,128)S(1)}, f32[2,16,3,2,128]{4,3,2,1,0:T(2,128)S(1)}, u32[]{:S(2)}, u32[]{:S(2)}) collective-permute-start(f32[2,16,3,2,128]{4,3,2,1,0:T(2,128)S(1)} %get-tuple-element.24), channel_id=1, source_target_pairs={{56,72},{57,73},{58,74},{59,75},{60,76},{61,77},{62,78},{63,79},{1... | collective-permute-start | bytes 294920 | tf_op jit(solution)/shard_map/ppermute | solution.py:403
  2.3 0.9 copy-start.5
  3.3 0.9 copy-start.6
  4.2 0.9 copy-start.7
  55.4 4.2 %collective-permute-start.2 = (f32[8,8,9,2,128]{4,3,2,1,0:T(2,128)S(1)}, f32[8,8,9,2,128]{4,3,2,1,0:T(2,128)S(1)}, u32[]{:S(2)}, u32[]{:S(2)}) collective-permute-start(f32[8,8,9,2,128]{4,3,2,1,0:T(2,128)S(1)} %bitcast.8), channel_id=1, source_target_pairs={{0,8},{8,0},{1,9},{9,1},{2,10},{10,2},{3,11},{11,3},{4,12},{12,4},... | collective-permute-start | bytes 1769480 | tf_op jit(solution)/shard_map/ppermute | solution.py:421
  59.9 8.5 %collective-permute-start.3 = (f32[4,8,24,128]{3,2,1,0:T(8,128)S(1)}, f32[4,8,24,128]{3,2,1,0:T(8,128)S(1)}, u32[]{:S(2)}, u32[]{:S(2)}) collective-permute-start(f32[4,8,24,128]{3,2,1,0:T(8,128)S(1)} %get-tuple-element.25), channel_id=1, source_target_pairs={{0,2},{2,4},{4,6},{6,22},{22,20},{20,18},{18,16},{16,32},{32,34},{... | collective-permute-start | bytes 1179656 | tf_op jit(solution)/shard_map/ppermute | solution.py:424
  68.4 3.6 %collective-permute-start.4 = (f32[4,8,24,128]{3,2,1,0:T(8,128)S(1)}, f32[4,8,24,128]{3,2,1,0:T(8,128)S(1)}, u32[]{:S(2)}, u32[]{:S(2)}) collective-permute-start(f32[4,8,24,128]{3,2,1,0:T(8,128)S(1)} %collective-permute-done.3.got_ref), channel_id=1, source_target_pairs={{0,8},{8,0},{1,9},{9,1},{2,10},{10,2},{3,11},{11,3},{4,12},{12,4},... | collective-permute-start | bytes 1179656 | tf_op jit(solution)/shard_map/ppermute | solution.py:421
  75.1 1.4 copy-start
  76.5 1.8 %copy-start.2 = (f32[3,8,24,128]{3,2,1,0:T(8,128)}, f32[3,8,24,128]{3,2,1,0:T(8,128)S(1)}, u32[]{:S(2)}) copy-start(f32[3,8,24,128]{3,2,1,0:T(8,128)S(1)} %get-tuple-element.34.own_ref) | copy-start | bytes 884740
  76.5 7.9 %collective-permute-start.5 = (f32[3,8,24,128]{3,2,1,0:T(8,128)S(1)}, f32[3,8,24,128]{3,2,1,0:T(8,128)}, u32[]{:S(2)}, u32[]{:S(2)}) collective-permute-start(f32[3,8,24,128]{3,2,1,0:T(8,128)S(1)} %get-tuple-element.34.own_ref), channel_id=1, source_target_pairs={{0,2},{2,4},{4,6},{6,22},{22,20},{20,18},{18,16},{16,32},{32,34},{... | collective-permute-start | bytes 884744 | tf_op jit(solution)/shard_map/ppermute | solution.py:424
  84.4 4.1 %collective-permute-start.6 = (f32[3,8,24,128]{3,2,1,0:T(8,128)}, f32[3,8,24,128]{3,2,1,0:T(8,128)}, u32[]{:S(2)}, u32[]{:S(2)}) collective-permute-start(f32[3,8,24,128]{3,2,1,0:T(8,128)} %collective-permute-done.5.got_ref), channel_id=1, source_target_pairs={{0,8},{8,0},{1,9},{9,1},{2,10},{10,2},{3,11},{11,3},{4,12},{12,4},... | collective-permute-start | bytes 884744 | tf_op jit(solution)/shard_map/ppermute | solution.py:421
  88.5 1.6 %copy-start.1 = (f32[7,16,40,128]{3,2,1,0:T(8,128)S(1)}, f32[7,16,40,128]{3,2,1,0:T(8,128)}, u32[]{:S(2)}) copy-start(f32[7,16,40,128]{3,2,1,0:T(8,128)} %copy-done) | copy-start | bytes 6881284
  90.2 1.0 copy-start.3
  94.8 6.2 %collective-permute-start.7 = (f32[1,8,24,128]{3,2,1,0:T(8,128)S(1)}, f32[1,8,24,128]{3,2,1,0:T(8,128)S(1)}, u32[]{:S(2)}, u32[]{:S(2)}) collective-permute-start(f32[1,8,24,128]{3,2,1,0:T(8,128)S(1)} %get-tuple-element.37.own_ref), channel_id=1, source_target_pairs={{0,2},{2,4},{4,6},{6,22},{22,20},{20,18},{18,16},{16,32},{32,34},{... | collective-permute-start | bytes 294920 | tf_op jit(solution)/shard_map/ppermute | solution.py:424

commit v13 on v12

--- a/solution.py
+++ b/solution.py
@@ -286,8 +286,8 @@
 
 
 def late_body(
-    core_ref, side_ref, fine_s, co_s, own_ref, got_ref, got2_ref, start_ref,
-    out_ref, pow_ref, next_ref, a_s, b_s, db_s, f_s, pow_s,
+    core_ref, fine_s, co_s, own_ref, got_ref, got2_ref, start_ref,
+    out_ref, pow_ref, next_ref, a_s, b_s, db_s, f_s,
 ):
     clear_ends(a_s, b_s)
     load_window(core_ref, a_s, 0, own_ref, got_ref, got2_ref)
@@ -303,19 +303,25 @@
         if n > 0:
             step(10 - 2 * n, a_s, b_s, co_s, db_s)
         for z in range(NZ):
-            pow_s[n, z] = a_s[z + 1, OWN:HIGH]
+            pow_ref[n, z] = a_s[z + 1, OWN:HIGH]
     for z in range(NZ):
         next_ref[0, z // 2, at(z, 0, STRIP)] = a_s[z + 1, OWN:HIGH]
 
-    def send(m, z, rows):
-        for n in range(5):
-            pow_ref[n, m * HALF : (m + 1) * HALF] = pow_s[n, z, rows]
-
-    cut(core_ref, side_ref, send)
+
+def early_powers_body(core_ref, side_ref, block_ref, early_ref, out_ref):
+    for b in range(NB):
+        power = b - block_ref[0]
+        live = (power >= 0) & (power < 5)
+        power = jnp.clip(power, 0, 4)
+
+        def send(m, z, rows, b=b, power=power, live=live):
+            out_ref[b, m * HALF : (m + 1) * HALF] = jnp.where(live, early_ref[power, z, rows], 0.0)
+
+        cut(core_ref, side_ref, send)
 
 
 def powers_body(
-    core_ref, side_ref, block_ref, co_s, own_ref, got_ref, early_ref, out_ref, a_s, b_s, db_s, pow_s, late_s
+    core_ref, side_ref, block_ref, co_s, own_ref, got_ref, base_ref, out_ref, a_s, b_s, db_s, late_s
 ):
     clear_ends(a_s, b_s)
     for z in range(NZ):
@@ -328,21 +334,21 @@
 
     pl.when(core_ref[0] == 0)(functools.partial(halo, slice(LOW, OWN)))
     pl.when(core_ref[0] == 1)(functools.partial(halo, slice(HIGH, WIN)))
-    for n in range(5):
-        pow_s[n] = early_ref[n]
     for n in range(3):
         step(6 - 2 * n, a_s, b_s, co_s, db_s)
         for z in range(NZ):
             late_s[n, z] = a_s[z + 1, OWN:HIGH]
-
-    def send(m, z, rows):
-        for n in range(3):
-            pow_s[5 + n, m * HALF : (m + 1) * HALF] = late_s[n, z, rows]
-
-    cut(core_ref, side_ref, send)
-    for b in range(NB):
-        power = jnp.clip(b - block_ref[0], 0, NB - 1)
-        out_ref[b] = jnp.where(b >= block_ref[0], pow_s[power], 0.0)
+    for n in range(3):
+        to = block_ref[0] + 5 + n
+
+        @pl.when(to < NB)
+        def _(n=n, to=to):
+            to = jnp.minimum(to, NB - 1)
+
+            def send(m, z, rows):
+                out_ref[to, m * HALF : (m + 1) * HALF] = late_s[n, z, rows]
+
+            cut(core_ref, side_ref, send)
 
 
 def cut(core_ref, side_ref, body):
@@ -450,15 +456,23 @@
     )
     state_got, state_got2, start_g = exchange(state, start_g)
     v_late, first_powers, last = call(
-        late_body, [sds(NZ, STRIP, LANES), sds(5, 8 * HALF, LANES), sds(1, 8, PAIR, LANES)],
-        core, side, fine, coarse, state, state_got, state_got2, start_g, smem=2, flops=12 * flops,
-        scratch=SWEEP_SCRATCH + (pltpu.VMEM((NZ + 2, WIN, LANES), F32), pltpu.VMEM((5, NZ, STRIP, LANES), F32)),
+        late_body, [sds(NZ, STRIP, LANES), sds(5, NZ, STRIP, LANES), sds(1, 8, PAIR, LANES)],
+        core, fine, coarse, state, state_got, state_got2, start_g, smem=1, flops=12 * flops,
+        scratch=SWEEP_SCRATCH + (pltpu.VMEM((NZ + 2, WIN, LANES), F32),),
     )
-    (powers,) = call(
-        powers_body, [sds(NB, 8 * HALF, LANES)],
-        core, side, block, coarse, last, from_neighbour(last), first_powers, smem=3, flops=6 * flops,
-        scratch=SWEEP_SCRATCH + (pltpu.VMEM((NB, 8 * HALF, LANES), F32), pltpu.VMEM((3, NZ, STRIP, LANES), F32)),
-    )
+    last_got = from_neighbour(last)
+    (base,) = call(early_powers_body, [sds(NB, 8 * HALF, LANES)], core, side, block, first_powers, smem=3)
+    last_got, base = lax.optimization_barrier((last_got, base))
+    smem = pl.BlockSpec(memory_space=pltpu.SMEM)
+    powers = pl.pallas_call(
+        powers_body,
+        out_shape=sds(NB, 8 * HALF, LANES),
+        in_specs=[smem] * 3 + [vmem] * 4,
+        out_specs=vmem,
+        scratch_shapes=SWEEP_SCRATCH + (pltpu.VMEM((3, NZ, STRIP, LANES), F32),),
+        input_output_aliases={6: 0},
+        compiler_params=pltpu.CompilerParams(vmem_limit_bytes=12 * 1024 * 1024),
+    )(core, side, block, coarse, last, last_got, base)
     arrived = lax.all_to_all(powers, BLOCKS, 0, 0, tiled=True)
     (back,) = call(collect_body, [sds(32, 6, 2, LANES)], core, side, arrived, v_early, v_late, smem=2)
     returned = lax.all_to_all(back, ("zl", "core", "y"), 0, 0, tiled=True)

time: 149 us -> 144 us (0.966)
  local copies, waits for them, and re-layouts: 7.72 us -> 5.61 us
  waiting for transfers between devices: 20 us -> 18.2 us
    unnamed x16 -> x12, local copies, waits for them, and re-layouts: 7.72 us -> 5.61 us
    pallas_call x10, Pallas kernels: 12.6 us -> 10.6 us  [call(): pl.pallas_call(body, out_shape=list(outs), in_specs=specs, out_specs=out_...]
where the time goes in v13:
time: 144 us
  blocking collectives  95.6 us (66%)
  waiting for transfers between devices  18.2 us (13%)
  starting transfers between devices  12.4 us (9%)
  Pallas kernels  11.6 us (8%)
  local copies, waits for them, and re-layouts  5.61 us (4%)
    all_to_all x1, blocking collectives, on_device(): lax.all_to_all(sent, BLOCK, 0, 0, tiled=True).reshape(8, 8, 9, 2, LANES)  50 us
    all_to_all x1, blocking collectives, on_device(): returned = lax.all_to_all(back, ('zl', 'core', 'y'), 0, 0, tiled=True)  23.3 us
    all_to_all x1, blocking collectives, on_device(): arrived = lax.all_to_all(powers, BLOCKS, 0, 0, tiled=True)  22.3 us
    ppermute x3, waiting for transfers between devices, from_neighbour(): return lax.ppermute(mine, ('zl', 'core', 'y'), neighbour_route())  13.7 us
    pallas_call x10, Pallas kernels, call(): pl.pallas_call(body, out_shape=list(outs), in_specs=specs, out_specs=out_...  10.6 us
    ppermute x3, starting transfers between devices, swap(): return lax.ppermute(mine, 'core', [(0, 1), (1, 0)])  7.16 us
    unnamed x12, local copies, waits for them, and re-layouts  5.61 us
    ppermute x3, waiting for transfers between devices, swap(): return lax.ppermute(mine, 'core', [(0, 1), (1, 0)])  4.47 us
  transfers between devices with their start and end apart: 8, of which 6 were waited for; matrix products, arithmetic and copies ran while one was open for 0% of the time, Pallas kernels for 3%

profile of v13, /device:TPU:1, one launch (start us, length us, event | category | flops | bytes accessed | tf_op | source)
XLA Modules:
  0.0 143.6 jit_solution(14859666807412108954)
XLA Ops:
  0.0 0.9 copy-done.2
  1.0 0.7 collective-permute-start
  1.7 0.7 collective-permute-start.1
  2.4 0.9 copy-done.3
  3.3 0.9 copy-done.4
  4.2 0.9 copy-done.5
  5.1 0.2 shard_map.47.base_ref
  5.4 50.0 %all_to_all.15 = f32[64,9,2,128]{3,2,1,0:T(2,128)S(1)} all-to-all(f32[64,9,2,128]{3,2,1,0:T(2,128)S(1)} %shard_map.48), channel_id=1, replica_groups=mesh['x'=4,'zh'=2,'zl'=4,'core'=2,'y'=4,'zhi'=2] {'zl','core','y','zhi'}, dimensions={0} | all-to-all | bytes 1179648 | tf_op jit(solution)/shard_map/all_to_all | solution.py:424
  55.4 2.6 %collective-permute-start.2 = (f32[8,8,9,2,128]{4,3,2,1,0:T(2,128)S(1)}, f32[8,8,9,2,128]{4,3,2,1,0:T(2,128)S(1)}, u32[]{:S(2)}, u32[]{:S(2)}) collective-permute-start(f32[8,8,9,2,128]{4,3,2,1,0:T(2,128)S(1)} %bitcast.8), channel_id=1, source_target_pairs={{0,8},{8,0},{1,9},{9,1},{2,10},{10,2},{3,11},{11,3},{4,12},{12,4},... | collective-permute-start | bytes 1769480 | tf_op jit(solution)/shard_map/ppermute | solution.py:427
  58.0 1.6 %collective-permute-done.2.other_ref = f32[8,8,9,2,128]{4,3,2,1,0:T(2,128)S(1)} collective-permute-done((f32[8,8,9,2,128]{4,3,2,1,0:T(2,128)S(1)}, f32[8,8,9,2,128]{4,3,2,1,0:T(2,128)S(1)}, u32[]{:S(2)}, u32[]{:S(2)}) %collective-permute-start.2) | collective-permute-done | bytes 589856 | tf_op jit(solution)/shard_map/ppermute | solution.py:427
  59.6 0.3 shard_map.49
  59.9 1.3 collective-permute-start.3
  61.2 3.1 %shard_map.50 = (f32[7,16,40,128]{3,2,1,0:T(8,128)S(1)}, f32[7,16,40,128]{3,2,1,0:T(8,128)S(1)}) custom-call(f32[16,40,128]{2,1,0:T(8,128)S(1)} %get-tuple-element.28.k_ref), custom_call_target="tpu_custom_call" | custom-call | flops 7372800 | bytes 4915200 | tf_op jit(solution)/shard_map/pallas_call | solution.py:57
  64.2 4.1 %collective-permute-done.3.got_ref = f32[4,8,24,128]{3,2,1,0:T(8,128)S(1)} collective-permute-done((f32[4,8,24,128]{3,2,1,0:T(8,128)S(1)}, f32[4,8,24,128]{3,2,1,0:T(8,128)S(1)}, u32[]{:S(2)}, u32[]{:S(2)}) %collective-permute-start.3) | collective-permute-done | bytes 393248 | tf_op jit(solution)/shard_map/ppermute | solution.py:430
  68.4 1.9 %collective-permute-start.4 = (f32[4,8,24,128]{3,2,1,0:T(8,128)S(1)}, f32[4,8,24,128]{3,2,1,0:T(8,128)S(1)}, u32[]{:S(2)}, u32[]{:S(2)}) collective-permute-start(f32[4,8,24,128]{3,2,1,0:T(8,128)S(1)} %collective-permute-done.3.got_ref), channel_id=1, source_target_pairs={{0,8},{8,0},{1,9},{9,1},{2,10},{10,2},{3,11},{11,3},{4,12},{12,4},... | collective-permute-start | bytes 1179656 | tf_op jit(solution)/shard_map/ppermute | solution.py:427
  70.3 1.7 %collective-permute-done.4.got2_ref = f32[4,8,24,128]{3,2,1,0:T(8,128)S(1)} collective-permute-done((f32[4,8,24,128]{3,2,1,0:T(8,128)S(1)}, f32[4,8,24,128]{3,2,1,0:T(8,128)S(1)}, u32[]{:S(2)}, u32[]{:S(2)}) %collective-permute-start.4) | collective-permute-done | bytes 393248 | tf_op jit(solution)/shard_map/ppermute | solution.py:427
  72.0 3.1 %shard_map.51 = (f32[6,16,12,128]{3,2,1,0:T(8,128)S(1)}, f32[3,8,24,128]{3,2,1,0:T(8,128)S(1)}) custom-call(s32[1]{0:T(128)} %bitcast.core_ref, f32[7,16,40,128]{3,2,1,0:T(8,128)S(1)} %get-tuple-element.32.co_s.fine_s, f32[8,16,12,128]{3,2,1,0:T(8,128)S(1)} %get-tuple-element.33.f_ref, f32[1,8,24,128]{3,2,1,0:T(8,128)S(1)} %get-tuple-element.34.own_ref, ...), custom_call_target="tpu_custom_call" | custom-call | flops 14745600 | bytes 4849668 | tf_op jit(solution)/shard_map/pallas_call | solution.py:57
  75.1 1.3 collective-permute-start.5
  76.4 0.5 shard_map.52.start_ref
  76.9 6.0 %collective-permute-done.5.got_ref = f32[3,8,24,128]{3,2,1,0:T(8,128)S(1)} collective-permute-done((f32[3,8,24,128]{3,2,1,0:T(8,128)S(1)}, f32[3,8,24,128]{3,2,1,0:T(8,128)S(1)}, u32[]{:S(2)}, u32[]{:S(2)}) %collective-permute-start.5) | collective-permute-done | bytes 294944 | tf_op jit(solution)/shard_map/ppermute | solution.py:430
  82.9 2.7 %collective-permute-start.6 = (f32[3,8,24,128]{3,2,1,0:T(8,128)S(1)}, f32[3,8,24,128]{3,2,1,0:T(8,128)S(1)}, u32[]{:S(2)}, u32[]{:S(2)}) collective-permute-start(f32[3,8,24,128]{3,2,1,0:T(8,128)S(1)} %collective-permute-done.5.got_ref), channel_id=1, source_target_pairs={{0,8},{8,0},{1,9},{9,1},{2,10},{10,2},{3,11},{11,3},{4,12},{12,4},... | collective-permute-start | bytes 884744 | tf_op jit(solution)/shard_map/ppermute | solution.py:427
  85.6 1.2 collective-permute-done.6.got2_ref
  86.8 2.6 %shard_map.53 = (f32[16,12,128]{2,1,0:T(8,128)S(1)}, f32[5,16,12,128]{3,2,1,0:T(8,128)S(1)}, f32[1,8,24,128]{3,2,1,0:T(8,128)S(1)}) custom-call(s32[1]{0:T(128)} %bitcast.core_ref, f32[7,16,40,128]{3,2,1,0:T(8,128)S(1)} %get-tuple-element.32.co_s.fine_s, f32[7,16,40,128]{3,2,1,0:T(8,128)S(1)} %get-tuple-element.31.co_s, ...), custom_call_target="tpu_custom_call" | custom-call | flops 14745600 | bytes 6488068 | tf_op jit(solution)/shard_map/pallas_call | solution.py:57
  89.3 0.8 copy-done
  90.2 1.3 collective-permute-start.7
  91.5 1.1 copy-done.1
  92.6 0.1 shard_map.54.base_ref
  92.7 3.6 %collective-permute-done.7.got_ref = f32[1,8,24,128]{3,2,1,0:T(8,128)S(1)} collective-permute-done((f32[1,8,24,128]{3,2,1,0:T(8,128)S(1)}, f32[1,8,24,128]{3,2,1,0:T(8,128)S(1)}, u32[]{:S(2)}, u32[]{:S(2)}) %collective-permute-start.7) | collective-permute-done | bytes 98336 | tf_op jit(solution)/shard_map/ppermute | solution.py:430
  96.3 1.0 shard_map.55
  97.2 22.3 %all_to_all.16.got_ref = f32[8,48,128]{2,1,0:T(8,128)S(1)} all-to-all(f32[8,48,128]{2,1,0:T(8,128)S(1)} %shard_map.55), channel_id=1, replica_groups=mesh['x'=4,'zh'=2,'zl'=4,'core'=2,'y'=4,'zhi'=2] {'x','zh'}, dimensions={0} | all-to-all | bytes 393216 | tf_op jit(solution)/shard_map/all_to_all | solution.py:476
  119.6 23.3 %all_to_all.17.got_ref = f32[32,6,2,128]{3,2,1,0:T(2,128)S(1)} all-to-all(f32[32,6,2,128]{3,2,1,0:T(2,128)S(1)} %shard_map.56), channel_id=1, replica_groups=mesh['x'=4,'zh'=2,'zl'=4,'core'=2,'y'=4,'zhi'=2] {'zl','core','y'}, dimensions={0} | all-to-all | bytes 393216 | tf_op jit(solution)/shard_map/all_to_all | solution.py:478
  142.9 0.7 shard_map.57
  (11 shorter events, 0.1 us)
Async XLA Ops:
  0.0 0.9 copy-start.2
  1.0 4.3 %collective-permute-start = (f32[2,16,3,2,128]{4,3,2,1,0:T(2,128)S(1)}, f32[2,16,3,2,128]{4,3,2,1,0:T(2,128)S(1)}, u32[]{:S(2)}, u32[]{:S(2)}) collective-permute-start(f32[2,16,3,2,128]{4,3,2,1,0:T(2,128)S(1)} %get-tuple-element.25), channel_id=1, source_target_pairs={{56,64},{57,65},{58,66},{59,67},{60,68},{61,69},{62,70},{63,71},{1... | collective-permute-start | bytes 294920 | tf_op jit(solution)/shard_map/ppermute | solution.py:409
  1.7 3.7 %collective-permute-start.1 = (f32[2,16,3,2,128]{4,3,2,1,0:T(2,128)S(1)}, f32[2,16,3,2,128]{4,3,2,1,0:T(2,128)S(1)}, u32[]{:S(2)}, u32[]{:S(2)}) collective-permute-start(f32[2,16,3,2,128]{4,3,2,1,0:T(2,128)S(1)} %get-tuple-element.26), channel_id=1, source_target_pairs={{56,72},{57,73},{58,74},{59,75},{60,76},{61,77},{62,78},{63,79},{1... | collective-permute-start | bytes 294920 | tf_op jit(solution)/shard_map/ppermute | solution.py:409
  2.3 0.9 copy-start.3
  3.3 0.9 copy-start.4
  4.2 0.9 copy-start.5
  55.4 4.2 %collective-permute-start.2 = (f32[8,8,9,2,128]{4,3,2,1,0:T(2,128)S(1)}, f32[8,8,9,2,128]{4,3,2,1,0:T(2,128)S(1)}, u32[]{:S(2)}, u32[]{:S(2)}) collective-permute-start(f32[8,8,9,2,128]{4,3,2,1,0:T(2,128)S(1)} %bitcast.8), channel_id=1, source_target_pairs={{0,8},{8,0},{1,9},{9,1},{2,10},{10,2},{3,11},{11,3},{4,12},{12,4},... | collective-permute-start | bytes 1769480 | tf_op jit(solution)/shard_map/ppermute | solution.py:427
  59.9 8.5 %collective-permute-start.3 = (f32[4,8,24,128]{3,2,1,0:T(8,128)S(1)}, f32[4,8,24,128]{3,2,1,0:T(8,128)S(1)}, u32[]{:S(2)}, u32[]{:S(2)}) collective-permute-start(f32[4,8,24,128]{3,2,1,0:T(8,128)S(1)} %get-tuple-element.27), channel_id=1, source_target_pairs={{0,2},{2,4},{4,6},{6,22},{22,20},{20,18},{18,16},{16,32},{32,34},{... | collective-permute-start | bytes 1179656 | tf_op jit(solution)/shard_map/ppermute | solution.py:430
  68.4 3.6 %collective-permute-start.4 = (f32[4,8,24,128]{3,2,1,0:T(8,128)S(1)}, f32[4,8,24,128]{3,2,1,0:T(8,128)S(1)}, u32[]{:S(2)}, u32[]{:S(2)}) collective-permute-start(f32[4,8,24,128]{3,2,1,0:T(8,128)S(1)} %collective-permute-done.3.got_ref), channel_id=1, source_target_pairs={{0,8},{8,0},{1,9},{9,1},{2,10},{10,2},{3,11},{11,3},{4,12},{12,4},... | collective-permute-start | bytes 1179656 | tf_op jit(solution)/shard_map/ppermute | solution.py:427
  75.1 7.8 %collective-permute-start.5 = (f32[3,8,24,128]{3,2,1,0:T(8,128)S(1)}, f32[3,8,24,128]{3,2,1,0:T(8,128)S(1)}, u32[]{:S(2)}, u32[]{:S(2)}) collective-permute-start(f32[3,8,24,128]{3,2,1,0:T(8,128)S(1)} %get-tuple-element.36.own_ref), channel_id=1, source_target_pairs={{0,2},{2,4},{4,6},{6,22},{22,20},{20,18},{18,16},{16,32},{32,34},{... | collective-permute-start | bytes 884744 | tf_op jit(solution)/shard_map/ppermute | solution.py:430
  82.9 3.9 %collective-permute-start.6 = (f32[3,8,24,128]{3,2,1,0:T(8,128)S(1)}, f32[3,8,24,128]{3,2,1,0:T(8,128)S(1)}, u32[]{:S(2)}, u32[]{:S(2)}) collective-permute-start(f32[3,8,24,128]{3,2,1,0:T(8,128)S(1)} %collective-permute-done.5.got_ref), channel_id=1, source_target_pairs={{0,8},{8,0},{1,9},{9,1},{2,10},{10,2},{3,11},{11,3},{4,12},{12,4},... | collective-permute-start | bytes 884744 | tf_op jit(solution)/shard_map/ppermute | solution.py:427
  89.3 0.8 copy-start
  90.2 6.1 %collective-permute-start.7 = (f32[1,8,24,128]{3,2,1,0:T(8,128)S(1)}, f32[1,8,24,128]{3,2,1,0:T(8,128)S(1)}, u32[]{:S(2)}, u32[]{:S(2)}) collective-permute-start(f32[1,8,24,128]{3,2,1,0:T(8,128)S(1)} %get-tuple-element.39.own_ref), channel_id=1, source_target_pairs={{0,2},{2,4},{4,6},{6,22},{22,20},{20,18},{18,16},{16,32},{32,34},{... | collective-permute-start | bytes 294920 | tf_op jit(solution)/shard_map/ppermute | solution.py:430
  91.5 1.1 copy-start.1

commit v14 on v13

--- a/solution.py
+++ b/solution.py
@@ -252,7 +252,6 @@
     load_window(core_ref, a_s, 0, own_ref, got_ref, got2_ref)
     for n in range(6):
         for z in range(NZ):
-            f_s[n, z] = jnp.zeros((WIN, LANES), F32)
             f_s[n, z, OWN:HIGH] = f_ref[n, z]
 
     def halos(below_ref, above_ref):

time: 144 us -> 144 us (level)
  no operation moved by 1% of the time
where the time goes in v14:
time: 144 us
  blocking collectives  95.6 us (66%)
  waiting for transfers between devices  18.2 us (13%)
  starting transfers between devices  12.4 us (9%)
  Pallas kernels  11.5 us (8%)
  local copies, waits for them, and re-layouts  5.61 us (4%)
    all_to_all x1, blocking collectives, on_device(): lax.all_to_all(sent, BLOCK, 0, 0, tiled=True).reshape(8, 8, 9, 2, LANES)  50 us
    all_to_all x1, blocking collectives, on_device(): returned = lax.all_to_all(back, ('zl', 'core', 'y'), 0, 0, tiled=True)  23.3 us
    all_to_all x1, blocking collectives, on_device(): arrived = lax.all_to_all(powers, BLOCKS, 0, 0, tiled=True)  22.3 us
    ppermute x3, waiting for transfers between devices, from_neighbour(): return lax.ppermute(mine, ('zl', 'core', 'y'), neighbour_route())  13.7 us
    pallas_call x10, Pallas kernels, call(): pl.pallas_call(body, out_shape=list(outs), in_specs=specs, out_specs=out_...  10.6 us
    ppermute x3, starting transfers between devices, swap(): return lax.ppermute(mine, 'core', [(0, 1), (1, 0)])  7.17 us
    unnamed x12, local copies, waits for them, and re-layouts  5.61 us
    ppermute x3, waiting for transfers between devices, swap(): return lax.ppermute(mine, 'core', [(0, 1), (1, 0)])  4.47 us
  transfers between devices with their start and end apart: 8, of which 6 were waited for; matrix products, arithmetic and copies ran while one was open for 0% of the time, Pallas kernels for 3%

profile of v14, /device:TPU:1, one launch (start us, length us, event | category | flops | bytes accessed | tf_op | source)
XLA Modules:
  0.0 143.6 jit_solution(14983509264739845657)
XLA Ops:
  0.0 0.9 copy-done.2
  1.0 0.7 collective-permute-start
  1.7 0.7 collective-permute-start.1
  2.4 0.9 copy-done.3
  3.3 0.9 copy-done.4
  4.2 0.9 copy-done.5
  5.1 0.2 shard_map.47.base_ref
  5.4 50.0 %all_to_all.15 = f32[64,9,2,128]{3,2,1,0:T(2,128)S(1)} all-to-all(f32[64,9,2,128]{3,2,1,0:T(2,128)S(1)} %shard_map.48), channel_id=1, replica_groups=mesh['x'=4,'zh'=2,'zl'=4,'core'=2,'y'=4,'zhi'=2] {'zl','core','y','zhi'}, dimensions={0} | all-to-all | bytes 1179648 | tf_op jit(solution)/shard_map/all_to_all | solution.py:423
  55.4 2.6 %collective-permute-start.2 = (f32[8,8,9,2,128]{4,3,2,1,0:T(2,128)S(1)}, f32[8,8,9,2,128]{4,3,2,1,0:T(2,128)S(1)}, u32[]{:S(2)}, u32[]{:S(2)}) collective-permute-start(f32[8,8,9,2,128]{4,3,2,1,0:T(2,128)S(1)} %bitcast.8), channel_id=1, source_target_pairs={{0,8},{8,0},{1,9},{9,1},{2,10},{10,2},{3,11},{11,3},{4,12},{12,4},... | collective-permute-start | bytes 1769480 | tf_op jit(solution)/shard_map/ppermute | solution.py:426
  58.0 1.6 %collective-permute-done.2.other_ref = f32[8,8,9,2,128]{4,3,2,1,0:T(2,128)S(1)} collective-permute-done((f32[8,8,9,2,128]{4,3,2,1,0:T(2,128)S(1)}, f32[8,8,9,2,128]{4,3,2,1,0:T(2,128)S(1)}, u32[]{:S(2)}, u32[]{:S(2)}) %collective-permute-start.2) | collective-permute-done | bytes 589856 | tf_op jit(solution)/shard_map/ppermute | solution.py:426
  59.6 0.3 shard_map.49
  59.9 1.3 collective-permute-start.3
  61.2 3.1 %shard_map.50 = (f32[7,16,40,128]{3,2,1,0:T(8,128)S(1)}, f32[7,16,40,128]{3,2,1,0:T(8,128)S(1)}) custom-call(f32[16,40,128]{2,1,0:T(8,128)S(1)} %get-tuple-element.28.k_ref), custom_call_target="tpu_custom_call" | custom-call | flops 7372800 | bytes 4915200 | tf_op jit(solution)/shard_map/pallas_call | solution.py:57
  64.2 4.1 %collective-permute-done.3.got_ref = f32[4,8,24,128]{3,2,1,0:T(8,128)S(1)} collective-permute-done((f32[4,8,24,128]{3,2,1,0:T(8,128)S(1)}, f32[4,8,24,128]{3,2,1,0:T(8,128)S(1)}, u32[]{:S(2)}, u32[]{:S(2)}) %collective-permute-start.3) | collective-permute-done | bytes 393248 | tf_op jit(solution)/shard_map/ppermute | solution.py:429
  68.4 1.9 %collective-permute-start.4 = (f32[4,8,24,128]{3,2,1,0:T(8,128)S(1)}, f32[4,8,24,128]{3,2,1,0:T(8,128)S(1)}, u32[]{:S(2)}, u32[]{:S(2)}) collective-permute-start(f32[4,8,24,128]{3,2,1,0:T(8,128)S(1)} %collective-permute-done.3.got_ref), channel_id=1, source_target_pairs={{0,8},{8,0},{1,9},{9,1},{2,10},{10,2},{3,11},{11,3},{4,12},{12,4},... | collective-permute-start | bytes 1179656 | tf_op jit(solution)/shard_map/ppermute | solution.py:426
  70.3 1.7 %collective-permute-done.4.got2_ref = f32[4,8,24,128]{3,2,1,0:T(8,128)S(1)} collective-permute-done((f32[4,8,24,128]{3,2,1,0:T(8,128)S(1)}, f32[4,8,24,128]{3,2,1,0:T(8,128)S(1)}, u32[]{:S(2)}, u32[]{:S(2)}) %collective-permute-start.4) | collective-permute-done | bytes 393248 | tf_op jit(solution)/shard_map/ppermute | solution.py:426
  72.0 3.0 %shard_map.51 = (f32[6,16,12,128]{3,2,1,0:T(8,128)S(1)}, f32[3,8,24,128]{3,2,1,0:T(8,128)S(1)}) custom-call(s32[1]{0:T(128)} %bitcast.core_ref, f32[7,16,40,128]{3,2,1,0:T(8,128)S(1)} %get-tuple-element.32.co_s.fine_s, f32[8,16,12,128]{3,2,1,0:T(8,128)S(1)} %get-tuple-element.33.f_ref, f32[1,8,24,128]{3,2,1,0:T(8,128)S(1)} %get-tuple-element.34.own_ref, ...), custom_call_target="tpu_custom_call" | custom-call | flops 14745600 | bytes 4849668 | tf_op jit(solution)/shard_map/pallas_call | solution.py:57
  75.0 1.3 collective-permute-start.5
  76.3 0.5 shard_map.52.start_ref
  76.8 6.0 %collective-permute-done.5.got_ref = f32[3,8,24,128]{3,2,1,0:T(8,128)S(1)} collective-permute-done((f32[3,8,24,128]{3,2,1,0:T(8,128)S(1)}, f32[3,8,24,128]{3,2,1,0:T(8,128)S(1)}, u32[]{:S(2)}, u32[]{:S(2)}) %collective-permute-start.5) | collective-permute-done | bytes 294944 | tf_op jit(solution)/shard_map/ppermute | solution.py:429
  82.8 2.7 %collective-permute-start.6 = (f32[3,8,24,128]{3,2,1,0:T(8,128)S(1)}, f32[3,8,24,128]{3,2,1,0:T(8,128)S(1)}, u32[]{:S(2)}, u32[]{:S(2)}) collective-permute-start(f32[3,8,24,128]{3,2,1,0:T(8,128)S(1)} %collective-permute-done.5.got_ref), channel_id=1, source_target_pairs={{0,8},{8,0},{1,9},{9,1},{2,10},{10,2},{3,11},{11,3},{4,12},{12,4},... | collective-permute-start | bytes 884744 | tf_op jit(solution)/shard_map/ppermute | solution.py:426
  85.5 1.2 collective-permute-done.6.got2_ref
  86.7 2.6 %shard_map.53 = (f32[16,12,128]{2,1,0:T(8,128)S(1)}, f32[5,16,12,128]{3,2,1,0:T(8,128)S(1)}, f32[1,8,24,128]{3,2,1,0:T(8,128)S(1)}) custom-call(s32[1]{0:T(128)} %bitcast.core_ref, f32[7,16,40,128]{3,2,1,0:T(8,128)S(1)} %get-tuple-element.32.co_s.fine_s, f32[7,16,40,128]{3,2,1,0:T(8,128)S(1)} %get-tuple-element.31.co_s, ...), custom_call_target="tpu_custom_call" | custom-call | flops 14745600 | bytes 6488068 | tf_op jit(solution)/shard_map/pallas_call | solution.py:57
  89.3 0.8 copy-done
  90.1 1.3 collective-permute-start.7
  91.4 1.1 copy-done.1
  92.5 0.1 shard_map.54.base_ref
  92.6 3.6 %collective-permute-done.7.got_ref = f32[1,8,24,128]{3,2,1,0:T(8,128)S(1)} collective-permute-done((f32[1,8,24,128]{3,2,1,0:T(8,128)S(1)}, f32[1,8,24,128]{3,2,1,0:T(8,128)S(1)}, u32[]{:S(2)}, u32[]{:S(2)}) %collective-permute-start.7) | collective-permute-done | bytes 98336 | tf_op jit(solution)/shard_map/ppermute | solution.py:429
  96.2 1.0 shard_map.55
  97.2 22.3 %all_to_all.16.got_ref = f32[8,48,128]{2,1,0:T(8,128)S(1)} all-to-all(f32[8,48,128]{2,1,0:T(8,128)S(1)} %shard_map.55), channel_id=1, replica_groups=mesh['x'=4,'zh'=2,'zl'=4,'core'=2,'y'=4,'zhi'=2] {'x','zh'}, dimensions={0} | all-to-all | bytes 393216 | tf_op jit(solution)/shard_map/all_to_all | solution.py:475
  119.5 23.3 %all_to_all.17.got_ref = f32[32,6,2,128]{3,2,1,0:T(2,128)S(1)} all-to-all(f32[32,6,2,128]{3,2,1,0:T(2,128)S(1)} %shard_map.56), channel_id=1, replica_groups=mesh['x'=4,'zh'=2,'zl'=4,'core'=2,'y'=4,'zhi'=2] {'zl','core','y'}, dimensions={0} | all-to-all | bytes 393216 | tf_op jit(solution)/shard_map/all_to_all | solution.py:477
  142.8 0.7 shard_map.57
  (11 shorter events, 0.1 us)
Async XLA Ops:
  0.0 0.9 copy-start.2
  1.0 4.3 %collective-permute-start = (f32[2,16,3,2,128]{4,3,2,1,0:T(2,128)S(1)}, f32[2,16,3,2,128]{4,3,2,1,0:T(2,128)S(1)}, u32[]{:S(2)}, u32[]{:S(2)}) collective-permute-start(f32[2,16,3,2,128]{4,3,2,1,0:T(2,128)S(1)} %get-tuple-element.25), channel_id=1, source_target_pairs={{56,64},{57,65},{58,66},{59,67},{60,68},{61,69},{62,70},{63,71},{1... | collective-permute-start | bytes 294920 | tf_op jit(solution)/shard_map/ppermute | solution.py:408
  1.7 3.7 %collective-permute-start.1 = (f32[2,16,3,2,128]{4,3,2,1,0:T(2,128)S(1)}, f32[2,16,3,2,128]{4,3,2,1,0:T(2,128)S(1)}, u32[]{:S(2)}, u32[]{:S(2)}) collective-permute-start(f32[2,16,3,2,128]{4,3,2,1,0:T(2,128)S(1)} %get-tuple-element.26), channel_id=1, source_target_pairs={{56,72},{57,73},{58,74},{59,75},{60,76},{61,77},{62,78},{63,79},{1... | collective-permute-start | bytes 294920 | tf_op jit(solution)/shard_map/ppermute | solution.py:408
  2.3 0.9 copy-start.3
  3.3 0.9 copy-start.4
  4.2 0.9 copy-start.5
  55.4 4.2 %collective-permute-start.2 = (f32[8,8,9,2,128]{4,3,2,1,0:T(2,128)S(1)}, f32[8,8,9,2,128]{4,3,2,1,0:T(2,128)S(1)}, u32[]{:S(2)}, u32[]{:S(2)}) collective-permute-start(f32[8,8,9,2,128]{4,3,2,1,0:T(2,128)S(1)} %bitcast.8), channel_id=1, source_target_pairs={{0,8},{8,0},{1,9},{9,1},{2,10},{10,2},{3,11},{11,3},{4,12},{12,4},... | collective-permute-start | bytes 1769480 | tf_op jit(solution)/shard_map/ppermute | solution.py:426
  59.9 8.5 %collective-permute-start.3 = (f32[4,8,24,128]{3,2,1,0:T(8,128)S(1)}, f32[4,8,24,128]{3,2,1,0:T(8,128)S(1)}, u32[]{:S(2)}, u32[]{:S(2)}) collective-permute-start(f32[4,8,24,128]{3,2,1,0:T(8,128)S(1)} %get-tuple-element.27), channel_id=1, source_target_pairs={{0,2},{2,4},{4,6},{6,22},{22,20},{20,18},{18,16},{16,32},{32,34},{... | collective-permute-start | bytes 1179656 | tf_op jit(solution)/shard_map/ppermute | solution.py:429
  68.4 3.6 %collective-permute-start.4 = (f32[4,8,24,128]{3,2,1,0:T(8,128)S(1)}, f32[4,8,24,128]{3,2,1,0:T(8,128)S(1)}, u32[]{:S(2)}, u32[]{:S(2)}) collective-permute-start(f32[4,8,24,128]{3,2,1,0:T(8,128)S(1)} %collective-permute-done.3.got_ref), channel_id=1, source_target_pairs={{0,8},{8,0},{1,9},{9,1},{2,10},{10,2},{3,11},{11,3},{4,12},{12,4},... | collective-permute-start | bytes 1179656 | tf_op jit(solution)/shard_map/ppermute | solution.py:426
  75.0 7.8 %collective-permute-start.5 = (f32[3,8,24,128]{3,2,1,0:T(8,128)S(1)}, f32[3,8,24,128]{3,2,1,0:T(8,128)S(1)}, u32[]{:S(2)}, u32[]{:S(2)}) collective-permute-start(f32[3,8,24,128]{3,2,1,0:T(8,128)S(1)} %get-tuple-element.36.own_ref), channel_id=1, source_target_pairs={{0,2},{2,4},{4,6},{6,22},{22,20},{20,18},{18,16},{16,32},{32,34},{... | collective-permute-start | bytes 884744 | tf_op jit(solution)/shard_map/ppermute | solution.py:429
  82.8 3.9 %collective-permute-start.6 = (f32[3,8,24,128]{3,2,1,0:T(8,128)S(1)}, f32[3,8,24,128]{3,2,1,0:T(8,128)S(1)}, u32[]{:S(2)}, u32[]{:S(2)}) collective-permute-start(f32[3,8,24,128]{3,2,1,0:T(8,128)S(1)} %collective-permute-done.5.got_ref), channel_id=1, source_target_pairs={{0,8},{8,0},{1,9},{9,1},{2,10},{10,2},{3,11},{11,3},{4,12},{12,4},... | collective-permute-start | bytes 884744 | tf_op jit(solution)/shard_map/ppermute | solution.py:426
  89.3 0.8 copy-start
  90.1 6.1 %collective-permute-start.7 = (f32[1,8,24,128]{3,2,1,0:T(8,128)S(1)}, f32[1,8,24,128]{3,2,1,0:T(8,128)S(1)}, u32[]{:S(2)}, u32[]{:S(2)}) collective-permute-start(f32[1,8,24,128]{3,2,1,0:T(8,128)S(1)} %get-tuple-element.39.own_ref), channel_id=1, source_target_pairs={{0,2},{2,4},{4,6},{6,22},{22,20},{20,18},{18,16},{16,32},{32,34},{... | collective-permute-start | bytes 294920 | tf_op jit(solution)/shard_map/ppermute | solution.py:429
  91.4 1.1 copy-start.1

commit v15 on v13

--- a/solution.py
+++ b/solution.py
@@ -287,7 +287,7 @@
 
 def late_body(
     core_ref, fine_s, co_s, own_ref, got_ref, got2_ref, start_ref,
-    out_ref, pow_ref, next_ref, a_s, b_s, db_s, f_s,
+    out_ref, pow_ref, next_ref, edge_ref, a_s, b_s, db_s, f_s,
 ):
     clear_ends(a_s, b_s)
     load_window(core_ref, a_s, 0, own_ref, got_ref, got2_ref)
@@ -307,6 +307,13 @@
     for z in range(NZ):
         next_ref[0, z // 2, at(z, 0, STRIP)] = a_s[z + 1, OWN:HIGH]
 
+    def edge(rows):
+        for z in range(NZ):
+            edge_ref[z // 4, HALF * (z % 4) : HALF * (z % 4) + HALF] = a_s[z + 1, rows]
+
+    pl.when(core_ref[0] == 0)(functools.partial(edge, slice(HIGH - HALF, HIGH)))
+    pl.when(core_ref[0] == 1)(functools.partial(edge, slice(OWN, OWN + HALF)))
+
 
 def early_powers_body(core_ref, side_ref, block_ref, early_ref, out_ref):
     for b in range(NB):
@@ -330,10 +337,10 @@
 
     def halo(rows):
         for z in range(NZ):
-            a_s[z + 1, rows] = got_ref[0, z // 2, at(z, 0, STRIP)]
-
-    pl.when(core_ref[0] == 0)(functools.partial(halo, slice(LOW, OWN)))
-    pl.when(core_ref[0] == 1)(functools.partial(halo, slice(HIGH, WIN)))
+            a_s[z + 1, rows] = got_ref[z // 4, HALF * (z % 4) : HALF * (z % 4) + HALF]
+
+    pl.when(core_ref[0] == 0)(functools.partial(halo, slice(OWN - HALF, OWN)))
+    pl.when(core_ref[0] == 1)(functools.partial(halo, slice(HIGH, HIGH + HALF)))
     for n in range(3):
         step(6 - 2 * n, a_s, b_s, co_s, db_s)
         for z in range(NZ):
@@ -455,12 +462,12 @@
         core, block, coarse, start, got, got2, smem=2, flops=2 * flops, scratch=SWEEP_SCRATCH,
     )
     state_got, state_got2, start_g = exchange(state, start_g)
-    v_late, first_powers, last = call(
-        late_body, [sds(NZ, STRIP, LANES), sds(5, NZ, STRIP, LANES), sds(1, 8, PAIR, LANES)],
+    v_late, first_powers, last, edge = call(
+        late_body, [sds(NZ, STRIP, LANES), sds(5, NZ, STRIP, LANES), sds(1, 8, PAIR, LANES), sds(4, 4 * HALF, LANES)],
         core, fine, coarse, state, state_got, state_got2, start_g, smem=1, flops=12 * flops,
         scratch=SWEEP_SCRATCH + (pltpu.VMEM((NZ + 2, WIN, LANES), F32),),
     )
-    last_got = from_neighbour(last)
+    last_got = from_neighbour(edge)
     (base,) = call(early_powers_body, [sds(NB, 8 * HALF, LANES)], core, side, block, first_powers, smem=3)
     last_got, base = lax.optimization_barrier((last_got, base))
     smem = pl.BlockSpec(memory_space=pltpu.SMEM)

time: 144 us -> 144 us (level)
  no operation moved by 1% of the time
where the time goes in v15:
time: 144 us; the launch traced here: 143 us
  blocking collectives  95.6 us (66%)
  waiting for transfers between devices  17.7 us (12%)
  starting transfers between devices  12.4 us (9%)
  Pallas kernels  11.6 us (8%)
  local copies, waits for them, and re-layouts  5.61 us (4%)
    all_to_all x1, blocking collectives, on_device(): lax.all_to_all(sent, BLOCK, 0, 0, tiled=True).reshape(8, 8, 9, 2, LANES)  50 us
    all_to_all x1, blocking collectives, on_device(): returned = lax.all_to_all(back, ('zl', 'core', 'y'), 0, 0, tiled=True)  23.3 us
    all_to_all x1, blocking collectives, on_device(): arrived = lax.all_to_all(powers, BLOCKS, 0, 0, tiled=True)  22.3 us
    ppermute x3, waiting for transfers between devices, from_neighbour(): return lax.ppermute(mine, ('zl', 'core', 'y'), neighbour_route())  13.2 us
    pallas_call x10, Pallas kernels, call(): pl.pallas_call(body, out_shape=list(outs), in_specs=specs, out_specs=out_...  10.7 us
    ppermute x3, starting transfers between devices, swap(): return lax.ppermute(mine, 'core', [(0, 1), (1, 0)])  7.16 us
    unnamed x12, local copies, waits for them, and re-layouts  5.61 us
    ppermute x3, waiting for transfers between devices, swap(): return lax.ppermute(mine, 'core', [(0, 1), (1, 0)])  4.47 us
  transfers between devices with their start and end apart: 8, of which 6 were waited for; matrix products, arithmetic and copies ran while one was open for 0% of the time, Pallas kernels for 3%

profile of v15, /device:TPU:1, one launch (start us, length us, event | category | flops | bytes accessed | tf_op | source)
XLA Modules:
  0.0 143.1 jit_solution(6166431633379137404)
XLA Ops:
  0.0 0.9 copy-done.2
  1.0 0.7 collective-permute-start
  1.7 0.7 collective-permute-start.1
  2.4 0.9 copy-done.3
  3.3 0.9 copy-done.4
  4.2 0.9 copy-done.5
  5.1 0.2 shard_map.47.base_ref
  5.4 50.0 %all_to_all.15 = f32[64,9,2,128]{3,2,1,0:T(2,128)S(1)} all-to-all(f32[64,9,2,128]{3,2,1,0:T(2,128)S(1)} %shard_map.48), channel_id=1, replica_groups=mesh['x'=4,'zh'=2,'zl'=4,'core'=2,'y'=4,'zhi'=2] {'zl','core','y','zhi'}, dimensions={0} | all-to-all | bytes 1179648 | tf_op jit(solution)/shard_map/all_to_all | solution.py:431
  55.4 2.6 %collective-permute-start.2 = (f32[8,8,9,2,128]{4,3,2,1,0:T(2,128)S(1)}, f32[8,8,9,2,128]{4,3,2,1,0:T(2,128)S(1)}, u32[]{:S(2)}, u32[]{:S(2)}) collective-permute-start(f32[8,8,9,2,128]{4,3,2,1,0:T(2,128)S(1)} %bitcast.8), channel_id=1, source_target_pairs={{0,8},{8,0},{1,9},{9,1},{2,10},{10,2},{3,11},{11,3},{4,12},{12,4},... | collective-permute-start | bytes 1769480 | tf_op jit(solution)/shard_map/ppermute | solution.py:434
  58.0 1.6 %collective-permute-done.2.other_ref = f32[8,8,9,2,128]{4,3,2,1,0:T(2,128)S(1)} collective-permute-done((f32[8,8,9,2,128]{4,3,2,1,0:T(2,128)S(1)}, f32[8,8,9,2,128]{4,3,2,1,0:T(2,128)S(1)}, u32[]{:S(2)}, u32[]{:S(2)}) %collective-permute-start.2) | collective-permute-done | bytes 589856 | tf_op jit(solution)/shard_map/ppermute | solution.py:434
  59.6 0.3 shard_map.49
  59.9 1.3 collective-permute-start.3
  61.2 3.1 %shard_map.50 = (f32[7,16,40,128]{3,2,1,0:T(8,128)S(1)}, f32[7,16,40,128]{3,2,1,0:T(8,128)S(1)}) custom-call(f32[16,40,128]{2,1,0:T(8,128)S(1)} %get-tuple-element.29.k_ref), custom_call_target="tpu_custom_call" | custom-call | flops 7372800 | bytes 4915200 | tf_op jit(solution)/shard_map/pallas_call | solution.py:57
  64.2 4.1 %collective-permute-done.3.got_ref = f32[4,8,24,128]{3,2,1,0:T(8,128)S(1)} collective-permute-done((f32[4,8,24,128]{3,2,1,0:T(8,128)S(1)}, f32[4,8,24,128]{3,2,1,0:T(8,128)S(1)}, u32[]{:S(2)}, u32[]{:S(2)}) %collective-permute-start.3) | collective-permute-done | bytes 393248 | tf_op jit(solution)/shard_map/ppermute | solution.py:437
  68.4 1.9 %collective-permute-start.4 = (f32[4,8,24,128]{3,2,1,0:T(8,128)S(1)}, f32[4,8,24,128]{3,2,1,0:T(8,128)S(1)}, u32[]{:S(2)}, u32[]{:S(2)}) collective-permute-start(f32[4,8,24,128]{3,2,1,0:T(8,128)S(1)} %collective-permute-done.3.got_ref), channel_id=1, source_target_pairs={{0,8},{8,0},{1,9},{9,1},{2,10},{10,2},{3,11},{11,3},{4,12},{12,4},... | collective-permute-start | bytes 1179656 | tf_op jit(solution)/shard_map/ppermute | solution.py:434
  70.3 1.7 %collective-permute-done.4.got2_ref = f32[4,8,24,128]{3,2,1,0:T(8,128)S(1)} collective-permute-done((f32[4,8,24,128]{3,2,1,0:T(8,128)S(1)}, f32[4,8,24,128]{3,2,1,0:T(8,128)S(1)}, u32[]{:S(2)}, u32[]{:S(2)}) %collective-permute-start.4) | collective-permute-done | bytes 393248 | tf_op jit(solution)/shard_map/ppermute | solution.py:434
  72.0 3.1 %shard_map.51 = (f32[6,16,12,128]{3,2,1,0:T(8,128)S(1)}, f32[3,8,24,128]{3,2,1,0:T(8,128)S(1)}) custom-call(s32[1]{0:T(128)} %bitcast.core_ref, f32[7,16,40,128]{3,2,1,0:T(8,128)S(1)} %get-tuple-element.33.co_s.fine_s, f32[8,16,12,128]{3,2,1,0:T(8,128)S(1)} %get-tuple-element.34.f_ref, f32[1,8,24,128]{3,2,1,0:T(8,128)S(1)} %get-tuple-element.35.own_ref, ...), custom_call_target="tpu_custom_call" | custom-call | flops 14745600 | bytes 4849668 | tf_op jit(solution)/shard_map/pallas_call | solution.py:57
  75.1 1.3 collective-permute-start.5
  76.4 0.5 shard_map.52.start_ref
  76.9 6.0 %collective-permute-done.5.got_ref = f32[3,8,24,128]{3,2,1,0:T(8,128)S(1)} collective-permute-done((f32[3,8,24,128]{3,2,1,0:T(8,128)S(1)}, f32[3,8,24,128]{3,2,1,0:T(8,128)S(1)}, u32[]{:S(2)}, u32[]{:S(2)}) %collective-permute-start.5) | collective-permute-done | bytes 294944 | tf_op jit(solution)/shard_map/ppermute | solution.py:437
  82.9 2.7 %collective-permute-start.6 = (f32[3,8,24,128]{3,2,1,0:T(8,128)S(1)}, f32[3,8,24,128]{3,2,1,0:T(8,128)S(1)}, u32[]{:S(2)}, u32[]{:S(2)}) collective-permute-start(f32[3,8,24,128]{3,2,1,0:T(8,128)S(1)} %collective-permute-done.5.got_ref), channel_id=1, source_target_pairs={{0,8},{8,0},{1,9},{9,1},{2,10},{10,2},{3,11},{11,3},{4,12},{12,4},... | collective-permute-start | bytes 884744 | tf_op jit(solution)/shard_map/ppermute | solution.py:434
  85.6 1.2 collective-permute-done.6.got2_ref
  86.8 2.6 %shard_map.53 = (f32[16,12,128]{2,1,0:T(8,128)S(1)}, f32[5,16,12,128]{3,2,1,0:T(8,128)S(1)}, f32[1,8,24,128]{3,2,1,0:T(8,128)S(1)}, f32[4,24,128]{2,1,0:T(8,128)S(1)}) custom-call(s32[1]{0:T(128)} %bitcast.core_ref, f32[7,16,40,128]{3,2,1,0:T(8,128)S(1)} %get-tuple-element.33.co_s.fine_s, f32[7,16,40,128]{3,2,1,0:T(8,128)S(1)} %get-tuple-element.32.co_s, ...), custom_call_target="tpu_custom_call" | custom-call | flops 14745600 | bytes 6537220 | tf_op jit(solution)/shard_map/pallas_call | solution.py:57
  89.4 0.8 copy-done
  90.2 1.3 collective-permute-start.7
  91.5 1.1 copy-done.1
  92.6 0.1 shard_map.54.base_ref
  92.7 3.0 %collective-permute-done.7.got_ref = f32[4,24,128]{2,1,0:T(8,128)S(1)} collective-permute-done((f32[4,24,128]{2,1,0:T(8,128)S(1)}, f32[4,24,128]{2,1,0:T(8,128)S(1)}, u32[]{:S(2)}, u32[]{:S(2)}) %collective-permute-start.7) | collective-permute-done | bytes 49184 | tf_op jit(solution)/shard_map/ppermute | solution.py:437
  95.8 0.9 shard_map.55
  96.7 22.3 %all_to_all.16.got_ref = f32[8,48,128]{2,1,0:T(8,128)S(1)} all-to-all(f32[8,48,128]{2,1,0:T(8,128)S(1)} %shard_map.55), channel_id=1, replica_groups=mesh['x'=4,'zh'=2,'zl'=4,'core'=2,'y'=4,'zhi'=2] {'x','zh'}, dimensions={0} | all-to-all | bytes 393216 | tf_op jit(solution)/shard_map/all_to_all | solution.py:483
  119.1 23.3 %all_to_all.17.got_ref = f32[32,6,2,128]{3,2,1,0:T(2,128)S(1)} all-to-all(f32[32,6,2,128]{3,2,1,0:T(2,128)S(1)} %shard_map.56), channel_id=1, replica_groups=mesh['x'=4,'zh'=2,'zl'=4,'core'=2,'y'=4,'zhi'=2] {'zl','core','y'}, dimensions={0} | all-to-all | bytes 393216 | tf_op jit(solution)/shard_map/all_to_all | solution.py:485
  142.3 0.7 shard_map.57
  (11 shorter events, 0.1 us)
Async XLA Ops:
  0.0 0.9 copy-start.2
  1.0 4.3 %collective-permute-start = (f32[2,16,3,2,128]{4,3,2,1,0:T(2,128)S(1)}, f32[2,16,3,2,128]{4,3,2,1,0:T(2,128)S(1)}, u32[]{:S(2)}, u32[]{:S(2)}) collective-permute-start(f32[2,16,3,2,128]{4,3,2,1,0:T(2,128)S(1)} %get-tuple-element.26), channel_id=1, source_target_pairs={{56,64},{57,65},{58,66},{59,67},{60,68},{61,69},{62,70},{63,71},{1... | collective-permute-start | bytes 294920 | tf_op jit(solution)/shard_map/ppermute | solution.py:416
  1.7 3.7 %collective-permute-start.1 = (f32[2,16,3,2,128]{4,3,2,1,0:T(2,128)S(1)}, f32[2,16,3,2,128]{4,3,2,1,0:T(2,128)S(1)}, u32[]{:S(2)}, u32[]{:S(2)}) collective-permute-start(f32[2,16,3,2,128]{4,3,2,1,0:T(2,128)S(1)} %get-tuple-element.27), channel_id=1, source_target_pairs={{56,72},{57,73},{58,74},{59,75},{60,76},{61,77},{62,78},{63,79},{1... | collective-permute-start | bytes 294920 | tf_op jit(solution)/shard_map/ppermute | solution.py:416
  2.3 0.9 copy-start.3
  3.3 0.9 copy-start.4
  4.2 0.9 copy-start.5
  55.4 4.2 %collective-permute-start.2 = (f32[8,8,9,2,128]{4,3,2,1,0:T(2,128)S(1)}, f32[8,8,9,2,128]{4,3,2,1,0:T(2,128)S(1)}, u32[]{:S(2)}, u32[]{:S(2)}) collective-permute-start(f32[8,8,9,2,128]{4,3,2,1,0:T(2,128)S(1)} %bitcast.8), channel_id=1, source_target_pairs={{0,8},{8,0},{1,9},{9,1},{2,10},{10,2},{3,11},{11,3},{4,12},{12,4},... | collective-permute-start | bytes 1769480 | tf_op jit(solution)/shard_map/ppermute | solution.py:434
  59.9 8.5 %collective-permute-start.3 = (f32[4,8,24,128]{3,2,1,0:T(8,128)S(1)}, f32[4,8,24,128]{3,2,1,0:T(8,128)S(1)}, u32[]{:S(2)}, u32[]{:S(2)}) collective-permute-start(f32[4,8,24,128]{3,2,1,0:T(8,128)S(1)} %get-tuple-element.28), channel_id=1, source_target_pairs={{0,2},{2,4},{4,6},{6,22},{22,20},{20,18},{18,16},{16,32},{32,34},{... | collective-permute-start | bytes 1179656 | tf_op jit(solution)/shard_map/ppermute | solution.py:437
  68.4 3.6 %collective-permute-start.4 = (f32[4,8,24,128]{3,2,1,0:T(8,128)S(1)}, f32[4,8,24,128]{3,2,1,0:T(8,128)S(1)}, u32[]{:S(2)}, u32[]{:S(2)}) collective-permute-start(f32[4,8,24,128]{3,2,1,0:T(8,128)S(1)} %collective-permute-done.3.got_ref), channel_id=1, source_target_pairs={{0,8},{8,0},{1,9},{9,1},{2,10},{10,2},{3,11},{11,3},{4,12},{12,4},... | collective-permute-start | bytes 1179656 | tf_op jit(solution)/shard_map/ppermute | solution.py:434
  75.1 7.8 %collective-permute-start.5 = (f32[3,8,24,128]{3,2,1,0:T(8,128)S(1)}, f32[3,8,24,128]{3,2,1,0:T(8,128)S(1)}, u32[]{:S(2)}, u32[]{:S(2)}) collective-permute-start(f32[3,8,24,128]{3,2,1,0:T(8,128)S(1)} %get-tuple-element.37.own_ref), channel_id=1, source_target_pairs={{0,2},{2,4},{4,6},{6,22},{22,20},{20,18},{18,16},{16,32},{32,34},{... | collective-permute-start | bytes 884744 | tf_op jit(solution)/shard_map/ppermute | solution.py:437
  82.9 3.9 %collective-permute-start.6 = (f32[3,8,24,128]{3,2,1,0:T(8,128)S(1)}, f32[3,8,24,128]{3,2,1,0:T(8,128)S(1)}, u32[]{:S(2)}, u32[]{:S(2)}) collective-permute-start(f32[3,8,24,128]{3,2,1,0:T(8,128)S(1)} %collective-permute-done.5.got_ref), channel_id=1, source_target_pairs={{0,8},{8,0},{1,9},{9,1},{2,10},{10,2},{3,11},{11,3},{4,12},{12,4},... | collective-permute-start | bytes 884744 | tf_op jit(solution)/shard_map/ppermute | solution.py:434
  89.3 0.8 copy-start
  90.2 5.6 %collective-permute-start.7 = (f32[4,24,128]{2,1,0:T(8,128)S(1)}, f32[4,24,128]{2,1,0:T(8,128)S(1)}, u32[]{:S(2)}, u32[]{:S(2)}) collective-permute-start(f32[4,24,128]{2,1,0:T(8,128)S(1)} %get-tuple-element.41), channel_id=1, source_target_pairs={{0,2},{2,4},{4,6},{6,22},{22,20},{20,18},{18,16},{16,32},{32,34},{... | collective-permute-start | bytes 147464 | tf_op jit(solution)/shard_map/ppermute | solution.py:437
  91.5 1.1 copy-start.1
